TPU v7x, 32 devices: a whole 2x2x4 slice. The times are simulated.
32 devices in a mesh: dp: 8 (over y, x, core), tensor: 4 (over z).
Axes of the slice: x: 2, y: 2, z: 4, core: 2. Of those that a mesh axis runs over, the one named last changes fastest.
Arguments:
- token_ids: int32 [2, 2048], P(None, 'dp'), may hold values from 0 to 50287
- labels: int32 [2, 2048], P(None, 'dp'), may hold values from 0 to 50287, as said below
- seq_lengths: int32 [2], replicated, may hold values from 1024 to 2048, as said below
- micro_batch: int32 [2], replicated, may hold values from 0 to 1, as said below
- step_count: int32 [1], replicated, may hold values from 1 to 20
- block_slot: int32 [4, 192], P('tensor'), may hold values from 0 to 191, as said below
- vocab_table: float32 [25144, 2048], P('tensor', 'dp'), may hold values from -0.375 to 0.375
- vocab_first: float32 [25144, 2048], P('tensor', 'dp'), may hold values from -2.7621359e-06 to 2.7621359e-06
- vocab_second: float32 [25144, 2048], P('tensor', 'dp'), may hold values from 1.0251999e-12 to 4.1246416e-12
- layer_blocks: float32 [8, 4, 24, 128, 128], P('dp', 'tensor'), may hold values from -0.1875 to 0.1875
- block_bases: float32 [8, 4, 24, 2, 128, 128], P('dp', 'tensor'), may hold values from -0.5 to 0.5
- block_first: float32 [8, 4, 24, 128, 128], P('dp', 'tensor'), may hold values from -1.8887924e-06 to 1.8887924e-06
- block_second: float32 [8, 4, 24, 128, 128], P('dp', 'tensor'), may hold values from 4.7683716e-13 to 1.9073486e-12
- side_proj: float32 [2, 1024, 288], P(None, ('dp', 'tensor')), may hold values from -0.1875 to 0.1875
- side_first: float32 [2, 1024, 288], P(None, ('dp', 'tensor')), may hold values from -5.2083333e-06 to 5.2083333e-06
- side_second: float32 [2, 1024, 288], P(None, ('dp', 'tensor')), may hold values from 3.729926e-12 to 1.4580621e-11
- shared_params: float32 [5632], P(('dp', 'tensor')), may hold values from 0.1 to 1.9
- shared_first: float32 [5632], P(('dp', 'tensor')), may hold values from -5.330018e-05 to 5.330018e-05
- shared_second: float32 [5632], P(('dp', 'tensor')), may hold values from 3.90625e-10 to 1.5269886e-09
- channel_params: float32 [2, 6, 2048], P(None, None, 'tensor'), may hold values from 0.1 to 1.9
- channel_first: float32 [2, 6, 2048], P(None, None, 'tensor'), may hold values from -2.5515517e-05 to 2.5515517e-05
- channel_second: float32 [2, 6, 2048], P(None, None, 'tensor'), may hold values from 8.951823e-12 to 3.499349e-11
- head_params: float32 [2, 3, 32], P(None, None, 'tensor'), may hold values from -7 to 2.5, as said below
- head_first: float32 [2, 3, 32], P(None, None, 'tensor'), may hold values from -0.00019485572 to 0.00019485572
- head_second: float32 [2, 3, 32], P(None, None, 'tensor'), may hold values from 1.9791667e-10 to 7.8125e-10
Outputs:
- seq_loss: float32 [2], replicated
- clip_norm: float32 [], replicated
- table_next: float32 [25144, 2048], P('tensor', 'dp')
- table_first_next: float32 [25144, 2048], P('tensor', 'dp')
- table_second_next: float32 [25144, 2048], P('tensor', 'dp')
- blocks_next: float32 [8, 4, 24, 128, 128], P('dp', 'tensor')
- blocks_copy: bfloat16 [8, 4, 24, 128, 128], P('dp', 'tensor')
- block_first_next: float32 [8, 4, 24, 128, 128], P('dp', 'tensor')
- block_second_next: float32 [8, 4, 24, 128, 128], P('dp', 'tensor')
- side_next: float32 [2, 1024, 288], P(None, ('dp', 'tensor'))
- side_first_next: float32 [2, 1024, 288], P(None, ('dp', 'tensor'))
- side_second_next: float32 [2, 1024, 288], P(None, ('dp', 'tensor'))
- shared_step: float32 [5632], P(('dp', 'tensor'))
- shared_first_next: float32 [5632], P(('dp', 'tensor'))
- shared_second_next: float32 [5632], P(('dp', 'tensor'))
- channel_step: float32 [2, 6, 2048], P(None, None, 'tensor')
- channel_first_next: float32 [2, 6, 2048], P(None, None, 'tensor')
- channel_second_next: float32 [2, 6, 2048], P(None, None, 'tensor')
- head_step: float32 [2, 3, 32], P(None, None, 'tensor')
- head_first_next: float32 [2, 3, 32], P(None, None, 'tensor')
- head_second_next: float32 [2, 3, 32], P(None, None, 'tensor')
Inputs may be any that keep to these rules, and one draw needn't show every extreme that they name: Some labels equal the input token at the same position. `seq_lengths`: one sequence in every draw is exactly 2048 long. `micro_batch`: each micro-batch holds exactly 1 sequence. `block_slot`: each row is a permutation of 0 to 191. `head_params`: row 0 lies in -7 to -2, row 1 in -3 to 2.5, row 2 in 0.5 to 1.5.
All inputs are finite; a program needn't handle non-finite values.
Results may differ from a plain program's by a relative error of at most 0.015.
Values may be sent and summed in bfloat16 or wider, within the bound.
A program may use at most 384 MiB of HBM per device.

v0:
```python
import jax
import jax.numpy as jnp
from jax import lax
from jax.sharding import PartitionSpec as P

D = 1024
DI = 2048
H = 32
P_SIZE = 64
N = 128
V = 50288
SPAN = 256
L = 2
MB = 2
BLK = 128


HIGHEST = lax.Precision.HIGHEST
NORM_EPS = 1e-05
SMOOTHING = 0.1
ZLOSS_WEIGHT = 0.005
CLIP_LIMIT = 0.02
BETA_FIRST = 0.9
BETA_SECOND = 0.95
ADAM_EPS = 1e-08
LEARN_RATE = 0.03
WEIGHT_DECAY = 0.01


def shifted(x, axis, by):
    size = lax.axis_size(axis)
    pairs = [(i, i + by) for i in range(size) if 0 <= i + by < size]
    return lax.ppermute(x, axis, pairs)


def prefix(x, axis, combine, identity):
    size, place = (lax.axis_size(axis), lax.axis_index(axis))
    everything = jax.tree.map(
        lambda part, kind: lax.all_gather(part.astype(kind), axis), x, (jnp.bfloat16, jnp.bfloat16)
    )
    start = jax.tree.map(
        lambda part, zero: jnp.broadcast_to(jnp.asarray(zero, part.dtype), part.shape), x, identity
    )

    def prefix_turn(k, before):
        reached = k < place
        new = combine(
            before, jax.tree.map(lambda part, own: part[k].astype(own.dtype), everything, x)
        )
        return jax.tree.map(lambda a, b: jnp.where(reached, a, b), new, before)

    return lax.fori_loop(0, size, prefix_turn, start)


def entering(x, axis, combine, identity):
    size, place = (lax.axis_size(axis), lax.axis_index(axis))
    everything = jax.tree.map(
        lambda part, kind: lax.all_gather(part.astype(kind), axis),
        x,
        jax.tree.map(lambda a: jnp.bfloat16 if a.dtype == jnp.float32 else a.dtype, x),
    )
    start = jax.tree.map(
        lambda part, zero: jnp.broadcast_to(jnp.asarray(zero, part.dtype), part.shape), x, identity
    )

    def entering_turn(k, before):
        at = size - 1 - k
        reached = at > place
        new = combine(
            before, jax.tree.map(lambda part, own: part[at].astype(own.dtype), everything, x)
        )
        return jax.tree.map(lambda a, b: jnp.where(reached, a, b), new, before)

    return lax.fori_loop(0, size, entering_turn, start)


def combined_all(part, axis, combine):
    gathered = jax.tree.map(lambda a: lax.all_gather(a, axis), part)

    def take(source):
        return jax.tree.map(lambda a: lax.dynamic_index_in_dim(a, source, 0, False), gathered)

    return lax.fori_loop(
        1, lax.axis_size(axis), lambda source, state: combine(state, take(source)), take(0)
    )


def rms_scale(values):
    return lax.rsqrt(jnp.mean(values * values, axis=-1, keepdims=True) + NORM_EPS)


def span_step(carry_state, pieces):
    inputs, keys_b, queries_c, step_sizes, decay_rates = pieces
    cumulative = jnp.cumsum(decay_rates, axis=0)
    spread = cumulative[:, None, :] - cumulative[None, :, :]
    positions = jnp.arange(cumulative.shape[0])
    lower_mask = (positions[:, None] >= positions[None, :])[:, :, None]
    decay_weights = jnp.where(lower_mask, jnp.exp(jnp.where(lower_mask, spread, 0.0)), 0.0)
    scores = jnp.dot(queries_c, keys_b.T, precision=HIGHEST)
    scaled = inputs * step_sizes[:, :, None]
    mixing = scores[:, :, None] * decay_weights
    within = jnp.einsum("qrh,rhp->qhp", mixing, scaled, precision=HIGHEST)
    carried = jnp.exp(cumulative)[:, :, None] * jnp.einsum(
        "qn,hpn->qhp", queries_c, carry_state, precision=HIGHEST
    )
    tail_decay = jnp.exp(cumulative[-1][None, :] - cumulative)
    fresh_state = jnp.einsum(
        "rhp,rn->hpn", scaled * tail_decay[:, :, None], keys_b, precision=HIGHEST
    )
    new_state = jnp.exp(cumulative[-1])[:, None, None] * carry_state + fresh_state
    return (new_state, within + carried)


def state_step(carry_in, pieces):
    total_decay, carry_state = carry_in
    inputs, keys_b, step_sizes, decay_rates = pieces
    cumulative = jnp.cumsum(decay_rates, axis=0)
    tail_decay = jnp.exp(cumulative[-1][None, :] - cumulative)
    weighted = inputs * (step_sizes * tail_decay)[:, :, None]
    fresh_state = jnp.einsum("rhp,rn->hpn", weighted, keys_b, precision=HIGHEST)
    span_decay = jnp.exp(cumulative[-1])
    return ((total_decay * span_decay, span_decay[:, None, None] * carry_state + fresh_state), None)


def link_states(earlier, later):
    return (earlier[0] * later[0], later[1] + later[0][..., None, None] * earlier[1])


def split_spans(array_in):
    seqs_here = array_in.shape[0]
    row_count = array_in.shape[1]
    return array_in.reshape((seqs_here, row_count // SPAN, SPAN) + array_in.shape[2:]).swapaxes(
        0, 1
    )


def prepare(raw_rows, rim_rows, dt_raw, channel_row, bc_taps, bc_offset, head_row):
    seqs_here = raw_rows.shape[0]
    row_count = raw_rows.shape[1]
    inner_here = channel_row.shape[1]
    heads_here = head_row.shape[1]
    padded = jnp.concatenate([rim_rows, raw_rows], axis=1)
    conv_taps = jnp.concatenate([channel_row[0:4], bc_taps], axis=1)
    offset = jnp.concatenate([channel_row[4], bc_offset])
    summed = offset[None, None, :] + conv_taps[0][None, None, :] * padded[:, 0:row_count]
    for tap_index in range(1, 4):
        summed = (
            summed
            + conv_taps[tap_index][None, None, :] * padded[:, tap_index : tap_index + row_count]
        )
    conv_out = jax.nn.silu(summed)
    inputs = conv_out[:, :, :inner_here].reshape(seqs_here, row_count, heads_here, P_SIZE)
    keys_b = conv_out[:, :, inner_here : inner_here + N]
    queries_c = conv_out[:, :, inner_here + N :]
    step_sizes = jax.nn.softplus(dt_raw + head_row[0][None, None, :])
    decay_rates = -step_sizes * jnp.exp(head_row[1])[None, None, :]
    return (inputs, keys_b, queries_c, step_sizes, decay_rates)


def local_totals(inputs, keys_b, step_sizes, decay_rates):
    seqs_here = inputs.shape[0]
    heads_here = inputs.shape[2]
    start_pair = (
        jnp.ones((seqs_here, heads_here), jnp.float32),
        jnp.zeros((seqs_here, heads_here, P_SIZE, N), jnp.float32),
    )
    result_pair, unused = lax.scan(
        jax.vmap(state_step),
        start_pair,
        (
            split_spans(inputs),
            split_spans(keys_b),
            split_spans(step_sizes),
            split_spans(decay_rates),
        ),
    )
    return result_pair


def local_outputs(inputs, keys_b, queries_c, step_sizes, decay_rates, incoming, skip_row, gate_z):
    final_state, outputs = lax.scan(
        jax.vmap(span_step),
        incoming,
        (
            split_spans(inputs),
            split_spans(keys_b),
            split_spans(queries_c),
            split_spans(step_sizes),
            split_spans(decay_rates),
        ),
    )
    outputs = outputs.swapaxes(0, 1).reshape(inputs.shape)
    mixed_out = outputs + skip_row[None, None, :, None] * inputs
    return mixed_out.reshape(gate_z.shape) * jax.nn.silu(gate_z)


def merge_stats(first_set, second_set):
    top_value = jnp.maximum(first_set[0], second_set[0])
    exp_total = first_set[1] * jnp.exp(first_set[0] - top_value) + second_set[1] * jnp.exp(
        second_set[0] - top_value
    )
    return (top_value, exp_total, first_set[2] + second_set[2], first_set[3] + second_set[3])


def to_blocks(matrix):
    row_count = matrix.shape[0]
    col_count = matrix.shape[1]
    return (
        matrix.reshape(row_count // BLK, BLK, col_count // BLK, BLK)
        .transpose(0, 2, 1, 3)
        .reshape(-1, BLK, BLK)
    )


def adam_update(weight_in, gradient, moment_one, moment_two, factor, fix_one, fix_two, decay_rate):
    gradient = gradient * factor
    one_next = BETA_FIRST * moment_one + (1.0 - BETA_FIRST) * gradient
    two_next = BETA_SECOND * moment_two + (1.0 - BETA_SECOND) * gradient * gradient
    direction = one_next / fix_one / (jnp.sqrt(two_next / fix_two) + ADAM_EPS)
    return (weight_in - LEARN_RATE * (direction + decay_rate * weight_in), one_next, two_next)


def soap_update(weight_in, gradient, bases, moment_one, moment_two, factor, fix_one, fix_two):
    gradient = gradient * factor
    left_basis = bases[..., 0, :, :]
    right_basis = bases[..., 1, :, :]
    half_turn = jnp.einsum("...ab,...ac->...bc", left_basis, gradient, precision=HIGHEST)
    rotated = jnp.einsum("...bc,...cd->...bd", half_turn, right_basis, precision=HIGHEST)
    one_next = BETA_FIRST * moment_one + (1.0 - BETA_FIRST) * rotated
    two_next = BETA_SECOND * moment_two + (1.0 - BETA_SECOND) * rotated * rotated
    direction = one_next / fix_one / (jnp.sqrt(two_next / fix_two) + ADAM_EPS)
    back_half = jnp.einsum("...ab,...bc->...ac", left_basis, direction, precision=HIGHEST)
    turned = jnp.einsum("...ac,...dc->...ad", back_half, right_basis, precision=HIGHEST)
    weight_next = weight_in - LEARN_RATE * (turned + WEIGHT_DECAY * weight_in)
    return (weight_next, weight_next.astype(jnp.bfloat16), one_next, two_next)


def shards(
    token_ids,
    labels,
    seq_lengths,
    micro_batch,
    step_count,
    block_slot,
    vocab_table,
    vocab_first,
    vocab_second,
    layer_blocks,
    block_bases,
    block_first,
    block_second,
    side_proj,
    side_first,
    side_second,
    shared_params,
    shared_first,
    shared_second,
    channel_params,
    channel_first,
    channel_second,
    head_params,
    head_first,
    head_second,
):
    tensor_size = lax.axis_size("tensor")
    tensor_index = lax.axis_index("tensor")
    data_index = lax.axis_index("dp")
    seqs_here = token_ids.shape[0]
    slots_here = token_ids.shape[1]
    total_rows = seqs_here * slots_here
    own_rows = total_rows // tensor_size
    vocab_here = vocab_table.shape[0] * 2
    inner_here = channel_params.shape[2]
    heads_here = head_params.shape[2]
    block_count = block_slot.shape[1]
    zx_count = D * 2 * inner_here // (BLK * BLK)
    per_layer = 3 * D * inner_here // (BLK * BLK)
    shared_stride = D + 10 * N
    slot_weights, table_pairs = (
        lax.all_gather(layer_blocks.astype(jnp.bfloat16), "dp", axis=0, tiled=True),
        lax.all_gather(vocab_table.astype(jnp.bfloat16), "dp", axis=1, tiled=True),
    )
    table_used = table_pairs.reshape(vocab_here, D)
    ordered = slot_weights.reshape(block_count, BLK, BLK)[block_slot[0]]
    side_used, shared_used = (
        lax.all_gather(side_proj.astype(jnp.bfloat16), ("dp", "tensor"), axis=1, tiled=True),
        lax.all_gather(shared_params.astype(jnp.bfloat16), ("dp", "tensor"), axis=0, tiled=True),
    )
    shared_full = shared_used.astype(jnp.float32)

    def layer_mats(layer_index):
        base_index = layer_index * per_layer
        zx_part = (
            ordered[base_index : base_index + zx_count]
            .reshape(D // BLK, 2 * inner_here // BLK, BLK, BLK)
            .transpose(0, 2, 1, 3)
            .reshape(D, 2 * inner_here)
        )
        out_part = (
            ordered[base_index + zx_count : base_index + per_layer]
            .reshape(inner_here // BLK, D // BLK, BLK, BLK)
            .transpose(0, 2, 1, 3)
            .reshape(inner_here, D)
        )
        return (zx_part, out_part)

    def layer_shared(layer_index):
        base_index = layer_index * shared_stride
        return (
            shared_full[base_index : base_index + D],
            shared_full[base_index + D : base_index + D + 8 * N].reshape(4, 2 * N),
            shared_full[base_index + D + 8 * N : base_index + shared_stride],
        )

    def spread_rows(rows_in):
        return lax.all_gather(rows_in, "tensor", axis=0, tiled=True)

    def reduce_rows(rows_in):
        return lax.psum_scatter(rows_in, "tensor", scatter_dimension=0, tiled=True)

    def tensor_total(values):
        return lax.psum(values, "tensor")

    member = micro_batch[:, None] == jnp.arange(MB, dtype=jnp.int32)[None, :]
    batch_tokens = jnp.sum(jnp.where(member, seq_lengths[:, None], 0), axis=0).astype(jnp.float32)
    seq_weight = 1.0 / (MB * jnp.sum(jnp.where(member, batch_tokens[None, :], 0.0), axis=1))
    positions = data_index * slots_here + jnp.arange(slots_here, dtype=jnp.int32)
    row_weight = (
        (positions[None, :] < seq_lengths[:, None]).astype(jnp.float32) * seq_weight[:, None]
    ).reshape(total_rows)
    flat_ids = token_ids.reshape(total_rows) - tensor_index * vocab_here
    in_vocab = (flat_ids >= 0) & (flat_ids < vocab_here)
    looked = jnp.where(
        in_vocab[:, None], table_used[jnp.where(in_vocab, flat_ids, 0)].astype(jnp.float32), 0.0
    )
    residual = reduce_rows(looked)
    saved_layers = []
    for layer_index in range(L):
        zx_part, out_part = layer_mats(layer_index)
        front_gain_in, front_bc_taps, front_bc_offset = layer_shared(layer_index)
        front_normed = spread_rows(
            (residual * rms_scale(residual) * front_gain_in[None, :]).astype(jnp.bfloat16)
        )
        front_gate_in = jnp.dot(front_normed, zx_part, preferred_element_type=jnp.float32)
        front_side_out = jnp.dot(
            front_normed, side_used[layer_index], preferred_element_type=jnp.float32
        )
        front_raw_rows = jnp.concatenate(
            [front_gate_in[:, inner_here:], front_side_out[:, : 2 * N]], axis=1
        ).reshape(seqs_here, slots_here, inner_here + 2 * N)
        front_rim_rows = shifted(front_raw_rows[:, slots_here - 3 :], "dp", 1)
        front_dt_raw = lax.dynamic_slice_in_dim(
            front_side_out, 2 * N + tensor_index * heads_here, heads_here, 1
        ).reshape(seqs_here, slots_here, heads_here)
        front_prepared = prepare(
            front_raw_rows,
            front_rim_rows,
            front_dt_raw,
            channel_params[layer_index],
            front_bc_taps,
            front_bc_offset,
            head_params[layer_index],
        )
        totals = local_totals(
            front_prepared[0], front_prepared[1], front_prepared[3], front_prepared[4]
        )
        ones_part = jnp.ones((seqs_here, heads_here), jnp.float32)
        zeros_part = jnp.zeros((seqs_here, heads_here, P_SIZE, N), jnp.float32)
        incoming = prefix((totals[0], totals[1]), "dp", link_states, (ones_part, zeros_part))
        front_gated_out = local_outputs(
            front_prepared[0],
            front_prepared[1],
            front_prepared[2],
            front_prepared[3],
            front_prepared[4],
            incoming[1],
            head_params[layer_index, 2],
            front_gate_in[:, :inner_here],
        )
        front_norm_factor = lax.rsqrt(
            tensor_total(jnp.sum(front_gated_out * front_gated_out, axis=1)) / DI + NORM_EPS
        )
        front_scaled_out = (
            front_gated_out * front_norm_factor[:, None] * channel_params[layer_index, 5][None, :]
        ).astype(jnp.bfloat16)
        kept_items = (
            residual,
            front_normed,
            front_gate_in,
            front_side_out,
            front_raw_rows,
            front_rim_rows,
            front_dt_raw,
            totals[0],
            incoming[1],
            front_gated_out,
            front_norm_factor,
            front_scaled_out,
        )
        residual = residual + reduce_rows(
            jnp.dot(kept_items[11], out_part, preferred_element_type=jnp.float32)
        )
        saved_layers.append(kept_items)
    final_gain = shared_full[L * shared_stride :]
    final_scale = rms_scale(residual)
    final_rows = spread_rows((residual * final_scale * final_gain[None, :]).astype(jnp.bfloat16))
    row_block = 512
    block_total = total_rows // row_block
    flat_labels = labels.reshape(total_rows) - tensor_index * vocab_here
    vocab_iota = jnp.arange(vocab_here, dtype=jnp.int32)
    blocked_rows = final_rows.reshape(block_total, row_block, D)
    blocked_labels = flat_labels.reshape(block_total, row_block)

    def block_stats(pieces):
        rows_in, label_rows = pieces
        logits = jnp.einsum("md,vd->mv", rows_in, table_used, preferred_element_type=jnp.float32)
        top_value = jnp.max(logits, axis=1)
        exp_total = jnp.sum(jnp.exp(logits - top_value[:, None]), axis=1)
        target_logit = jnp.sum(
            jnp.where(vocab_iota[None, :] == label_rows[:, None], logits, 0.0), axis=1
        )
        logit_total = jnp.sum(logits, axis=1)
        return (top_value, exp_total, target_logit, logit_total)

    vocab_stats = lax.map(block_stats, (blocked_rows, blocked_labels))
    merged = combined_all(
        (
            vocab_stats[0].reshape(total_rows),
            vocab_stats[1].reshape(total_rows),
            vocab_stats[2].reshape(total_rows),
            vocab_stats[3].reshape(total_rows),
        ),
        "tensor",
        merge_stats,
    )
    log_total = merged[0] + jnp.log(merged[1])
    token_loss = (
        log_total
        - (1.0 - SMOOTHING) * merged[2]
        - SMOOTHING / V * merged[3]
        + ZLOSS_WEIGHT * log_total * log_total
    )
    row_index = jnp.arange(total_rows, dtype=jnp.int32)
    mine = (row_index >= tensor_index * own_rows) & (row_index < (tensor_index + 1) * own_rows)
    seq_part = jnp.sum(
        jnp.where(mine, row_weight * token_loss, 0.0).reshape(seqs_here, slots_here), axis=1
    )
    soft_weight = row_weight * (1.0 + 2.0 * ZLOSS_WEIGHT * log_total)

    def block_back(table_grad, pieces):
        rows_in, label_rows, soft_rows, weight_rows, total_logs = pieces
        logits = jnp.einsum("md,vd->mv", rows_in, table_used, preferred_element_type=jnp.float32)
        label_hits = (vocab_iota[None, :] == label_rows[:, None]).astype(jnp.float32)
        grad_logits = (
            soft_rows[:, None] * jnp.exp(logits - total_logs[:, None])
            - weight_rows[:, None] * ((1.0 - SMOOTHING) * label_hits + SMOOTHING / V)
        ).astype(jnp.bfloat16)
        grad_rows = jnp.dot(grad_logits, table_used, preferred_element_type=jnp.float32)
        return (
            table_grad
            + jnp.einsum("mv,md->vd", grad_logits, rows_in, preferred_element_type=jnp.float32),
            grad_rows,
        )

    table_grad, grad_final = lax.scan(
        block_back,
        jnp.zeros((vocab_here, D), jnp.float32),
        (
            blocked_rows,
            blocked_labels,
            soft_weight.reshape(block_total, row_block),
            row_weight.reshape(block_total, row_block),
            log_total.reshape(block_total, row_block),
        ),
    )
    grad_final = reduce_rows(grad_final.reshape(total_rows, D))
    grad_final_gain = jnp.sum(grad_final * residual * final_scale, axis=0)
    scaled_grad = grad_final * final_gain[None, :]
    grad_res = final_scale * scaled_grad - residual * (
        final_scale * final_scale * final_scale
    ) * jnp.mean(scaled_grad * residual, axis=1, keepdims=True)
    layer_results = [None] * L
    for layer_index in reversed(range(L)):
        zx_part, out_part = layer_mats(layer_index)
        kept_items = saved_layers[layer_index]
        (
            residual_in,
            normed,
            gate_in,
            side_out,
            raw_rows,
            rim_rows,
            dt_raw,
            span_decay,
            incoming_state,
            gated_out,
            norm_factor,
            scaled_out,
        ) = kept_items
        gain_in, bc_taps, bc_offset = layer_shared(layer_index)
        norm_gain = channel_params[layer_index, 5]
        grad_branch = spread_rows(grad_res.astype(jnp.bfloat16))
        grad_out_w = jnp.einsum(
            "mc,md->cd", scaled_out, grad_branch, preferred_element_type=jnp.float32
        )
        grad_scaled = jnp.einsum(
            "md,cd->mc", grad_branch, out_part, preferred_element_type=jnp.float32
        )
        grad_norm_gain = jnp.sum(grad_scaled * gated_out * norm_factor[:, None], axis=0)
        grad_normed_in = grad_scaled * norm_gain[None, :]
        inner_rows = tensor_total(jnp.sum(grad_normed_in * gated_out, axis=1))
        cube_factor = norm_factor * norm_factor * norm_factor
        grad_gated = (
            norm_factor[:, None] * grad_normed_in
            - gated_out * (cube_factor * inner_rows / DI)[:, None]
        )
        prepared, prepare_back = jax.vjp(
            prepare,
            raw_rows,
            rim_rows,
            dt_raw,
            channel_params[layer_index],
            bc_taps,
            bc_offset,
            head_params[layer_index],
        )
        unused_out, outputs_back = jax.vjp(
            local_outputs,
            prepared[0],
            prepared[1],
            prepared[2],
            prepared[3],
            prepared[4],
            incoming_state,
            head_params[layer_index, 2],
            gate_in[:, :inner_here],
        )
        output_grads = outputs_back(grad_gated)
        back_state = entering(
            (span_decay, output_grads[5]),
            "dp",
            link_states,
            (jnp.ones_like(span_decay), jnp.zeros_like(incoming_state)),
        )
        grad_state = back_state[1]
        grad_decay = jnp.sum(grad_state * incoming_state, axis=(2, 3))
        unused_totals, totals_back = jax.vjp(
            local_totals, prepared[0], prepared[1], prepared[3], prepared[4]
        )
        total_grads = totals_back((grad_decay, grad_state))
        prepared_grads = prepare_back(
            (
                output_grads[0] + total_grads[0],
                output_grads[1] + total_grads[1],
                output_grads[2],
                output_grads[3] + total_grads[2],
                output_grads[4] + total_grads[3],
            )
        )
        from_next = shifted(prepared_grads[1], "dp", -1)
        grad_raw = (
            prepared_grads[0]
            .at[:, slots_here - 3 :]
            .add(from_next)
            .reshape(total_rows, inner_here + 2 * N)
        )
        grad_gate = jnp.concatenate([output_grads[7], grad_raw[:, :inner_here]], axis=1).astype(
            jnp.bfloat16
        )
        grad_dt = lax.dynamic_update_slice(
            jnp.zeros((total_rows, H), jnp.float32),
            prepared_grads[2].reshape(total_rows, heads_here),
            (jnp.zeros((), jnp.int32), tensor_index * heads_here),
        )
        grad_side = jnp.concatenate([grad_raw[:, inner_here:], grad_dt], axis=1)
        side_full = side_used[layer_index].astype(jnp.float32)
        grad_normed = jnp.einsum(
            "mc,dc->md", grad_gate, zx_part, preferred_element_type=jnp.float32
        ) + jnp.einsum("mc,dc->md", grad_side, side_full, precision=HIGHEST)
        grad_zx_w = jnp.einsum("md,mc->dc", normed, grad_gate, preferred_element_type=jnp.float32)
        grad_side_w = jnp.einsum(
            "md,mc->dc", normed.astype(jnp.float32), grad_side, precision=HIGHEST
        )
        grad_local = reduce_rows(grad_normed)
        inv_scale = rms_scale(residual_in)
        grad_gain_in = jnp.sum(grad_local * residual_in * inv_scale, axis=0)
        grad_scaled_in = grad_local * gain_in[None, :]
        grad_res_new = (
            grad_res
            + inv_scale * grad_scaled_in
            - residual_in
            * (inv_scale * inv_scale * inv_scale)
            * jnp.mean(grad_scaled_in * residual_in, axis=1, keepdims=True)
        )
        channel_grad = prepared_grads[3].at[5].add(grad_norm_gain)
        head_grad = prepared_grads[6].at[2].add(output_grads[6])
        shared_part = jnp.concatenate(
            [grad_gain_in, prepared_grads[4].reshape(8 * N), prepared_grads[5]]
        )
        results = (
            grad_res_new,
            grad_zx_w,
            grad_out_w,
            grad_side_w,
            channel_grad,
            head_grad,
            shared_part,
        )
        grad_res = results[0]
        layer_results[layer_index] = results
    grad_embed = spread_rows(grad_res.astype(jnp.bfloat16))
    table_grad = (
        table_grad
        + jax.ops.segment_sum(
            grad_embed.astype(jnp.float32),
            jnp.where(in_vocab, flat_ids, vocab_here),
            num_segments=vocab_here + 1,
        )[:vocab_here]
    )
    block_pieces = []
    side_pieces = []
    channel_pieces = []
    head_pieces = []
    shared_pieces = []
    for layer_index in range(L):
        results = layer_results[layer_index]
        block_pieces.append(to_blocks(results[1]))
        block_pieces.append(to_blocks(results[2]))
        side_pieces.append(results[3])
        channel_pieces.append(results[4])
        head_pieces.append(results[5])
        shared_pieces.append(results[6])
    shared_pieces.append(grad_final_gain)
    ordered_grads = jnp.concatenate(block_pieces, axis=0)
    slot_grads = jnp.zeros_like(ordered_grads).at[block_slot[0]].set(ordered_grads)
    table_grad_pairs = table_grad.reshape(vocab_here // 2, 2 * D)
    block_grads, table_share = (
        lax.psum_scatter(
            slot_grads.astype(jnp.bfloat16), "dp", scatter_dimension=0, tiled=True
        ).astype(jnp.float32),
        lax.psum_scatter(
            table_grad_pairs.astype(jnp.bfloat16), "dp", scatter_dimension=1, tiled=True
        ).astype(jnp.float32),
    )
    side_share, shared_share = (
        lax.psum_scatter(jnp.stack(side_pieces), ("dp", "tensor"), scatter_dimension=1, tiled=True),
        lax.psum_scatter(
            jnp.concatenate(shared_pieces), ("dp", "tensor"), scatter_dimension=0, tiled=True
        ),
    )
    channel_sum, head_sum = lax.psum((jnp.stack(channel_pieces), jnp.stack(head_pieces)), "dp")
    first_copy = (data_index == 0).astype(jnp.float32)
    square_part = (
        jnp.sum(block_grads * block_grads)
        + jnp.sum(table_share * table_share)
        + jnp.sum(side_share * side_share)
        + jnp.sum(shared_share * shared_share)
        + first_copy * (jnp.sum(channel_sum * channel_sum) + jnp.sum(head_sum * head_sum))
    )
    seq_loss, square_sum = lax.psum((seq_part, square_part), ("dp", "tensor"))
    clip_norm = jnp.sqrt(square_sum)
    factor = jnp.minimum(1.0, CLIP_LIMIT / (clip_norm + 1e-06))
    steps_done = step_count[0].astype(jnp.float32)
    fix_one = 1.0 - jnp.power(BETA_FIRST, steps_done)
    fix_two = 1.0 - jnp.power(BETA_SECOND, steps_done)
    table_out = adam_update(
        vocab_table, table_share, vocab_first, vocab_second, factor, fix_one, fix_two, WEIGHT_DECAY
    )
    block_out = soap_update(
        layer_blocks,
        block_grads.reshape(layer_blocks.shape),
        block_bases,
        block_first,
        block_second,
        factor,
        fix_one,
        fix_two,
    )
    side_next = adam_update(
        side_proj, side_share, side_first, side_second, factor, fix_one, fix_two, WEIGHT_DECAY
    )
    shared_next = adam_update(
        shared_params, shared_share, shared_first, shared_second, factor, fix_one, fix_two, 0.0
    )
    channel_next = adam_update(
        channel_params, channel_sum, channel_first, channel_second, factor, fix_one, fix_two, 0.0
    )
    head_next = adam_update(
        head_params, head_sum, head_first, head_second, factor, fix_one, fix_two, 0.0
    )
    shared_step = shared_next[0] - shared_params
    channel_step = channel_next[0] - channel_params
    head_step = head_next[0] - head_params
    return (
        seq_loss,
        clip_norm,
        table_out[0],
        table_out[1],
        table_out[2],
        block_out[0],
        block_out[1],
        block_out[2],
        block_out[3],
        side_next[0],
        side_next[1],
        side_next[2],
        shared_step,
        shared_next[1],
        shared_next[2],
        channel_step,
        channel_next[1],
        channel_next[2],
        head_step,
        head_next[1],
        head_next[2],
    )


def solution(mesh):
    in_specs = (
        P(None, "dp"),
        P(None, "dp"),
        P(),
        P(),
        P(),
        P("tensor", None),
        P("tensor", "dp"),
        P("tensor", "dp"),
        P("tensor", "dp"),
        P("dp", "tensor", None, None, None),
        P("dp", "tensor", None, None, None, None),
        P("dp", "tensor", None, None, None),
        P("dp", "tensor", None, None, None),
        P(None, ("dp", "tensor"), None),
        P(None, ("dp", "tensor"), None),
        P(None, ("dp", "tensor"), None),
        P(("dp", "tensor")),
        P(("dp", "tensor")),
        P(("dp", "tensor")),
        P(None, None, "tensor"),
        P(None, None, "tensor"),
        P(None, None, "tensor"),
        P(None, None, "tensor"),
        P(None, None, "tensor"),
        P(None, None, "tensor"),
    )
    out_specs = (
        P(),
        P(),
        P("tensor", "dp"),
        P("tensor", "dp"),
        P("tensor", "dp"),
        P("dp", "tensor", None, None, None),
        P("dp", "tensor", None, None, None),
        P("dp", "tensor", None, None, None),
        P("dp", "tensor", None, None, None),
        P(None, ("dp", "tensor"), None),
        P(None, ("dp", "tensor"), None),
        P(None, ("dp", "tensor"), None),
        P(("dp", "tensor")),
        P(("dp", "tensor")),
        P(("dp", "tensor")),
        P(None, None, "tensor"),
        P(None, None, "tensor"),
        P(None, None, "tensor"),
        P(None, None, "tensor"),
        P(None, None, "tensor"),
        P(None, None, "tensor"),
    )
    return jax.shard_map(shards, mesh=mesh, in_specs=in_specs, out_specs=out_specs, check_vma=False)
```

profile of v0, /device:TPU:0, one launch (start us, length us, event | category | flops | bytes accessed | tf_op | source)
XLA Modules:
  0.0 1775.7 jit_solution(14890505987251590288)
XLA Ops:
  13.4 134.5 %all-gather.28.cloned.1.call-done = bf16[6286,2048]{1,0:T(8,128)(2,1)} async-done(((bf16[6286,256]{1,0:T(8,128)(2,1)}), bf16[6286,2048]{1,0:T(8,128)(2,1)}) %all-gather.28.cloned.1.call-update) | async-done | bytes 25747472 | tf_op jit(solution)/shard_map/all_gather | solution.py:281
  147.8 37.3 %reshape.1462 = bf16[12572,1024]{1,0:T(8,128)(2,1)} reshape(bf16[6286,2048]{1,0:T(8,128)(2,1)} %all-gather.28.cloned.1.call-done) | data formatting | bytes 51494912 | tf_op jit(solution)/shard_map/reshape | solution.py:283
  204.6 42.4 %all-reduce.38 = bf16[5632]{0:T(1024)(128)(2,1)S(1)} all-reduce(bf16[5632]{0:T(1024)(128)(2,1)S(1)} %dynamic-update-slice.22), channel_id=1, replica_groups=mesh['dp'=8,'tensor'=4] {'dp','tensor'}, use_global_device_ids=true, to_apply=%add.38 | all-reduce | flops 5632 | bytes 22528
  252.8 40.7 %all-gather.32.cloned.1.call-done = bf16[8,1,24,128,128]{4,3,2,1,0:T(8,128)(2,1)} async-done(((bf16[1,1,24,128,128]{4,3,2,1,0:T(8,128)(2,1)}), bf16[8,1,24,128,128]{4,3,2,1,0:T(8,128)(2,1)}) %all-gather.32.cloned.1.call-update) | async-done | bytes 6291472 | tf_op jit(solution)/shard_map/all_gather | solution.py:280
  311.3 41.1 %all-gather.34.cloned.1.call-done = bf16[2,1024,288]{2,1,0:T(8,128)(2,1)} async-done(((bf16[2,32,288]{2,1,0:T(8,128)(2,1)}), bf16[2,1024,288]{2,1,0:T(8,128)(2,1)}) %all-gather.34.cloned.1.call-update) | async-done | bytes 1179664 | tf_op jit(solution)/shard_map/all_gather | solution.py:286
  352.4 28.9 %all-gather.30.cloned.1.call-done = bf16[512,1024]{1,0:T(8,128)(2,1)} async-done(((bf16[128,1024]{1,0:T(8,128)(2,1)}), bf16[512,1024]{1,0:T(8,128)(2,1)}) %all-gather.30.cloned.1.call-update) | async-done | bytes 1048592 | tf_op jit(solution)/shard_map/all_gather | solution.py:316
  470.9 41.2 %reduce-scatter.11.cloned.1.call-done = f32[128,1024]{1,0:T(8,128)} async-done(((f32[512,1024]{1,0:T(8,128)}), f32[128,1024]{1,0:T(8,128)}) %reduce-scatter.11.cloned.1.call-update) | async-done | bytes 524304 | tf_op jit(solution)/shard_map/reduce_scatter | solution.py:319
  645.2 41.2 %reduce-scatter.13.cloned.1.call-done = f32[128,1024]{1,0:T(8,128)} async-done(((f32[512,1024]{1,0:T(8,128)}), f32[128,1024]{1,0:T(8,128)}) %reduce-scatter.13.cloned.1.call-update) | async-done | bytes 524304 | tf_op jit(solution)/shard_map/reduce_scatter | solution.py:319
  692.5 24.1 %all-gather.38.cloned.1.call-done = bf16[512,1024]{1,0:T(8,128)(2,1)} async-done(((bf16[128,1024]{1,0:T(8,128)(2,1)}), bf16[512,1024]{1,0:T(8,128)(2,1)}) %all-gather.38.cloned.1.call-update) | async-done | bytes 1048592 | tf_op jit(solution)/shard_map/all_gather | solution.py:316
  716.7 23.4 %fusion.355 = (f32[512]{0:T(512)S(1)}, f32[512,12572]{0,1:T(8,128)}) fusion(bf16[512,1024]{1,0:T(8,128)(2,1)} %all-gather.38.cloned.1.call-done, bf16[12572,1024]{1,0:T(8,128)(2,1)} %reshape.1462), kind=kOutput, calls=%fused_computation.636 | convolution fusion | flops 13189134336 | bytes 52545536 | tf_op jit(solution)/shard_map/while/body/eval_jaxpr/md,vd->mv/dot_general | solution.py:416
  800.9 33.8 %fusion.328 = f32[512,1024]{1,0:T(8,128)} fusion(bf16[12572,1024]{1,0:T(8,128)(2,1)} %reshape.1462, f32[512,12572]{0,1:T(8,128)} %get-tuple-element.2238, f32[512]{0:T(512)S(1)} %bitcast.685, f32[512]{0:T(512)S(1)} %get-tuple-element.2141, f32[512]{0:T(512)S(1)} %get-tuple-element.2140, s32[512]{0:T(512)S(1)} %bitcast.701), kind=kOutput, calls=%fused_computation.625 | convolution fusion | flops 13234192384 | bytes 53600256 | tf_op jit(solution)/shard_map/while/body/eval_jaxpr/dot_general | solution.py:458
  834.7 42.5 %reduce-scatter.15.cloned.1.call-done = f32[128,1024]{1,0:T(8,128)} async-done(((f32[512,1024]{1,0:T(8,128)}), f32[128,1024]{1,0:T(8,128)}) %reduce-scatter.15.cloned.1.call-update) | async-done | bytes 524304 | tf_op jit(solution)/shard_map/reduce_scatter | solution.py:319
  881.6 27.4 %all-gather.40.cloned.1.call-done = bf16[512,1024]{1,0:T(8,128)(2,1)} async-done(((bf16[128,1024]{1,0:T(8,128)(2,1)}), bf16[512,1024]{1,0:T(8,128)(2,1)}) %all-gather.40.cloned.1.call-update) | async-done | bytes 1048592 | tf_op jit(solution)/shard_map/all_gather | solution.py:316
  1035.6 43.5 %reduce-scatter.17.cloned.1.call-done = f32[128,1024]{1,0:T(8,128)} async-done(((f32[512,1024]{1,0:T(8,128)}), f32[128,1024]{1,0:T(8,128)}) %reduce-scatter.17.cloned.1.call-update) | async-done | bytes 524304 | tf_op jit(solution)/shard_map/reduce_scatter | solution.py:319
  1083.6 27.3 %all-gather.42.cloned.1.call-done = bf16[512,1024]{1,0:T(8,128)(2,1)} async-done(((bf16[128,1024]{1,0:T(8,128)(2,1)}), bf16[512,1024]{1,0:T(8,128)(2,1)}) %all-gather.42.cloned.1.call-update) | async-done | bytes 1048592 | tf_op jit(solution)/shard_map/all_gather | solution.py:316
  1238.1 46.3 %reduce-scatter.21.cloned.1.call-done = f32[128,1024]{1,0:T(8,128)} async-done(((f32[512,1024]{1,0:T(8,128)}), f32[128,1024]{1,0:T(8,128)}) %reduce-scatter.21.cloned.1.call-update) | async-done | bytes 524304 | tf_op jit(solution)/shard_map/reduce_scatter | solution.py:319
  1321.4 35.5 %scatter_fusion = f32[192,128,128]{2,1,0:T(8,128)} fusion(f32[192,128,128]{2,1,0:T(8,128)} %broadcast_in_dim.608, s32[192]{0:T(256)S(1)} %bitcast.695, f32[192,128,128]{2,1,0:T(8,128)} %pad_maximum_fusion), kind=kCustom, calls=%fused_computation.2 | custom fusion | bytes 37749504 | tf_op jit(solution)/shard_map/scatter | solution.py:635
  1366.2 26.0 %scatter_custom_fusion.1 = f32[12573,1024]{1,0:T(8,128)} fusion(s32[512]{0:T(512)} %bitcast.715, f32[]{:T(128)} %constant.793.clone.1, bf16[512,1024]{1,0:T(8,128)(2,1)} %all-gather.44.cloned.1.call-done), kind=kCustom, calls=%fused_computation.23 | custom fusion | flops 1048576 | bytes 52548096 | tf_op jit(solution)/shard_map/scatter-add | solution.py:614
  1392.4 37.7 %fusion.4 = bf16[12572,1024]{1,0:T(8,128)(2,1)} fusion(f32[12573,1024]{1,0:T(8,128)} %scatter_custom_fusion.1, bf16[512,1024]{1,0:T(8,128)(2,1)S(1)} %copy-done.240, f32[512,12572]{0,1:T(8,128)} %get-tuple-element.2238, f32[512]{0:T(512)S(1)} %bitcast.686, f32[512]{0:T(512)S(1)} %copy-done.203, f32[512]{0:T(512)S(1)} %copy-done.230, s32[512]{0:T(512)S(1)} %bitcast.702), kind=kOutput, calls=%fused_computation.22 | convolution fusion | flops 13259939840 | bytes 104046592 | tf_op jit(solution)/shard_map/while/body/eval_jaxpr/mv,md->vd/dot_general | solution.py:461
  1430.0 37.5 %convert_element_type.264 = bf16[6286,2048]{1,0:T(8,128)(2,1)} reshape(bf16[12572,1024]{1,0:T(8,128)(2,1)} %fusion.4) | data formatting | bytes 51494912 | tf_op jit(solution)/shard_map/convert_element_type | solution.py:642
  1469.9 24.2 %all-reduce.42 = (f32[2,6,512]{2,1,0:T(8,128)S(1)}, f32[2,3,8]{2,1,0:T(4,128)S(1)}) all-reduce(f32[2,6,512]{2,1,0:T(8,128)S(1)} %pad_maximum_fusion.18, f32[2,3,8]{2,1,0:T(4,128)S(1)} %pad_maximum_fusion.21), channel_id=1, replica_groups=mesh['dp'=8,'tensor'=4] {'dp'}, use_global_device_ids=true, to_apply=%region_103.105 | all-reduce | flops 6192 | bytes 49536 | tf_op jit(solution)/shard_map/psum | solution.py:651
  1498.3 39.3 %all-reduce.40 = f32[5632]{0:T(1024)S(1)} all-reduce(f32[5632]{0:T(1024)S(1)} %constant_dynamic-update-slice_fusion), channel_id=21, replica_groups=mesh['dp'=8,'tensor'=4] {'dp','tensor'}, use_global_device_ids=true, to_apply=%region_99.101.clone | all-reduce | flops 5632 | bytes 45056
  1540.5 147.7 %reduce-scatter.23.cloned.1.call-done = bf16[6286,256]{1,0:T(8,128)(2,1)} async-done(((bf16[6286,2048]{1,0:T(8,128)(2,1)}), bf16[6286,256]{1,0:T(8,128)(2,1)}) %reduce-scatter.23.cloned.1.call-update) | async-done | bytes 3218448 | tf_op jit(solution)/shard_map/reduce_scatter | solution.py:641
  1695.0 39.6 %all-reduce.41 = (f32[2]{0:T(128)}, f32[]{:T(128)}) all-reduce(f32[2]{0:T(128)S(1)} %reduce_sum.858, f32[]{:T(128)S(6)} %add.944), channel_id=1, replica_groups=mesh['dp'=8,'tensor'=4] {'dp','tensor'}, use_global_device_ids=true, to_apply=%region_27.28 | all-reduce | flops 3 | bytes 24 | tf_op jit(solution)/shard_map/psum | solution.py:660
  (1012 shorter events, 738.1 us)
Async XLA Ops:
  7.2 140.6 %all-gather.28.cloned.1.call-start = ((), (), s32[]{:S(2)}) async-start(), calls=%async_computation.8 | async-start | bytes 28975104 | tf_op jit(solution)/shard_map/all_gather | solution.py:281
  12.1 234.9 %reduce-scatter.9.cloned.1.call-start = ((), (), s32[]{:S(2)}) async-start(), calls=%async_computation.9 | async-start | bytes 2621440 | tf_op jit(solution)/shard_map/reduce_scatter | solution.py:319
  201.1 92.4 %all-gather.32.cloned.1.call-start = ((), (), s32[]{:S(2)}) async-start(), calls=%async_computation.11 | async-start | bytes 7077888 | tf_op jit(solution)/shard_map/all_gather | solution.py:280
  203.5 148.9 %all-gather.34.cloned.1.call-start = ((), (), s32[]{:S(2)}) async-start(), calls=%async_computation.12 | async-start | bytes 1622016 | tf_op jit(solution)/shard_map/all_gather | solution.py:286
  204.2 177.1 %all-gather.30.cloned.1.call-start = ((), (), s32[]{:S(2)}) async-start(), calls=%async_computation.10 | async-start | bytes 1310720 | tf_op jit(solution)/shard_map/all_gather | solution.py:316
  250.7 179.2 %all-gather.46.cloned.1.call-start = ((), (), s32[]{:S(2)}) async-start(), calls=%async_computation.25 | async-start | bytes 2359296 | tf_op jit(solution)/shard_map/all_gather | solution.py:39
  400.0 112.1 %reduce-scatter.11.cloned.1.call-start = ((), (), s32[]{:S(2)}) async-start(), calls=%async_computation.13 | async-start | bytes 2621440 | tf_op jit(solution)/shard_map/reduce_scatter | solution.py:319
  470.9 71.5 %all-gather.36.cloned.1.call-start = ((), (), s32[]{:S(2)}) async-start(), calls=%async_computation.14 | async-start | bytes 1310720 | tf_op jit(solution)/shard_map/all_gather | solution.py:316
  514.9 82.7 %all-gather.48.cloned.1.call-start = ((), (), s32[]{:S(2)}) async-start(), calls=%async_computation.26 | async-start | bytes 2359296 | tf_op jit(solution)/shard_map/all_gather | solution.py:39
  568.3 118.1 %reduce-scatter.13.cloned.1.call-start = ((), (), s32[]{:S(2)}) async-start(), calls=%async_computation.15 | async-start | bytes 2621440 | tf_op jit(solution)/shard_map/reduce_scatter | solution.py:319
  645.1 71.5 %all-gather.38.cloned.1.call-start = ((), (), s32[]{:S(2)}) async-start(), calls=%async_computation.16 | async-start | bytes 1310720 | tf_op jit(solution)/shard_map/all_gather | solution.py:316
  689.2 188.0 %reduce-scatter.15.cloned.1.call-start = ((), (), s32[]{:S(2)}) async-start(), calls=%async_computation.17 | async-start | bytes 2621440 | tf_op jit(solution)/shard_map/reduce_scatter | solution.py:319
  834.7 74.3 %all-gather.40.cloned.1.call-start = ((), (), s32[]{:S(2)}) async-start(), calls=%async_computation.18 | async-start | bytes 1310720 | tf_op jit(solution)/shard_map/all_gather | solution.py:316
  881.5 85.2 %all-gather.50.cloned.1.call-start = ((), (), s32[]{:S(2)}) async-start(), calls=%async_computation.27 | async-start | bytes 2359296 | tf_op jit(solution)/shard_map/all_gather | solution.py:58
  937.1 142.1 %reduce-scatter.17.cloned.1.call-start = ((), (), s32[]{:S(2)}) async-start(), calls=%async_computation.19 | async-start | bytes 2621440 | tf_op jit(solution)/shard_map/reduce_scatter | solution.py:319
  1003.9 21.5 %collective-permute-start.2 = (f32[2,3,768]{2,1,0:T(4,128)}, f32[2,3,768]{2,1,0:T(4,128)}, u32[]{:S(2)}, u32[]{:S(2)}) collective-permute-start(f32[2,3,768]{2,1,0:T(4,128)} %pad_add_fusion.5), channel_id=1, source_target_pairs={{4,0},{8,4},{12,8},{16,12},{20,16},{24,20},{28,24},{5,1},{9,5},{13... | collective-permute-start | bytes 55304 | tf_op jit(solution)/shard_map/ppermute | solution.py:33
  1035.6 75.3 %all-gather.42.cloned.1.call-start = ((), (), s32[]{:S(2)}) async-start(), calls=%async_computation.20 | async-start | bytes 1310720 | tf_op jit(solution)/shard_map/all_gather | solution.py:316
  1083.5 77.4 %all-gather.52.cloned.1.call-start = ((), (), s32[]{:S(2)}) async-start(), calls=%async_computation.28 | async-start | bytes 2359296 | tf_op jit(solution)/shard_map/all_gather | solution.py:58
  1134.7 149.6 %reduce-scatter.21.cloned.1.call-start = ((), (), s32[]{:S(2)}) async-start(), calls=%async_computation.22 | async-start | bytes 2621440 | tf_op jit(solution)/shard_map/reduce_scatter | solution.py:319
  1192.9 34.2 %collective-permute-start.3 = (f32[2,3,768]{2,1,0:T(4,128)}, f32[2,3,768]{2,1,0:T(4,128)S(1)}, u32[]{:S(2)}, u32[]{:S(2)}) collective-permute-start(f32[2,3,768]{2,1,0:T(4,128)} %pad_add_fusion.4), channel_id=1, source_target_pairs={{4,0},{8,4},{12,8},{16,12},{20,16},{24,20},{28,24},{5,1},{9,5},{13... | collective-permute-start | bytes 55304 | tf_op jit(solution)/shard_map/ppermute | solution.py:33
  1238.0 128.2 %all-gather.44.cloned.1.call-start = ((), (), s32[]{:S(2)}) async-start(), calls=%async_computation.23 | async-start | bytes 1310720 | tf_op jit(solution)/shard_map/all_gather | solution.py:316
  1287.6 209.1 %all-reduce.45.cloned.1.call-start = ((), (), s32[]{:S(2)}) async-start(), calls=%async_computation.29 | async-start | bytes 6291456
  1298.5 239.8 %reduce-scatter.19.cloned.1.call-start = ((), (), s32[]{:S(2)}) async-start(), calls=%async_computation.21 | async-start | bytes 7077888 | tf_op jit(solution)/shard_map/reduce_scatter | solution.py:638
  1365.9 322.3 %reduce-scatter.23.cloned.1.call-start = ((), (), s32[]{:S(2)}) async-start(), calls=%async_computation.24 | async-start | bytes 28975104 | tf_op jit(solution)/shard_map/reduce_scatter | solution.py:641
  (245 other events, 5421.7 us)
Sparse Core Ops, SparseCore 0:
  12.2 135.5 all-gather.27
  201.2 44.7 reduce-scatter.8
  248.7 44.8 all-gather.31
  297.3 55.0 all-gather.33
  354.5 26.8 all-gather.29
  400.1 29.6 all-gather.45
  471.0 41.0 reduce-scatter.10
  515.1 27.2 all-gather.35
  568.4 29.2 all-gather.47
  645.3 41.0 reduce-scatter.12
  689.4 27.2 all-gather.37
  834.8 42.3 reduce-scatter.14
  881.6 27.2 all-gather.39
  937.2 26.0 all-gather.49
  1035.7 43.3 reduce-scatter.16
  1083.6 27.2 all-gather.41
  1134.8 26.0 all-gather.51
  1238.1 46.1 reduce-scatter.20
  1287.7 27.2 all-gather.43
  1320.9 137.1 all-reduce.44
  1462.5 61.2 reduce-scatter.18
  1527.4 160.7 reduce-scatter.22
where the time goes:
time: 1790 us; the launch traced here: 1780 us
  waiting for transfers between devices  734 us (41%)
  local copies, waits for them, and re-layouts  265 us (15%)
  blocking collectives  261 us (15%)
  matrix products  243 us (14%)
  other arithmetic  239 us (13%)
  between operations  24.8 us (1%)
    reduce_scatter x6, waiting for transfers between devices, reduce_rows(): return lax.psum_scatter(rows_in, 'tensor', scatter_dimension=0, tiled=True)  215 us
    reduce_scatter x1, waiting for transfers between devices, shards(): lax.psum_scatter(table_grad_pairs.astype(jnp.bfloat16), 'dp', scatter_dim...  148 us
    all_gather x1, waiting for transfers between devices, shards(): lax.all_gather(vocab_table.astype(jnp.bfloat16), 'dp', axis=1, tiled=True)  134 us
    all_gather x6, waiting for transfers between devices, spread_rows(): return lax.all_gather(rows_in, 'tensor', axis=0, tiled=True)  131 us
    unnamed x2, blocking collectives  81.7 us
    all_gather x4, blocking collectives, combined_all(): gathered = jax.tree.map(lambda a: lax.all_gather(a, axis), part)  47.7 us
    psum x4, blocking collectives, tensor_total(): return lax.psum(values, 'tensor')  44.1 us
    all_gather x1, waiting for transfers between devices, shards(): lax.all_gather(side_proj.astype(jnp.bfloat16), ('dp', 'tensor'), axis=1,...  41.1 us
  transfers between devices with their start and end apart: 26, of which 17 were waited for; matrix products, arithmetic and copies ran while one was open for 19% of the time, Pallas kernels for 0%

commit v1 on v0

v1 whole, which is shorter than its diff:
```python
import functools

import jax
import jax.numpy as jnp
from jax import lax
from jax.experimental import pallas as pl
from jax.experimental.pallas import tpu as pltpu
from jax.sharding import PartitionSpec as P

D = 1024
DI = 2048
H = 32
P_SIZE = 64
N = 128
V = 50288
SPAN = 256
L = 2
MB = 2
BLK = 128
RIM = 16
PAIRS = 640
LANES = 128

HIGHEST = lax.Precision.HIGHEST
NORM_EPS = 1e-05
SMOOTHING = 0.1
ZLOSS_WEIGHT = 0.005
CLIP_LIMIT = 0.02
BETA_FIRST = 0.9
BETA_SECOND = 0.95
ADAM_EPS = 1e-08
LEARN_RATE = 0.03
WEIGHT_DECAY = 0.01

BF = jnp.bfloat16
F32 = jnp.float32
MIB = 1 << 20


def nn(a, b, precision=None):
    return lax.dot_general(
        a, b, (((1,), (0,)), ((), ())), precision=precision, preferred_element_type=F32
    )


def nt_dot(a, b, precision=None):
    return lax.dot_general(
        a, b, (((1,), (1,)), ((), ())), precision=precision, preferred_element_type=F32
    )


def tn(a, b, precision=None):
    return lax.dot_general(
        a, b, (((0,), (0,)), ((), ())), precision=precision, preferred_element_type=F32
    )


def iota(shape, dim):
    return lax.broadcasted_iota(jnp.int32, shape, dim)


def head_map(inner):
    return (iota((LANES, inner), 0) == iota((LANES, inner), 1) // P_SIZE).astype(F32)


def swap(x, axis, offset):
    size = lax.axis_size(axis)
    return lax.ppermute(x, axis, [(i, i ^ offset) for i in range(size)])


def sigmoid(x):
    return 1.0 / (1.0 + jnp.exp(-x))


def softplus(x):
    return jnp.maximum(x, 0.0) + jnp.log1p(jnp.exp(-jnp.abs(x)))


def call(kernel, name, out_shape, args, smem=(), scratch=(), mib=48, flops=0, moved=0, **extra):
    specs = [
        pl.BlockSpec(memory_space=pltpu.SMEM if i in smem else pltpu.VMEM)
        for i in range(len(args))
    ]
    return pl.pallas_call(
        kernel,
        out_shape=out_shape,
        in_specs=specs,
        out_specs=jax.tree.map(lambda _: pl.BlockSpec(memory_space=pltpu.VMEM), out_shape),
        scratch_shapes=list(scratch),
        compiler_params=pltpu.CompilerParams(vmem_limit_bytes=mib * MIB),
        cost_estimate=pl.CostEstimate(flops=flops, bytes_accessed=moved, transcendentals=0),
        name=name,
        **extra,
    )(*args)


def sds(shape, dtype):
    return jax.ShapeDtypeStruct(shape, dtype)


def look_kernel(groups, rows, scal, idx, mask_ref, table, *rest):
    outs, work = rest[:groups], rest[groups]
    place = scal[0]
    for off in range(groups):
        base = (place ^ off) * rows

        def turn(step, carry):
            for lane in range(8):
                at = step * 8 + lane
                work[pl.ds(at, 1), :] = table[pl.ds(idx[base + at], 1), :]
            return carry

        lax.fori_loop(0, rows // 8, turn, 0)
        keep = mask_ref[pl.ds(pl.multiple_of(base, rows), rows), :]
        outs[off][...] = jnp.where(keep > 0, work[...], 0.0).astype(BF)


def gather_rows(scal, idx, keep, table, groups, rows):
    cols = table.shape[1]
    return call(
        functools.partial(look_kernel, groups, rows),
        "look",
        [sds((rows, cols), BF)] * groups,
        (scal, idx, keep, table),
        smem=(0, 1),
        scratch=[pltpu.VMEM((rows, cols), F32)],
        moved=30 * MIB,
    )


def join_kernel(groups, shards, own, scal, *rest):
    parts, outs, work = rest[:groups], rest[groups : groups + shards], rest[-1]
    place, shard = scal[0], scal[1]
    half = groups // 2
    cols = parts[0].shape[1]
    for off in range(half):
        at = ((place ^ off) % half) * cols
        work[:, pl.ds(pl.multiple_of(at, cols), cols)] = parts[off][...] + parts[off + half][...]
    for off in range(shards):
        at = pl.multiple_of((shard ^ off) * own, own)
        outs[off][...] = work[pl.ds(at, own), :]


def join_parts(scal, parts, shards, own):
    rows = parts[0].shape[0]
    return call(
        functools.partial(join_kernel, len(parts), shards, own),
        "join",
        [sds((own, D), BF)] * shards,
        (scal, *parts),
        smem=(0,),
        scratch=[pltpu.VMEM((rows, D), BF)],
        moved=4 * MIB,
    )


def cut_kernel(groups, shards, own, scal, *rest):
    parts, outs, work = rest[:shards], rest[shards : shards + groups], rest[-1]
    place, shard = scal[0], scal[1]
    half = groups // 2
    cols = outs[0].shape[1]
    for off in range(shards):
        at = pl.multiple_of((shard ^ off) * own, own)
        work[pl.ds(at, own), :] = parts[off][...]
    for off in range(groups):
        at = ((place ^ off) % half) * cols
        outs[off][...] = work[:, pl.ds(pl.multiple_of(at, cols), cols)]


def cut_parts(scal, parts, groups):
    own = parts[0].shape[0]
    shards = len(parts)
    cols = 2 * D // groups
    return call(
        functools.partial(cut_kernel, groups, shards, own),
        "cut",
        [sds((own * shards, cols), BF)] * groups,
        (scal, *parts),
        smem=(0,),
        scratch=[pltpu.VMEM((own * shards, D), BF)],
        moved=4 * MIB,
    )


def add_kernel(groups, rows, vrows, scal, idx, share, *rest):
    parts, out, square, work, bins = (rest[:groups], rest[groups], rest[groups + 1], rest[-2], rest[-1])
    place = scal[0]
    bins[0:vrows, :] = share[0:vrows, :].astype(F32)
    for off in range(groups):
        base = (place ^ off) * rows
        work[...] = parts[off][...].astype(F32)

        def turn(step, carry):
            for lane in range(8):
                at = step * 8 + lane
                to = pl.ds(idx[base + at], 1)
                bins[to, :] = bins[to, :] + work[pl.ds(at, 1), :]
            return carry

        lax.fori_loop(0, rows // 8, turn, 0)
    total = bins[0:vrows, :]
    out[...] = total
    square[...] = jnp.sum(total * total, axis=0, keepdims=True)


def add_rows(scal, idx, share, parts, vrows):
    cols = share.shape[1]
    rows = parts[0].shape[0]
    return call(
        functools.partial(add_kernel, len(parts), rows, vrows),
        "addrows",
        [sds((vrows, cols), F32), sds((1, cols), F32)],
        (scal, idx, share, *parts),
        smem=(0, 1),
        scratch=[pltpu.VMEM((rows, cols), F32), pltpu.VMEM((vrows + 8, cols), F32)],
        moved=30 * MIB,
    )


def conv_sum(raw, params, rows, lanes):
    total = params[4:5, :] + params[0:1, :] * raw[pl.ds(RIM - 3, rows), lanes]
    for k in range(1, 4):
        total = total + params[k : k + 1, :] * raw[pl.ds(RIM - 3 + k, rows), lanes]
    return total


def front_kernel(shards, own, scal, *rest):
    blocks, rest = rest[:shards], rest[shards:]
    rims, rest = rest[:shards], rest[shards:]
    wzx, wside, chan, bcp, head = rest[:5]
    normed, zx, side, yloc, final, tot_out, c_out, cum_out, xs_scr = rest[5:]
    shard = scal[0]
    rows = own * shards
    inner = chan.shape[1]
    rim = rims[0][...]
    for other in rims[1:]:
        rim = rim + other[...]
    normed[0:RIM, :] = rim
    for off in range(shards):
        at = pl.multiple_of(RIM + (shard ^ off) * own, RIM)
        normed[pl.ds(at, own), :] = blocks[off][...]
    zx[...] = nn(normed[...], wzx[...])
    side[...] = nn(normed[...], wside[...])
    pre = conv_sum(zx, chan, rows, pl.ds(inner, inner))
    xs_scr[...] = pre * sigmoid(pre)
    pre = conv_sum(side, bcp, rows, pl.ds(0, 2 * N))
    bc = (pre * sigmoid(pre)).astype(BF)
    c_out[...] = bc[:, N:]
    dt = softplus(side[RIM:, 2 * N :] + head[0:1, :])
    rate = -dt * jnp.exp(head[1:2, :])
    expand = head_map(inner)
    skip = nn(head[...], expand, HIGHEST)[2:3, :]
    lower = (iota((SPAN, SPAN), 0) >= iota((SPAN, SPAN), 1)).astype(F32)
    first_half = iota((SPAN, LANES), 1) < P_SIZE
    state = None
    base = jnp.zeros((1, LANES), F32)
    for span in range(rows // SPAN):
        here = slice(span * SPAN, (span + 1) * SPAN)
        cum = nn(lower, rate[here], HIGHEST)
        cum_t = cum.T
        tot = cum[SPAN - 1 : SPAN, :]
        keys = bc[here, :N]
        queries = bc[here, N:]
        scores = nt_dot(queries, keys)
        xs = xs_scr[here, :]
        scaled = xs * nn(dt[here], expand, HIGHEST)
        scaled_low = scaled.astype(BF)
        pieces = []
        for pair in range(inner // LANES):
            values = scaled_low[:, pair * LANES : (pair + 1) * LANES]
            both = []
            for h in (2 * pair, 2 * pair + 1):
                gap = cum[:, h : h + 1] - cum_t[h : h + 1, :]
                decay = jnp.exp(jnp.minimum(gap, 0.0)) * lower
                both.append(nn((scores * decay).astype(BF), values))
            pieces.append(jnp.where(first_half, both[0], both[1]))
        y = jnp.concatenate(pieces, axis=1) + skip * xs
        if state is not None:
            y = y + nn(jnp.exp(cum), expand, HIGHEST) * nn(queries, state.astype(BF))
        yloc[here, :] = y
        tail = nn(jnp.exp(tot - cum), expand, HIGHEST)
        fresh = tn(keys, (scaled * tail).astype(BF))
        if state is not None:
            fresh = fresh + nn(jnp.exp(tot), expand, HIGHEST) * state
        state = fresh
        cum_out[here, :] = cum + base
        base = base + tot
    final[...] = state.astype(BF)
    tot_out[...] = jnp.broadcast_to(base, tot_out.shape)


def mixer_front(scal, blocks, rims, wzx, wside, chan, bcp, head):
    shards = len(blocks)
    own = blocks[0].shape[0]
    rows = own * shards
    inner = chan.shape[1]
    return call(
        functools.partial(front_kernel, shards, own),
        "front",
        [
            sds((rows + RIM, D), BF),
            sds((rows + RIM, 2 * inner), F32),
            sds((rows + RIM, 2 * N + LANES), F32),
            sds((rows, inner), F32),
            sds((N, inner), BF),
            sds((8, LANES), F32),
            sds((rows, N), BF),
            sds((rows, LANES), F32),
        ],
        (scal, *blocks, *rims, wzx, wside, chan, bcp, head),
        smem=(0,),
        scratch=[pltpu.VMEM((rows, inner), F32)],
        flops=8 * rows * D * inner,
        moved=12 * MIB,
    )


def chain(parts, tots, expand):
    total = None
    past = jnp.zeros((1, LANES), F32)
    for part, tot in zip(parts, tots):
        term = nn(jnp.exp(past), expand, HIGHEST) * part[...].astype(F32)
        total = term if total is None else total + term
        past = past + tot[0:1, :]
    return total


def middle_kernel(shards, own, hops, scal, *rest):
    states, tots, rest = rest[:hops], rest[hops : 2 * hops], rest[2 * hops :]
    yloc, zx, c_in, cum, wout, chan = rest[:6]
    y_out, s_out, square = rest[6:9]
    parts, work = rest[9 : 9 + shards], rest[-1]
    shard = scal[0]
    rows, inner = yloc.shape
    expand = head_map(inner)
    state = chain(states, tots, expand)
    s_out[...] = state
    y = yloc[...] + nn(jnp.exp(cum[...]), expand, HIGHEST) * nn(c_in[...], state.astype(BF))
    y_out[...] = y
    z = zx[RIM:, :inner]
    gated = y * (z * sigmoid(z))
    square[...] = nt_dot(jnp.ones((8, inner), F32), gated * gated, HIGHEST)
    work[...] = nn((gated * chan[5:6, :]).astype(BF), wout[...]).astype(BF)
    for off in range(shards):
        at = pl.multiple_of((shard ^ off) * own, own)
        parts[off][...] = work[pl.ds(at, own), :]


def mixer_middle(scal, states, tots, yloc, zx, c_in, cum, wout, chan, shards):
    rows, inner = yloc.shape
    own = rows // shards
    return call(
        functools.partial(middle_kernel, shards, own, len(states)),
        "middle",
        [sds((rows, inner), F32), sds((N, inner), F32), sds((8, rows), F32)]
        + [sds((own, D), BF)] * shards,
        (scal, *states, *tots, yloc, zx, c_in, cum, wout, chan),
        smem=(0,),
        scratch=[pltpu.VMEM((rows, D), BF)],
        flops=2 * rows * D * inner,
        moved=8 * MIB,
    )


def gate_back_kernel(shards, own, scal, *rest):
    blocks, rest = rest[:shards], rest[shards:]
    coef, wout, y_in, zx, c_in, cum, chan = rest[:7]
    grads, u_out, dy_out, dz_out, state_out, gain_out = rest[7:]
    shard = scal[0]
    inner = chan.shape[1]
    for off in range(shards):
        at = pl.multiple_of((shard ^ off) * own, own)
        grads[pl.ds(at, own), :] = blocks[off][...]
    du = nt_dot(grads[...], wout[...])
    z = zx[RIM:, :inner]
    y = y_in[...]
    sig = sigmoid(z)
    silu = z * sig
    gated = y * silu
    gain_out[...] = jnp.sum(du * gated, axis=0, keepdims=True)
    gain = chan[5:6, :]
    u_out[...] = (gated * gain).astype(BF)
    dgated = du * gain - gated * coef[...]
    dy = dgated * silu
    dy_out[...] = dy
    dz_out[...] = (dgated * y * (sig * (1.0 + z * (1.0 - sig)))).astype(BF)
    grown = nn(jnp.exp(cum[...]), head_map(inner), HIGHEST)
    state_out[...] = tn(c_in[...], (dy * grown).astype(BF)).astype(BF)


def gate_back(scal, blocks, coef, wout, y, zx, c_in, cum, chan):
    shards = len(blocks)
    own = blocks[0].shape[0]
    rows, inner = y.shape
    return call(
        functools.partial(gate_back_kernel, shards, own),
        "gateback",
        [
            sds((rows, D), BF),
            sds((rows, inner), BF),
            sds((rows, inner), F32),
            sds((rows, inner), BF),
            sds((N, inner), BF),
            sds((1, inner), F32),
        ],
        (scal, *blocks, coef, wout, y, zx, c_in, cum, chan),
        smem=(0,),
        flops=2 * rows * D * inner,
        moved=10 * MIB,
    )


def silu_slope(pre):
    sig = sigmoid(pre)
    return sig * (1.0 + pre * (1.0 - sig))


def conv_back(ds_scr, raw, params, rows, lanes, width, low_out, out_lanes):
    ext = rows + RIM
    total = params[0:1, :] * ds_scr[pl.ds(3, ext), :]
    for k in range(1, 4):
        total = total + params[k : k + 1, :] * ds_scr[pl.ds(3 - k, ext), :]
    low_out[:, out_lanes] = total.astype(BF)
    ds = ds_scr[pl.ds(RIM, rows), :]
    grads = [
        jnp.sum(ds * raw[pl.ds(RIM - 3 + k, rows), lanes], axis=0, keepdims=True) for k in range(4)
    ]
    grads.append(jnp.sum(ds, axis=0, keepdims=True))
    grads.append(jnp.zeros((3, width), F32))
    return jnp.concatenate(grads, axis=0)


def back_kernel(shards, own, hops, scal, *rest):
    states, tots, rest = rest[:hops], rest[hops : 2 * hops], rest[2 * hops :]
    s_in, zx, side, dy_in, dz_in, y_in, wzx, wside, chan, bcp, head = rest[:11]
    dzx, dside, chan_out, bcp_out, head_out, rim_out = rest[11:17]
    parts, rest = rest[17 : 17 + shards], rest[17 + shards :]
    xs_scr, dsx, dsbc, work = rest
    shard = scal[0]
    rows, inner = dy_in.shape
    expand = head_map(inner)
    pre_x = conv_sum(zx, chan, rows, pl.ds(inner, inner))
    xs_scr[...] = pre_x * sigmoid(pre_x)
    pre_bc = conv_sum(side, bcp, rows, pl.ds(0, 2 * N))
    bc = (pre_bc * sigmoid(pre_bc)).astype(BF)
    raw_dt = side[RIM:, 2 * N :] + head[0:1, :]
    dt = softplus(raw_dt)
    grow = jnp.exp(head[1:2, :])
    rate = -dt * grow
    skip = nn(head[...], expand, HIGHEST)[2:3, :]
    lower = (iota((SPAN, SPAN), 0) >= iota((SPAN, SPAN), 1)).astype(F32)
    upper = (iota((SPAN, SPAN), 0) <= iota((SPAN, SPAN), 1)).astype(F32)
    first_half = iota((SPAN, LANES), 1) < P_SIZE
    spans = rows // SPAN
    cums, starts = [], [s_in[...]]
    for span in range(spans):
        here = slice(span * SPAN, (span + 1) * SPAN)
        cum = nn(lower, rate[here], HIGHEST)
        cums.append(cum)
        if span + 1 < spans:
            tot = cum[SPAN - 1 : SPAN, :]
            scale = nn(dt[here] * jnp.exp(tot - cum), expand, HIGHEST)
            fresh = tn(bc[here, :N], (xs_scr[here, :] * scale).astype(BF))
            starts.append(nn(jnp.exp(tot), expand, HIGHEST) * starts[-1] + fresh)
    dstate = chain(states, tots, expand)
    dsx[0:RIM, :] = jnp.zeros((RIM, inner), F32)
    dsx[RIM + rows :, :] = jnp.zeros((RIM, inner), F32)
    dsbc[0:RIM, :] = jnp.zeros((RIM, 2 * N), F32)
    dsbc[RIM + rows :, :] = jnp.zeros((RIM, 2 * N), F32)
    dside[0:RIM, 2 * N :] = jnp.zeros((RIM, LANES), BF)
    dzx[0:RIM, :inner] = jnp.zeros((RIM, inner), BF)
    dzx[RIM:, :inner] = dz_in[...]
    dbias = jnp.zeros((1, LANES), F32)
    dgrow = jnp.zeros((1, LANES), F32)
    dskip = jnp.zeros((1, LANES), F32)
    for span in reversed(range(spans)):
        here = slice(span * SPAN, (span + 1) * SPAN)
        there = slice(RIM + span * SPAN, RIM + (span + 1) * SPAN)
        cum = cums[span]
        cum_t = cum.T
        tot = cum[SPAN - 1 : SPAN, :]
        keys = bc[here, :N]
        queries = bc[here, N:]
        start = starts[span]
        scores_t = nt_dot(keys, queries)
        xs = xs_scr[here, :]
        dy = dy_in[here, :]
        dy_low = dy.astype(BF)
        dt_wide = nn(dt[here], expand, HIGHEST)
        scaled = xs * dt_wide
        scaled_low = scaled.astype(BF)
        dscores_t = jnp.zeros((SPAN, SPAN), F32)
        pieces = []
        for pair in range(inner // LANES):
            values = scaled_low[:, pair * LANES : (pair + 1) * LANES]
            dpair = dy_low[:, pair * LANES : (pair + 1) * LANES]
            both = []
            for h in (2 * pair, 2 * pair + 1):
                gap = cum_t[h : h + 1, :] - cum[:, h : h + 1]
                decay = jnp.exp(jnp.minimum(gap, 0.0)) * upper
                mine = first_half if h % 2 == 0 else jnp.logical_not(first_half)
                outer = nt_dot(jnp.where(mine, values, jnp.zeros_like(values)), dpair)
                dscores_t = dscores_t + outer * decay
                both.append(nn((scores_t * decay).astype(BF), dpair))
            pieces.append(jnp.where(first_half, both[0], both[1]))
        dscaled = jnp.concatenate(pieces, axis=1)
        dscores_low = dscores_t.astype(BF)
        grown = nn(jnp.exp(cum), expand, HIGHEST)
        tail = nn(jnp.exp(tot - cum), expand, HIGHEST)
        dy_grown = (dy * grown).astype(BF)
        dstate_low = dstate.astype(BF)
        through = tail * nn(keys, dstate_low)
        dscaled = dscaled + through
        dqueries = tn(dscores_low, keys) + nt_dot(dy_grown, start.astype(BF))
        dkeys = nn(dscores_low, queries) + nt_dot((scaled * tail).astype(BF), dstate_low)
        plain = y_in[here, :] - skip * xs
        held = scaled_low.astype(F32)
        dcum = nt_dot(dy_low.astype(F32) * plain - held * dscaled, expand, HIGHEST)
        tot_wide = nn(jnp.exp(tot), expand, HIGHEST)
        over = jnp.sum(held * through, axis=0, keepdims=True) + jnp.sum(
            tot_wide * dstate * start, axis=0, keepdims=True
        )
        dtot = nt_dot(jnp.broadcast_to(over, (8, inner)), expand, HIGHEST)[0:1, :]
        drate = nn(upper, dcum, HIGHEST) + dtot
        ddt = nt_dot(dscaled * xs, expand, HIGHEST) - drate * grow
        dgrow = dgrow + jnp.sum(drate * rate[here], axis=0, keepdims=True)
        draw = ddt * sigmoid(raw_dt[here])
        dbias = dbias + jnp.sum(draw, axis=0, keepdims=True)
        dside[there, 2 * N :] = draw.astype(BF)
        over = jnp.sum(dy * xs, axis=0, keepdims=True)
        dskip = dskip + nt_dot(jnp.broadcast_to(over, (8, inner)), expand, HIGHEST)[0:1, :]
        dsx[there, :] = dscaled * dt_wide + skip * dy
        dsbc[there, :N] = dkeys
        dsbc[there, N:] = dqueries
        if span > 0:
            dstate = tot_wide * dstate + tn(queries, dy_grown)
    body = pl.ds(RIM, rows)
    pre_x = conv_sum(zx, chan, rows, pl.ds(inner, inner))
    dsx[body, :] = dsx[body, :] * silu_slope(pre_x)
    pre_bc = conv_sum(side, bcp, rows, pl.ds(0, 2 * N))
    dsbc[body, :] = dsbc[body, :] * silu_slope(pre_bc)
    chan_out[...] = conv_back(
        dsx, zx, chan, rows, pl.ds(inner, inner), inner, dzx, pl.ds(inner, inner)
    )
    bcp_out[...] = conv_back(dsbc, side, bcp, rows, pl.ds(0, 2 * N), 2 * N, dside, pl.ds(0, 2 * N))
    head_out[...] = jnp.concatenate([dbias, dgrow, dskip, jnp.zeros((5, LANES), F32)], axis=0)
    work[...] = (nt_dot(dzx[...], wzx[...]) + nt_dot(dside[...], wside[...])).astype(BF)
    rim_out[...] = work[0:RIM, :]
    for off in range(shards):
        at = pl.multiple_of(RIM + (shard ^ off) * own, RIM)
        parts[off][...] = work[pl.ds(at, own), :]


def mixer_back(scal, states, tots, s_in, zx, side, dy, dz, y, wzx, wside, chan, bcp, head, shards):
    rows, inner = dy.shape
    own = rows // shards
    ext = rows + RIM
    return call(
        functools.partial(back_kernel, shards, own, len(states)),
        "back",
        [
            sds((ext, 2 * inner), BF),
            sds((ext, 2 * N + LANES), BF),
            sds((8, inner), F32),
            sds((8, 2 * N), F32),
            sds((8, LANES), F32),
            sds((RIM, D), BF),
        ]
        + [sds((own, D), BF)] * shards,
        (scal, *states, *tots, s_in, zx, side, dy, dz, y, wzx, wside, chan, bcp, head),
        smem=(0,),
        scratch=[
            pltpu.VMEM((rows, inner), F32),
            pltpu.VMEM((ext + RIM, inner), F32),
            pltpu.VMEM((ext + RIM, 2 * N), F32),
            pltpu.VMEM((ext, D), BF),
        ],
        flops=8 * rows * D * inner,
        moved=16 * MIB,
    )


def logits_kernel(shards, own, vrows, label, table, *rest):
    blocks, rest = rest[:shards], rest[shards:]
    p_out, tops, stats, rows_scr, top, total, target, plain = rest
    step = pl.program_id(0)
    rows = own * shards

    @pl.when(step == 0)
    def _():
        for off in range(shards):
            rows_scr[off * own : (off + 1) * own, :] = blocks[off][...]
        top[...] = jnp.full((1, rows), -1e30, F32)
        total[...] = jnp.zeros((1, rows), F32)
        target[...] = jnp.zeros((1, rows), F32)
        plain[...] = jnp.zeros((1, rows), F32)

    at = step * PAIRS + iota((PAIRS, rows), 0)
    valid = at < vrows
    logits = []
    highest = top[...]
    for half in range(2):
        raw = nt_dot(table[:, half * D : (half + 1) * D], rows_scr[...])
        highest = jnp.maximum(
            highest, jnp.max(jnp.where(valid, raw, -1e30), axis=0, keepdims=True)
        )
        logits.append(raw)
    summed = total[...] * jnp.exp(top[...] - highest)
    hit = target[...]
    whole = plain[...]
    for half in range(2):
        raw = logits[half]
        part = jnp.where(valid, jnp.exp(raw - highest), 0.0)
        summed = summed + jnp.sum(part, axis=0, keepdims=True)
        hit = hit + jnp.sum(
            jnp.where(2 * at + half == label[...], raw, 0.0), axis=0, keepdims=True
        )
        whole = whole + jnp.sum(raw, axis=0, keepdims=True)
        p_out[half] = part.astype(BF)
    top[...] = highest
    total[...] = summed
    target[...] = hit
    plain[...] = whole
    tops[...] = jnp.broadcast_to(highest, (1, 8, rows))
    stats[...] = jnp.concatenate([highest, summed, hit, whole, jnp.zeros((4, rows), F32)], axis=0)


def vocab_logits(label, table, blocks, vrows):
    shards = len(blocks)
    own = blocks[0].shape[0]
    rows = own * shards
    padded = table.shape[0]
    steps = padded // PAIRS
    whole = lambda i: (0, 0)
    return pl.pallas_call(
        functools.partial(logits_kernel, shards, own, vrows),
        grid=(steps,),
        out_shape=[
            sds((2, padded, rows), BF),
            sds((steps, 8, rows), F32),
            sds((8, rows), F32),
        ],
        in_specs=[
            pl.BlockSpec((1, rows), whole),
            pl.BlockSpec((PAIRS, 2 * D), lambda i: (i, 0)),
        ]
        + [pl.BlockSpec((own, D), whole)] * shards,
        out_specs=[
            pl.BlockSpec((2, PAIRS, rows), lambda i: (0, i, 0)),
            pl.BlockSpec((1, 8, rows), lambda i: (i, 0, 0)),
            pl.BlockSpec((8, rows), whole),
        ],
        scratch_shapes=[pltpu.VMEM((rows, D), BF)] + [pltpu.VMEM((1, rows), F32)] * 4,
        compiler_params=pltpu.CompilerParams(
            dimension_semantics=("arbitrary",), vmem_limit_bytes=48 * MIB
        ),
        cost_estimate=pl.CostEstimate(
            flops=4 * rows * D * padded, bytes_accessed=40 * MIB, transcendentals=2 * rows * padded
        ),
        name="logits",
    )(label, table, *blocks)


def rows_kernel(shards, own, vrows, label, scale, weight, p_in, table, *rest):
    q_out, parts, acc = rest[0], rest[1 : 1 + shards], rest[-1]
    step = pl.program_id(0)
    rows = own * shards

    @pl.when(step == 0)
    def _():
        acc[...] = jnp.zeros_like(acc)

    at = step * PAIRS + iota((PAIRS, rows), 0)
    keep = jnp.where(at < vrows, weight[...], 0.0)
    factor = scale[0, 0:1, :]
    term = None
    for half in range(2):
        share = jnp.where(2 * at + half == label[...], 1.0 - SMOOTHING + SMOOTHING / V, SMOOTHING / V)
        q = (p_in[half].astype(F32) * factor - keep * share).astype(BF)
        q_out[half] = q
        part = tn(q, table[:, half * D : (half + 1) * D])
        term = part if term is None else term + part
    acc[...] += term

    @pl.when(step == pl.num_programs(0) - 1)
    def _():
        for off in range(shards):
            parts[off][...] = acc[off * own : (off + 1) * own, :].astype(BF)


def vocab_rows(label, scale, weight, p_in, table, vrows, shards):
    _, padded, rows = p_in.shape
    steps = padded // PAIRS
    own = rows // shards
    whole = lambda i: (0, 0)
    return pl.pallas_call(
        functools.partial(rows_kernel, shards, own, vrows),
        grid=(steps,),
        out_shape=[sds((2, padded, rows), BF)] + [sds((own, D), BF)] * shards,
        in_specs=[
            pl.BlockSpec((1, rows), whole),
            pl.BlockSpec((1, 8, rows), lambda i: (i, 0, 0)),
            pl.BlockSpec((1, rows), whole),
            pl.BlockSpec((2, PAIRS, rows), lambda i: (0, i, 0)),
            pl.BlockSpec((PAIRS, 2 * D), lambda i: (i, 0)),
        ],
        out_specs=[pl.BlockSpec((2, PAIRS, rows), lambda i: (0, i, 0))]
        + [pl.BlockSpec((own, D), whole)] * shards,
        scratch_shapes=[pltpu.VMEM((rows, D), F32)],
        compiler_params=pltpu.CompilerParams(
            dimension_semantics=("arbitrary",), vmem_limit_bytes=48 * MIB
        ),
        cost_estimate=pl.CostEstimate(
            flops=4 * rows * D * padded, bytes_accessed=52 * MIB, transcendentals=0
        ),
        name="rowgrads",
    )(label, scale, weight, p_in, table)


def table_kernel(shards, own, q_in, *rest):
    blocks, out, rows_scr = rest[:shards], rest[shards], rest[-1]

    @pl.when(pl.program_id(0) == 0)
    def _():
        for off in range(shards):
            rows_scr[off * own : (off + 1) * own, :] = blocks[off][...]

    for half in range(2):
        out[:, half * D : (half + 1) * D] = nn(q_in[half], rows_scr[...]).astype(BF)


def vocab_table_grad(q_in, blocks):
    _, padded, rows = q_in.shape
    shards = len(blocks)
    own = blocks[0].shape[0]
    whole = lambda i: (0, 0)
    return pl.pallas_call(
        functools.partial(table_kernel, shards, own),
        grid=(padded // PAIRS,),
        out_shape=sds((padded, 2 * D), BF),
        in_specs=[pl.BlockSpec((2, PAIRS, rows), lambda i: (0, i, 0))]
        + [pl.BlockSpec((own, D), whole)] * shards,
        out_specs=pl.BlockSpec((PAIRS, 2 * D), lambda i: (i, 0)),
        scratch_shapes=[pltpu.VMEM((rows, D), BF)],
        compiler_params=pltpu.CompilerParams(
            dimension_semantics=("arbitrary",), vmem_limit_bytes=48 * MIB
        ),
        cost_estimate=pl.CostEstimate(
            flops=4 * rows * D * padded, bytes_accessed=40 * MIB, transcendentals=0
        ),
        name="tablegrads",
    )(q_in, *blocks)


def adam_update(weight_in, gradient, moment_one, moment_two, factor, fix_one, fix_two, decay_rate):
    gradient = gradient * factor
    one_next = BETA_FIRST * moment_one + (1.0 - BETA_FIRST) * gradient
    two_next = BETA_SECOND * moment_two + (1.0 - BETA_SECOND) * gradient * gradient
    direction = one_next / fix_one / (jnp.sqrt(two_next / fix_two) + ADAM_EPS)
    return (weight_in - LEARN_RATE * (direction + decay_rate * weight_in), one_next, two_next)


def soap_update(weight_in, gradient, bases, moment_one, moment_two, factor, fix_one, fix_two):
    gradient = gradient * factor
    left_basis = bases[..., 0, :, :]
    right_basis = bases[..., 1, :, :]
    half_turn = jnp.einsum("...ab,...ac->...bc", left_basis, gradient, precision=HIGHEST)
    rotated = jnp.einsum("...bc,...cd->...bd", half_turn, right_basis, precision=HIGHEST)
    one_next = BETA_FIRST * moment_one + (1.0 - BETA_FIRST) * rotated
    two_next = BETA_SECOND * moment_two + (1.0 - BETA_SECOND) * rotated * rotated
    direction = one_next / fix_one / (jnp.sqrt(two_next / fix_two) + ADAM_EPS)
    back_half = jnp.einsum("...ab,...bc->...ac", left_basis, direction, precision=HIGHEST)
    turned = jnp.einsum("...ac,...dc->...ad", back_half, right_basis, precision=HIGHEST)
    weight_next = weight_in - LEARN_RATE * (turned + WEIGHT_DECAY * weight_in)
    return (weight_next, weight_next.astype(BF), one_next, two_next)


def to_blocks(matrix):
    row_count, col_count = matrix.shape
    return (
        matrix.reshape(row_count // BLK, BLK, col_count // BLK, BLK)
        .transpose(0, 2, 1, 3)
        .reshape(-1, BLK, BLK)
    )


def total_over(x, axis):
    out = x
    for off in range(1, lax.axis_size(axis)):
        out = out + swap(x, axis, off)
    return out


def rms_scale(values):
    return lax.rsqrt(jnp.mean(values * values, axis=-1, keepdims=True) + NORM_EPS)


def shards(
    token_ids,
    labels,
    seq_lengths,
    micro_batch,
    step_count,
    block_slot,
    vocab_table,
    vocab_first,
    vocab_second,
    layer_blocks,
    block_bases,
    block_first,
    block_second,
    side_proj,
    side_first,
    side_second,
    shared_params,
    shared_first,
    shared_second,
    channel_params,
    channel_first,
    channel_second,
    head_params,
    head_first,
    head_second,
):
    nt = lax.axis_size("tensor")
    nd = lax.axis_size("dp")
    shard = lax.axis_index("tensor")
    place = lax.axis_index("dp")
    seqs = token_ids.shape[0]
    length = token_ids.shape[1] * nd
    chunks = nd // seqs
    rows = seqs * length // nd
    own = rows // nt
    vrows = vocab_table.shape[0]
    padded = -(-vrows // PAIRS) * PAIRS
    half = nd // 2
    inner = channel_params.shape[2]
    heads = head_params.shape[2]
    tiles = block_slot.shape[1]
    zx_count = D * 2 * inner // (BLK * BLK)
    per_layer = 3 * D * inner // (BLK * BLK)
    stride = D + 10 * N
    both = ("dp", "tensor")
    side_rows = side_proj.shape[1]
    share_size = shared_params.shape[0]
    share_pad = -(-share_size // 2048) * 2048

    piece = jnp.concatenate(
        [
            jnp.pad(side_proj.astype(BF), ((0, 0), (0, 0), (0, LANES - H))).reshape(-1, LANES),
            jnp.pad(shared_params.astype(BF), (0, share_pad - share_size)).reshape(-1, LANES),
        ],
        axis=0,
    )
    piece_rows = piece.shape[0]
    side_part = piece_rows - share_pad // LANES
    pieces = jnp.zeros((nt, piece_rows, LANES), BF)
    for off in range(nt):
        pieces = lax.dynamic_update_index_in_dim(
            pieces, piece if off == 0 else swap(piece, "tensor", off), shard ^ off, 0
        )
    own_tiles = layer_blocks.shape[2]
    carried = jnp.concatenate(
        [layer_blocks.astype(BF).reshape(own_tiles * BLK, BLK), pieces.reshape(-1, LANES)], axis=0
    )
    gathered = lax.all_gather(carried, "dp", axis=0, tiled=False)
    ids_all = lax.all_gather(jnp.concatenate([token_ids, labels], axis=0), "dp", axis=1, tiled=True)
    table_low = jnp.pad(vocab_table.astype(BF), ((0, padded - vrows), (0, 0)))

    slot_tiles = gathered[:, : own_tiles * BLK].reshape(tiles, BLK, BLK)
    ordered = slot_tiles[block_slot[0]]
    small = gathered[:, own_tiles * BLK :].reshape(nd, nt, piece_rows, LANES)
    side_full = (
        small[:, :, :side_part]
        .reshape(nd, nt, L, side_rows, 2 * N + LANES)
        .transpose(2, 0, 1, 3, 4)
        .reshape(L, D, 2 * N + LANES)
    )
    shared_full = small[:, :, side_part:].reshape(nd * nt, share_pad)[:, :share_size].reshape(-1)
    shared_full = shared_full.astype(F32)

    all_ids = ids_all[:seqs].reshape(-1)
    local_row = all_ids // 2 - shard * vrows
    held = (local_row >= 0) & (local_row < vrows) & (all_ids % 2 == place // half)
    scal = jnp.stack([place, shard]).astype(jnp.int32)
    scal_shard = shard.astype(jnp.int32).reshape(1)
    parts = gather_rows(
        scal,
        jnp.where(held, local_row, 0),
        jnp.broadcast_to(held[:, None], (held.shape[0], 1)).astype(F32),
        vocab_table,
        nd,
        rows,
    )
    parts = [parts[0]] + [swap(parts[off], "dp", off) for off in range(1, nd)]
    parts = join_parts(scal, parts, nt, own)
    residual = parts[0]
    for off in range(1, nt):
        residual = residual + swap(parts[off], "tensor", off)
    residual = residual.astype(F32)
    table_all = lax.all_gather(table_low, "dp", axis=1, tiled=True)

    def layer_mats(layer_index):
        base_index = layer_index * per_layer
        zx_part = (
            ordered[base_index : base_index + zx_count]
            .reshape(D // BLK, 2 * inner // BLK, BLK, BLK)
            .transpose(0, 2, 1, 3)
            .reshape(D, 2 * inner)
        )
        out_part = (
            ordered[base_index + zx_count : base_index + per_layer]
            .reshape(inner // BLK, D // BLK, BLK, BLK)
            .transpose(0, 2, 1, 3)
            .reshape(inner, D)
        )
        dt_part = lax.dynamic_slice_in_dim(
            side_full[layer_index], 2 * N + shard * heads, heads, 1
        )
        side_here = jnp.concatenate(
            [
                side_full[layer_index][:, : 2 * N],
                jnp.pad(dt_part, ((0, 0), (0, LANES - heads))),
            ],
            axis=1,
        )
        base = layer_index * stride
        gain = shared_full[base : base + D]
        taps = shared_full[base + D : base + D + 8 * N].reshape(4, 2 * N)
        bias = shared_full[base + D + 8 * N : base + stride].reshape(1, 2 * N)
        bcp = jnp.concatenate([taps, bias, jnp.zeros((3, 2 * N), F32)], axis=0)
        chan = jnp.pad(channel_params[layer_index], ((0, 2), (0, 0)))
        head = jnp.pad(head_params[layer_index], ((0, 5), (0, LANES - heads)))
        return (zx_part, out_part, side_here, gain, bcp, chan, head)

    def spread(x):
        return [x] + [swap(x, "tensor", off) for off in range(1, nt)]

    def rim_pairs(to):
        return [
            (k * nt + nt - 1, (k + 1) * nt + to) for k in range(nd) if k % chunks + 1 < chunks
        ]

    def hop(x, distance):
        pairs = [
            (k, k + distance)
            for k in range(nd)
            if 0 <= k % chunks + distance < chunks
        ]
        return lax.ppermute(x, "dp", pairs)

    def collect(parts):
        total = parts[0].astype(F32)
        for off in range(1, nt):
            total = total + swap(parts[off], "tensor", off).astype(F32)
        return total

    hops = range(1, chunks)
    mats = [layer_mats(layer_index) for layer_index in range(L)]
    saved = []
    for layer_index in range(L):
        wzx, wout, wside, gain, bcp, chan, head = mats[layer_index]
        normed_own = (residual * rms_scale(residual) * gain[None, :]).astype(BF)
        edge = normed_own[own - RIM :]
        rims = [lax.ppermute(edge, both, rim_pairs(to)) for to in range(nt)]
        normed, zx, side, yloc, final, tot, c_out, cum = mixer_front(
            scal_shard, spread(normed_own), rims, wzx, wside, chan, bcp, head
        )
        states = [hop(final, k) for k in hops]
        tots = [hop(tot, k) for k in hops]
        result = mixer_middle(scal_shard, states, tots, yloc, zx, c_out, cum, wout, chan, nt)
        y, s_in, square = result[:3]
        square = total_over(square, "tensor")[0]
        square = lax.dynamic_slice_in_dim(square, shard * own, own)
        factor = lax.rsqrt(square / DI + NORM_EPS)[:, None]
        branch = collect(result[3:])
        saved.append((residual, normed, zx, side, tot, c_out, cum, y, s_in, factor, branch))
        residual = residual + factor * branch
    final_gain = shared_full[L * stride :]
    final_scale = rms_scale(residual)
    final_rows = spread((residual * final_scale * final_gain[None, :]).astype(BF))

    member = micro_batch[:, None] == jnp.arange(MB, dtype=jnp.int32)[None, :]
    batch_tokens = jnp.sum(jnp.where(member, seq_lengths[:, None], 0), axis=0).astype(F32)
    seq_weight = 1.0 / (MB * jnp.sum(jnp.where(member, batch_tokens[None, :], 0.0), axis=1))
    block_order = shard ^ jnp.arange(nt, dtype=jnp.int32)
    row_at = (
        place * rows + block_order[:, None] * own + jnp.arange(own, dtype=jnp.int32)[None, :]
    ).reshape(rows)
    my_seq = place // chunks
    weight = jnp.where(row_at % length < seq_lengths[my_seq], seq_weight[my_seq], 0.0)
    all_labels = ids_all[seqs:].reshape(-1)
    label = (all_labels[row_at] - 2 * shard * vrows).reshape(1, rows)

    p_low, tops, stats = vocab_logits(label, table_all, final_rows, vrows)
    stats = stats.reshape(8, nt, own)
    merged = (stats[0], stats[1], stats[2], stats[3])
    others = [swap(stats, "tensor", off) for off in range(1, nt)]
    best = stats[0]
    for off in range(1, nt):
        best = jnp.maximum(best, jnp.stack([others[off - 1][0, o ^ off] for o in range(nt)]))
    summed = stats[1] * jnp.exp(stats[0] - best)
    target = stats[2]
    plain = stats[3]
    for off in range(1, nt):
        them = jnp.stack([others[off - 1][:, o ^ off] for o in range(nt)], axis=1)
        summed = summed + them[1] * jnp.exp(them[0] - best)
        target = target + them[2]
        plain = plain + them[3]
    log_total = best + jnp.log(summed)
    token_loss = (
        log_total
        - (1.0 - SMOOTHING) * target
        - SMOOTHING / V * plain
        + ZLOSS_WEIGHT * log_total * log_total
    )
    loss_here = jnp.sum(weight[:own] * token_loss[0])
    seq_part = jnp.where(jnp.arange(seqs) == my_seq, loss_here, 0.0)
    soft = (weight.reshape(nt, own) * (1.0 + 2.0 * ZLOSS_WEIGHT * log_total)).reshape(1, 1, rows)
    scale = soft * jnp.exp(tops - log_total.reshape(1, 1, rows))
    result = vocab_rows(label, scale, weight.reshape(1, rows), p_low, table_all, vrows, nt)
    q_low = result[0]
    grad_final = collect(result[1:])
    table_grad = vocab_table_grad(q_low, final_rows)
    table_share = lax.psum_scatter(table_grad, "dp", scatter_dimension=1, tiled=True)

    grad_final_gain = jnp.sum(grad_final * residual * final_scale, axis=0)
    scaled_grad = grad_final * final_gain[None, :]
    grad_res = final_scale * scaled_grad - residual * (
        final_scale * final_scale * final_scale
    ) * jnp.mean(scaled_grad * residual, axis=1, keepdims=True)

    block_pieces = [None] * (2 * L)
    side_pieces = [None] * L
    channel_pieces = [None] * L
    head_pieces = [None] * L
    shared_pieces = [None] * L
    for layer_index in reversed(range(L)):
        wzx, wout, wside, gain, bcp, chan, head = mats[layer_index]
        residual_in, normed, zx, side, tot, c_out, cum, y, s_in, factor, branch = saved[layer_index]
        inner_rows = jnp.sum(grad_res * branch, axis=1)
        coef_own = factor[:, 0] * factor[:, 0] * factor[:, 0] * inner_rows / DI
        coef = jnp.zeros((rows,), F32)
        for off in range(nt):
            coef = lax.dynamic_update_slice_in_dim(
                coef, coef_own if off == 0 else swap(coef_own, "tensor", off), (shard ^ off) * own, 0
            )
        grads, u_low, dy, dz, dstate, gain_grad = gate_back(
            scal_shard,
            spread((factor * grad_res).astype(BF)),
            coef[:, None],
            wout,
            y,
            zx,
            c_out,
            cum,
            chan,
        )
        states = [hop(dstate, -k) for k in hops]
        tots = [hop(tot, -k) for k in hops]
        grad_out_w = tn(u_low, grads)
        result = mixer_back(
            scal_shard, states, tots, s_in, zx, side, dy, dz, y, wzx, wside, chan, bcp, head, nt
        )
        dzx, dside, chan_grad, bcp_grad, head_grad, rim_grad = result[:6]
        grad_local = collect(result[6:])
        rim_sum = jnp.zeros((RIM, D), F32)
        for to in range(nt):
            pairs = [(b, a) for a, b in rim_pairs(to)]
            rim_sum = rim_sum + lax.ppermute(rim_grad, both, pairs).astype(F32)
        grad_local = grad_local + jnp.pad(rim_sum, ((own - RIM, 0), (0, 0)))
        grad_zx_w = tn(normed, dzx)
        grad_side_w = tn(normed, dside)
        inv_scale = rms_scale(residual_in)
        grad_gain_in = jnp.sum(grad_local * residual_in * inv_scale, axis=0)
        scaled_in = grad_local * gain[None, :]
        grad_res = (
            grad_res
            + inv_scale * scaled_in
            - residual_in
            * (inv_scale * inv_scale * inv_scale)
            * jnp.mean(scaled_in * residual_in, axis=1, keepdims=True)
        )
        block_pieces[2 * layer_index] = to_blocks(grad_zx_w.astype(BF))
        block_pieces[2 * layer_index + 1] = to_blocks(grad_out_w.astype(BF))
        spaced = lax.dynamic_update_slice(
            jnp.zeros((D, LANES), F32),
            grad_side_w[:, 2 * N : 2 * N + heads],
            (jnp.zeros((), jnp.int32), shard * heads),
        )
        side_pieces[layer_index] = jnp.concatenate([grad_side_w[:, : 2 * N], spaced], axis=1)
        channel_pieces[layer_index] = jnp.concatenate([chan_grad[:5], gain_grad], axis=0)
        head_pieces[layer_index] = head_grad[:3, :heads]
        shared_pieces[layer_index] = jnp.concatenate(
            [grad_gain_in, bcp_grad[:4].reshape(-1), bcp_grad[4]]
        )

    embed = cut_parts(scal, spread(grad_res.astype(BF)), nd)
    embed = [embed[0]] + [swap(embed[off], "dp", off) for off in range(1, nd)]

    inverse = jnp.zeros((tiles,), jnp.int32).at[block_slot[0]].set(jnp.arange(tiles, dtype=jnp.int32))
    ordered_grads = jnp.concatenate(block_pieces, axis=0)
    slot_grads = ordered_grads[inverse].reshape(nd, own_tiles * BLK, BLK)
    side_grads = (
        jnp.stack(side_pieces)
        .astype(BF)
        .reshape(L, nd, nt, side_rows, 2 * N + LANES)
        .transpose(1, 2, 0, 3, 4)
        .reshape(nd, nt, side_part, LANES)
    )
    shared_grads = jnp.concatenate(shared_pieces + [grad_final_gain]).astype(BF)
    shared_grads = jnp.pad(
        shared_grads.reshape(nd, nt, share_size), ((0, 0), (0, 0), (0, share_pad - share_size))
    ).reshape(nd, nt, share_pad // LANES, LANES)
    small_grads = jnp.concatenate([side_grads, shared_grads], axis=2).reshape(nd, -1, LANES)
    block_share = lax.psum_scatter(
        jnp.concatenate([slot_grads, small_grads], axis=1), "dp", scatter_dimension=0, tiled=True
    )[0]
    block_grads = block_share[: own_tiles * BLK].astype(F32)
    small_share = block_share[own_tiles * BLK :].reshape(nt, piece_rows, LANES)
    mine = jnp.zeros((piece_rows, LANES), F32)
    for off in range(nt):
        sent = lax.dynamic_index_in_dim(small_share, shard ^ off, 0, False)
        mine = mine + (sent if off == 0 else swap(sent, "tensor", off)).astype(F32)
    side_share = mine[:side_part].reshape(L, side_rows, 2 * N + LANES)[:, :, : 2 * N + H]
    shared_share = mine[side_part:].reshape(-1)[:share_size]
    lines = jnp.concatenate(
        [
            jnp.stack(channel_pieces).reshape(-1, LANES),
            jnp.pad(jnp.stack(head_pieces).reshape(-1), (0, LANES - L * 3 * heads)).reshape(1, LANES),
        ],
        axis=0,
    )
    lines = total_over(lines, "dp")
    channel_sum = lines[:-1].reshape(channel_params.shape)
    head_sum = lines[-1, : L * 3 * heads].reshape(head_params.shape)

    grad_table, table_square = add_rows(
        scal, jnp.where(held, local_row, vrows), table_share, embed, vrows
    )
    first_copy = (place == 0).astype(F32)
    square_part = (
        jnp.sum(block_grads * block_grads)
        + jnp.sum(table_square)
        + jnp.sum(side_share * side_share)
        + jnp.sum(shared_share * shared_share)
        + first_copy * (jnp.sum(channel_sum * channel_sum) + jnp.sum(head_sum * head_sum))
    )
    packed = jnp.concatenate([seq_part, square_part[None]])
    packed = total_over(total_over(packed, "tensor"), "dp")
    seq_loss = packed[:seqs]
    clip_norm = jnp.sqrt(packed[seqs])
    factor = jnp.minimum(1.0, CLIP_LIMIT / (clip_norm + 1e-06))
    steps_done = step_count[0].astype(F32)
    fix_one = 1.0 - jnp.power(BETA_FIRST, steps_done)
    fix_two = 1.0 - jnp.power(BETA_SECOND, steps_done)
    table_out = adam_update(
        vocab_table, grad_table, vocab_first, vocab_second, factor, fix_one, fix_two, WEIGHT_DECAY
    )
    block_out = soap_update(
        layer_blocks,
        block_grads.reshape(layer_blocks.shape),
        block_bases,
        block_first,
        block_second,
        factor,
        fix_one,
        fix_two,
    )
    side_next = adam_update(
        side_proj, side_share, side_first, side_second, factor, fix_one, fix_two, WEIGHT_DECAY
    )
    shared_next = adam_update(
        shared_params, shared_share, shared_first, shared_second, factor, fix_one, fix_two, 0.0
    )
    channel_next = adam_update(
        channel_params, channel_sum, channel_first, channel_second, factor, fix_one, fix_two, 0.0
    )
    head_next = adam_update(
        head_params, head_sum, head_first, head_second, factor, fix_one, fix_two, 0.0
    )
    return (
        seq_loss,
        clip_norm,
        table_out[0],
        table_out[1],
        table_out[2],
        block_out[0],
        block_out[1],
        block_out[2],
        block_out[3],
        side_next[0],
        side_next[1],
        side_next[2],
        shared_next[0] - shared_params,
        shared_next[1],
        shared_next[2],
        channel_next[0] - channel_params,
        channel_next[1],
        channel_next[2],
        head_next[0] - head_params,
        head_next[1],
        head_next[2],
    )


def solution(mesh):
    table = P("tensor", "dp")
    block = P("dp", "tensor", None, None, None)
    side = P(None, ("dp", "tensor"), None)
    shared = P(("dp", "tensor"))
    channel = P(None, None, "tensor")
    in_specs = (
        P(None, "dp"),
        P(None, "dp"),
        P(),
        P(),
        P(),
        P("tensor", None),
        *[table] * 3,
        block,
        P("dp", "tensor", None, None, None, None),
        block,
        block,
        *[side] * 3,
        *[shared] * 3,
        *[channel] * 6,
    )
    out_specs = (
        P(),
        P(),
        *[table] * 3,
        *[block] * 4,
        *[side] * 3,
        *[shared] * 3,
        *[channel] * 6,
    )
    return jax.shard_map(shards, mesh=mesh, in_specs=in_specs, out_specs=out_specs, check_vma=False)
```

time: 1790 us -> 1030 us (0.58)
  waiting for transfers between devices: 734 us -> 336 us
  blocking collectives: 261 us -> 9.08 us
  matrix products: 243 us -> 23 us
  Pallas kernels: 0 us -> 206 us
  starting transfers between devices: 8.13 us -> 195 us
  other arithmetic: 239 us -> 80.2 us
  local copies, waits for them, and re-layouts: 265 us -> 146 us
    all_gather x13 -> x2, waiting for transfers between devices: 371 us -> 0.01 us  [the longest x1 0.01 us: shards(): gathered = lax.all_gather(carried, 'dp', axis=0, tiled=False)]
    dot_general x49 -> x6, matrix products: 229 us -> 9.29 us  [tn(): lax.dot_general(a, b, (((0,), (0,)), ((), ())), precision=precision, pref...]
    reduce_scatter x8 -> x2, waiting for transfers between devices: 362 us -> 152 us  [the longest x1 134 us: shards(): lax.psum_scatter(table_grad, 'dp', scatter_dimension=1, tiled=True)]
    pallas_call x0 -> x15, Pallas kernels: none -> 206 us  [the longest x12 126 us: call(): pl.pallas_call(kernel, out_shape=out_shape, in_specs=specs, out_specs=jax...]
    ppermute x4 -> x128, starting transfers between devices: 6.3 us -> 195 us  [the longest x88 139 us: swap(): return lax.ppermute(x, axis, [(i, i ^ offset) for i in range(size)])]
    ppermute x4 -> x128, waiting for transfers between devices: 0.01 us -> 184 us  [the longest x88 169 us: swap(): return lax.ppermute(x, axis, [(i, i ^ offset) for i in range(size)])]
    psum x6 -> x0, blocking collectives: 108 us -> none  [the longest x4 44.1 us: tensor_total(): return lax.psum(values, 'tensor')]
    unnamed x2 -> x0, blocking collectives: 81.7 us -> none
  transfers between devices with their start and end apart: 26 -> 132, of which waited for: 17 -> 43; matrix products, arithmetic and copies ran while one was open for 19% -> 17% of each run, Pallas kernels for 0% -> 8%
where the time goes in v1:
time: 1030 us; the launch traced here: 1020 us
  waiting for transfers between devices  336 us (33%)
  Pallas kernels  206 us (20%)
  starting transfers between devices  195 us (19%)
  local copies, waits for them, and re-layouts  146 us (14%)
  other arithmetic  80.2 us (8%)
  between operations  24.1 us (2%)
  matrix products  23 us (2%)
    ppermute x88, waiting for transfers between devices, swap(): return lax.ppermute(x, axis, [(i, i ^ offset) for i in range(size)])  169 us
    ppermute x88, starting transfers between devices, swap(): return lax.ppermute(x, axis, [(i, i ^ offset) for i in range(size)])  139 us
    reduce_scatter x1, waiting for transfers between devices, shards(): lax.psum_scatter(table_grad, 'dp', scatter_dimension=1, tiled=True)  134 us
    pallas_call x12, Pallas kernels, call(): pl.pallas_call(kernel, out_shape=out_shape, in_specs=specs, out_specs=jax...  126 us
    ppermute x24, starting transfers between devices, hop(): return lax.ppermute(x, 'dp', pairs)  43.5 us
    unnamed x431, local copies, waits for them, and re-layouts  36.4 us
    pallas_call x1, Pallas kernels, vocab_logits(): pl.pallas_call(functools.partial(logits_kernel, shards, own, vrows), grid...  30.3 us
    pallas_call x1, Pallas kernels, vocab_rows(): pl.pallas_call(functools.partial(rows_kernel, shards, own, vrows), grid=(...  26.6 us
  transfers between devices with their start and end apart: 132, of which 43 were waited for; matrix products, arithmetic and copies ran while one was open for 17% of the time, Pallas kernels for 8%

profile of v1, /device:TPU:0, one launch (start us, length us, event | category | flops | bytes accessed | tf_op | source)
XLA Modules:
  0.0 1019.3 jit_solution(12865446199466281927)
XLA Ops:
  27.4 9.1 all_gather.12
  43.6 20.4 %look.1 = (bf16[512,256]{1,0:T(8,128)(2,1)S(1)}, bf16[512,256]{1,0:T(8,128)(2,1)S(1)}, bf16[512,256]{1,0:T(8,128)(2,1)S(1)}, bf16[512,256]{1,0:T(8,128)(2,1)}, b...) custom-call(s32[2]{0:T(128)S(1)} %pad_add_fusion.3.scal, ...), custom_call_target="tpu_custom_call" | custom-call | bytes 31457280 | tf_op jit(solution)/shard_map/look/pallas_call | solution.py:84
  99.5 8.9 collective-permute-done.7
  108.4 9.5 collective-permute-done.8
  142.1 11.1 %gather_fusion.1 = bf16[192,128,128]{2,1,0:T(8,128)(2,1)} fusion(bf16[192,128,128]{2,1,0:T(8,128)(2,1)} %bitcast.445, s32[1024]{0:T(1024)S(1)} %pad_clamp_fusion.1), kind=kCustom, calls=%fused_computation.1 | custom fusion | bytes 12583680 | tf_op jit(solution)/shard_map/gather | solution.py:871
  169.1 9.3 front.2
  223.1 11.5 %collective-permute-done.30 = bf16[128,1024]{1,0:T(8,128)(2,1)S(1)} collective-permute-done((bf16[128,1024]{1,0:T(8,128)(2,1)}, bf16[128,1024]{1,0:T(8,128)(2,1)S(1)}, u32[]{:S(2)}, u32[]{:S(2)}) %collective-permute-start.30) | collective-permute-done | bytes 262176 | tf_op jit(solution)/shard_map/ppermute | solution.py:68
  254.8 8.9 collective-permute-done.33.rest_2_
  263.8 9.3 front.3
  313.9 18.9 %collective-permute-done.46 = f32[8,512]{1,0:T(8,128)S(1)} collective-permute-done((f32[8,512]{1,0:T(8,128)S(1)}, f32[8,512]{1,0:T(8,128)S(1)}, u32[]{:S(2)}, u32[]{:S(2)}) %collective-permute-start.46) | collective-permute-done | bytes 16416 | tf_op jit(solution)/shard_map/ppermute | solution.py:68
  356.5 30.3 %logits.1 = (bf16[2,6400,512]{2,1,0:T(8,128)(2,1)}, f32[10,8,512]{2,1,0:T(8,128)S(1)}, f32[8,512]{1,0:T(8,128)S(1)}) custom-call(s32[1,512]{1,0:T(1,128)S(1)} %bitcast.440, bf16[6400,2048]{1,0:T(8,128)(2,1)} %all-gather.4.cloned.1.call-done.table, bf16[128,1024]{1,0:T(8,128)(2,1)} %multiply_convert_fusion.2.rest_0_, ...), custom_call_target="tpu_custom_call" | custom-call | flops 13421772800 | bytes 41943040 | tf_op jit(solution)/shard_map/logits/pallas_call | solution.py:635
  399.2 26.6 %rowgrads.1 = (bf16[2,6400,512]{2,1,0:T(8,128)(2,1)}, bf16[128,1024]{1,0:T(8,128)(2,1)S(1)}, bf16[128,1024]{1,0:T(8,128)(2,1)}, bf16[128,1024]{1,0:T(8,128)(2,1)}, bf16[128,1024]{1,0:T(8,128)(2,1)}) custom-call(s32[1,512]{1,0:T(1,128)S(1)} %bitcast.441, f32[10,8,512]{2,1,0:T(8,128)S(1)} %exponential_multiply_fusion.scale, f32[1,512]{1,0:T(1,128)S(1)} %copy-done.51, ...), custom_call_target="tpu_custom_call" | custom-call | flops 13421772800 | bytes 54525952 | tf_op jit(solution)/shard_map/rowgrads/pallas_call | solution.py:696
  437.9 9.1 collective-permute-done.58
  498.7 19.2 %back.2 = (bf16[528,1024]{1,0:T(8,128)(2,1)}, bf16[528,384]{1,0:T(8,128)(2,1)S(1)}, f32[8,512]{1,0:T(8,128)S(1)}, f32[8,256]{1,0:T(8,128)S(1)}, f32[8,128]{1,0:T...) custom-call(s32[1]{0:T(128)} %bitcast.7.scal, ...), custom_call_target="tpu_custom_call" | custom-call | flops 2147483648 | bytes 16777216 | tf_op jit(solution)/shard_map/back/pallas_call | solution.py:84
  539.6 11.9 %collective-permute-done.73 = bf16[128,1024]{1,0:T(8,128)(2,1)S(1)} collective-permute-done((bf16[128,1024]{1,0:T(8,128)(2,1)}, bf16[128,1024]{1,0:T(8,128)(2,1)S(1)}, u32[]{:S(2)}, u32[]{:S(2)}) %collective-permute-start.73) | collective-permute-done | bytes 262176 | tf_op jit(solution)/shard_map/ppermute | solution.py:68
  602.4 18.9 %back.3 = (bf16[528,1024]{1,0:T(8,128)(2,1)}, bf16[528,384]{1,0:T(8,128)(2,1)S(1)}, f32[8,512]{1,0:T(8,128)S(1)}, f32[8,256]{1,0:T(8,128)S(1)}, f32[8,128]{1,0:T...) custom-call(s32[1]{0:T(128)} %bitcast.7.scal, ...), custom_call_target="tpu_custom_call" | custom-call | flops 2147483648 | bytes 16777216 | tf_op jit(solution)/shard_map/back/pallas_call | solution.py:84
  649.7 11.1 %gather_fusion.2 = bf16[192,128,128]{2,1,0:T(8,128)(2,1)} fusion(bf16[192,128,128]{2,1,0:T(8,128)(2,1)} %pad_maximum_fusion.1, s32[1024]{0:T(1024)} %pad_clamp_fusion), kind=kCustom, calls=%fused_computation.2 | custom fusion | bytes 12583680 | tf_op jit(solution)/shard_map/gather | solution.py:1103
  674.2 22.4 %tablegrads.1 = bf16[6400,2048]{1,0:T(8,128)(2,1)} custom-call(bf16[2,6400,512]{2,1,0:T(8,128)(2,1)} %get-tuple-element.188.q_in, bf16[128,1024]{1,0:T(8,128)(2,1)} %multiply_convert_fusion.2.rest_0_, bf16[128,1024]{1,0:T(8,128)(2,1)} %collective-permute-done.51.rest_1_, bf16[128,1024]{1,0:T(8,128)(2,1)} %collective-permute-done.52.rest_2_, ...), custom_call_target="tpu_custom_call" | custom-call | flops 13421772800 | bytes 41943040 | tf_op jit(solution)/shard_map/tablegrads/pallas_call | solution.py:737
  723.2 11.2 %collective-permute-done.99.rest_2_ = bf16[128,1024]{1,0:T(8,128)(2,1)S(1)} collective-permute-done((bf16[128,1024]{1,0:T(8,128)(2,1)S(1)}, bf16[128,1024]{1,0:T(8,128)(2,1)S(1)}, u32[]{:S(2)}, u32[]{:S(2)}) %collective-permute-start.99) | collective-permute-done | bytes 262176 | tf_op jit(solution)/shard_map/ppermute | solution.py:68
  735.9 17.9 %reduce-scatter.3.cloned.1.call-done = bf16[1,3904,128]{2,1,0:T(8,128)(2,1)} async-done(((bf16[8,3904,128]{2,1,0:T(8,128)(2,1)}), bf16[1,3904,128]{2,1,0:T(8,128)(2,1)}) %reduce-scatter.3.cloned.1.call-update) | async-done | bytes 999440 | tf_op jit(solution)/shard_map/reduce_scatter | solution.py:1116
  772.8 9.9 collective-permute-done.104.rest_4_
  786.1 134.1 %reduce-scatter.5.cloned.1.call-done.share = bf16[6400,256]{1,0:T(8,128)(2,1)} async-done(((bf16[6400,2048]{1,0:T(8,128)(2,1)}), bf16[6400,256]{1,0:T(8,128)(2,1)}) %reduce-scatter.5.cloned.1.call-update) | async-done | bytes 3276816 | tf_op jit(solution)/shard_map/reduce_scatter | solution.py:1025
  922.2 28.5 %addrows.1 = (f32[6286,256]{1,0:T(8,128)}, f32[1,256]{1,0:T(1,128)S(1)}) custom-call(s32[2]{0:T(128)S(1)} %copy-done.40, s32[4096]{0:T(1024)S(1)} %copy-done.28, bf16[6400,256]{1,0:T(8,128)(2,1)S(1)} %copy-done.2, bf16[512,256]{1,0:T(8,128)(2,1)S(1)} %get-tuple-element.189.rest_0_, bf16[512,256]{1,0:T(8,128)(2,1)S(1)} %collective-permute-done.101.rest_1_, ...), custom_call_target="tpu_custom_call" | custom-call | bytes 31457280 | tf_op jit(solution)/shard_map/addrows/pallas_call | solution.py:84
  997.5 13.8 %multiply_subtract_fusion = (f32[6286,256]{1,0:T(8,128)}, f32[6286,256]{1,0:T(8,128)}, f32[6286,256]{1,0:T(8,128)}) fusion(f32[6286,256]{1,0:T(8,128)S(1)} %bitcast.444, f32[]{:T(128)} %bitcast.116, f32[]{:T(128)} %bitcast.115, f32[6286,256]{1,0:T(8,128)} %get-tuple-element.204, f32[]{:T(128)S(6)} %min.3, f32[6286,256]{1,0:T(8,128)} %param.33, ...), kind=kLoop, calls=%fused_computation.7 | loop fusion | flops 25747456 | bytes 45058060 | tf_op jit(solution)/shard_map/sub | solution.py:760
  (911 shorter events, 513.7 us)
Async XLA Ops:
  7.2 111.6 %all-gather.6.cloned.1.call-start = ((), (), s32[]{:S(2)}) async-start(), calls=%async_computation.5 | async-start | bytes 8994816 | tf_op jit(solution)/shard_map/all_gather | solution.py:866
  21.6 334.3 %all-gather.4.cloned.1.call-start = ((), (), s32[]{:S(2)}) async-start(), calls=%async_computation.2 | async-start | bytes 29491200 | tf_op jit(solution)/shard_map/all_gather | solution.py:901
  26.7 727.1 %reduce-scatter.3.cloned.1.call-start = ((), (), s32[]{:S(2)}) async-start(), calls=%async_computation.3 | async-start | bytes 8994816 | tf_op jit(solution)/shard_map/reduce_scatter | solution.py:1116
  121.3 42.8 %collective-permute-start.13 = (bf16[128,1024]{1,0:T(8,128)(2,1)S(1)}, bf16[128,1024]{1,0:T(8,128)(2,1)S(1)}, u32[]{:S(2)}, u32[]{:S(2)}) collective-permute-start(bf16[128,1024]{1,0:T(8,128)(2,1)S(1)} %fusion.43.rest_0_), channel_id=1, source_target_pairs={{0,1},{1,0},{2,3},{3,2},{4,5},{5,4},{6,7},{7,6},{8,9},{9,8},{10,11... | collective-permute-start | bytes 786440 | tf_op jit(solution)/shard_map/ppermute | solution.py:68
  126.5 38.4 %collective-permute-start.14 = (bf16[128,1024]{1,0:T(8,128)(2,1)S(1)}, bf16[128,1024]{1,0:T(8,128)(2,1)S(1)}, u32[]{:S(2)}, u32[]{:S(2)}) collective-permute-start(bf16[128,1024]{1,0:T(8,128)(2,1)S(1)} %fusion.43.rest_0_), channel_id=1, source_target_pairs={{0,2},{1,3},{2,0},{3,1},{4,6},{5,7},{6,4},{7,5},{8,10},{9,11},{10,... | collective-permute-start | bytes 786440 | tf_op jit(solution)/shard_map/ppermute | solution.py:68
  127.5 38.1 %collective-permute-start.15 = (bf16[128,1024]{1,0:T(8,128)(2,1)S(1)}, bf16[128,1024]{1,0:T(8,128)(2,1)S(1)}, u32[]{:S(2)}, u32[]{:S(2)}) collective-permute-start(bf16[128,1024]{1,0:T(8,128)(2,1)S(1)} %fusion.43.rest_0_), channel_id=1, source_target_pairs={{0,3},{1,2},{2,1},{3,0},{4,7},{5,6},{6,5},{7,4},{8,11},{9,10},{10,... | collective-permute-start | bytes 786440 | tf_op jit(solution)/shard_map/ppermute | solution.py:68
  128.9 30.3 %collective-permute-start.16 = (bf16[16,1024]{1,0:T(8,128)(2,1)S(1)}, bf16[16,1024]{1,0:T(8,128)(2,1)S(1)}, u32[]{:S(2)}, u32[]{:S(2)}) collective-permute-start(bf16[16,1024]{1,0:T(8,128)(2,1)S(1)} %slice.411), channel_id=1, source_target_pairs={{3,4},{7,8},{11,12},{19,20},{23,24},{27,28}} | collective-permute-start | bytes 98312 | tf_op jit(solution)/shard_map/ppermute | solution.py:965
  129.6 30.4 %collective-permute-start.17 = (bf16[16,1024]{1,0:T(8,128)(2,1)S(1)}, bf16[16,1024]{1,0:T(8,128)(2,1)S(1)}, u32[]{:S(2)}, u32[]{:S(2)}) collective-permute-start(bf16[16,1024]{1,0:T(8,128)(2,1)S(1)} %slice.411), channel_id=1, source_target_pairs={{3,5},{7,9},{11,13},{19,21},{23,25},{27,29}} | collective-permute-start | bytes 98312 | tf_op jit(solution)/shard_map/ppermute | solution.py:965
  241.9 21.8 %collective-permute-start.33 = (bf16[128,1024]{1,0:T(8,128)(2,1)S(1)}, bf16[128,1024]{1,0:T(8,128)(2,1)S(1)}, u32[]{:S(2)}, u32[]{:S(2)}) collective-permute-start(bf16[128,1024]{1,0:T(8,128)(2,1)S(1)} %multiply_convert_fusion.3.rest_0_), channel_id=1, source_target_pairs={{0,2},{1,3},{2,0},{3,1},{4,6},{5,7},{6,4},{7,5},{8,10},{9,11},{10,... | collective-permute-start | bytes 786440 | tf_op jit(solution)/shard_map/ppermute | solution.py:68
  307.5 25.8 %collective-permute-start.48 = (bf16[128,1024]{1,0:T(8,128)(2,1)S(1)}, bf16[128,1024]{1,0:T(8,128)(2,1)S(1)}, u32[]{:S(2)}, u32[]{:S(2)}) collective-permute-start(bf16[128,1024]{1,0:T(8,128)(2,1)S(1)} %get-tuple-element.144), channel_id=1, source_target_pairs={{0,1},{1,0},{2,3},{3,2},{4,5},{5,4},{6,7},{7,6},{8,9},{9,8},{10,11... | collective-permute-start | bytes 786440 | tf_op jit(solution)/shard_map/ppermute | solution.py:68
  307.6 25.7 %collective-permute-start.49 = (bf16[128,1024]{1,0:T(8,128)(2,1)S(1)}, bf16[128,1024]{1,0:T(8,128)(2,1)S(1)}, u32[]{:S(2)}, u32[]{:S(2)}) collective-permute-start(bf16[128,1024]{1,0:T(8,128)(2,1)S(1)} %get-tuple-element.145), channel_id=1, source_target_pairs={{0,2},{1,3},{2,0},{3,1},{4,6},{5,7},{6,4},{7,5},{8,10},{9,11},{10,... | collective-permute-start | bytes 786440 | tf_op jit(solution)/shard_map/ppermute | solution.py:68
  309.4 23.9 %collective-permute-start.50 = (bf16[128,1024]{1,0:T(8,128)(2,1)S(1)}, bf16[128,1024]{1,0:T(8,128)(2,1)S(1)}, u32[]{:S(2)}, u32[]{:S(2)}) collective-permute-start(bf16[128,1024]{1,0:T(8,128)(2,1)S(1)} %get-tuple-element.146), channel_id=1, source_target_pairs={{0,3},{1,2},{2,1},{3,0},{4,7},{5,6},{6,5},{7,4},{8,11},{9,10},{10,... | collective-permute-start | bytes 786440 | tf_op jit(solution)/shard_map/ppermute | solution.py:68
  530.1 21.4 %collective-permute-start.73 = (bf16[128,1024]{1,0:T(8,128)(2,1)}, bf16[128,1024]{1,0:T(8,128)(2,1)S(1)}, u32[]{:S(2)}, u32[]{:S(2)}) collective-permute-start(bf16[128,1024]{1,0:T(8,128)(2,1)} %get-tuple-element.163), channel_id=1, source_target_pairs={{0,2},{1,3},{2,0},{3,1},{4,6},{5,7},{6,4},{7,5},{8,10},{9,11},{10,... | collective-permute-start | bytes 786440 | tf_op jit(solution)/shard_map/ppermute | solution.py:68
  564.7 21.4 %collective-permute-start.80 = (bf16[128,1024]{1,0:T(8,128)(2,1)S(1)}, bf16[128,1024]{1,0:T(8,128)(2,1)S(1)}, u32[]{:S(2)}, u32[]{:S(2)}) collective-permute-start(bf16[128,1024]{1,0:T(8,128)(2,1)S(1)} %multiply_convert_fusion.rest_0_), channel_id=1, source_target_pairs={{0,2},{1,3},{2,0},{3,1},{4,6},{5,7},{6,4},{7,5},{8,10},{9,11},{10,... | collective-permute-start | bytes 786440 | tf_op jit(solution)/shard_map/ppermute | solution.py:68
  572.0 22.0 %collective-permute-start.88 = (f32[8,128]{1,0:T(8,128)}, f32[8,128]{1,0:T(8,128)}, u32[]{:S(2)}, u32[]{:S(2)}) collective-permute-start(f32[8,128]{1,0:T(8,128)} %get-tuple-element.126), channel_id=1, source_target_pairs={{4,0},{8,4},{12,8},{20,16},{24,20},{28,24},{5,1},{9,5},{13,9},{21,... | collective-permute-start | bytes 12296 | tf_op jit(solution)/shard_map/ppermute | solution.py:950
  574.6 23.3 %collective-permute-start.89 = (f32[8,128]{1,0:T(8,128)}, f32[8,128]{1,0:T(8,128)}, u32[]{:S(2)}, u32[]{:S(2)}) collective-permute-start(f32[8,128]{1,0:T(8,128)} %get-tuple-element.126), channel_id=1, source_target_pairs={{8,0},{12,4},{24,16},{28,20},{9,1},{13,5},{25,17},{29,21},{10,2},{... | collective-permute-start | bytes 12296 | tf_op jit(solution)/shard_map/ppermute | solution.py:950
  622.6 38.2 %collective-permute-start.96 = (bf16[16,1024]{1,0:T(8,128)(2,1)S(1)}, bf16[16,1024]{1,0:T(8,128)(2,1)S(1)}, u32[]{:S(2)}, u32[]{:S(2)}) collective-permute-start(bf16[16,1024]{1,0:T(8,128)(2,1)S(1)} %get-tuple-element.185), channel_id=1, source_target_pairs={{6,3},{10,7},{14,11},{22,19},{26,23},{30,27}} | collective-permute-start | bytes 98312 | tf_op jit(solution)/shard_map/ppermute | solution.py:1070
  623.3 37.5 %collective-permute-start.97 = (bf16[16,1024]{1,0:T(8,128)(2,1)S(1)}, bf16[16,1024]{1,0:T(8,128)(2,1)S(1)}, u32[]{:S(2)}, u32[]{:S(2)}) collective-permute-start(bf16[16,1024]{1,0:T(8,128)(2,1)S(1)} %get-tuple-element.185), channel_id=1, source_target_pairs={{7,3},{11,7},{15,11},{23,19},{27,23},{31,27}} | collective-permute-start | bytes 98312 | tf_op jit(solution)/shard_map/ppermute | solution.py:1070
  631.8 29.1 %collective-permute-start.91 = (bf16[128,1024]{1,0:T(8,128)(2,1)S(1)}, bf16[128,1024]{1,0:T(8,128)(2,1)S(1)}, u32[]{:S(2)}, u32[]{:S(2)}) collective-permute-start(bf16[128,1024]{1,0:T(8,128)(2,1)S(1)} %get-tuple-element.182), channel_id=1, source_target_pairs={{0,1},{1,0},{2,3},{3,2},{4,5},{5,4},{6,7},{7,6},{8,9},{9,8},{10,11... | collective-permute-start | bytes 786440 | tf_op jit(solution)/shard_map/ppermute | solution.py:68
  673.9 246.3 %reduce-scatter.5.cloned.1.call-start = ((), (), s32[]{:S(2)}) async-start(), calls=%async_computation.4 | async-start | bytes 29491200 | tf_op jit(solution)/shard_map/reduce_scatter | solution.py:1025
  735.4 29.4 %collective-permute-start.101 = (bf16[512,256]{1,0:T(8,128)(2,1)S(1)}, bf16[512,256]{1,0:T(8,128)(2,1)S(1)}, u32[]{:S(2)}, u32[]{:S(2)}) collective-permute-start(bf16[512,256]{1,0:T(8,128)(2,1)S(1)} %get-tuple-element.190), channel_id=1, source_target_pairs={{0,4},{4,0},{8,12},{12,8},{16,20},{20,16},{24,28},{28,24},{1,5},{5... | collective-permute-start | bytes 786440 | tf_op jit(solution)/shard_map/ppermute | solution.py:68
  735.5 30.8 %collective-permute-start.102 = (bf16[512,256]{1,0:T(8,128)(2,1)S(1)}, bf16[512,256]{1,0:T(8,128)(2,1)S(1)}, u32[]{:S(2)}, u32[]{:S(2)}) collective-permute-start(bf16[512,256]{1,0:T(8,128)(2,1)S(1)} %get-tuple-element.191), channel_id=1, source_target_pairs={{0,8},{4,12},{8,0},{12,4},{16,24},{20,28},{24,16},{28,20},{1,9},{5... | collective-permute-start | bytes 786440 | tf_op jit(solution)/shard_map/ppermute | solution.py:68
  764.7 21.4 %collective-permute-start.105 = (bf16[512,256]{1,0:T(8,128)(2,1)S(1)}, bf16[512,256]{1,0:T(8,128)(2,1)S(1)}, u32[]{:S(2)}, u32[]{:S(2)}) collective-permute-start(bf16[512,256]{1,0:T(8,128)(2,1)S(1)} %get-tuple-element.194), channel_id=1, source_target_pairs={{0,20},{4,16},{8,28},{12,24},{16,4},{20,0},{24,12},{28,8},{1,21},{... | collective-permute-start | bytes 786440 | tf_op jit(solution)/shard_map/ppermute | solution.py:68
  764.8 21.4 %collective-permute-start.106 = (bf16[512,256]{1,0:T(8,128)(2,1)S(1)}, bf16[512,256]{1,0:T(8,128)(2,1)S(1)}, u32[]{:S(2)}, u32[]{:S(2)}) collective-permute-start(bf16[512,256]{1,0:T(8,128)(2,1)S(1)} %get-tuple-element.195), channel_id=1, source_target_pairs={{0,24},{4,28},{8,16},{12,20},{16,8},{20,12},{24,0},{28,4},{1,25},{... | collective-permute-start | bytes 786440 | tf_op jit(solution)/shard_map/ppermute | solution.py:68
  (307 other events, 3522.0 us)
Sparse Core Ops, SparseCore 0:
  21.7 55.0 all-gather.5
  79.3 137.2 all-gather.3
  674.0 79.7 reduce-scatter.2
  757.8 162.3 reduce-scatter.4

commit v2 on v1

--- a/solution.py
+++ b/solution.py
@@ -60,12 +60,65 @@
 
 
 def head_map(inner):
-    return (iota((LANES, inner), 0) == iota((LANES, inner), 1) // P_SIZE).astype(F32)
+    return (iota((LANES, inner), 0) == iota((LANES, inner), 1) // P_SIZE).astype(F32).astype(BF)
 
 
 def swap(x, axis, offset):
     size = lax.axis_size(axis)
     return lax.ppermute(x, axis, [(i, i ^ offset) for i in range(size)])
+
+
+def halves(x):
+    high = x.astype(BF)
+    return high, (x - high.astype(F32)).astype(BF)
+
+
+def thirds(x):
+    high = x.astype(BF)
+    rest = x - high.astype(F32)
+    mid = rest.astype(BF)
+    return high, mid, (rest - mid.astype(F32)).astype(BF)
+
+
+def widen(x, expand):
+    high, low = halves(x)
+    twice = jnp.concatenate([expand, expand], axis=0)
+    return nn(jnp.concatenate([high, low], axis=1), twice)
+
+
+def narrow(x, expand):
+    high, low = halves(x)
+    return nt_dot(high, expand) + nt_dot(low, expand)
+
+
+def tri_sum(tri, x):
+    wide = nn(tri, jnp.concatenate(thirds(x), axis=1))
+    size = x.shape[1]
+    return wide[:, :size] + wide[:, size : 2 * size] + wide[:, 2 * size :]
+
+
+def lanes3(column):
+    high, mid, low = thirds(column)
+    lane = iota((column.shape[0], LANES), 1)
+    zero = jnp.zeros((column.shape[0], LANES), F32)
+    wide = jnp.where(lane == 0, high.astype(F32), zero)
+    wide = jnp.where(lane == 1, mid.astype(F32), wide)
+    return jnp.where(lane == 2, low.astype(F32), wide).astype(BF)
+
+
+def column3(wide):
+    return wide[:, 0:1] + wide[:, 1:2] + wide[:, 2:3]
+
+
+def rows3(line, inner):
+    high, mid, low = thirds(line)
+    at = iota((RIM, LANES), 0)
+    wide = jnp.where(at == 0, high.astype(F32), 0.0)
+    wide = jnp.where(at == 1, mid.astype(F32), wide)
+    wide = jnp.where(at == 2, low.astype(F32), wide)
+    if inner > LANES:
+        wide = jnp.concatenate([wide, jnp.zeros((RIM, inner - LANES), F32)], axis=1)
+    return wide.astype(BF)
 
 
 def sigmoid(x):
@@ -98,34 +151,56 @@
     return jax.ShapeDtypeStruct(shape, dtype)
 
 
-def look_kernel(groups, rows, scal, idx, mask_ref, table, *rest):
-    outs, work = rest[:groups], rest[groups]
+def look_kernel(groups, rows, scal, code, table, *rest):
+    outs, listed, count, work = rest[:groups], rest[groups], rest[groups + 1], rest[groups + 2]
     place = scal[0]
+    total = groups * rows
+
+    def fill(step, carry):
+        work[pl.ds(pl.multiple_of(step * rows, rows), rows), :] = jnp.zeros((rows, table.shape[1]), F32)
+        return carry
+
+    lax.fori_loop(0, groups, fill, 0)
+
+    def note(step, found):
+        for lane in range(8):
+            at = step * 8 + lane
+            listed[found] = at
+            found = found + 1 + lax.shift_right_arithmetic(code[at], 31)
+        return found
+
+    found = lax.fori_loop(0, total // 8, note, 0)
+    for lane in range(8):
+        listed[found + lane] = total
+    count[0] = found
+
+    def turn(step, carry):
+        for lane in range(8):
+            at = listed[step * 8 + lane]
+            work[pl.ds(at, 1), :] = table[pl.ds(code[at], 1), :]
+        return carry
+
+    lax.fori_loop(0, (found + 7) // 8, turn, 0)
     for off in range(groups):
-        base = (place ^ off) * rows
-
-        def turn(step, carry):
-            for lane in range(8):
-                at = step * 8 + lane
-                work[pl.ds(at, 1), :] = table[pl.ds(idx[base + at], 1), :]
-            return carry
-
-        lax.fori_loop(0, rows // 8, turn, 0)
-        keep = mask_ref[pl.ds(pl.multiple_of(base, rows), rows), :]
-        outs[off][...] = jnp.where(keep > 0, work[...], 0.0).astype(BF)
-
-
-def gather_rows(scal, idx, keep, table, groups, rows):
+        base = pl.multiple_of((place ^ off) * rows, rows)
+        outs[off][...] = work[pl.ds(base, rows), :].astype(BF)
+
+
+def gather_rows(scal, code, table, groups, rows):
     cols = table.shape[1]
-    return call(
+    total = groups * rows
+    vmem = pl.BlockSpec(memory_space=pltpu.VMEM)
+    smem = pl.BlockSpec(memory_space=pltpu.SMEM)
+    return pl.pallas_call(
         functools.partial(look_kernel, groups, rows),
-        "look",
-        [sds((rows, cols), BF)] * groups,
-        (scal, idx, keep, table),
-        smem=(0, 1),
-        scratch=[pltpu.VMEM((rows, cols), F32)],
-        moved=30 * MIB,
-    )
+        out_shape=[sds((rows, cols), BF)] * groups + [sds((total + 8,), jnp.int32), sds((1,), jnp.int32)],
+        in_specs=[smem, smem, vmem],
+        out_specs=[vmem] * groups + [smem, smem],
+        scratch_shapes=[pltpu.VMEM((total + 8, cols), F32)],
+        compiler_params=pltpu.CompilerParams(vmem_limit_bytes=48 * MIB),
+        cost_estimate=pl.CostEstimate(flops=0, bytes_accessed=30 * MIB, transcendentals=0),
+        name="look",
+    )(scal, code, table)
 
 
 def join_kernel(groups, shards, own, scal, *rest):
@@ -182,39 +257,233 @@
     )
 
 
-def add_kernel(groups, rows, vrows, scal, idx, share, *rest):
-    parts, out, square, work, bins = (rest[:groups], rest[groups], rest[groups + 1], rest[-2], rest[-1])
+def add_kernel(groups, rows, vrows, scal, code, listed, count, share, *rest):
+    parts, out, square, work = rest[:groups], rest[groups], rest[groups + 1], rest[groups + 2]
     place = scal[0]
-    bins[0:vrows, :] = share[0:vrows, :].astype(F32)
+    out[...] = share[0:vrows, :].astype(F32)
     for off in range(groups):
-        base = (place ^ off) * rows
-        work[...] = parts[off][...].astype(F32)
-
-        def turn(step, carry):
-            for lane in range(8):
-                at = step * 8 + lane
-                to = pl.ds(idx[base + at], 1)
-                bins[to, :] = bins[to, :] + work[pl.ds(at, 1), :]
-            return carry
-
-        lax.fori_loop(0, rows // 8, turn, 0)
-    total = bins[0:vrows, :]
-    out[...] = total
+        base = pl.multiple_of((place ^ off) * rows, rows)
+        work[pl.ds(base, rows), :] = parts[off][...].astype(F32)
+    work[groups * rows :, :] = jnp.zeros((8, work.shape[1]), F32)
+
+    def turn(step, carry):
+        for lane in range(8):
+            at = listed[step * 8 + lane]
+            to = pl.ds(code[at], 1)
+            out[to, :] = out[to, :] + work[pl.ds(at, 1), :]
+        return carry
+
+    lax.fori_loop(0, (count[0] + 7) // 8, turn, 0)
+    total = out[...]
     square[...] = jnp.sum(total * total, axis=0, keepdims=True)
 
 
-def add_rows(scal, idx, share, parts, vrows):
+def add_rows(scal, code, listed, count, share, parts, vrows):
     cols = share.shape[1]
     rows = parts[0].shape[0]
     return call(
         functools.partial(add_kernel, len(parts), rows, vrows),
         "addrows",
         [sds((vrows, cols), F32), sds((1, cols), F32)],
-        (scal, idx, share, *parts),
-        smem=(0, 1),
-        scratch=[pltpu.VMEM((rows, cols), F32), pltpu.VMEM((vrows + 8, cols), F32)],
+        (scal, code, listed, count, share, *parts),
+        smem=(0, 1, 2, 3),
+        scratch=[pltpu.VMEM((rows * len(parts) + 8, cols), F32)],
         moved=30 * MIB,
     )
+
+
+def tiles_kernel(slots_each, zx_count, per_layer, layers, slot, tiles, *outs):
+    for layer in range(layers):
+        for at in range(per_layer):
+            where = slot[0, layer * per_layer + at]
+            owner = where // slots_each
+            first = pl.multiple_of((where % slots_each) * BLK, BLK)
+            tile = tiles[owner, pl.ds(first, BLK), :]
+            if at < zx_count:
+                wide = outs[2 * layer].shape[1] // BLK
+                row, col = at // wide, at % wide
+                out = outs[2 * layer]
+            else:
+                wide = D // BLK
+                row, col = (at - zx_count) // wide, (at - zx_count) % wide
+                out = outs[2 * layer + 1]
+            out[row * BLK : (row + 1) * BLK, col * BLK : (col + 1) * BLK] = tile
+
+
+def place_tiles(slot, tiles, slots_each, inner, zx_count, per_layer):
+    return call(
+        functools.partial(tiles_kernel, slots_each, zx_count, per_layer, L),
+        "placetiles",
+        [sds((D, 2 * inner), BF), sds((inner, D), BF)] * L,
+        (slot, tiles),
+        smem=(0,),
+        moved=14 * MIB,
+    )
+
+
+def norm_rows(values, gain):
+    return values * lax.rsqrt(jnp.mean(values * values, axis=-1, keepdims=True) + NORM_EPS) * gain
+
+
+def total_of(parts):
+    total = parts[0][...].astype(F32)
+    for part in parts[1:]:
+        total = total + part[...].astype(F32)
+    return total
+
+
+def enter_kernel(count, *refs):
+    parts, (gain, residual, normed) = refs[:count], refs[count:]
+    total = total_of(parts)
+    residual[...] = total
+    normed[...] = norm_rows(total, gain[...]).astype(BF)
+
+
+def enter(parts, gain):
+    own = parts[0].shape[0]
+    return call(
+        functools.partial(enter_kernel, len(parts)),
+        "enter",
+        [sds((own, D), F32), sds((own, D), BF)],
+        (*parts, gain),
+        moved=2 * MIB,
+    )
+
+
+def join_residual_kernel(count, *refs):
+    parts, (before, gain, residual, branch, factor, normed) = refs[:count], refs[count:]
+    total = total_of(parts)
+    scale = lax.rsqrt(column3(total[:, D:]) / DI + NORM_EPS)
+    branch[...] = total[:, :D]
+    factor[...] = scale
+    after = before[...] + scale * total[:, :D]
+    residual[...] = after
+    normed[...] = norm_rows(after, gain[...]).astype(BF)
+
+
+def join_residual(parts, before, gain):
+    own = before.shape[0]
+    return call(
+        functools.partial(join_residual_kernel, len(parts)),
+        "residual",
+        [sds((own, D), F32), sds((own, D), F32), sds((own, 1), F32), sds((own, D), BF)],
+        (*parts, before, gain),
+        moved=3 * MIB,
+    )
+
+
+def back_rows_kernel(count, rim_count, last, *refs):
+    parts, refs = refs[:count], refs[count:]
+    rims, refs = refs[:rim_count], refs[rim_count:]
+    residual, gain, refs = refs[0], refs[1], refs[2:]
+    grad_in = None
+    if rim_count:
+        grad_in, refs = refs[0], refs[1:]
+    if not last:
+        branch, factor, refs = refs[0], refs[1], refs[2:]
+    if rim_count:
+        grad_out, payload, gain_grad, work = refs
+    else:
+        grad_out, payload, gain_grad = refs
+    grad = total_of(parts)
+    if rim_count:
+        work[...] = grad
+        own = work.shape[0]
+        work[own - RIM :, :] += total_of(rims)
+        grad = work[...]
+    values = residual[...]
+    inv = lax.rsqrt(jnp.mean(values * values, axis=-1, keepdims=True) + NORM_EPS)
+    gain_grad[...] = jnp.sum(grad * values * inv, axis=0, keepdims=True)
+    scaled = grad * gain[...]
+    result = inv * scaled - values * (inv * inv * inv) * jnp.mean(
+        scaled * values, axis=-1, keepdims=True
+    )
+    if grad_in is not None:
+        result = grad_in[...] + result
+    grad_out[...] = result
+    if last:
+        payload[...] = result.astype(BF)
+    else:
+        scale = factor[...]
+        payload[:, :D] = (scale * result).astype(BF)
+        inner_rows = jnp.sum(result * branch[...], axis=-1, keepdims=True)
+        payload[:, D:] = lanes3(scale * scale * scale * inner_rows / DI)
+
+
+def back_rows(parts, rims, residual, gain, grad_in, below):
+    own = residual.shape[0]
+    last = below is None
+    args = (*parts, *rims, residual, gain)
+    if rims:
+        args = (*args, grad_in)
+    if not last:
+        args = (*args, *below)
+    return call(
+        functools.partial(back_rows_kernel, len(parts), len(rims), last),
+        "backrows",
+        [
+            sds((own, D), F32),
+            sds((own, D if last else D + LANES), BF),
+            sds((1, D), F32),
+        ],
+        args,
+        scratch=[pltpu.VMEM((own, D), F32)] if rims else [],
+        moved=4 * MIB,
+    )
+
+
+def sum_kernel(groups, shards, x_ref, o_ref, mid, from_shards, from_groups, send, recv):
+    place, shard = lax.axis_index("dp"), lax.axis_index("tensor")
+    peers = [(place, shard ^ off) for off in range(1, shards)]
+    peers += [(place ^ off, shard) for off in range(1, groups)]
+    barrier = pltpu.get_barrier_semaphore()
+    for peer in peers:
+        pl.semaphore_signal(barrier, inc=1, device_id=peer, device_id_type=pl.DeviceIdType.MESH)
+    pl.semaphore_wait(barrier, len(peers))
+
+    def exchange(source, slots, first, some):
+        copies = []
+        for i, peer in enumerate(some):
+            copy = pltpu.make_async_remote_copy(
+                src_ref=source,
+                dst_ref=slots.at[i],
+                send_sem=send.at[first + i],
+                recv_sem=recv.at[first + i],
+                device_id=peer,
+                device_id_type=pl.DeviceIdType.MESH,
+            )
+            copy.start()
+            copies.append(copy)
+        for copy in copies:
+            copy.wait()
+        total = source[...]
+        for i in range(len(some)):
+            total = total + slots[i]
+        return total
+
+    mid[...] = exchange(x_ref, from_shards, 0, peers[: shards - 1])
+    o_ref[...] = exchange(mid, from_groups, shards - 1, peers[shards - 1 :])
+
+
+def sum_everywhere(x, groups, shards):
+    count = groups + shards - 2
+    return pl.pallas_call(
+        functools.partial(sum_kernel, groups, shards),
+        out_shape=sds((8, LANES), F32),
+        in_specs=[pl.BlockSpec(memory_space=pltpu.VMEM)],
+        out_specs=pl.BlockSpec(memory_space=pltpu.VMEM),
+        scratch_shapes=[
+            pltpu.VMEM((8, LANES), F32),
+            pltpu.VMEM((shards - 1, 8, LANES), F32),
+            pltpu.VMEM((groups - 1, 8, LANES), F32),
+            pltpu.SemaphoreType.DMA((count,)),
+            pltpu.SemaphoreType.DMA((count,)),
+        ],
+        compiler_params=pltpu.CompilerParams(
+            collective_id=1, has_side_effects=True, vmem_limit_bytes=8 * MIB
+        ),
+        name="sumall",
+    )(x)
 
 
 def conv_sum(raw, params, rows, lanes):
@@ -228,7 +497,7 @@
     blocks, rest = rest[:shards], rest[shards:]
     rims, rest = rest[:shards], rest[shards:]
     wzx, wside, chan, bcp, head = rest[:5]
-    normed, zx, side, yloc, final, tot_out, c_out, cum_out, xs_scr = rest[5:]
+    normed, zx, side, yloc, final, c_out, cum_out, xs_scr = rest[5:]
     shard = scal[0]
     rows = own * shards
     inner = chan.shape[1]
@@ -249,21 +518,22 @@
     dt = softplus(side[RIM:, 2 * N :] + head[0:1, :])
     rate = -dt * jnp.exp(head[1:2, :])
     expand = head_map(inner)
-    skip = nn(head[...], expand, HIGHEST)[2:3, :]
+    skip = widen(head[...], expand)[2:3, :]
     lower = (iota((SPAN, SPAN), 0) >= iota((SPAN, SPAN), 1)).astype(F32)
+    lower_low = lower.astype(BF)
     first_half = iota((SPAN, LANES), 1) < P_SIZE
     state = None
     base = jnp.zeros((1, LANES), F32)
     for span in range(rows // SPAN):
         here = slice(span * SPAN, (span + 1) * SPAN)
-        cum = nn(lower, rate[here], HIGHEST)
+        cum = tri_sum(lower_low, rate[here])
         cum_t = cum.T
         tot = cum[SPAN - 1 : SPAN, :]
         keys = bc[here, :N]
         queries = bc[here, N:]
         scores = nt_dot(queries, keys)
         xs = xs_scr[here, :]
-        scaled = xs * nn(dt[here], expand, HIGHEST)
+        scaled = xs * widen(dt[here], expand)
         scaled_low = scaled.astype(BF)
         pieces = []
         for pair in range(inner // LANES):
@@ -276,17 +546,17 @@
             pieces.append(jnp.where(first_half, both[0], both[1]))
         y = jnp.concatenate(pieces, axis=1) + skip * xs
         if state is not None:
-            y = y + nn(jnp.exp(cum), expand, HIGHEST) * nn(queries, state.astype(BF))
+            y = y + widen(jnp.exp(cum), expand) * nn(queries, state.astype(BF))
         yloc[here, :] = y
-        tail = nn(jnp.exp(tot - cum), expand, HIGHEST)
+        tail = widen(jnp.exp(tot - cum), expand)
         fresh = tn(keys, (scaled * tail).astype(BF))
         if state is not None:
-            fresh = fresh + nn(jnp.exp(tot), expand, HIGHEST) * state
+            fresh = fresh + widen(jnp.exp(tot), expand) * state
         state = fresh
         cum_out[here, :] = cum + base
         base = base + tot
-    final[...] = state.astype(BF)
-    tot_out[...] = jnp.broadcast_to(base, tot_out.shape)
+    final[0:N, :] = state.astype(BF)
+    final[N:, :] = rows3(base, inner)
 
 
 def mixer_front(scal, blocks, rims, wzx, wside, chan, bcp, head):
@@ -302,8 +572,7 @@
             sds((rows + RIM, 2 * inner), F32),
             sds((rows + RIM, 2 * N + LANES), F32),
             sds((rows, inner), F32),
-            sds((N, inner), BF),
-            sds((8, LANES), F32),
+            sds((N + RIM, inner), BF),
             sds((rows, N), BF),
             sds((rows, LANES), F32),
         ],
@@ -315,48 +584,48 @@
     )
 
 
-def chain(parts, tots, expand):
+def chain(parts, expand):
     total = None
     past = jnp.zeros((1, LANES), F32)
-    for part, tot in zip(parts, tots):
-        term = nn(jnp.exp(past), expand, HIGHEST) * part[...].astype(F32)
+    for part in parts:
+        term = widen(jnp.exp(past), expand) * part[0:N, :].astype(F32)
         total = term if total is None else total + term
-        past = past + tot[0:1, :]
+        past = past + jnp.sum(part[N:, :LANES].astype(F32), axis=0, keepdims=True)
     return total
 
 
 def middle_kernel(shards, own, hops, scal, *rest):
-    states, tots, rest = rest[:hops], rest[hops : 2 * hops], rest[2 * hops :]
+    states, rest = rest[:hops], rest[hops:]
     yloc, zx, c_in, cum, wout, chan = rest[:6]
-    y_out, s_out, square = rest[6:9]
-    parts, work = rest[9 : 9 + shards], rest[-1]
+    y_out, s_out = rest[6:8]
+    parts, work = rest[8 : 8 + shards], rest[-1]
     shard = scal[0]
     rows, inner = yloc.shape
     expand = head_map(inner)
-    state = chain(states, tots, expand)
+    state = chain(states, expand)
     s_out[...] = state
-    y = yloc[...] + nn(jnp.exp(cum[...]), expand, HIGHEST) * nn(c_in[...], state.astype(BF))
+    y = yloc[...] + widen(jnp.exp(cum[...]), expand) * nn(c_in[...], state.astype(BF))
     y_out[...] = y
     z = zx[RIM:, :inner]
     gated = y * (z * sigmoid(z))
-    square[...] = nt_dot(jnp.ones((8, inner), F32), gated * gated, HIGHEST)
-    work[...] = nn((gated * chan[5:6, :]).astype(BF), wout[...]).astype(BF)
+    work[:, :D] = nn((gated * chan[5:6, :]).astype(BF), wout[...]).astype(BF)
+    work[:, D:] = lanes3(jnp.sum(gated * gated, axis=1, keepdims=True))
     for off in range(shards):
         at = pl.multiple_of((shard ^ off) * own, own)
         parts[off][...] = work[pl.ds(at, own), :]
 
 
-def mixer_middle(scal, states, tots, yloc, zx, c_in, cum, wout, chan, shards):
+def mixer_middle(scal, states, yloc, zx, c_in, cum, wout, chan, shards):
     rows, inner = yloc.shape
     own = rows // shards
     return call(
         functools.partial(middle_kernel, shards, own, len(states)),
         "middle",
-        [sds((rows, inner), F32), sds((N, inner), F32), sds((8, rows), F32)]
-        + [sds((own, D), BF)] * shards,
-        (scal, *states, *tots, yloc, zx, c_in, cum, wout, chan),
+        [sds((rows, inner), F32), sds((N, inner), F32)]
+        + [sds((own, D + LANES), BF)] * shards,
+        (scal, *states, yloc, zx, c_in, cum, wout, chan),
         smem=(0,),
-        scratch=[pltpu.VMEM((rows, D), BF)],
+        scratch=[pltpu.VMEM((rows, D + LANES), BF)],
         flops=2 * rows * D * inner,
         moved=8 * MIB,
     )
@@ -364,13 +633,14 @@
 
 def gate_back_kernel(shards, own, scal, *rest):
     blocks, rest = rest[:shards], rest[shards:]
-    coef, wout, y_in, zx, c_in, cum, chan = rest[:7]
-    grads, u_out, dy_out, dz_out, state_out, gain_out = rest[7:]
+    wout, y_in, zx, c_in, cum, chan = rest[:6]
+    grads, u_out, dy_out, dz_out, state_out, gain_out, coef = rest[6:]
     shard = scal[0]
     inner = chan.shape[1]
     for off in range(shards):
         at = pl.multiple_of((shard ^ off) * own, own)
-        grads[pl.ds(at, own), :] = blocks[off][...]
+        grads[pl.ds(at, own), :] = blocks[off][:, :D]
+        coef[pl.ds(at, own), :] = column3(blocks[off][:, D:].astype(F32))
     du = nt_dot(grads[...], wout[...])
     z = zx[RIM:, :inner]
     y = y_in[...]
@@ -384,11 +654,13 @@
     dy = dgated * silu
     dy_out[...] = dy
     dz_out[...] = (dgated * y * (sig * (1.0 + z * (1.0 - sig)))).astype(BF)
-    grown = nn(jnp.exp(cum[...]), head_map(inner), HIGHEST)
-    state_out[...] = tn(c_in[...], (dy * grown).astype(BF)).astype(BF)
-
-
-def gate_back(scal, blocks, coef, wout, y, zx, c_in, cum, chan):
+    grown = widen(jnp.exp(cum[...]), head_map(inner))
+    state_out[0:N, :] = tn(c_in[...], (dy * grown).astype(BF)).astype(BF)
+    rows = dy.shape[0]
+    state_out[N:, :] = rows3(cum[rows - 1 : rows, :], inner)
+
+
+def gate_back(scal, blocks, wout, y, zx, c_in, cum, chan):
     shards = len(blocks)
     own = blocks[0].shape[0]
     rows, inner = y.shape
@@ -400,11 +672,12 @@
             sds((rows, inner), BF),
             sds((rows, inner), F32),
             sds((rows, inner), BF),
-            sds((N, inner), BF),
+            sds((N + RIM, inner), BF),
             sds((1, inner), F32),
         ],
-        (scal, *blocks, coef, wout, y, zx, c_in, cum, chan),
+        (scal, *blocks, wout, y, zx, c_in, cum, chan),
         smem=(0,),
+        scratch=[pltpu.VMEM((rows, 1), F32)],
         flops=2 * rows * D * inner,
         moved=10 * MIB,
     )
@@ -431,7 +704,7 @@
 
 
 def back_kernel(shards, own, hops, scal, *rest):
-    states, tots, rest = rest[:hops], rest[hops : 2 * hops], rest[2 * hops :]
+    states, rest = rest[:hops], rest[hops:]
     s_in, zx, side, dy_in, dz_in, y_in, wzx, wside, chan, bcp, head = rest[:11]
     dzx, dside, chan_out, bcp_out, head_out, rim_out = rest[11:17]
     parts, rest = rest[17 : 17 + shards], rest[17 + shards :]
@@ -447,22 +720,23 @@
     dt = softplus(raw_dt)
     grow = jnp.exp(head[1:2, :])
     rate = -dt * grow
-    skip = nn(head[...], expand, HIGHEST)[2:3, :]
-    lower = (iota((SPAN, SPAN), 0) >= iota((SPAN, SPAN), 1)).astype(F32)
+    skip = widen(head[...], expand)[2:3, :]
+    lower_low = (iota((SPAN, SPAN), 0) >= iota((SPAN, SPAN), 1)).astype(F32).astype(BF)
     upper = (iota((SPAN, SPAN), 0) <= iota((SPAN, SPAN), 1)).astype(F32)
+    upper_low = upper.astype(BF)
     first_half = iota((SPAN, LANES), 1) < P_SIZE
     spans = rows // SPAN
     cums, starts = [], [s_in[...]]
     for span in range(spans):
         here = slice(span * SPAN, (span + 1) * SPAN)
-        cum = nn(lower, rate[here], HIGHEST)
+        cum = tri_sum(lower_low, rate[here])
         cums.append(cum)
         if span + 1 < spans:
             tot = cum[SPAN - 1 : SPAN, :]
-            scale = nn(dt[here] * jnp.exp(tot - cum), expand, HIGHEST)
+            scale = widen(dt[here] * jnp.exp(tot - cum), expand)
             fresh = tn(bc[here, :N], (xs_scr[here, :] * scale).astype(BF))
-            starts.append(nn(jnp.exp(tot), expand, HIGHEST) * starts[-1] + fresh)
-    dstate = chain(states, tots, expand)
+            starts.append(widen(jnp.exp(tot), expand) * starts[-1] + fresh)
+    dstate = chain(states, expand)
     dsx[0:RIM, :] = jnp.zeros((RIM, inner), F32)
     dsx[RIM + rows :, :] = jnp.zeros((RIM, inner), F32)
     dsbc[0:RIM, :] = jnp.zeros((RIM, 2 * N), F32)
@@ -486,7 +760,7 @@
         xs = xs_scr[here, :]
         dy = dy_in[here, :]
         dy_low = dy.astype(BF)
-        dt_wide = nn(dt[here], expand, HIGHEST)
+        dt_wide = widen(dt[here], expand)
         scaled = xs * dt_wide
         scaled_low = scaled.astype(BF)
         dscores_t = jnp.zeros((SPAN, SPAN), F32)
@@ -505,8 +779,8 @@
             pieces.append(jnp.where(first_half, both[0], both[1]))
         dscaled = jnp.concatenate(pieces, axis=1)
         dscores_low = dscores_t.astype(BF)
-        grown = nn(jnp.exp(cum), expand, HIGHEST)
-        tail = nn(jnp.exp(tot - cum), expand, HIGHEST)
+        grown = widen(jnp.exp(cum), expand)
+        tail = widen(jnp.exp(tot - cum), expand)
         dy_grown = (dy * grown).astype(BF)
         dstate_low = dstate.astype(BF)
         through = tail * nn(keys, dstate_low)
@@ -515,20 +789,20 @@
         dkeys = nn(dscores_low, queries) + nt_dot((scaled * tail).astype(BF), dstate_low)
         plain = y_in[here, :] - skip * xs
         held = scaled_low.astype(F32)
-        dcum = nt_dot(dy_low.astype(F32) * plain - held * dscaled, expand, HIGHEST)
-        tot_wide = nn(jnp.exp(tot), expand, HIGHEST)
+        dcum = narrow(dy_low.astype(F32) * plain - held * dscaled, expand)
+        tot_wide = widen(jnp.exp(tot), expand)
         over = jnp.sum(held * through, axis=0, keepdims=True) + jnp.sum(
             tot_wide * dstate * start, axis=0, keepdims=True
         )
-        dtot = nt_dot(jnp.broadcast_to(over, (8, inner)), expand, HIGHEST)[0:1, :]
-        drate = nn(upper, dcum, HIGHEST) + dtot
-        ddt = nt_dot(dscaled * xs, expand, HIGHEST) - drate * grow
+        dtot = narrow(jnp.broadcast_to(over, (8, inner)), expand)[0:1, :]
+        drate = tri_sum(upper_low, dcum) + dtot
+        ddt = narrow(dscaled * xs, expand) - drate * grow
         dgrow = dgrow + jnp.sum(drate * rate[here], axis=0, keepdims=True)
         draw = ddt * sigmoid(raw_dt[here])
         dbias = dbias + jnp.sum(draw, axis=0, keepdims=True)
         dside[there, 2 * N :] = draw.astype(BF)
         over = jnp.sum(dy * xs, axis=0, keepdims=True)
-        dskip = dskip + nt_dot(jnp.broadcast_to(over, (8, inner)), expand, HIGHEST)[0:1, :]
+        dskip = dskip + narrow(jnp.broadcast_to(over, (8, inner)), expand)[0:1, :]
         dsx[there, :] = dscaled * dt_wide + skip * dy
         dsbc[there, :N] = dkeys
         dsbc[there, N:] = dqueries
@@ -551,7 +825,7 @@
         parts[off][...] = work[pl.ds(at, own), :]
 
 
-def mixer_back(scal, states, tots, s_in, zx, side, dy, dz, y, wzx, wside, chan, bcp, head, shards):
+def mixer_back(scal, states, s_in, zx, side, dy, dz, y, wzx, wside, chan, bcp, head, shards):
     rows, inner = dy.shape
     own = rows // shards
     ext = rows + RIM
@@ -567,7 +841,7 @@
             sds((RIM, D), BF),
         ]
         + [sds((own, D), BF)] * shards,
-        (scal, *states, *tots, s_in, zx, side, dy, dz, y, wzx, wside, chan, bcp, head),
+        (scal, *states, s_in, zx, side, dy, dz, y, wzx, wside, chan, bcp, head),
         smem=(0,),
         scratch=[
             pltpu.VMEM((rows, inner), F32),
@@ -589,39 +863,32 @@
     @pl.when(step == 0)
     def _():
         for off in range(shards):
-            rows_scr[off * own : (off + 1) * own, :] = blocks[off][...]
+            rows_scr[:, off * own : (off + 1) * own] = blocks[off][...].T
         top[...] = jnp.full((1, rows), -1e30, F32)
         total[...] = jnp.zeros((1, rows), F32)
         target[...] = jnp.zeros((1, rows), F32)
         plain[...] = jnp.zeros((1, rows), F32)
 
-    at = step * PAIRS + iota((PAIRS, rows), 0)
-    valid = at < vrows
-    logits = []
-    highest = top[...]
+    padding = jnp.where(step * PAIRS + iota((PAIRS, LANES), 0) < vrows, 0.0, -1e30)
+    padding = jnp.concatenate([padding] * (rows // LANES), axis=1)
+    highest, summed, hit, whole = top[...], total[...], target[...], plain[...]
+    wanted = label[...] - 2 * step * PAIRS
+    line = 2 * iota((PAIRS, rows), 0)
     for half in range(2):
-        raw = nt_dot(table[:, half * D : (half + 1) * D], rows_scr[...])
-        highest = jnp.maximum(
-            highest, jnp.max(jnp.where(valid, raw, -1e30), axis=0, keepdims=True)
-        )
-        logits.append(raw)
-    summed = total[...] * jnp.exp(top[...] - highest)
-    hit = target[...]
-    whole = plain[...]
-    for half in range(2):
-        raw = logits[half]
-        part = jnp.where(valid, jnp.exp(raw - highest), 0.0)
-        summed = summed + jnp.sum(part, axis=0, keepdims=True)
-        hit = hit + jnp.sum(
-            jnp.where(2 * at + half == label[...], raw, 0.0), axis=0, keepdims=True
-        )
+        raw = nn(table[:, half * D : (half + 1) * D], rows_scr[...])
+        shown = raw + padding
+        before = highest
+        highest = jnp.maximum(before, jnp.max(shown, axis=0, keepdims=True))
+        part = jnp.exp(shown - highest)
+        summed = summed * jnp.exp(before - highest) + jnp.sum(part, axis=0, keepdims=True)
+        hit = hit + jnp.sum(jnp.where(line == wanted - half, raw, 0.0), axis=0, keepdims=True)
         whole = whole + jnp.sum(raw, axis=0, keepdims=True)
         p_out[half] = part.astype(BF)
+        tops[0, 8 * half : 8 * half + 8, :] = jnp.broadcast_to(highest, (8, rows))
     top[...] = highest
     total[...] = summed
     target[...] = hit
     plain[...] = whole
-    tops[...] = jnp.broadcast_to(highest, (1, 8, rows))
     stats[...] = jnp.concatenate([highest, summed, hit, whole, jnp.zeros((4, rows), F32)], axis=0)
 
 
@@ -637,7 +904,7 @@
         grid=(steps,),
         out_shape=[
             sds((2, padded, rows), BF),
-            sds((steps, 8, rows), F32),
+            sds((steps, 16, rows), F32),
             sds((8, rows), F32),
         ],
         in_specs=[
@@ -647,10 +914,10 @@
         + [pl.BlockSpec((own, D), whole)] * shards,
         out_specs=[
             pl.BlockSpec((2, PAIRS, rows), lambda i: (0, i, 0)),
-            pl.BlockSpec((1, 8, rows), lambda i: (i, 0, 0)),
+            pl.BlockSpec((1, 16, rows), lambda i: (i, 0, 0)),
             pl.BlockSpec((8, rows), whole),
         ],
-        scratch_shapes=[pltpu.VMEM((rows, D), BF)] + [pltpu.VMEM((1, rows), F32)] * 4,
+        scratch_shapes=[pltpu.VMEM((D, rows), BF)] + [pltpu.VMEM((1, rows), F32)] * 4,
         compiler_params=pltpu.CompilerParams(
             dimension_semantics=("arbitrary",), vmem_limit_bytes=48 * MIB
         ),
@@ -670,13 +937,14 @@
     def _():
         acc[...] = jnp.zeros_like(acc)
 
-    at = step * PAIRS + iota((PAIRS, rows), 0)
-    keep = jnp.where(at < vrows, weight[...], 0.0)
-    factor = scale[0, 0:1, :]
+    wanted = label[...] - 2 * step * PAIRS
+    line = 2 * iota((PAIRS, rows), 0)
+    usual = (SMOOTHING / V) * weight[...]
+    special = (1.0 - SMOOTHING + SMOOTHING / V) * weight[...]
     term = None
     for half in range(2):
-        share = jnp.where(2 * at + half == label[...], 1.0 - SMOOTHING + SMOOTHING / V, SMOOTHING / V)
-        q = (p_in[half].astype(F32) * factor - keep * share).astype(BF)
+        share = jnp.where(line == wanted - half, special, usual)
+        q = (p_in[half].astype(F32) * scale[0, 8 * half : 8 * half + 1, :] - share).astype(BF)
         q_out[half] = q
         part = tn(q, table[:, half * D : (half + 1) * D])
         term = part if term is None else term + part
@@ -699,7 +967,7 @@
         out_shape=[sds((2, padded, rows), BF)] + [sds((own, D), BF)] * shards,
         in_specs=[
             pl.BlockSpec((1, rows), whole),
-            pl.BlockSpec((1, 8, rows), lambda i: (i, 0, 0)),
+            pl.BlockSpec((1, 16, rows), lambda i: (i, 0, 0)),
             pl.BlockSpec((1, rows), whole),
             pl.BlockSpec((2, PAIRS, rows), lambda i: (0, i, 0)),
             pl.BlockSpec((PAIRS, 2 * D), lambda i: (i, 0)),
@@ -760,12 +1028,17 @@
     return (weight_in - LEARN_RATE * (direction + decay_rate * weight_in), one_next, two_next)
 
 
-def soap_update(weight_in, gradient, bases, moment_one, moment_two, factor, fix_one, fix_two):
-    gradient = gradient * factor
+def soap_turn(gradient, bases):
     left_basis = bases[..., 0, :, :]
     right_basis = bases[..., 1, :, :]
     half_turn = jnp.einsum("...ab,...ac->...bc", left_basis, gradient, precision=HIGHEST)
-    rotated = jnp.einsum("...bc,...cd->...bd", half_turn, right_basis, precision=HIGHEST)
+    return jnp.einsum("...bc,...cd->...bd", half_turn, right_basis, precision=HIGHEST)
+
+
+def soap_update(weight_in, turned_grad, bases, moment_one, moment_two, factor, fix_one, fix_two):
+    left_basis = bases[..., 0, :, :]
+    right_basis = bases[..., 1, :, :]
+    rotated = turned_grad * factor
     one_next = BETA_FIRST * moment_one + (1.0 - BETA_FIRST) * rotated
     two_next = BETA_SECOND * moment_two + (1.0 - BETA_SECOND) * rotated * rotated
     direction = one_next / fix_one / (jnp.sqrt(two_next / fix_two) + ADAM_EPS)
@@ -867,8 +1140,7 @@
     ids_all = lax.all_gather(jnp.concatenate([token_ids, labels], axis=0), "dp", axis=1, tiled=True)
     table_low = jnp.pad(vocab_table.astype(BF), ((0, padded - vrows), (0, 0)))
 
-    slot_tiles = gathered[:, : own_tiles * BLK].reshape(tiles, BLK, BLK)
-    ordered = slot_tiles[block_slot[0]]
+    placed = place_tiles(block_slot, gathered, own_tiles, inner, zx_count, per_layer)
     small = gathered[:, own_tiles * BLK :].reshape(nd, nt, piece_rows, LANES)
     side_full = (
         small[:, :, :side_part]
@@ -884,36 +1156,15 @@
     held = (local_row >= 0) & (local_row < vrows) & (all_ids % 2 == place // half)
     scal = jnp.stack([place, shard]).astype(jnp.int32)
     scal_shard = shard.astype(jnp.int32).reshape(1)
-    parts = gather_rows(
-        scal,
-        jnp.where(held, local_row, 0),
-        jnp.broadcast_to(held[:, None], (held.shape[0], 1)).astype(F32),
-        vocab_table,
-        nd,
-        rows,
-    )
+    code = jnp.concatenate([jnp.where(held, local_row, -1), jnp.zeros((8,), jnp.int32)])
+    parts = gather_rows(scal, code, vocab_table, nd, rows)
+    listed, count = parts[nd], parts[nd + 1]
     parts = [parts[0]] + [swap(parts[off], "dp", off) for off in range(1, nd)]
     parts = join_parts(scal, parts, nt, own)
-    residual = parts[0]
-    for off in range(1, nt):
-        residual = residual + swap(parts[off], "tensor", off)
-    residual = residual.astype(F32)
     table_all = lax.all_gather(table_low, "dp", axis=1, tiled=True)
 
     def layer_mats(layer_index):
-        base_index = layer_index * per_layer
-        zx_part = (
-            ordered[base_index : base_index + zx_count]
-            .reshape(D // BLK, 2 * inner // BLK, BLK, BLK)
-            .transpose(0, 2, 1, 3)
-            .reshape(D, 2 * inner)
-        )
-        out_part = (
-            ordered[base_index + zx_count : base_index + per_layer]
-            .reshape(inner // BLK, D // BLK, BLK, BLK)
-            .transpose(0, 2, 1, 3)
-            .reshape(inner, D)
-        )
+        zx_part, out_part = placed[2 * layer_index], placed[2 * layer_index + 1]
         dt_part = lax.dynamic_slice_in_dim(
             side_full[layer_index], 2 * N + shard * heads, heads, 1
         )
@@ -949,36 +1200,31 @@
         ]
         return lax.ppermute(x, "dp", pairs)
 
-    def collect(parts):
-        total = parts[0].astype(F32)
-        for off in range(1, nt):
-            total = total + swap(parts[off], "tensor", off).astype(F32)
-        return total
+    def returned(parts):
+        return [parts[0]] + [swap(parts[off], "tensor", off) for off in range(1, nt)]
 
     hops = range(1, chunks)
     mats = [layer_mats(layer_index) for layer_index in range(L)]
+    final_gain = shared_full[L * stride :][None, :]
+    gains = [mats[layer_index][3][None, :] for layer_index in range(L)] + [final_gain]
     saved = []
+    residual, normed_own = enter(returned(parts), gains[0])
     for layer_index in range(L):
         wzx, wout, wside, gain, bcp, chan, head = mats[layer_index]
-        normed_own = (residual * rms_scale(residual) * gain[None, :]).astype(BF)
         edge = normed_own[own - RIM :]
         rims = [lax.ppermute(edge, both, rim_pairs(to)) for to in range(nt)]
-        normed, zx, side, yloc, final, tot, c_out, cum = mixer_front(
+        normed, zx, side, yloc, final, c_out, cum = mixer_front(
             scal_shard, spread(normed_own), rims, wzx, wside, chan, bcp, head
         )
         states = [hop(final, k) for k in hops]
-        tots = [hop(tot, k) for k in hops]
-        result = mixer_middle(scal_shard, states, tots, yloc, zx, c_out, cum, wout, chan, nt)
-        y, s_in, square = result[:3]
-        square = total_over(square, "tensor")[0]
-        square = lax.dynamic_slice_in_dim(square, shard * own, own)
-        factor = lax.rsqrt(square / DI + NORM_EPS)[:, None]
-        branch = collect(result[3:])
-        saved.append((residual, normed, zx, side, tot, c_out, cum, y, s_in, factor, branch))
-        residual = residual + factor * branch
-    final_gain = shared_full[L * stride :]
-    final_scale = rms_scale(residual)
-    final_rows = spread((residual * final_scale * final_gain[None, :]).astype(BF))
+        result = mixer_middle(scal_shard, states, yloc, zx, c_out, cum, wout, chan, nt)
+        y, s_in = result[:2]
+        before = residual
+        residual, branch, factor, normed_own = join_residual(
+            returned(result[2:]), before, gains[layer_index + 1]
+        )
+        saved.append((before, normed, zx, side, c_out, cum, y, s_in, factor, branch))
+    final_rows = spread(normed_own)
 
     member = micro_batch[:, None] == jnp.arange(MB, dtype=jnp.int32)[None, :]
     batch_tokens = jnp.sum(jnp.where(member, seq_lengths[:, None], 0), axis=0).astype(F32)
@@ -1020,15 +1266,13 @@
     scale = soft * jnp.exp(tops - log_total.reshape(1, 1, rows))
     result = vocab_rows(label, scale, weight.reshape(1, rows), p_low, table_all, vrows, nt)
     q_low = result[0]
-    grad_final = collect(result[1:])
+    sent = returned(result[1:])
     table_grad = vocab_table_grad(q_low, final_rows)
+    sent, table_grad = lax.optimization_barrier((sent, table_grad))
     table_share = lax.psum_scatter(table_grad, "dp", scatter_dimension=1, tiled=True)
-
-    grad_final_gain = jnp.sum(grad_final * residual * final_scale, axis=0)
-    scaled_grad = grad_final * final_gain[None, :]
-    grad_res = final_scale * scaled_grad - residual * (
-        final_scale * final_scale * final_scale
-    ) * jnp.mean(scaled_grad * residual, axis=1, keepdims=True)
+    grad_res, payload, grad_final_gain = back_rows(
+        sent, [], residual, final_gain, None, (saved[L - 1][9], saved[L - 1][8])
+    )
 
     block_pieces = [None] * (2 * L)
     side_pieces = [None] * L
@@ -1037,50 +1281,25 @@
     shared_pieces = [None] * L
     for layer_index in reversed(range(L)):
         wzx, wout, wside, gain, bcp, chan, head = mats[layer_index]
-        residual_in, normed, zx, side, tot, c_out, cum, y, s_in, factor, branch = saved[layer_index]
-        inner_rows = jnp.sum(grad_res * branch, axis=1)
-        coef_own = factor[:, 0] * factor[:, 0] * factor[:, 0] * inner_rows / DI
-        coef = jnp.zeros((rows,), F32)
-        for off in range(nt):
-            coef = lax.dynamic_update_slice_in_dim(
-                coef, coef_own if off == 0 else swap(coef_own, "tensor", off), (shard ^ off) * own, 0
-            )
+        residual_in, normed, zx, side, c_out, cum, y, s_in, factor, branch = saved[layer_index]
         grads, u_low, dy, dz, dstate, gain_grad = gate_back(
-            scal_shard,
-            spread((factor * grad_res).astype(BF)),
-            coef[:, None],
-            wout,
-            y,
-            zx,
-            c_out,
-            cum,
-            chan,
+            scal_shard, spread(payload), wout, y, zx, c_out, cum, chan
         )
         states = [hop(dstate, -k) for k in hops]
-        tots = [hop(tot, -k) for k in hops]
         grad_out_w = tn(u_low, grads)
         result = mixer_back(
-            scal_shard, states, tots, s_in, zx, side, dy, dz, y, wzx, wside, chan, bcp, head, nt
+            scal_shard, states, s_in, zx, side, dy, dz, y, wzx, wside, chan, bcp, head, nt
         )
         dzx, dside, chan_grad, bcp_grad, head_grad, rim_grad = result[:6]
-        grad_local = collect(result[6:])
-        rim_sum = jnp.zeros((RIM, D), F32)
-        for to in range(nt):
-            pairs = [(b, a) for a, b in rim_pairs(to)]
-            rim_sum = rim_sum + lax.ppermute(rim_grad, both, pairs).astype(F32)
-        grad_local = grad_local + jnp.pad(rim_sum, ((own - RIM, 0), (0, 0)))
+        rims = [
+            lax.ppermute(rim_grad, both, [(b, a) for a, b in rim_pairs(to)]) for to in range(nt)
+        ]
+        below = (saved[layer_index - 1][9], saved[layer_index - 1][8]) if layer_index else None
+        grad_res, payload, grad_gain_in = back_rows(
+            returned(result[6:]), rims, residual_in, gains[layer_index], grad_res, below
+        )
         grad_zx_w = tn(normed, dzx)
         grad_side_w = tn(normed, dside)
-        inv_scale = rms_scale(residual_in)
-        grad_gain_in = jnp.sum(grad_local * residual_in * inv_scale, axis=0)
-        scaled_in = grad_local * gain[None, :]
-        grad_res = (
-            grad_res
-            + inv_scale * scaled_in
-            - residual_in
-            * (inv_scale * inv_scale * inv_scale)
-            * jnp.mean(scaled_in * residual_in, axis=1, keepdims=True)
-        )
         block_pieces[2 * layer_index] = to_blocks(grad_zx_w.astype(BF))
         block_pieces[2 * layer_index + 1] = to_blocks(grad_out_w.astype(BF))
         spaced = lax.dynamic_update_slice(
@@ -1092,10 +1311,10 @@
         channel_pieces[layer_index] = jnp.concatenate([chan_grad[:5], gain_grad], axis=0)
         head_pieces[layer_index] = head_grad[:3, :heads]
         shared_pieces[layer_index] = jnp.concatenate(
-            [grad_gain_in, bcp_grad[:4].reshape(-1), bcp_grad[4]]
+            [grad_gain_in[0], bcp_grad[:4].reshape(-1), bcp_grad[4]]
         )
 
-    embed = cut_parts(scal, spread(grad_res.astype(BF)), nd)
+    embed = cut_parts(scal, spread(payload), nd)
     embed = [embed[0]] + [swap(embed[off], "dp", off) for off in range(1, nd)]
 
     inverse = jnp.zeros((tiles,), jnp.int32).at[block_slot[0]].set(jnp.arange(tiles, dtype=jnp.int32))
@@ -1108,14 +1327,14 @@
         .transpose(1, 2, 0, 3, 4)
         .reshape(nd, nt, side_part, LANES)
     )
-    shared_grads = jnp.concatenate(shared_pieces + [grad_final_gain]).astype(BF)
+    shared_grads = jnp.concatenate(shared_pieces + [grad_final_gain[0]]).astype(BF)
     shared_grads = jnp.pad(
         shared_grads.reshape(nd, nt, share_size), ((0, 0), (0, 0), (0, share_pad - share_size))
     ).reshape(nd, nt, share_pad // LANES, LANES)
     small_grads = jnp.concatenate([side_grads, shared_grads], axis=2).reshape(nd, -1, LANES)
-    block_share = lax.psum_scatter(
-        jnp.concatenate([slot_grads, small_grads], axis=1), "dp", scatter_dimension=0, tiled=True
-    )[0]
+    tile_grads = jnp.concatenate([slot_grads, small_grads], axis=1)
+    tile_grads, table_share = lax.optimization_barrier((tile_grads, table_share))
+    block_share = lax.psum_scatter(tile_grads, "dp", scatter_dimension=0, tiled=True)[0]
     block_grads = block_share[: own_tiles * BLK].astype(F32)
     small_share = block_share[own_tiles * BLK :].reshape(nt, piece_rows, LANES)
     mine = jnp.zeros((piece_rows, LANES), F32)
@@ -1136,8 +1355,9 @@
     head_sum = lines[-1, : L * 3 * heads].reshape(head_params.shape)
 
     grad_table, table_square = add_rows(
-        scal, jnp.where(held, local_row, vrows), table_share, embed, vrows
-    )
+        scal, jnp.maximum(code, 0), listed, count, table_share, embed, vrows
+    )
+    rotated = soap_turn(block_grads.reshape(layer_blocks.shape), block_bases)
     first_copy = (place == 0).astype(F32)
     square_part = (
         jnp.sum(block_grads * block_grads)
@@ -1146,8 +1366,9 @@
         + jnp.sum(shared_share * shared_share)
         + first_copy * (jnp.sum(channel_sum * channel_sum) + jnp.sum(head_sum * head_sum))
     )
-    packed = jnp.concatenate([seq_part, square_part[None]])
-    packed = total_over(total_over(packed, "tensor"), "dp")
+    packed = jnp.pad(jnp.concatenate([seq_part, square_part[None]]), (0, 8 * LANES - seqs - 1))
+    packed, rotated = lax.optimization_barrier((packed, rotated))
+    packed = sum_everywhere(packed.reshape(8, LANES), nd, nt)[0]
     seq_loss = packed[:seqs]
     clip_norm = jnp.sqrt(packed[seqs])
     factor = jnp.minimum(1.0, CLIP_LIMIT / (clip_norm + 1e-06))
@@ -1159,7 +1380,7 @@
     )
     block_out = soap_update(
         layer_blocks,
-        block_grads.reshape(layer_blocks.shape),
+        rotated,
         block_bases,
         block_first,
         block_second,

time: 1030 us -> 828 us (0.80)
  waiting for transfers between devices: 336 us -> 241 us
  starting transfers between devices: 195 us -> 149 us
  local copies, waits for them, and re-layouts: 146 us -> 113 us
  Pallas kernels: 206 us -> 193 us
    reduce_scatter x1, waiting for transfers between devices: 134 us -> 0.01 us  [shards(): lax.psum_scatter(table_grad, 'dp', scatter_dimension=1, tiled=True)]
    pallas_call x12 -> x18, Pallas kernels: 126 us -> 87.2 us  [call(): pl.pallas_call(kernel, out_shape=out_shape, in_specs=specs, out_specs=jax...]
    ppermute x88 -> x66, waiting for transfers between devices: 169 us -> 208 us  [swap(): return lax.ppermute(x, axis, [(i, i ^ offset) for i in range(size)])]
    ppermute x88 -> x66, starting transfers between devices: 139 us -> 106 us  [swap(): return lax.ppermute(x, axis, [(i, i ^ offset) for i in range(size)])]
    pallas_call x0 -> x2, Pallas kernels: none -> 30.9 us  [the longest x1 20.1 us: gather_rows(): pl.pallas_call(functools.partial(look_kernel, groups, rows), out_shape=[s...]
    ppermute x24 -> x12, waiting for transfers between devices: 14.8 us -> 33.7 us  [hop(): return lax.ppermute(x, 'dp', pairs)]
    unnamed x431 -> x367, local copies, waits for them, and re-layouts: 36.4 us -> 54.5 us
    reduce_scatter x1, waiting for transfers between devices: 17.9 us -> 0.01 us  [shards(): lax.psum_scatter(tile_grads, 'dp', scatter_dimension=0, tiled=True)[0]]
  transfers between devices with their start and end apart: 132 -> 98, of which waited for: 43 -> 39; matrix products, arithmetic and copies ran while one was open for 17% -> 14% of each run, Pallas kernels for 8% -> 16%
where the time goes in v2:
time: 828 us; the launch traced here: 820 us
  waiting for transfers between devices  241 us (29%)
  Pallas kernels  193 us (23%)
  starting transfers between devices  149 us (18%)
  local copies, waits for them, and re-layouts  113 us (14%)
  other arithmetic  71.1 us (9%)
  between operations  23 us (3%)
  matrix products  21.1 us (3%)
  blocking collectives  9.08 us (1%)
    ppermute x66, waiting for transfers between devices, swap(): return lax.ppermute(x, axis, [(i, i ^ offset) for i in range(size)])  208 us
    ppermute x66, starting transfers between devices, swap(): return lax.ppermute(x, axis, [(i, i ^ offset) for i in range(size)])  106 us
    pallas_call x18, Pallas kernels, call(): pl.pallas_call(kernel, out_shape=out_shape, in_specs=specs, out_specs=jax...  87.2 us
    unnamed x367, local copies, waits for them, and re-layouts  54.5 us
    ppermute x12, waiting for transfers between devices, hop(): return lax.ppermute(x, 'dp', pairs)  33.7 us
    ppermute x12, starting transfers between devices, hop(): return lax.ppermute(x, 'dp', pairs)  30.1 us
    pallas_call x1, Pallas kernels, vocab_logits(): pl.pallas_call(functools.partial(logits_kernel, shards, own, vrows), grid...  26.5 us
    pallas_call x1, Pallas kernels, vocab_rows(): pl.pallas_call(functools.partial(rows_kernel, shards, own, vrows), grid=(...  26.1 us
  transfers between devices with their start and end apart: 98, of which 39 were waited for; matrix products, arithmetic and copies ran while one was open for 14% of the time, Pallas kernels for 16%

profile of v2, /device:TPU:0, one launch (start us, length us, event | category | flops | bytes accessed | tf_op | source)
XLA Modules:
  0.0 819.7 jit_solution(1999467191144052006)
XLA Ops:
  27.4 9.1 %all_gather.12 = s32[4,2048]{1,0:T(4,128)S(1)} all-gather(s32[4,256]{1,0:T(4,128)S(1)} %pad_add_fusion), channel_id=1, replica_groups=mesh['dp'=8,'tensor'=4] {'dp'}, dimensions={1}, use_global_device_ids=true | all-gather | bytes 36864 | tf_op jit(solution)/shard_map/all_gather | solution.py:1140
  37.8 20.1 %look.1 = (bf16[512,256]{1,0:T(8,128)(2,1)S(1)}, bf16[512,256]{1,0:T(8,128)(2,1)S(1)}, bf16[512,256]{1,0:T(8,128)(2,1)S(1)}, bf16[512,256]{1,0:T(8,128)(2,1)S(1)...) custom-call(s32[2]{0:T(128)S(1)} %pad_add_fusion.1.scal, ...), custom_call_target="tpu_custom_call" | custom-call | bytes 31457280 | tf_op jit(solution)/shard_map/look/pallas_call | solution.py:194
  64.0 9.6 %collective-permute-done.1.rest_2_ = bf16[512,256]{1,0:T(8,128)(2,1)S(1)} collective-permute-done((bf16[512,256]{1,0:T(8,128)(2,1)S(1)}, bf16[512,256]{1,0:T(8,128)(2,1)S(1)}, u32[]{:S(2)}, u32[]{:S(2)}) %collective-permute-start.1) | collective-permute-done | bytes 262176 | tf_op jit(solution)/shard_map/ppermute | solution.py:68
  108.4 9.5 %collective-permute-done.8.refs_2_ = bf16[128,1024]{1,0:T(8,128)(2,1)S(1)} collective-permute-done((bf16[128,1024]{1,0:T(8,128)(2,1)S(1)}, bf16[128,1024]{1,0:T(8,128)(2,1)S(1)}, u32[]{:S(2)}, u32[]{:S(2)}) %collective-permute-start.8) | collective-permute-done | bytes 262176 | tf_op jit(solution)/shard_map/ppermute | solution.py:68
  159.7 10.3 %collective-permute-start.20 = (bf16[144,512]{1,0:T(8,128)(2,1)}, bf16[144,512]{1,0:T(8,128)(2,1)}, u32[]{:S(2)}, u32[]{:S(2)}) collective-permute-start(bf16[144,512]{1,0:T(8,128)(2,1)} %get-tuple-element.156), channel_id=1, source_target_pairs={{0,4},{4,8},{8,12},{16,20},{20,24},{24,28},{1,5},{5,9},{9,13},{17,... | collective-permute-start | bytes 442376 | tf_op jit(solution)/shard_map/ppermute | solution.py:1201
  204.4 11.1 %collective-permute-done.24.refs_2_ = bf16[128,1152]{1,0:T(8,128)(2,1)S(1)} collective-permute-done((bf16[128,1152]{1,0:T(8,128)(2,1)S(1)}, bf16[128,1152]{1,0:T(8,128)(2,1)S(1)}, u32[]{:S(2)}, u32[]{:S(2)}) %collective-permute-start.24) | collective-permute-done | bytes 294944 | tf_op jit(solution)/shard_map/ppermute | solution.py:68
  227.1 14.4 %collective-permute-done.27.rest_2_ = bf16[128,1024]{1,0:T(8,128)(2,1)S(1)} collective-permute-done((bf16[128,1024]{1,0:T(8,128)(2,1)S(1)}, bf16[128,1024]{1,0:T(8,128)(2,1)S(1)}, u32[]{:S(2)}, u32[]{:S(2)}) %collective-permute-start.27) | collective-permute-done | bytes 262176 | tf_op jit(solution)/shard_map/ppermute | solution.py:68
  291.2 13.2 %collective-permute-done.37.refs_2_ = bf16[128,1152]{1,0:T(8,128)(2,1)S(1)} collective-permute-done((bf16[128,1152]{1,0:T(8,128)(2,1)S(1)}, bf16[128,1152]{1,0:T(8,128)(2,1)S(1)}, u32[]{:S(2)}, u32[]{:S(2)}) %collective-permute-start.37) | collective-permute-done | bytes 294944 | tf_op jit(solution)/shard_map/ppermute | solution.py:68
  321.4 10.7 %collective-permute-done.40.rest_2_ = bf16[128,1024]{1,0:T(8,128)(2,1)} collective-permute-done((bf16[128,1024]{1,0:T(8,128)(2,1)}, bf16[128,1024]{1,0:T(8,128)(2,1)}, u32[]{:S(2)}, u32[]{:S(2)}) %collective-permute-start.40) | collective-permute-done | bytes 262176 | tf_op jit(solution)/shard_map/ppermute | solution.py:68
  332.8 26.5 %logits.1 = (bf16[2,6400,512]{2,1,0:T(8,128)(2,1)}, f32[10,16,512]{2,1,0:T(8,128)S(1)}, f32[8,512]{1,0:T(8,128)S(1)}) custom-call(s32[1,512]{1,0:T(1,128)S(1)} %bitcast.373, bf16[6400,2048]{1,0:T(8,128)(2,1)} %all-gather.4.cloned.1.call-done.table, bf16[128,1024]{1,0:T(8,128)(2,1)} %get-tuple-element.180.rest_0_, ...), custom_call_target="tpu_custom_call" | custom-call | flops 13421772800 | bytes 41943040 | tf_op jit(solution)/shard_map/logits/pallas_call | solution.py:902
  371.8 26.1 %rowgrads.1 = (bf16[2,6400,512]{2,1,0:T(8,128)(2,1)}, bf16[128,1024]{1,0:T(8,128)(2,1)S(1)}, bf16[128,1024]{1,0:T(8,128)(2,1)}, bf16[128,1024]{1,0:T(8,128)(2,1)}, bf16[128,1024]{1,0:T(8,128)(2,1)}) custom-call(s32[1,512]{1,0:T(1,128)S(1)} %bitcast.374, f32[10,16,512]{2,1,0:T(8,128)S(1)} %exponential_multiply_fusion.scale, f32[1,512]{1,0:T(1,128)S(1)} %copy-done.92, ...), custom_call_target="tpu_custom_call" | custom-call | flops 13421772800 | bytes 54525952 | tf_op jit(solution)/shard_map/rowgrads/pallas_call | solution.py:964
  403.0 22.0 %tablegrads.1 = bf16[6400,2048]{1,0:T(8,128)(2,1)} custom-call(bf16[2,6400,512]{2,1,0:T(8,128)(2,1)} %get-tuple-element.189.q_in, bf16[128,1024]{1,0:T(8,128)(2,1)} %get-tuple-element.180.rest_0_, bf16[128,1024]{1,0:T(8,128)(2,1)} %collective-permute-done.39.rest_1_, bf16[128,1024]{1,0:T(8,128)(2,1)} %collective-permute-done.40.rest_2_, ...), custom_call_target="tpu_custom_call" | custom-call | flops 13421772800 | bytes 41943040 | tf_op jit(solution)/shard_map/tablegrads/pallas_call | solution.py:1005
  449.2 10.4 %collective-permute-done.49.rest_2_ = bf16[128,1152]{1,0:T(8,128)(2,1)} collective-permute-done((bf16[128,1152]{1,0:T(8,128)(2,1)}, bf16[128,1152]{1,0:T(8,128)(2,1)}, u32[]{:S(2)}, u32[]{:S(2)}) %collective-permute-start.49) | collective-permute-done | bytes 294944 | tf_op jit(solution)/shard_map/ppermute | solution.py:68
  484.1 15.1 %back.2 = (bf16[528,1024]{1,0:T(8,128)(2,1)}, bf16[528,384]{1,0:T(8,128)(2,1)S(1)}, f32[8,512]{1,0:T(8,128)S(1)}, f32[8,256]{1,0:T(8,128)S(1)}, f32[8,128]{1,0:T...) custom-call(s32[1]{0:T(128)} %bitcast.6.scal, ...), custom_call_target="tpu_custom_call" | custom-call | flops 2147483648 | bytes 16777216 | tf_op jit(solution)/shard_map/back/pallas_call | solution.py:137
  514.6 10.9 %collective-permute-done.55.refs_2_ = bf16[128,1024]{1,0:T(8,128)(2,1)S(1)} collective-permute-done((bf16[128,1024]{1,0:T(8,128)(2,1)S(1)}, bf16[128,1024]{1,0:T(8,128)(2,1)S(1)}, u32[]{:S(2)}, u32[]{:S(2)}) %collective-permute-start.55) | collective-permute-done | bytes 262176 | tf_op jit(solution)/shard_map/ppermute | solution.py:68
  544.5 11.7 %collective-permute-done.62.rest_2_ = bf16[128,1152]{1,0:T(8,128)(2,1)S(1)} collective-permute-done((bf16[128,1152]{1,0:T(8,128)(2,1)S(1)}, bf16[128,1152]{1,0:T(8,128)(2,1)S(1)}, u32[]{:S(2)}, u32[]{:S(2)}) %collective-permute-start.62) | collective-permute-done | bytes 294944 | tf_op jit(solution)/shard_map/ppermute | solution.py:68
  582.8 14.7 %back.3 = (bf16[528,1024]{1,0:T(8,128)(2,1)}, bf16[528,384]{1,0:T(8,128)(2,1)S(1)}, f32[8,512]{1,0:T(8,128)S(1)}, f32[8,256]{1,0:T(8,128)S(1)}, f32[8,128]{1,0:T...) custom-call(s32[1]{0:T(128)} %bitcast.6.scal, ...), custom_call_target="tpu_custom_call" | custom-call | flops 2147483648 | bytes 16777216 | tf_op jit(solution)/shard_map/back/pallas_call | solution.py:137
  629.1 11.1 %gather_fusion.1 = bf16[192,128,128]{2,1,0:T(8,128)(2,1)} fusion(bf16[192,128,128]{2,1,0:T(8,128)(2,1)} %pad_maximum_fusion.1, s32[1024]{0:T(1024)} %pad_clamp_fusion), kind=kCustom, calls=%fused_computation.1 | custom fusion | bytes 12583680 | tf_op jit(solution)/shard_map/gather | solution.py:1322
  667.6 11.1 %collective-permute-done.75.rest_2_ = bf16[128,1024]{1,0:T(8,128)(2,1)} collective-permute-done((bf16[128,1024]{1,0:T(8,128)(2,1)S(1)}, bf16[128,1024]{1,0:T(8,128)(2,1)}, u32[]{:S(2)}, u32[]{:S(2)}) %collective-permute-start.75) | collective-permute-done | bytes 262176 | tf_op jit(solution)/shard_map/ppermute | solution.py:68
  687.6 11.1 %collective-permute-done.88 = f32[49,128]{1,0:T(8,128)S(1)} collective-permute-done((f32[49,128]{1,0:T(8,128)S(1)}, f32[49,128]{1,0:T(8,128)S(1)}, u32[]{:S(2)}, u32[]{:S(2)}) %collective-permute-start.88) | collective-permute-done | bytes 25120 | tf_op jit(solution)/shard_map/ppermute | solution.py:68
  721.5 12.9 %collective-permute-done.81.rest_5_ = bf16[512,256]{1,0:T(8,128)(2,1)} collective-permute-done((bf16[512,256]{1,0:T(8,128)(2,1)}, bf16[512,256]{1,0:T(8,128)(2,1)}, u32[]{:S(2)}, u32[]{:S(2)}) %collective-permute-start.81) | collective-permute-done | bytes 262176 | tf_op jit(solution)/shard_map/ppermute | solution.py:68
  737.7 9.7 %addrows.1 = (f32[6286,256]{1,0:T(8,128)}, f32[1,256]{1,0:T(1,128)S(1)}) custom-call(s32[2]{0:T(128)S(1)} %copy-done.85, s32[4104]{0:T(1024)S(1)} %copy-done.59, s32[4104]{0:T(1024)S(1)} %copy-done.75, s32[1]{0:T(128)} %get-tuple-element.242.count, bf16[6400,256]{1,0:T(8,128)(2,1)S(1)} %copy-done.2, bf16[512,256]{1,0:T(8,128)(2,1)S(1)} %get-tuple-element.245.rest_0_, ...), custom_call_target="tpu_custom_call" | custom-call | bytes 31457280 | tf_op jit(solution)/shard_map/addrows/pallas_call | solution.py:137
  768.0 10.8 %sumall.1 = f32[8,128]{1,0:T(8,128)S(1)} custom-call(f32[8,128]{1,0:T(8,128)S(1)} %bitcast.370), custom_call_target="tpu_custom_call" | custom-call | tf_op jit(solution)/shard_map/sumall/pallas_call | solution.py:470
  797.8 14.0 %multiply_subtract_fusion = (f32[6286,256]{1,0:T(8,128)}, f32[6286,256]{1,0:T(8,128)}, f32[6286,256]{1,0:T(8,128)}) fusion(f32[6286,256]{1,0:T(8,128)S(1)} %bitcast.377, f32[]{:T(128)} %bitcast.104, f32[]{:T(128)} %bitcast.103, f32[6286,256]{1,0:T(8,128)} %get-tuple-element.261, f32[]{:T(128)S(6)} %min.3, f32[6286,256]{1,0:T(8,128)} %param.33, ...), kind=kLoop, calls=%fused_computation.6 | loop fusion | flops 25747456 | bytes 45058060 | tf_op jit(solution)/shard_map/sub | solution.py:1028
  (727 shorter events, 470.7 us)
Async XLA Ops:
  7.2 92.3 %all-gather.6.cloned.1.call-start = ((), (), s32[]{:S(2)}) async-start(), calls=%async_computation.5 | async-start | bytes 8994816 | tf_op jit(solution)/shard_map/all_gather | solution.py:1139
  21.6 310.6 %all-gather.4.cloned.1.call-start = ((), (), s32[]{:S(2)}) async-start(), calls=%async_computation.2 | async-start | bytes 29491200 | tf_op jit(solution)/shard_map/all_gather | solution.py:1164
  26.7 625.0 %reduce-scatter.3.cloned.1.call-start = ((), (), s32[]{:S(2)}) async-start(), calls=%async_computation.3 | async-start | bytes 29491200 | tf_op jit(solution)/shard_map/reduce_scatter | solution.py:1272
  62.3 26.9 %collective-permute-start.5 = (bf16[512,256]{1,0:T(8,128)(2,1)S(1)}, bf16[512,256]{1,0:T(8,128)(2,1)S(1)}, u32[]{:S(2)}, u32[]{:S(2)}) collective-permute-start(bf16[512,256]{1,0:T(8,128)(2,1)S(1)} %get-tuple-element.148), channel_id=1, source_target_pairs={{0,24},{4,28},{8,16},{12,20},{16,8},{20,12},{24,0},{28,4},{1,25},{... | collective-permute-start | bytes 786440 | tf_op jit(solution)/shard_map/ppermute | solution.py:68
  118.9 28.8 %collective-permute-start.13 = (bf16[128,1024]{1,0:T(8,128)(2,1)}, bf16[128,1024]{1,0:T(8,128)(2,1)}, u32[]{:S(2)}, u32[]{:S(2)}) collective-permute-start(bf16[128,1024]{1,0:T(8,128)(2,1)} %get-tuple-element.154.rest_0_), channel_id=1, source_target_pairs={{0,1},{1,0},{2,3},{3,2},{4,5},{5,4},{6,7},{7,6},{8,9},{9,8},{10,11... | collective-permute-start | bytes 786440 | tf_op jit(solution)/shard_map/ppermute | solution.py:68
  124.0 23.7 %collective-permute-start.14 = (bf16[128,1024]{1,0:T(8,128)(2,1)}, bf16[128,1024]{1,0:T(8,128)(2,1)}, u32[]{:S(2)}, u32[]{:S(2)}) collective-permute-start(bf16[128,1024]{1,0:T(8,128)(2,1)} %get-tuple-element.154.rest_0_), channel_id=1, source_target_pairs={{0,2},{1,3},{2,0},{3,1},{4,6},{5,7},{6,4},{7,5},{8,10},{9,11},{10,... | collective-permute-start | bytes 786440 | tf_op jit(solution)/shard_map/ppermute | solution.py:68
  281.3 23.1 %collective-permute-start.37 = (bf16[128,1152]{1,0:T(8,128)(2,1)S(1)}, bf16[128,1152]{1,0:T(8,128)(2,1)S(1)}, u32[]{:S(2)}, u32[]{:S(2)}) collective-permute-start(bf16[128,1152]{1,0:T(8,128)(2,1)S(1)} %get-tuple-element.177), channel_id=1, source_target_pairs={{0,2},{1,3},{2,0},{3,1},{4,6},{5,7},{6,4},{7,5},{8,10},{9,11},{10,... | collective-permute-start | bytes 884744 | tf_op jit(solution)/shard_map/ppermute | solution.py:68
  281.3 23.1 %collective-permute-start.38 = (bf16[128,1152]{1,0:T(8,128)(2,1)S(1)}, bf16[128,1152]{1,0:T(8,128)(2,1)S(1)}, u32[]{:S(2)}, u32[]{:S(2)}) collective-permute-start(bf16[128,1152]{1,0:T(8,128)(2,1)S(1)} %get-tuple-element.178), channel_id=1, source_target_pairs={{0,3},{1,2},{2,1},{3,0},{4,7},{5,6},{6,5},{7,4},{8,11},{9,10},{10,... | collective-permute-start | bytes 884744 | tf_op jit(solution)/shard_map/ppermute | solution.py:68
  398.6 26.4 %collective-permute-start.45 = (bf16[128,1024]{1,0:T(8,128)(2,1)}, bf16[128,1024]{1,0:T(8,128)(2,1)}, u32[]{:S(2)}, u32[]{:S(2)}) collective-permute-start(bf16[128,1024]{1,0:T(8,128)(2,1)} %get-tuple-element.186), channel_id=1, source_target_pairs={{0,1},{1,0},{2,3},{3,2},{4,5},{5,4},{6,7},{7,6},{8,9},{9,8},{10,11... | collective-permute-start | bytes 786440 | tf_op jit(solution)/shard_map/ppermute | solution.py:68
  398.6 26.4 %collective-permute-start.46 = (bf16[128,1024]{1,0:T(8,128)(2,1)}, bf16[128,1024]{1,0:T(8,128)(2,1)}, u32[]{:S(2)}, u32[]{:S(2)}) collective-permute-start(bf16[128,1024]{1,0:T(8,128)(2,1)} %get-tuple-element.187), channel_id=1, source_target_pairs={{0,2},{1,3},{2,0},{3,1},{4,6},{5,7},{6,4},{7,5},{8,10},{9,11},{10,... | collective-permute-start | bytes 786440 | tf_op jit(solution)/shard_map/ppermute | solution.py:68
  401.6 23.4 %collective-permute-start.47 = (bf16[128,1024]{1,0:T(8,128)(2,1)}, bf16[128,1024]{1,0:T(8,128)(2,1)}, u32[]{:S(2)}, u32[]{:S(2)}) collective-permute-start(bf16[128,1024]{1,0:T(8,128)(2,1)} %get-tuple-element.188), channel_id=1, source_target_pairs={{0,3},{1,2},{2,1},{3,0},{4,7},{5,6},{6,5},{7,4},{8,11},{9,10},{10,... | collective-permute-start | bytes 786440 | tf_op jit(solution)/shard_map/ppermute | solution.py:68
  425.0 323.0 %reduce-scatter.5.cloned.1.call-start = ((), (), s32[]{:S(2)}) async-start(), calls=%async_computation.4 | async-start | bytes 8994816 | tf_op jit(solution)/shard_map/reduce_scatter | solution.py:1337
  532.7 23.5 %collective-permute-start.62 = (bf16[128,1152]{1,0:T(8,128)(2,1)S(1)}, bf16[128,1152]{1,0:T(8,128)(2,1)S(1)}, u32[]{:S(2)}, u32[]{:S(2)}) collective-permute-start(bf16[128,1152]{1,0:T(8,128)(2,1)S(1)} %get-tuple-element.212.rest_0_), channel_id=1, source_target_pairs={{0,2},{1,3},{2,0},{3,1},{4,6},{5,7},{6,4},{7,5},{8,10},{9,11},{10,... | collective-permute-start | bytes 884744 | tf_op jit(solution)/shard_map/ppermute | solution.py:68
  532.7 24.2 %collective-permute-start.63 = (bf16[128,1152]{1,0:T(8,128)(2,1)S(1)}, bf16[128,1152]{1,0:T(8,128)(2,1)}, u32[]{:S(2)}, u32[]{:S(2)}) collective-permute-start(bf16[128,1152]{1,0:T(8,128)(2,1)S(1)} %get-tuple-element.212.rest_0_), channel_id=1, source_target_pairs={{0,3},{1,2},{2,1},{3,0},{4,7},{5,6},{6,5},{7,4},{8,11},{9,10},{10,... | collective-permute-start | bytes 884744 | tf_op jit(solution)/shard_map/ppermute | solution.py:68
  597.4 25.2 %collective-permute-start.70 = (bf16[16,1024]{1,0:T(8,128)(2,1)S(1)}, bf16[16,1024]{1,0:T(8,128)(2,1)S(1)}, u32[]{:S(2)}, u32[]{:S(2)}) collective-permute-start(bf16[16,1024]{1,0:T(8,128)(2,1)S(1)} %get-tuple-element.232), channel_id=1, source_target_pairs={{4,3},{8,7},{12,11},{20,19},{24,23},{28,27}} | collective-permute-start | bytes 98312 | tf_op jit(solution)/shard_map/ppermute | solution.py:1295
  598.1 25.2 %collective-permute-start.71 = (bf16[16,1024]{1,0:T(8,128)(2,1)S(1)}, bf16[16,1024]{1,0:T(8,128)(2,1)S(1)}, u32[]{:S(2)}, u32[]{:S(2)}) collective-permute-start(bf16[16,1024]{1,0:T(8,128)(2,1)S(1)} %get-tuple-element.232), channel_id=1, source_target_pairs={{5,3},{9,7},{13,11},{21,19},{25,23},{29,27}} | collective-permute-start | bytes 98312 | tf_op jit(solution)/shard_map/ppermute | solution.py:1295
  608.7 31.5 %collective-permute-start.67 = (bf16[128,1024]{1,0:T(8,128)(2,1)S(1)}, bf16[128,1024]{1,0:T(8,128)(2,1)S(1)}, u32[]{:S(2)}, u32[]{:S(2)}) collective-permute-start(bf16[128,1024]{1,0:T(8,128)(2,1)S(1)} %get-tuple-element.229), channel_id=1, source_target_pairs={{0,1},{1,0},{2,3},{3,2},{4,5},{5,4},{6,7},{7,6},{8,9},{9,8},{10,11... | collective-permute-start | bytes 786440 | tf_op jit(solution)/shard_map/ppermute | solution.py:68
  613.9 26.4 %collective-permute-start.68 = (bf16[128,1024]{1,0:T(8,128)(2,1)S(1)}, bf16[128,1024]{1,0:T(8,128)(2,1)S(1)}, u32[]{:S(2)}, u32[]{:S(2)}) collective-permute-start(bf16[128,1024]{1,0:T(8,128)(2,1)S(1)} %get-tuple-element.230), channel_id=1, source_target_pairs={{0,2},{1,3},{2,0},{3,1},{4,6},{5,7},{6,4},{7,5},{8,10},{9,11},{10,... | collective-permute-start | bytes 786440 | tf_op jit(solution)/shard_map/ppermute | solution.py:68
  613.9 26.4 %collective-permute-start.69 = (bf16[128,1024]{1,0:T(8,128)(2,1)S(1)}, bf16[128,1024]{1,0:T(8,128)(2,1)S(1)}, u32[]{:S(2)}, u32[]{:S(2)}) collective-permute-start(bf16[128,1024]{1,0:T(8,128)(2,1)S(1)} %get-tuple-element.231), channel_id=1, source_target_pairs={{0,3},{1,2},{2,1},{3,0},{4,7},{5,6},{6,5},{7,4},{8,11},{9,10},{10,... | collective-permute-start | bytes 786440 | tf_op jit(solution)/shard_map/ppermute | solution.py:68
  682.7 23.8 %collective-permute-start.77 = (bf16[512,256]{1,0:T(8,128)(2,1)S(1)}, bf16[512,256]{1,0:T(8,128)(2,1)S(1)}, u32[]{:S(2)}, u32[]{:S(2)}) collective-permute-start(bf16[512,256]{1,0:T(8,128)(2,1)S(1)} %get-tuple-element.246), channel_id=1, source_target_pairs={{0,4},{4,0},{8,12},{12,8},{16,20},{20,16},{24,28},{28,24},{1,5},{5... | collective-permute-start | bytes 786440 | tf_op jit(solution)/shard_map/ppermute | solution.py:68
  682.7 26.0 %collective-permute-start.78 = (bf16[512,256]{1,0:T(8,128)(2,1)S(1)}, bf16[512,256]{1,0:T(8,128)(2,1)S(1)}, u32[]{:S(2)}, u32[]{:S(2)}) collective-permute-start(bf16[512,256]{1,0:T(8,128)(2,1)S(1)} %get-tuple-element.247), channel_id=1, source_target_pairs={{0,8},{4,12},{8,0},{12,4},{16,24},{20,28},{24,16},{28,20},{1,9},{5... | collective-permute-start | bytes 786440 | tf_op jit(solution)/shard_map/ppermute | solution.py:68
  705.8 28.5 %collective-permute-start.81 = (bf16[512,256]{1,0:T(8,128)(2,1)}, bf16[512,256]{1,0:T(8,128)(2,1)}, u32[]{:S(2)}, u32[]{:S(2)}) collective-permute-start(bf16[512,256]{1,0:T(8,128)(2,1)} %get-tuple-element.250), channel_id=1, source_target_pairs={{0,20},{4,16},{8,28},{12,24},{16,4},{20,0},{24,12},{28,8},{1,21},{... | collective-permute-start | bytes 786440 | tf_op jit(solution)/shard_map/ppermute | solution.py:68
  707.2 27.2 %collective-permute-start.82 = (bf16[512,256]{1,0:T(8,128)(2,1)}, bf16[512,256]{1,0:T(8,128)(2,1)}, u32[]{:S(2)}, u32[]{:S(2)}) collective-permute-start(bf16[512,256]{1,0:T(8,128)(2,1)} %get-tuple-element.251), channel_id=1, source_target_pairs={{0,24},{4,28},{8,16},{12,20},{16,8},{20,12},{24,0},{28,4},{1,25},{... | collective-permute-start | bytes 786440 | tf_op jit(solution)/shard_map/ppermute | solution.py:68
  709.4 25.0 %collective-permute-start.83 = (bf16[512,256]{1,0:T(8,128)(2,1)}, bf16[512,256]{1,0:T(8,128)(2,1)}, u32[]{:S(2)}, u32[]{:S(2)}) collective-permute-start(bf16[512,256]{1,0:T(8,128)(2,1)} %get-tuple-element.252), channel_id=1, source_target_pairs={{0,28},{4,24},{8,20},{12,16},{16,12},{20,8},{24,4},{28,0},{1,29},{... | collective-permute-start | bytes 786440 | tf_op jit(solution)/shard_map/ppermute | solution.py:68
  (246 other events, 2630.9 us)
Sparse Core Ops, SparseCore 0:
  21.7 60.6 all-gather.5
  84.8 140.6 all-gather.3
  425.2 173.1 reduce-scatter.2
  651.8 90.2 reduce-scatter.4

commit v3 on v2

--- a/solution.py
+++ b/solution.py
@@ -18,7 +18,8 @@
 MB = 2
 BLK = 128
 RIM = 16
-PAIRS = 640
+PAIRS = 1280
+PART = 320
 LANES = 128
 
 HIGHEST = lax.Precision.HIGHEST
@@ -129,7 +130,7 @@
     return jnp.maximum(x, 0.0) + jnp.log1p(jnp.exp(-jnp.abs(x)))
 
 
-def call(kernel, name, out_shape, args, smem=(), scratch=(), mib=48, flops=0, moved=0, **extra):
+def call(kernel, name, out_shape, args, smem=(), scratch=(), mib=60, flops=0, moved=0, **extra):
     specs = [
         pl.BlockSpec(memory_space=pltpu.SMEM if i in smem else pltpu.VMEM)
         for i in range(len(args))
@@ -151,10 +152,34 @@
     return jax.ShapeDtypeStruct(shape, dtype)
 
 
-def look_kernel(groups, rows, scal, code, table, *rest):
-    outs, listed, count, work = rest[:groups], rest[groups], rest[groups + 1], rest[groups + 2]
+def list_held(held, total):
+    runs = held.reshape(-1, LANES)
+    upper = iota((LANES, LANES), 0) <= iota((LANES, LANES), 1)
+    rank = nn(runs.astype(BF), upper.astype(BF)).astype(jnp.int32) - 1
+    here = (rank[:, :, None] == iota((1, 1, LANES), 2)) & runs[:, :, None]
+    at = jnp.sum(jnp.where(here, iota((1, LANES, 1), 1), 0), axis=1)
+    counts = rank[:, -1] + 1
+    first = iota(at.shape, 0) * LANES
+    listed = jnp.where(iota(at.shape, 1) < counts[:, None], at + first, total)
+    return listed.reshape(-1), counts
+
+
+def over_listed(listed, count, body):
+    def run(at_run, carry):
+        def turn(step, inner_carry):
+            for lane in range(8):
+                body(listed[at_run * LANES + step * 8 + lane])
+            return inner_carry
+
+        lax.fori_loop(0, (count[at_run] + 7) // 8, turn, 0)
+        return carry
+
+    lax.fori_loop(0, count.shape[0], run, 0)
+
+
+def look_kernel(groups, rows, scal, code, listed, count, table, *rest):
+    outs, work = rest[:groups], rest[groups]
     place = scal[0]
-    total = groups * rows
 
     def fill(step, carry):
         work[pl.ds(pl.multiple_of(step * rows, rows), rows), :] = jnp.zeros((rows, table.shape[1]), F32)
@@ -162,45 +187,26 @@
 
     lax.fori_loop(0, groups, fill, 0)
 
-    def note(step, found):
-        for lane in range(8):
-            at = step * 8 + lane
-            listed[found] = at
-            found = found + 1 + lax.shift_right_arithmetic(code[at], 31)
-        return found
-
-    found = lax.fori_loop(0, total // 8, note, 0)
-    for lane in range(8):
-        listed[found + lane] = total
-    count[0] = found
-
-    def turn(step, carry):
-        for lane in range(8):
-            at = listed[step * 8 + lane]
-            work[pl.ds(at, 1), :] = table[pl.ds(code[at], 1), :]
-        return carry
-
-    lax.fori_loop(0, (found + 7) // 8, turn, 0)
+    def take(at):
+        work[pl.ds(at, 1), :] = table[pl.ds(code[at], 1), :]
+
+    over_listed(listed, count, take)
     for off in range(groups):
         base = pl.multiple_of((place ^ off) * rows, rows)
         outs[off][...] = work[pl.ds(base, rows), :].astype(BF)
 
 
-def gather_rows(scal, code, table, groups, rows):
+def gather_rows(scal, code, listed, count, table, groups, rows):
     cols = table.shape[1]
-    total = groups * rows
-    vmem = pl.BlockSpec(memory_space=pltpu.VMEM)
-    smem = pl.BlockSpec(memory_space=pltpu.SMEM)
-    return pl.pallas_call(
+    return call(
         functools.partial(look_kernel, groups, rows),
-        out_shape=[sds((rows, cols), BF)] * groups + [sds((total + 8,), jnp.int32), sds((1,), jnp.int32)],
-        in_specs=[smem, smem, vmem],
-        out_specs=[vmem] * groups + [smem, smem],
-        scratch_shapes=[pltpu.VMEM((total + 8, cols), F32)],
-        compiler_params=pltpu.CompilerParams(vmem_limit_bytes=48 * MIB),
-        cost_estimate=pl.CostEstimate(flops=0, bytes_accessed=30 * MIB, transcendentals=0),
-        name="look",
-    )(scal, code, table)
+        "look",
+        [sds((rows, cols), BF)] * groups,
+        (scal, code, listed, count, table),
+        smem=(0, 1, 2, 3),
+        scratch=[pltpu.VMEM((groups * rows + 8, cols), F32)],
+        moved=30 * MIB,
+    )
 
 
 def join_kernel(groups, shards, own, scal, *rest):
@@ -229,65 +235,35 @@
     )
 
 
-def cut_kernel(groups, shards, own, scal, *rest):
-    parts, outs, work = rest[:shards], rest[shards : shards + groups], rest[-1]
-    place, shard = scal[0], scal[1]
-    half = groups // 2
-    cols = outs[0].shape[1]
-    for off in range(shards):
-        at = pl.multiple_of((shard ^ off) * own, own)
-        work[pl.ds(at, own), :] = parts[off][...]
-    for off in range(groups):
-        at = ((place ^ off) % half) * cols
-        outs[off][...] = work[:, pl.ds(pl.multiple_of(at, cols), cols)]
-
-
-def cut_parts(scal, parts, groups):
-    own = parts[0].shape[0]
-    shards = len(parts)
-    cols = 2 * D // groups
-    return call(
-        functools.partial(cut_kernel, groups, shards, own),
-        "cut",
-        [sds((own * shards, cols), BF)] * groups,
-        (scal, *parts),
-        smem=(0,),
-        scratch=[pltpu.VMEM((own * shards, D), BF)],
-        moved=4 * MIB,
-    )
-
-
-def add_kernel(groups, rows, vrows, scal, code, listed, count, share, *rest):
-    parts, out, square, work = rest[:groups], rest[groups], rest[groups + 1], rest[groups + 2]
+def add_kernel(groups, rows, vrows, scal, code, listed, count, share, parts, *rest):
+    out, square, work, bins = rest
     place = scal[0]
-    out[...] = share[0:vrows, :].astype(F32)
+    bins[...] = share[0:vrows, :].astype(F32)
     for off in range(groups):
         base = pl.multiple_of((place ^ off) * rows, rows)
-        work[pl.ds(base, rows), :] = parts[off][...].astype(F32)
+        work[pl.ds(base, rows), :] = parts[off].astype(F32)
     work[groups * rows :, :] = jnp.zeros((8, work.shape[1]), F32)
 
-    def turn(step, carry):
-        for lane in range(8):
-            at = listed[step * 8 + lane]
-            to = pl.ds(code[at], 1)
-            out[to, :] = out[to, :] + work[pl.ds(at, 1), :]
-        return carry
-
-    lax.fori_loop(0, (count[0] + 7) // 8, turn, 0)
-    total = out[...]
-    square[...] = jnp.sum(total * total, axis=0, keepdims=True)
+    def add(at):
+        to = pl.ds(code[at], 1)
+        bins[to, :] = bins[to, :] + work[pl.ds(at, 1), :]
+
+    over_listed(listed, count, add)
+    total = bins[...]
+    out[...] = total.astype(BF)
+    square[...] = jnp.sqrt(jnp.sum(total * total, axis=0, keepdims=True))
 
 
 def add_rows(scal, code, listed, count, share, parts, vrows):
     cols = share.shape[1]
-    rows = parts[0].shape[0]
+    groups, rows, _ = parts.shape
     return call(
-        functools.partial(add_kernel, len(parts), rows, vrows),
+        functools.partial(add_kernel, groups, rows, vrows),
         "addrows",
-        [sds((vrows, cols), F32), sds((1, cols), F32)],
-        (scal, code, listed, count, share, *parts),
+        [sds((vrows, cols), BF), sds((1, cols), F32)],
+        (scal, code, listed, count, share, parts),
         smem=(0, 1, 2, 3),
-        scratch=[pltpu.VMEM((rows * len(parts) + 8, cols), F32)],
+        scratch=[pltpu.VMEM((rows * groups + 8, cols), F32), pltpu.VMEM((vrows, cols), F32)],
         moved=30 * MIB,
     )
 
@@ -317,6 +293,62 @@
         [sds((D, 2 * inner), BF), sds((inner, D), BF)] * L,
         (slot, tiles),
         smem=(0,),
+        moved=14 * MIB,
+    )
+
+
+def pack_kernel(slots_each, per_layer, layers, shards, heads, scal, slot, *refs):
+    mats, sides, refs = refs[: 2 * layers], refs[2 * layers : 3 * layers], refs[3 * layers :]
+    shared, lines, out, work = refs
+    for layer in range(layers):
+        zx, wout = mats[2 * layer], mats[2 * layer + 1]
+        zx_wide, out_wide = zx.shape[1] // BLK, wout.shape[1] // BLK
+        zx_count = zx.shape[0] // BLK * zx_wide
+        for at in range(per_layer):
+            where = slot[0, layer * per_layer + at]
+            if at < zx_count:
+                source, row, col = zx, at // zx_wide, at % zx_wide
+            else:
+                source = wout
+                row, col = (at - zx_count) // out_wide, (at - zx_count) % out_wide
+            first = pl.multiple_of((where % slots_each) * BLK, BLK)
+            out[where // slots_each, pl.ds(first, BLK), :] = source[
+                row * BLK : (row + 1) * BLK, col * BLK : (col + 1) * BLK
+            ]
+        work[layer, :, : 2 * N] = sides[layer][:, : 2 * N]
+        work[layer, :, 2 * N :] = pltpu.roll(sides[layer][:, 2 * N :], scal[0] * heads, 1)
+    groups = out.shape[0]
+    each = work.shape[1] // (groups * shards)
+    piece = layers * each * work.shape[2] // LANES
+    base = slots_each * BLK
+    for group in range(groups):
+        for shard in range(shards):
+            first = (group * shards + shard) * each
+            blocks = [
+                work[layer, first : first + each, col : col + LANES]
+                for layer in range(layers)
+                for col in range(0, work.shape[2], LANES)
+            ]
+            at = base + shard * piece
+            out[group, at : at + piece, :] = jnp.concatenate(blocks, axis=0).astype(BF)
+    base += shards * piece
+    out[:, base : base + shared.shape[1], :] = shared[...]
+    for group in range(groups):
+        out[group, base + shared.shape[1] :, :] = lines[...]
+
+
+def pack_tiles(scal, slot, mats, sides, shared, lines, slots_each, per_layer, shards, heads):
+    groups = shared.shape[0]
+    layers = len(sides)
+    depth, width = sides[0].shape
+    extra = layers * depth * width // (groups * LANES) + shared.shape[1] + lines.shape[0]
+    return call(
+        functools.partial(pack_kernel, slots_each, per_layer, layers, shards, heads),
+        "packtiles",
+        sds((groups, slots_each * BLK + extra, LANES), BF),
+        (scal, slot, *mats, *sides, shared, lines),
+        smem=(0, 1),
+        scratch=[pltpu.VMEM((layers, depth, width), F32)],
         moved=14 * MIB,
     )
 
@@ -432,13 +464,238 @@
     )
 
 
-def sum_kernel(groups, shards, x_ref, o_ref, mid, from_shards, from_groups, send, recv):
+def send(source, target, send_sem, recv_sem, device):
+    copy = pltpu.make_async_remote_copy(
+        src_ref=source,
+        dst_ref=target,
+        send_sem=send_sem,
+        recv_sem=recv_sem,
+        device_id=device,
+        device_id_type=pl.DeviceIdType.MESH,
+    )
+    copy.start()
+    return copy
+
+
+def finish_kernel(groups, shards, chunks, own, *refs):
+    parts, rim, residual, gain, grad_in, out = refs[:shards], *refs[shards : shards + 5]
+    (from_shards, from_rims, payload, full, work, term_sems, rim_sems, row_sems, out_sems) = refs[
+        shards + 5 :
+    ]
+    place, shard = lax.axis_index("dp"), lax.axis_index("tensor")
+    half = groups // 2
+    cols = out.shape[2]
+    chunk = lax.rem(place, chunks)
+    last = shard == shards - 1
+    shard_peers = [(place, shard ^ off) for off in range(1, shards)]
+    group_peers = [(place ^ off, shard) for off in range(1, groups)]
+    barrier = pltpu.get_barrier_semaphore()
+
+    def greet(device):
+        pl.semaphore_signal(barrier, inc=1, device_id=device, device_id_type=pl.DeviceIdType.MESH)
+
+    for peer in shard_peers + group_peers:
+        greet(peer)
+
+    @pl.when(jnp.logical_not(last))
+    def _():
+        greet((lax.rem(place + groups - 1, groups), shards - 1))
+
+    @pl.when(last)
+    def _():
+        for other in range(shards - 1):
+            greet((lax.rem(place + 1, groups), other))
+
+    pl.semaphore_wait(barrier, shards + groups - 2 + jnp.where(last, shards - 1, 1))
+
+    def rim_copy():
+        return pltpu.make_async_remote_copy(
+            src_ref=rim,
+            dst_ref=from_rims.at[shard],
+            send_sem=rim_sems.at[0, shard],
+            recv_sem=rim_sems.at[1, shard],
+            device_id=(place - 1, shards - 1),
+            device_id_type=pl.DeviceIdType.MESH,
+        )
+
+    @pl.when(chunk > 0)
+    def _():
+        rim_copy().start()
+
+    terms = [
+        send(
+            parts[off],
+            from_shards.at[off - 1],
+            term_sems.at[0, off],
+            term_sems.at[1, off],
+            shard_peers[off - 1],
+        )
+        for off in range(1, shards)
+    ]
+    values = residual[...]
+    inv = lax.rsqrt(jnp.mean(values * values, axis=-1, keepdims=True) + NORM_EPS)
+    for term in terms:
+        term.wait()
+    total = parts[0][...].astype(F32)
+    for off in range(1, shards):
+        total = total + from_shards[off - 1].astype(F32)
+    work[...] = total
+
+    @pl.when(jnp.logical_and(chunk + 1 < chunks, last))
+    def _():
+        for other in range(shards):
+            pltpu.make_async_remote_copy(
+                src_ref=rim,
+                dst_ref=from_rims.at[other],
+                send_sem=rim_sems.at[0, other],
+                recv_sem=rim_sems.at[1, other],
+                device_id=(place + 1, other),
+                device_id_type=pl.DeviceIdType.MESH,
+            ).wait_recv()
+        edge = from_rims[0].astype(F32)
+        for other in range(1, shards):
+            edge = edge + from_rims[other].astype(F32)
+        work[own - RIM :, :] += edge
+
+    @pl.when(chunk > 0)
+    def _():
+        rim_copy().wait_send()
+
+    scaled = work[...] * gain[...]
+    result = (
+        grad_in[...]
+        + inv * scaled
+        - values * (inv * inv * inv) * jnp.mean(scaled * values, axis=-1, keepdims=True)
+    ).astype(BF)
+    payload[...] = result
+    rows_out = [
+        send(
+            payload,
+            full.at[off],
+            row_sems.at[0, off],
+            row_sems.at[1, off],
+            shard_peers[off - 1],
+        )
+        for off in range(1, shards)
+    ]
+    full[0] = result
+
+    def first_col(group):
+        return pl.multiple_of(lax.rem(group, half) * cols, cols)
+
+    cuts = []
+    for off in range(shards):
+        if off > 0:
+            rows_out[off - 1].wait()
+        at = pl.ds(pl.multiple_of((shard ^ off) * own, own), own)
+        for other in range(1, groups):
+            cuts.append(
+                send(
+                    full.at[off, :, pl.ds(first_col(place ^ other), cols)],
+                    out.at[other, at, :],
+                    out_sems.at[0, off, other],
+                    out_sems.at[1, off, other],
+                    group_peers[other - 1],
+                )
+            )
+        out[0, at, :] = full[off, :, pl.ds(first_col(place), cols)]
+    for cut in cuts:
+        cut.wait()
+
+
+def finish_rows(parts, rim, residual, gain, grad_in, groups, chunks):
+    shards = len(parts)
+    own = parts[0].shape[0]
+    vmem = pl.BlockSpec(memory_space=pltpu.VMEM)
+    args = (*parts, rim, residual, gain, grad_in)
+    return pl.pallas_call(
+        functools.partial(finish_kernel, groups, shards, chunks, own),
+        out_shape=sds((groups, own * shards, 2 * D // groups), BF),
+        in_specs=[vmem] * len(args),
+        out_specs=vmem,
+        scratch_shapes=[
+            pltpu.VMEM((shards - 1, own, D), BF),
+            pltpu.VMEM((shards, RIM, D), BF),
+            pltpu.VMEM((own, D), BF),
+            pltpu.VMEM((shards, own, D), BF),
+            pltpu.VMEM((own, D), F32),
+            pltpu.SemaphoreType.DMA((2, shards)),
+            pltpu.SemaphoreType.DMA((2, shards)),
+            pltpu.SemaphoreType.DMA((2, shards)),
+            pltpu.SemaphoreType.DMA((2, shards, groups)),
+        ],
+        compiler_params=pltpu.CompilerParams(
+            collective_id=3, has_side_effects=True, vmem_limit_bytes=32 * MIB
+        ),
+        name="finish",
+    )(*args)
+
+
+def open_kernel(groups, shards, ids, piece, ids_out, pieces_out, send, recv):
     place, shard = lax.axis_index("dp"), lax.axis_index("tensor")
     peers = [(place, shard ^ off) for off in range(1, shards)]
     peers += [(place ^ off, shard) for off in range(1, groups)]
     barrier = pltpu.get_barrier_semaphore()
     for peer in peers:
         pl.semaphore_signal(barrier, inc=1, device_id=peer, device_id_type=pl.DeviceIdType.MESH)
+    pl.semaphore_wait(barrier, len(peers))
+    copies = []
+    for i, peer in enumerate(peers):
+        copy = pltpu.make_async_remote_copy(
+            src_ref=piece if i < shards - 1 else ids,
+            dst_ref=pieces_out.at[shard] if i < shards - 1 else ids_out.at[place],
+            send_sem=send.at[i],
+            recv_sem=recv.at[i],
+            device_id=peer,
+            device_id_type=pl.DeviceIdType.MESH,
+        )
+        copy.start()
+        copies.append(copy)
+    ids_out[place] = ids[...]
+    pieces_out[shard] = piece[...]
+    for copy in copies:
+        copy.wait()
+
+
+def open_exchange(ids, piece, groups, shards):
+    count = groups + shards - 2
+    vmem = pl.BlockSpec(memory_space=pltpu.VMEM)
+    return pl.pallas_call(
+        functools.partial(open_kernel, groups, shards),
+        out_shape=[sds((groups, *ids.shape), jnp.int32), sds((shards, *piece.shape), BF)],
+        in_specs=[vmem, vmem],
+        out_specs=[vmem, vmem],
+        scratch_shapes=[pltpu.SemaphoreType.DMA((count,)), pltpu.SemaphoreType.DMA((count,))],
+        compiler_params=pltpu.CompilerParams(
+            collective_id=2, has_side_effects=True, vmem_limit_bytes=8 * MIB
+        ),
+        name="open",
+    )(ids, piece)
+
+
+def sum_kernel(groups, shards, once, split, *refs):
+    loss = refs[0]
+    refs = refs[1:]
+    count = once + split
+    ones, many, refs = refs[:once], refs[once:count], refs[count:]
+    o_ref, start, mid, from_shards, from_groups, send, recv = refs
+    place, shard = lax.axis_index("dp"), lax.axis_index("tensor")
+    peers = [(place, shard ^ off) for off in range(1, shards)]
+    peers += [(place ^ off, shard) for off in range(1, groups)]
+    barrier = pltpu.get_barrier_semaphore()
+    for peer in peers:
+        pl.semaphore_signal(barrier, inc=1, device_id=peer, device_id_type=pl.DeviceIdType.MESH)
+
+    def square(refs):
+        total = jnp.zeros((1, 1), F32)
+        for ref in refs:
+            flat = jnp.sum(ref[...] * ref[...], axis=0, keepdims=True)
+            total = total + jnp.sum(flat, axis=1, keepdims=True)
+        return total
+
+    first = (place == 0).astype(F32)
+    part = square(many) + first * square(ones)
+    start[...] = loss[...] + jnp.where(iota((8, LANES), 1) == LANES - 1, part, 0.0)
     pl.semaphore_wait(barrier, len(peers))
 
     def exchange(source, slots, first, some):
@@ -461,18 +718,25 @@
             total = total + slots[i]
         return total
 
-    mid[...] = exchange(x_ref, from_shards, 0, peers[: shards - 1])
-    o_ref[...] = exchange(mid, from_groups, shards - 1, peers[shards - 1 :])
-
-
-def sum_everywhere(x, groups, shards):
+    mid[...] = exchange(start, from_shards, 0, peers[: shards - 1])
+    total = exchange(mid, from_groups, shards - 1, peers[shards - 1 :])
+    norm = jnp.sqrt(total[0:1, LANES - 1 : LANES])
+    factor = jnp.minimum(1.0, CLIP_LIMIT / (norm + 1e-06))
+    row = iota((8, LANES), 0)
+    o_ref[...] = jnp.where(row == 0, total, jnp.where(row == 1, norm, factor))
+
+
+def sum_everywhere(loss, ones, many, groups, shards):
     count = groups + shards - 2
+    args = (loss, *ones, *many)
+    vmem = pl.BlockSpec(memory_space=pltpu.VMEM)
     return pl.pallas_call(
-        functools.partial(sum_kernel, groups, shards),
+        functools.partial(sum_kernel, groups, shards, len(ones), len(many)),
         out_shape=sds((8, LANES), F32),
-        in_specs=[pl.BlockSpec(memory_space=pltpu.VMEM)],
-        out_specs=pl.BlockSpec(memory_space=pltpu.VMEM),
+        in_specs=[vmem] * len(args),
+        out_specs=vmem,
         scratch_shapes=[
+            pltpu.VMEM((8, LANES), F32),
             pltpu.VMEM((8, LANES), F32),
             pltpu.VMEM((shards - 1, 8, LANES), F32),
             pltpu.VMEM((groups - 1, 8, LANES), F32),
@@ -483,7 +747,7 @@
             collective_id=1, has_side_effects=True, vmem_limit_bytes=8 * MIB
         ),
         name="sumall",
-    )(x)
+    )(*args)
 
 
 def conv_sum(raw, params, rows, lanes):
@@ -703,39 +967,98 @@
     return jnp.concatenate(grads, axis=0)
 
 
+def within_kernel(s_in, zx, side, dy_in, chan, bcp, head, *outs):
+    xs_out, bc_out, cum_out, starts_out, dscaled_out, dbc_out = outs
+    rows, inner = dy_in.shape
+    expand = head_map(inner)
+    pre_x = conv_sum(zx, chan, rows, pl.ds(inner, inner))
+    xs_out[...] = pre_x * sigmoid(pre_x)
+    pre_bc = conv_sum(side, bcp, rows, pl.ds(0, 2 * N))
+    bc = (pre_bc * sigmoid(pre_bc)).astype(BF)
+    bc_out[...] = bc
+    dt = softplus(side[RIM:, 2 * N :] + head[0:1, :])
+    rate = -dt * jnp.exp(head[1:2, :])
+    lower_low = (iota((SPAN, SPAN), 0) >= iota((SPAN, SPAN), 1)).astype(F32).astype(BF)
+    upper = (iota((SPAN, SPAN), 0) <= iota((SPAN, SPAN), 1)).astype(F32)
+    first_half = iota((SPAN, LANES), 1) < P_SIZE
+    spans = rows // SPAN
+    start = s_in[...]
+    for span in range(spans):
+        here = slice(span * SPAN, (span + 1) * SPAN)
+        cum = tri_sum(lower_low, rate[here])
+        cum_out[here, :] = cum
+        cum_t = cum.T
+        keys = bc[here, :N]
+        queries = bc[here, N:]
+        xs = xs_out[here, :]
+        starts_out[span] = start
+        start_low = start.astype(BF)
+        if span + 1 < spans:
+            tot = cum[SPAN - 1 : SPAN, :]
+            scale = widen(dt[here] * jnp.exp(tot - cum), expand)
+            fresh = tn(keys, (xs * scale).astype(BF))
+            start = widen(jnp.exp(tot), expand) * start + fresh
+        scores_t = nt_dot(keys, queries)
+        dy = dy_in[here, :]
+        dy_low = dy.astype(BF)
+        scaled_low = (xs * widen(dt[here], expand)).astype(BF)
+        dscores_t = jnp.zeros((SPAN, SPAN), F32)
+        for pair in range(inner // LANES):
+            lanes = slice(pair * LANES, (pair + 1) * LANES)
+            values = scaled_low[:, lanes]
+            dpair = dy_low[:, lanes]
+            both = []
+            for h in (2 * pair, 2 * pair + 1):
+                gap = cum_t[h : h + 1, :] - cum[:, h : h + 1]
+                decay = jnp.exp(jnp.minimum(gap, 0.0)) * upper
+                mine = first_half if h % 2 == 0 else jnp.logical_not(first_half)
+                outer = nt_dot(jnp.where(mine, values, jnp.zeros_like(values)), dpair)
+                dscores_t = dscores_t + outer * decay
+                both.append(nn((scores_t * decay).astype(BF), dpair))
+            dscaled_out[here, lanes] = jnp.where(first_half, both[0], both[1])
+        dscores_low = dscores_t.astype(BF)
+        dy_grown = (dy * widen(jnp.exp(cum), expand)).astype(BF)
+        dbc_out[here, :N] = nn(dscores_low, queries)
+        dbc_out[here, N:] = tn(dscores_low, keys) + nt_dot(dy_grown, start_low)
+
+
+def mixer_within(s_in, zx, side, dy, chan, bcp, head):
+    rows, inner = dy.shape
+    return call(
+        within_kernel,
+        "within",
+        [
+            sds((rows, inner), F32),
+            sds((rows, 2 * N), BF),
+            sds((rows, LANES), F32),
+            sds((rows // SPAN, N, inner), F32),
+            sds((rows, inner), F32),
+            sds((rows, 2 * N), F32),
+        ],
+        (s_in, zx, side, dy, chan, bcp, head),
+        flops=8 * rows * D * inner,
+        moved=16 * MIB,
+    )
+
+
 def back_kernel(shards, own, hops, scal, *rest):
     states, rest = rest[:hops], rest[hops:]
-    s_in, zx, side, dy_in, dz_in, y_in, wzx, wside, chan, bcp, head = rest[:11]
-    dzx, dside, chan_out, bcp_out, head_out, rim_out = rest[11:17]
-    parts, rest = rest[17 : 17 + shards], rest[17 + shards :]
-    xs_scr, dsx, dsbc, work = rest
+    xs_in, bc_in, cum_in, starts, dscaled_in, dbc_in, rest = *rest[:6], rest[6:]
+    zx, side, dy_in, dz_in, y_in, wzx, wside, chan, bcp, head = rest[:10]
+    normed, gain = rest[10:12]
+    dzx, dside, chan_out, bcp_out, head_out, rim_out, gain_out = rest[12:19]
+    parts, rest = rest[19 : 19 + shards], rest[19 + shards :]
+    dsx, dsbc, work = rest
     shard = scal[0]
     rows, inner = dy_in.shape
     expand = head_map(inner)
-    pre_x = conv_sum(zx, chan, rows, pl.ds(inner, inner))
-    xs_scr[...] = pre_x * sigmoid(pre_x)
-    pre_bc = conv_sum(side, bcp, rows, pl.ds(0, 2 * N))
-    bc = (pre_bc * sigmoid(pre_bc)).astype(BF)
     raw_dt = side[RIM:, 2 * N :] + head[0:1, :]
     dt = softplus(raw_dt)
     grow = jnp.exp(head[1:2, :])
     rate = -dt * grow
     skip = widen(head[...], expand)[2:3, :]
-    lower_low = (iota((SPAN, SPAN), 0) >= iota((SPAN, SPAN), 1)).astype(F32).astype(BF)
-    upper = (iota((SPAN, SPAN), 0) <= iota((SPAN, SPAN), 1)).astype(F32)
-    upper_low = upper.astype(BF)
-    first_half = iota((SPAN, LANES), 1) < P_SIZE
+    upper_low = (iota((SPAN, SPAN), 0) <= iota((SPAN, SPAN), 1)).astype(F32).astype(BF)
     spans = rows // SPAN
-    cums, starts = [], [s_in[...]]
-    for span in range(spans):
-        here = slice(span * SPAN, (span + 1) * SPAN)
-        cum = tri_sum(lower_low, rate[here])
-        cums.append(cum)
-        if span + 1 < spans:
-            tot = cum[SPAN - 1 : SPAN, :]
-            scale = widen(dt[here] * jnp.exp(tot - cum), expand)
-            fresh = tn(bc[here, :N], (xs_scr[here, :] * scale).astype(BF))
-            starts.append(widen(jnp.exp(tot), expand) * starts[-1] + fresh)
     dstate = chain(states, expand)
     dsx[0:RIM, :] = jnp.zeros((RIM, inner), F32)
     dsx[RIM + rows :, :] = jnp.zeros((RIM, inner), F32)
@@ -750,49 +1073,26 @@
     for span in reversed(range(spans)):
         here = slice(span * SPAN, (span + 1) * SPAN)
         there = slice(RIM + span * SPAN, RIM + (span + 1) * SPAN)
-        cum = cums[span]
-        cum_t = cum.T
+        cum = cum_in[here, :]
         tot = cum[SPAN - 1 : SPAN, :]
-        keys = bc[here, :N]
-        queries = bc[here, N:]
-        start = starts[span]
-        scores_t = nt_dot(keys, queries)
-        xs = xs_scr[here, :]
+        keys = bc_in[here, :N]
+        queries = bc_in[here, N:]
+        xs = xs_in[here, :]
         dy = dy_in[here, :]
         dy_low = dy.astype(BF)
         dt_wide = widen(dt[here], expand)
         scaled = xs * dt_wide
         scaled_low = scaled.astype(BF)
-        dscores_t = jnp.zeros((SPAN, SPAN), F32)
-        pieces = []
-        for pair in range(inner // LANES):
-            values = scaled_low[:, pair * LANES : (pair + 1) * LANES]
-            dpair = dy_low[:, pair * LANES : (pair + 1) * LANES]
-            both = []
-            for h in (2 * pair, 2 * pair + 1):
-                gap = cum_t[h : h + 1, :] - cum[:, h : h + 1]
-                decay = jnp.exp(jnp.minimum(gap, 0.0)) * upper
-                mine = first_half if h % 2 == 0 else jnp.logical_not(first_half)
-                outer = nt_dot(jnp.where(mine, values, jnp.zeros_like(values)), dpair)
-                dscores_t = dscores_t + outer * decay
-                both.append(nn((scores_t * decay).astype(BF), dpair))
-            pieces.append(jnp.where(first_half, both[0], both[1]))
-        dscaled = jnp.concatenate(pieces, axis=1)
-        dscores_low = dscores_t.astype(BF)
-        grown = widen(jnp.exp(cum), expand)
         tail = widen(jnp.exp(tot - cum), expand)
-        dy_grown = (dy * grown).astype(BF)
         dstate_low = dstate.astype(BF)
         through = tail * nn(keys, dstate_low)
-        dscaled = dscaled + through
-        dqueries = tn(dscores_low, keys) + nt_dot(dy_grown, start.astype(BF))
-        dkeys = nn(dscores_low, queries) + nt_dot((scaled * tail).astype(BF), dstate_low)
+        dscaled = dscaled_in[here, :] + through
         plain = y_in[here, :] - skip * xs
         held = scaled_low.astype(F32)
         dcum = narrow(dy_low.astype(F32) * plain - held * dscaled, expand)
         tot_wide = widen(jnp.exp(tot), expand)
         over = jnp.sum(held * through, axis=0, keepdims=True) + jnp.sum(
-            tot_wide * dstate * start, axis=0, keepdims=True
+            tot_wide * dstate * starts[span], axis=0, keepdims=True
         )
         dtot = narrow(jnp.broadcast_to(over, (8, inner)), expand)[0:1, :]
         drate = tri_sum(upper_low, dcum) + dtot
@@ -804,10 +1104,11 @@
         over = jnp.sum(dy * xs, axis=0, keepdims=True)
         dskip = dskip + narrow(jnp.broadcast_to(over, (8, inner)), expand)[0:1, :]
         dsx[there, :] = dscaled * dt_wide + skip * dy
-        dsbc[there, :N] = dkeys
-        dsbc[there, N:] = dqueries
+        dsbc[there, :N] = dbc_in[here, :N] + nt_dot((scaled * tail).astype(BF), dstate_low)
+        dsbc[there, N:] = dbc_in[here, N:]
         if span > 0:
-            dstate = tot_wide * dstate + tn(queries, dy_grown)
+            grown = widen(jnp.exp(cum), expand)
+            dstate = tot_wide * dstate + tn(queries, (dy * grown).astype(BF))
     body = pl.ds(RIM, rows)
     pre_x = conv_sum(zx, chan, rows, pl.ds(inner, inner))
     dsx[body, :] = dsx[body, :] * silu_slope(pre_x)
@@ -818,14 +1119,18 @@
     )
     bcp_out[...] = conv_back(dsbc, side, bcp, rows, pl.ds(0, 2 * N), 2 * N, dside, pl.ds(0, 2 * N))
     head_out[...] = jnp.concatenate([dbias, dgrow, dskip, jnp.zeros((5, LANES), F32)], axis=0)
-    work[...] = (nt_dot(dzx[...], wzx[...]) + nt_dot(dside[...], wside[...])).astype(BF)
+    dnormed = nt_dot(dzx[...], wzx[...]) + nt_dot(dside[...], wside[...])
+    work[...] = dnormed.astype(BF)
+    gain_out[...] = jnp.sum(dnormed * normed[...].astype(F32), axis=0, keepdims=True) / gain[...]
     rim_out[...] = work[0:RIM, :]
     for off in range(shards):
         at = pl.multiple_of(RIM + (shard ^ off) * own, RIM)
         parts[off][...] = work[pl.ds(at, own), :]
 
 
-def mixer_back(scal, states, s_in, zx, side, dy, dz, y, wzx, wside, chan, bcp, head, shards):
+def mixer_back(
+    scal, states, inside, zx, side, dy, dz, y, wzx, wside, chan, bcp, head, normed, gain, shards
+):
     rows, inner = dy.shape
     own = rows // shards
     ext = rows + RIM
@@ -839,12 +1144,12 @@
             sds((8, 2 * N), F32),
             sds((8, LANES), F32),
             sds((RIM, D), BF),
+            sds((1, D), F32),
         ]
         + [sds((own, D), BF)] * shards,
-        (scal, *states, s_in, zx, side, dy, dz, y, wzx, wside, chan, bcp, head),
+        (scal, *states, *inside, zx, side, dy, dz, y, wzx, wside, chan, bcp, head, normed, gain),
         smem=(0,),
         scratch=[
-            pltpu.VMEM((rows, inner), F32),
             pltpu.VMEM((ext + RIM, inner), F32),
             pltpu.VMEM((ext + RIM, 2 * N), F32),
             pltpu.VMEM((ext, D), BF),
@@ -869,22 +1174,26 @@
         target[...] = jnp.zeros((1, rows), F32)
         plain[...] = jnp.zeros((1, rows), F32)
 
-    padding = jnp.where(step * PAIRS + iota((PAIRS, LANES), 0) < vrows, 0.0, -1e30)
-    padding = jnp.concatenate([padding] * (rows // LANES), axis=1)
     highest, summed, hit, whole = top[...], total[...], target[...], plain[...]
-    wanted = label[...] - 2 * step * PAIRS
-    line = 2 * iota((PAIRS, rows), 0)
+    line = 2 * iota((PART, rows), 0)
     for half in range(2):
-        raw = nn(table[:, half * D : (half + 1) * D], rows_scr[...])
-        shown = raw + padding
-        before = highest
-        highest = jnp.maximum(before, jnp.max(shown, axis=0, keepdims=True))
-        part = jnp.exp(shown - highest)
-        summed = summed * jnp.exp(before - highest) + jnp.sum(part, axis=0, keepdims=True)
-        hit = hit + jnp.sum(jnp.where(line == wanted - half, raw, 0.0), axis=0, keepdims=True)
-        whole = whole + jnp.sum(raw, axis=0, keepdims=True)
-        p_out[half] = part.astype(BF)
-        tops[0, 8 * half : 8 * half + 8, :] = jnp.broadcast_to(highest, (8, rows))
+        for part_at in range(PAIRS // PART):
+            first = step * PAIRS + part_at * PART
+            here = slice(part_at * PART, (part_at + 1) * PART)
+            padding = jnp.where(first + iota((PART, LANES), 0) < vrows, 0.0, -1e30)
+            padding = jnp.concatenate([padding] * (rows // LANES), axis=1)
+            raw = nn(table[here, half * D : (half + 1) * D], rows_scr[...])
+            shown = raw + padding
+            before = highest
+            highest = jnp.maximum(before, jnp.max(shown, axis=0, keepdims=True))
+            part = jnp.exp(shown - highest)
+            summed = summed * jnp.exp(before - highest) + jnp.sum(part, axis=0, keepdims=True)
+            wanted = label[...] - 2 * first - half
+            hit = hit + jnp.sum(jnp.where(line == wanted, raw, 0.0), axis=0, keepdims=True)
+            whole = whole + jnp.sum(raw, axis=0, keepdims=True)
+            p_out[half, here, :] = part.astype(BF)
+            at = 8 * (half * (PAIRS // PART) + part_at)
+            tops[0, at : at + 8, :] = jnp.broadcast_to(highest, (8, rows))
     top[...] = highest
     total[...] = summed
     target[...] = hit
@@ -904,7 +1213,7 @@
         grid=(steps,),
         out_shape=[
             sds((2, padded, rows), BF),
-            sds((steps, 16, rows), F32),
+            sds((steps, 16 * (PAIRS // PART), rows), F32),
             sds((8, rows), F32),
         ],
         in_specs=[
@@ -914,12 +1223,12 @@
         + [pl.BlockSpec((own, D), whole)] * shards,
         out_specs=[
             pl.BlockSpec((2, PAIRS, rows), lambda i: (0, i, 0)),
-            pl.BlockSpec((1, 16, rows), lambda i: (i, 0, 0)),
+            pl.BlockSpec((1, 16 * (PAIRS // PART), rows), lambda i: (i, 0, 0)),
             pl.BlockSpec((8, rows), whole),
         ],
         scratch_shapes=[pltpu.VMEM((D, rows), BF)] + [pltpu.VMEM((1, rows), F32)] * 4,
         compiler_params=pltpu.CompilerParams(
-            dimension_semantics=("arbitrary",), vmem_limit_bytes=48 * MIB
+            dimension_semantics=("arbitrary",), vmem_limit_bytes=56 * MIB
         ),
         cost_estimate=pl.CostEstimate(
             flops=4 * rows * D * padded, bytes_accessed=40 * MIB, transcendentals=2 * rows * padded
@@ -928,27 +1237,32 @@
     )(label, table, *blocks)
 
 
-def rows_kernel(shards, own, vrows, label, scale, weight, p_in, table, *rest):
-    q_out, parts, acc = rest[0], rest[1 : 1 + shards], rest[-1]
+def logit_grads(step, label, scale, weight, p_in):
+    pairs, rows = p_in.shape[1:]
+    line = 2 * iota((PART, rows), 0)
+    usual = (SMOOTHING / V) * weight[...]
+    special = (1.0 - SMOOTHING + SMOOTHING / V) * weight[...]
+    for half in range(2):
+        pieces = []
+        for part_at in range(pairs // PART):
+            wanted = label[...] - 2 * (step * pairs + part_at * PART) - half
+            share = jnp.where(line == wanted, special, usual)
+            at = 8 * (half * (pairs // PART) + part_at)
+            grown = p_in[half, part_at * PART : (part_at + 1) * PART, :].astype(F32)
+            pieces.append((grown * scale[0, at : at + 1, :] - share).astype(BF))
+        yield half, jnp.concatenate(pieces, axis=0)
+
+
+def rows_kernel(shards, own, label, scale, weight, p_in, table, *rest):
+    parts, acc = rest[:shards], rest[-1]
     step = pl.program_id(0)
-    rows = own * shards
 
     @pl.when(step == 0)
     def _():
         acc[...] = jnp.zeros_like(acc)
 
-    wanted = label[...] - 2 * step * PAIRS
-    line = 2 * iota((PAIRS, rows), 0)
-    usual = (SMOOTHING / V) * weight[...]
-    special = (1.0 - SMOOTHING + SMOOTHING / V) * weight[...]
-    term = None
-    for half in range(2):
-        share = jnp.where(line == wanted - half, special, usual)
-        q = (p_in[half].astype(F32) * scale[0, 8 * half : 8 * half + 1, :] - share).astype(BF)
-        q_out[half] = q
-        part = tn(q, table[:, half * D : (half + 1) * D])
-        term = part if term is None else term + part
-    acc[...] += term
+    for half, q in logit_grads(step, label, scale, weight, p_in):
+        acc[...] += tn(q, table[:, half * D : (half + 1) * D])
 
     @pl.when(step == pl.num_programs(0) - 1)
     def _():
@@ -956,49 +1270,52 @@
             parts[off][...] = acc[off * own : (off + 1) * own, :].astype(BF)
 
 
-def vocab_rows(label, scale, weight, p_in, table, vrows, shards):
+def vocab_specs(rows):
+    whole = lambda i: (0, 0)
+    return [
+        pl.BlockSpec((1, rows), whole),
+        pl.BlockSpec((1, 16 * (PAIRS // PART), rows), lambda i: (i, 0, 0)),
+        pl.BlockSpec((1, rows), whole),
+        pl.BlockSpec((2, PAIRS, rows), lambda i: (0, i, 0)),
+    ]
+
+
+def vocab_rows(label, scale, weight, p_in, table, shards):
     _, padded, rows = p_in.shape
-    steps = padded // PAIRS
     own = rows // shards
     whole = lambda i: (0, 0)
     return pl.pallas_call(
-        functools.partial(rows_kernel, shards, own, vrows),
-        grid=(steps,),
-        out_shape=[sds((2, padded, rows), BF)] + [sds((own, D), BF)] * shards,
-        in_specs=[
-            pl.BlockSpec((1, rows), whole),
-            pl.BlockSpec((1, 16, rows), lambda i: (i, 0, 0)),
-            pl.BlockSpec((1, rows), whole),
-            pl.BlockSpec((2, PAIRS, rows), lambda i: (0, i, 0)),
-            pl.BlockSpec((PAIRS, 2 * D), lambda i: (i, 0)),
-        ],
-        out_specs=[pl.BlockSpec((2, PAIRS, rows), lambda i: (0, i, 0))]
-        + [pl.BlockSpec((own, D), whole)] * shards,
+        functools.partial(rows_kernel, shards, own),
+        grid=(padded // PAIRS,),
+        out_shape=[sds((own, D), BF)] * shards,
+        in_specs=vocab_specs(rows) + [pl.BlockSpec((PAIRS, 2 * D), lambda i: (i, 0))],
+        out_specs=[pl.BlockSpec((own, D), whole)] * shards,
         scratch_shapes=[pltpu.VMEM((rows, D), F32)],
         compiler_params=pltpu.CompilerParams(
-            dimension_semantics=("arbitrary",), vmem_limit_bytes=48 * MIB
+            dimension_semantics=("arbitrary",), vmem_limit_bytes=56 * MIB
         ),
         cost_estimate=pl.CostEstimate(
-            flops=4 * rows * D * padded, bytes_accessed=52 * MIB, transcendentals=0
+            flops=4 * rows * D * padded, bytes_accessed=40 * MIB, transcendentals=0
         ),
         name="rowgrads",
     )(label, scale, weight, p_in, table)
 
 
-def table_kernel(shards, own, q_in, *rest):
+def table_kernel(shards, own, label, scale, weight, p_in, *rest):
     blocks, out, rows_scr = rest[:shards], rest[shards], rest[-1]
-
-    @pl.when(pl.program_id(0) == 0)
+    step = pl.program_id(0)
+
+    @pl.when(step == 0)
     def _():
         for off in range(shards):
             rows_scr[off * own : (off + 1) * own, :] = blocks[off][...]
 
-    for half in range(2):
-        out[:, half * D : (half + 1) * D] = nn(q_in[half], rows_scr[...]).astype(BF)
-
-
-def vocab_table_grad(q_in, blocks):
-    _, padded, rows = q_in.shape
+    for half, q in logit_grads(step, label, scale, weight, p_in):
+        out[:, half * D : (half + 1) * D] = nn(q, rows_scr[...]).astype(BF)
+
+
+def vocab_table_grad(label, scale, weight, p_in, blocks):
+    _, padded, rows = p_in.shape
     shards = len(blocks)
     own = blocks[0].shape[0]
     whole = lambda i: (0, 0)
@@ -1006,18 +1323,17 @@
         functools.partial(table_kernel, shards, own),
         grid=(padded // PAIRS,),
         out_shape=sds((padded, 2 * D), BF),
-        in_specs=[pl.BlockSpec((2, PAIRS, rows), lambda i: (0, i, 0))]
-        + [pl.BlockSpec((own, D), whole)] * shards,
+        in_specs=vocab_specs(rows) + [pl.BlockSpec((own, D), whole)] * shards,
         out_specs=pl.BlockSpec((PAIRS, 2 * D), lambda i: (i, 0)),
         scratch_shapes=[pltpu.VMEM((rows, D), BF)],
         compiler_params=pltpu.CompilerParams(
-            dimension_semantics=("arbitrary",), vmem_limit_bytes=48 * MIB
+            dimension_semantics=("arbitrary",), vmem_limit_bytes=56 * MIB
         ),
         cost_estimate=pl.CostEstimate(
             flops=4 * rows * D * padded, bytes_accessed=40 * MIB, transcendentals=0
         ),
         name="tablegrads",
-    )(q_in, *blocks)
+    )(label, scale, weight, p_in, *blocks)
 
 
 def adam_update(weight_in, gradient, moment_one, moment_two, factor, fix_one, fix_two, decay_rate):
@@ -1028,32 +1344,105 @@
     return (weight_in - LEARN_RATE * (direction + decay_rate * weight_in), one_next, two_next)
 
 
-def soap_turn(gradient, bases):
-    left_basis = bases[..., 0, :, :]
-    right_basis = bases[..., 1, :, :]
-    half_turn = jnp.einsum("...ab,...ac->...bc", left_basis, gradient, precision=HIGHEST)
-    return jnp.einsum("...bc,...cd->...bd", half_turn, right_basis, precision=HIGHEST)
-
-
-def soap_update(weight_in, turned_grad, bases, moment_one, moment_two, factor, fix_one, fix_two):
-    left_basis = bases[..., 0, :, :]
-    right_basis = bases[..., 1, :, :]
-    rotated = turned_grad * factor
-    one_next = BETA_FIRST * moment_one + (1.0 - BETA_FIRST) * rotated
-    two_next = BETA_SECOND * moment_two + (1.0 - BETA_SECOND) * rotated * rotated
-    direction = one_next / fix_one / (jnp.sqrt(two_next / fix_two) + ADAM_EPS)
-    back_half = jnp.einsum("...ab,...bc->...ac", left_basis, direction, precision=HIGHEST)
-    turned = jnp.einsum("...ac,...dc->...ad", back_half, right_basis, precision=HIGHEST)
-    weight_next = weight_in - LEARN_RATE * (turned + WEIGHT_DECAY * weight_in)
-    return (weight_next, weight_next.astype(BF), one_next, two_next)
-
-
-def to_blocks(matrix):
-    row_count, col_count = matrix.shape
-    return (
-        matrix.reshape(row_count // BLK, BLK, col_count // BLK, BLK)
-        .transpose(0, 2, 1, 3)
-        .reshape(-1, BLK, BLK)
+def turn_kernel(share, bases, turned, root):
+    count = bases.shape[0]
+    total = jnp.zeros((1, BLK), F32)
+
+    def turn(at, total):
+        grad = share[pl.ds(pl.multiple_of(at * BLK, BLK), BLK), :].astype(F32)
+        half_turn = tn(bases[at, 0], grad, HIGHEST)
+        turned[at] = nn(half_turn, bases[at, 1], HIGHEST)
+        return total + jnp.sum(grad * grad, axis=0, keepdims=True)
+
+    for at in range(count):
+        total = turn(at, total)
+    root[...] = jnp.sqrt(total)
+
+
+def turn_tiles(share, bases):
+    count = bases.shape[0]
+    return call(
+        turn_kernel,
+        "turn",
+        [sds((count, BLK, BLK), F32), sds((1, BLK), F32)],
+        (share, bases),
+        moved=6 * MIB,
+    )
+
+
+def last_kernel(small, fixes, sums, *refs):
+    tiles, turned, bases, tile_one, tile_two = refs[:5]
+    little, refs = refs[5 : 5 + 4 * small], refs[5 + 4 * small :]
+    tiles_out, copy_out, tile_one_out, tile_two_out = refs[:4]
+    little_out = refs[4:]
+    factor, fix_one, fix_two = sums[2:3, 0:1], fixes[0], fixes[1]
+    for at in range(tiles.shape[0]):
+        rotated = turned[at] * factor
+        one_next = BETA_FIRST * tile_one[at] + (1.0 - BETA_FIRST) * rotated
+        two_next = BETA_SECOND * tile_two[at] + (1.0 - BETA_SECOND) * rotated * rotated
+        direction = one_next / fix_one / (jnp.sqrt(two_next / fix_two) + ADAM_EPS)
+        back_half = nn(bases[at, 0], direction, HIGHEST)
+        back = nt_dot(back_half, bases[at, 1], HIGHEST)
+        after = tiles[at] - LEARN_RATE * (back + WEIGHT_DECAY * tiles[at])
+        tiles_out[at] = after
+        copy_out[at] = after.astype(BF)
+        tile_one_out[at] = one_next
+        tile_two_out[at] = two_next
+
+    @pl.when(pl.program_id(0) == 0)
+    def _():
+        for which in range(small):
+            before, gradient, first, second = (ref[...] for ref in little[4 * which : 4 * which + 4])
+            results = adam_update(
+                before,
+                gradient,
+                first,
+                second,
+                factor,
+                fix_one,
+                fix_two,
+                WEIGHT_DECAY if which == 0 else 0.0,
+            )
+            outs = little_out[3 * which : 3 * which + 3]
+            outs[0][...] = results[0] if which == 0 else results[0] - before
+            outs[1][...], outs[2][...] = results[1], results[2]
+
+
+def last_update(fixes, sums, tiles, turned, bases, tile_one, tile_two, little):
+    count = tiles.shape[0]
+    each = 4 if count % 4 == 0 else 2
+    tile_spec = pl.BlockSpec((each, BLK, BLK), lambda i: (i, 0, 0))
+    base_spec = pl.BlockSpec((each, 2, BLK, BLK), lambda i: (i, 0, 0, 0))
+    whole = [pl.BlockSpec(x.shape, lambda i: (0, 0)) for group in little for x in group]
+    return pl.pallas_call(
+        functools.partial(last_kernel, len(little)),
+        grid=(count // each,),
+        out_shape=[sds(tiles.shape, F32), sds(tiles.shape, BF), sds(tiles.shape, F32), sds(tiles.shape, F32)]
+        + [sds(group[0].shape, F32) for group in little for _ in range(3)],
+        in_specs=[
+            pl.BlockSpec(memory_space=pltpu.SMEM),
+            pl.BlockSpec(sums.shape, lambda i: (0, 0)),
+        ]
+        + [tile_spec, tile_spec, base_spec, tile_spec, tile_spec]
+        + whole,
+        out_specs=[tile_spec] * 4
+        + [spec for which in range(len(little)) for spec in whole[4 * which : 4 * which + 3]],
+        compiler_params=pltpu.CompilerParams(
+            dimension_semantics=("arbitrary",), vmem_limit_bytes=48 * MIB
+        ),
+        cost_estimate=pl.CostEstimate(
+            flops=24 * count * BLK * BLK * BLK, bytes_accessed=16 * MIB, transcendentals=0
+        ),
+        name="update",
+    )(
+        fixes,
+        sums,
+        tiles,
+        turned,
+        bases,
+        tile_one,
+        tile_two,
+        *[x for group in little for x in group],
     )
 
 
@@ -1062,10 +1451,6 @@
     for off in range(1, lax.axis_size(axis)):
         out = out + swap(x, axis, off)
     return out
-
-
-def rms_scale(values):
-    return lax.rsqrt(jnp.mean(values * values, axis=-1, keepdims=True) + NORM_EPS)
 
 
 def shards(
@@ -1127,19 +1512,29 @@
     )
     piece_rows = piece.shape[0]
     side_part = piece_rows - share_pad // LANES
-    pieces = jnp.zeros((nt, piece_rows, LANES), BF)
-    for off in range(nt):
-        pieces = lax.dynamic_update_index_in_dim(
-            pieces, piece if off == 0 else swap(piece, "tensor", off), shard ^ off, 0
-        )
+    ids = jnp.pad(jnp.concatenate([token_ids, labels], axis=0), ((0, 8 - 2 * seqs), (0, 0)))
+    ids_all, pieces = open_exchange(ids, piece, nd, nt)
+    ids_all = ids_all.transpose(1, 0, 2).reshape(8, length)
+    all_ids = ids_all[:seqs].reshape(-1)
+    local_row = all_ids // 2 - shard * vrows
+    held = (local_row >= 0) & (local_row < vrows) & (all_ids % 2 == place // half)
+    scal = jnp.stack([place, shard]).astype(jnp.int32)
+    scal_shard = shard.astype(jnp.int32).reshape(1)
+    code = jnp.concatenate([jnp.where(held, local_row, 0), jnp.zeros((8,), jnp.int32)])
+    listed, count = list_held(held, nd * rows)
     own_tiles = layer_blocks.shape[2]
-    carried = jnp.concatenate(
-        [layer_blocks.astype(BF).reshape(own_tiles * BLK, BLK), pieces.reshape(-1, LANES)], axis=0
-    )
-    gathered = lax.all_gather(carried, "dp", axis=0, tiled=False)
-    ids_all = lax.all_gather(jnp.concatenate([token_ids, labels], axis=0), "dp", axis=1, tiled=True)
-    table_low = jnp.pad(vocab_table.astype(BF), ((0, padded - vrows), (0, 0)))
-
+    gathered = lax.all_gather(
+        jnp.concatenate(
+            [layer_blocks.astype(BF).reshape(own_tiles * BLK, BLK), pieces.reshape(-1, LANES)], axis=0
+        ),
+        "dp",
+        axis=0,
+        tiled=False,
+    )
+    parts = gather_rows(scal, code, listed, count, vocab_table, nd, rows)
+    table_now, parts = lax.optimization_barrier((vocab_table, parts))
+    parts = [parts[0]] + [swap(parts[off], "dp", off) for off in range(1, nd)]
+    table_low = jnp.pad(table_now.astype(BF), ((0, padded - vrows), (0, 0)))
     placed = place_tiles(block_slot, gathered, own_tiles, inner, zx_count, per_layer)
     small = gathered[:, own_tiles * BLK :].reshape(nd, nt, piece_rows, LANES)
     side_full = (
@@ -1151,15 +1546,6 @@
     shared_full = small[:, :, side_part:].reshape(nd * nt, share_pad)[:, :share_size].reshape(-1)
     shared_full = shared_full.astype(F32)
 
-    all_ids = ids_all[:seqs].reshape(-1)
-    local_row = all_ids // 2 - shard * vrows
-    held = (local_row >= 0) & (local_row < vrows) & (all_ids % 2 == place // half)
-    scal = jnp.stack([place, shard]).astype(jnp.int32)
-    scal_shard = shard.astype(jnp.int32).reshape(1)
-    code = jnp.concatenate([jnp.where(held, local_row, -1), jnp.zeros((8,), jnp.int32)])
-    parts = gather_rows(scal, code, vocab_table, nd, rows)
-    listed, count = parts[nd], parts[nd + 1]
-    parts = [parts[0]] + [swap(parts[off], "dp", off) for off in range(1, nd)]
     parts = join_parts(scal, parts, nt, own)
     table_all = lax.all_gather(table_low, "dp", axis=1, tiled=True)
 
@@ -1235,7 +1621,7 @@
     ).reshape(rows)
     my_seq = place // chunks
     weight = jnp.where(row_at % length < seq_lengths[my_seq], seq_weight[my_seq], 0.0)
-    all_labels = ids_all[seqs:].reshape(-1)
+    all_labels = ids_all[seqs : 2 * seqs].reshape(-1)
     label = (all_labels[row_at] - 2 * shard * vrows).reshape(1, rows)
 
     p_low, tops, stats = vocab_logits(label, table_all, final_rows, vrows)
@@ -1261,13 +1647,14 @@
         + ZLOSS_WEIGHT * log_total * log_total
     )
     loss_here = jnp.sum(weight[:own] * token_loss[0])
-    seq_part = jnp.where(jnp.arange(seqs) == my_seq, loss_here, 0.0)
+    seq_part = jnp.where(
+        (iota((8, LANES), 0) == 0) & (iota((8, LANES), 1) == my_seq), loss_here, 0.0
+    )
     soft = (weight.reshape(nt, own) * (1.0 + 2.0 * ZLOSS_WEIGHT * log_total)).reshape(1, 1, rows)
     scale = soft * jnp.exp(tops - log_total.reshape(1, 1, rows))
-    result = vocab_rows(label, scale, weight.reshape(1, rows), p_low, table_all, vrows, nt)
-    q_low = result[0]
-    sent = returned(result[1:])
-    table_grad = vocab_table_grad(q_low, final_rows)
+    row_weight = weight.reshape(1, rows)
+    sent = returned(vocab_rows(label, scale, row_weight, p_low, table_all, nt))
+    table_grad = vocab_table_grad(label, scale, row_weight, p_low, final_rows)
     sent, table_grad = lax.optimization_barrier((sent, table_grad))
     table_share = lax.psum_scatter(table_grad, "dp", scatter_dimension=1, tiled=True)
     grad_res, payload, grad_final_gain = back_rows(
@@ -1287,119 +1674,156 @@
         )
         states = [hop(dstate, -k) for k in hops]
         grad_out_w = tn(u_low, grads)
+        inside = mixer_within(s_in, zx, side, dy, chan, bcp, head)
         result = mixer_back(
-            scal_shard, states, s_in, zx, side, dy, dz, y, wzx, wside, chan, bcp, head, nt
+            scal_shard,
+            states,
+            inside,
+            zx,
+            side,
+            dy,
+            dz,
+            y,
+            wzx,
+            wside,
+            chan,
+            bcp,
+            head,
+            normed,
+            gains[layer_index],
+            nt,
         )
-        dzx, dside, chan_grad, bcp_grad, head_grad, rim_grad = result[:6]
-        rims = [
-            lax.ppermute(rim_grad, both, [(b, a) for a, b in rim_pairs(to)]) for to in range(nt)
-        ]
-        below = (saved[layer_index - 1][9], saved[layer_index - 1][8]) if layer_index else None
-        grad_res, payload, grad_gain_in = back_rows(
-            returned(result[6:]), rims, residual_in, gains[layer_index], grad_res, below
-        )
+        dzx, dside, chan_grad, bcp_grad, head_grad, rim_grad, grad_gain_in = result[:7]
+        parts_out = result[7:]
         grad_zx_w = tn(normed, dzx)
         grad_side_w = tn(normed, dside)
-        block_pieces[2 * layer_index] = to_blocks(grad_zx_w.astype(BF))
-        block_pieces[2 * layer_index + 1] = to_blocks(grad_out_w.astype(BF))
-        spaced = lax.dynamic_update_slice(
-            jnp.zeros((D, LANES), F32),
-            grad_side_w[:, 2 * N : 2 * N + heads],
-            (jnp.zeros((), jnp.int32), shard * heads),
-        )
-        side_pieces[layer_index] = jnp.concatenate([grad_side_w[:, : 2 * N], spaced], axis=1)
-        channel_pieces[layer_index] = jnp.concatenate([chan_grad[:5], gain_grad], axis=0)
-        head_pieces[layer_index] = head_grad[:3, :heads]
+        block_pieces[2 * layer_index] = grad_zx_w.astype(BF)
+        block_pieces[2 * layer_index + 1] = grad_out_w.astype(BF)
+        side_pieces[layer_index] = grad_side_w
         shared_pieces[layer_index] = jnp.concatenate(
             [grad_gain_in[0], bcp_grad[:4].reshape(-1), bcp_grad[4]]
         )
-
-    embed = cut_parts(scal, spread(payload), nd)
-    embed = [embed[0]] + [swap(embed[off], "dp", off) for off in range(1, nd)]
-
-    inverse = jnp.zeros((tiles,), jnp.int32).at[block_slot[0]].set(jnp.arange(tiles, dtype=jnp.int32))
-    ordered_grads = jnp.concatenate(block_pieces, axis=0)
-    slot_grads = ordered_grads[inverse].reshape(nd, own_tiles * BLK, BLK)
-    side_grads = (
-        jnp.stack(side_pieces)
-        .astype(BF)
-        .reshape(L, nd, nt, side_rows, 2 * N + LANES)
-        .transpose(1, 2, 0, 3, 4)
-        .reshape(nd, nt, side_part, LANES)
-    )
-    shared_grads = jnp.concatenate(shared_pieces + [grad_final_gain[0]]).astype(BF)
-    shared_grads = jnp.pad(
-        shared_grads.reshape(nd, nt, share_size), ((0, 0), (0, 0), (0, share_pad - share_size))
-    ).reshape(nd, nt, share_pad // LANES, LANES)
-    small_grads = jnp.concatenate([side_grads, shared_grads], axis=2).reshape(nd, -1, LANES)
-    tile_grads = jnp.concatenate([slot_grads, small_grads], axis=1)
-    tile_grads, table_share = lax.optimization_barrier((tile_grads, table_share))
-    block_share = lax.psum_scatter(tile_grads, "dp", scatter_dimension=0, tiled=True)[0]
-    block_grads = block_share[: own_tiles * BLK].astype(F32)
-    small_share = block_share[own_tiles * BLK :].reshape(nt, piece_rows, LANES)
+        channel_pieces[layer_index] = jnp.concatenate([chan_grad[:5], gain_grad], axis=0)
+        head_pieces[layer_index] = head_grad[:3, :heads]
+        if layer_index == 0:
+            shared_grads = jnp.concatenate(shared_pieces + [grad_final_gain[0]]).astype(BF)
+            shared_grads = jnp.pad(
+                shared_grads.reshape(nd * nt, share_size), ((0, 0), (0, share_pad - share_size))
+            ).reshape(nd, nt * share_pad // LANES, LANES)
+            lines = jnp.concatenate(
+                [
+                    jnp.stack(channel_pieces).reshape(-1, LANES),
+                    jnp.pad(jnp.stack(head_pieces).reshape(-1), (0, LANES - L * 3 * heads)).reshape(
+                        1, LANES
+                    ),
+                ],
+                axis=0,
+            ).astype(BF)
+            line_count = lines.shape[0]
+            line_rows = -(-line_count // RIM) * RIM
+            lines = jnp.pad(lines, ((0, line_rows - line_count), (0, 0)))
+            tile_grads = pack_tiles(
+                scal_shard,
+                block_slot,
+                block_pieces,
+                side_pieces,
+                shared_grads,
+                lines,
+                own_tiles,
+                per_layer,
+                nt,
+                heads,
+            )
+            tile_grads, table_share, parts_out, rim_grad = lax.optimization_barrier(
+                (tile_grads, table_share, parts_out, rim_grad)
+            )
+            block_share = lax.psum_scatter(tile_grads, "dp", scatter_dimension=0, tiled=True)[0]
+        if layer_index:
+            rims = [
+                lax.ppermute(rim_grad, both, [(b, a) for a, b in rim_pairs(to)]) for to in range(nt)
+            ]
+            grad_res, payload, _ = back_rows(
+                returned(parts_out),
+                rims,
+                residual_in,
+                gains[layer_index],
+                grad_res,
+                (saved[layer_index - 1][9], saved[layer_index - 1][8]),
+            )
+        else:
+            embed = finish_rows(
+                parts_out, rim_grad, residual_in, gains[0], grad_res, nd, chunks
+            )
+
+    side_count = nt * side_part
+    small_share = jnp.concatenate(
+        [
+            block_share[own_tiles * BLK : own_tiles * BLK + side_count].reshape(nt, side_part, LANES),
+            block_share[own_tiles * BLK + side_count : own_tiles * BLK + nt * piece_rows].reshape(
+                nt, piece_rows - side_part, LANES
+            ),
+        ],
+        axis=1,
+    )
     mine = jnp.zeros((piece_rows, LANES), F32)
     for off in range(nt):
-        sent = lax.dynamic_index_in_dim(small_share, shard ^ off, 0, False)
-        mine = mine + (sent if off == 0 else swap(sent, "tensor", off)).astype(F32)
-    side_share = mine[:side_part].reshape(L, side_rows, 2 * N + LANES)[:, :, : 2 * N + H]
-    shared_share = mine[side_part:].reshape(-1)[:share_size]
-    lines = jnp.concatenate(
-        [
-            jnp.stack(channel_pieces).reshape(-1, LANES),
-            jnp.pad(jnp.stack(head_pieces).reshape(-1), (0, LANES - L * 3 * heads)).reshape(1, LANES),
-        ],
-        axis=0,
-    )
-    lines = total_over(lines, "dp")
-    channel_sum = lines[:-1].reshape(channel_params.shape)
-    head_sum = lines[-1, : L * 3 * heads].reshape(head_params.shape)
-
-    grad_table, table_square = add_rows(
-        scal, jnp.maximum(code, 0), listed, count, table_share, embed, vrows
-    )
-    rotated = soap_turn(block_grads.reshape(layer_blocks.shape), block_bases)
-    first_copy = (place == 0).astype(F32)
-    square_part = (
-        jnp.sum(block_grads * block_grads)
-        + jnp.sum(table_square)
-        + jnp.sum(side_share * side_share)
-        + jnp.sum(shared_share * shared_share)
-        + first_copy * (jnp.sum(channel_sum * channel_sum) + jnp.sum(head_sum * head_sum))
-    )
-    packed = jnp.pad(jnp.concatenate([seq_part, square_part[None]]), (0, 8 * LANES - seqs - 1))
-    packed, rotated = lax.optimization_barrier((packed, rotated))
-    packed = sum_everywhere(packed.reshape(8, LANES), nd, nt)[0]
-    seq_loss = packed[:seqs]
-    clip_norm = jnp.sqrt(packed[seqs])
-    factor = jnp.minimum(1.0, CLIP_LIMIT / (clip_norm + 1e-06))
+        piece = lax.dynamic_index_in_dim(small_share, shard ^ off, 0, False)
+        mine = mine + (piece if off == 0 else swap(piece, "tensor", off)).astype(F32)
+    side_share = (
+        mine[:side_part]
+        .reshape(L, 2 * N // LANES + 1, side_rows, LANES)
+        .transpose(0, 2, 1, 3)
+        .reshape(L * side_rows, 2 * N + LANES)[:, : 2 * N + H]
+    )
+    shared_share = mine[side_part:].reshape(1, -1)[:, :share_size]
+    lines = block_share[own_tiles * BLK + nt * piece_rows :].astype(F32)
+    channel_sum = lines[: line_count - 1].reshape(L * 6, inner)
+    head_sum = lines[line_count - 1, : L * 3 * heads].reshape(L * 3, heads)
+    rotated, tile_root = turn_tiles(block_share, block_bases.reshape(own_tiles, 2, BLK, BLK))
+    grad_table, table_root = add_rows(scal, code, listed, count, table_share, embed, vrows)
+    sums = sum_everywhere(
+        seq_part,
+        [channel_sum, head_sum],
+        [table_root, tile_root, side_share, shared_share],
+        nd,
+        nt,
+    )
+    seq_loss = sums[0, :seqs]
+    clip_norm = sums[1, 0]
     steps_done = step_count[0].astype(F32)
     fix_one = 1.0 - jnp.power(BETA_FIRST, steps_done)
     fix_two = 1.0 - jnp.power(BETA_SECOND, steps_done)
+    tile_shape = layer_blocks.shape[2:]
+    flat = lambda x: x.reshape((-1, x.shape[-1]))
+    little = [
+        [flat(side_proj), side_share, flat(side_first), flat(side_second)],
+        [flat(shared_params), shared_share, flat(shared_first), flat(shared_second)],
+        [flat(channel_params), channel_sum, flat(channel_first), flat(channel_second)],
+        [flat(head_params), head_sum, flat(head_first), flat(head_second)],
+    ]
+    updated = last_update(
+        jnp.stack([fix_one, fix_two]),
+        sums,
+        layer_blocks.reshape(tile_shape),
+        rotated,
+        block_bases.reshape((own_tiles, 2, BLK, BLK)),
+        block_first.reshape(tile_shape),
+        block_second.reshape(tile_shape),
+        little,
+    )
     table_out = adam_update(
-        vocab_table, grad_table, vocab_first, vocab_second, factor, fix_one, fix_two, WEIGHT_DECAY
-    )
-    block_out = soap_update(
-        layer_blocks,
-        rotated,
-        block_bases,
-        block_first,
-        block_second,
-        factor,
+        vocab_table,
+        grad_table.astype(F32),
+        vocab_first,
+        vocab_second,
+        sums[2, 0],
         fix_one,
         fix_two,
-    )
-    side_next = adam_update(
-        side_proj, side_share, side_first, side_second, factor, fix_one, fix_two, WEIGHT_DECAY
-    )
-    shared_next = adam_update(
-        shared_params, shared_share, shared_first, shared_second, factor, fix_one, fix_two, 0.0
-    )
-    channel_next = adam_update(
-        channel_params, channel_sum, channel_first, channel_second, factor, fix_one, fix_two, 0.0
-    )
-    head_next = adam_update(
-        head_params, head_sum, head_first, head_second, factor, fix_one, fix_two, 0.0
-    )
+        WEIGHT_DECAY,
+    )
+    block_out = [x.reshape(layer_blocks.shape) for x in updated[:4]]
+    like = [side_proj] * 3 + [shared_params] * 3 + [channel_params] * 3 + [head_params] * 3
+    small_out = [x.reshape(y.shape) for x, y in zip(updated[4:], like)]
     return (
         seq_loss,
         clip_norm,
@@ -1410,18 +1834,7 @@
         block_out[1],
         block_out[2],
         block_out[3],
-        side_next[0],
-        side_next[1],
-        side_next[2],
-        shared_next[0] - shared_params,
-        shared_next[1],
-        shared_next[2],
-        channel_next[0] - channel_params,
-        channel_next[1],
-        channel_next[2],
-        head_next[0] - head_params,
-        head_next[1],
-        head_next[2],
+        *small_out,
     )
 
 

time: 828 us -> 751 us (0.907)
  Pallas kernels: 193 us -> 315 us
  local copies, waits for them, and re-layouts: 113 us -> 40.5 us
  waiting for transfers between devices: 241 us -> 195 us
  starting transfers between devices: 149 us -> 114 us
  other arithmetic: 71.1 us -> 44 us
  blocking collectives: 9.08 us -> 0 us
    pallas_call x3 -> x5, Pallas kernels: 56.9 us -> 126 us  [the longest x1 73 us: finish_rows(): pl.pallas_call(functools.partial(finish_kernel, groups, shards, chunks, o...]
    pallas_call x18 -> x21, Pallas kernels: 87.2 us -> 144 us  [call(): pl.pallas_call(kernel, out_shape=out_shape, in_specs=specs, out_specs=jax...]
    ppermute x66 -> x43, waiting for transfers between devices: 208 us -> 165 us  [swap(): return lax.ppermute(x, axis, [(i, i ^ offset) for i in range(size)])]
    unnamed x367 -> x236, local copies, waits for them, and re-layouts: 54.5 us -> 19.9 us
    ppermute x66 -> x43, starting transfers between devices: 106 us -> 76.7 us  [swap(): return lax.ppermute(x, axis, [(i, i ^ offset) for i in range(size)])]
    concatenate x6 -> x0, other arithmetic: 16.3 us -> none  [the longest x1 6.61 us: shards(): tile_grads = jnp.concatenate([slot_grads, small_grads], axis=1)]
    dot_general x4 -> x1, matrix products: 13.1 us -> 0.14 us  [nn(): lax.dot_general(a, b, (((1,), (0,)), ((), ())), precision=precision, pref...]
    ppermute x12, waiting for transfers between devices: 33.7 us -> 21.6 us  [hop(): return lax.ppermute(x, 'dp', pairs)]
  transfers between devices with their start and end apart: 98 -> 71, of which waited for: 39 -> 30; matrix products, arithmetic and copies ran while one was open for 14% -> 8% of each run, Pallas kernels for 16% -> 32%
where the time goes in v3:
time: 751 us; the launch traced here: 744 us
  Pallas kernels  315 us (42%)
  waiting for transfers between devices  195 us (26%)
  starting transfers between devices  114 us (15%)
  other arithmetic  44 us (6%)
  local copies, waits for them, and re-layouts  40.5 us (5%)
  matrix products  19.2 us (3%)
  between operations  16.7 us (2%)
    ppermute x43, waiting for transfers between devices, swap(): return lax.ppermute(x, axis, [(i, i ^ offset) for i in range(size)])  165 us
    pallas_call x21, Pallas kernels, call(): pl.pallas_call(kernel, out_shape=out_shape, in_specs=specs, out_specs=jax...  144 us
    ppermute x43, starting transfers between devices, swap(): return lax.ppermute(x, axis, [(i, i ^ offset) for i in range(size)])  76.7 us
    pallas_call x1, Pallas kernels, finish_rows(): pl.pallas_call(functools.partial(finish_kernel, groups, shards, chunks, o...  73 us
    ppermute x12, starting transfers between devices, hop(): return lax.ppermute(x, 'dp', pairs)  28.6 us
    pallas_call x1, Pallas kernels, vocab_logits(): pl.pallas_call(functools.partial(logits_kernel, shards, own, vrows), grid...  24.7 us
    ppermute x12, waiting for transfers between devices, hop(): return lax.ppermute(x, 'dp', pairs)  21.6 us
    pallas_call x1, Pallas kernels, vocab_table_grad(): pl.pallas_call(functools.partial(table_kernel, shards, own), grid=(padded...  20.8 us
  transfers between devices with their start and end apart: 71, of which 30 were waited for; matrix products, arithmetic and copies ran while one was open for 8% of the time, Pallas kernels for 32%

profile of v3, /device:TPU:0, one launch (start us, length us, event | category | flops | bytes accessed | tf_op | source)
XLA Modules:
  0.0 744.2 jit_solution(7626396974171032875)
XLA Ops:
  10.5 12.3 %open.1 = (s32[8,8,256]{2,1,0:T(8,128)S(1)}, bf16[4,208,128]{2,1,0:T(8,128)(2,1)S(1)}) custom-call(s32[8,256]{1,0:T(8,128)S(1)} %pad.51.ids, bf16[208,128]{1,0:T(8,128)(2,1)S(1)} %pad_maximum_fusion.1.piece), custom_call_target="tpu_custom_call" | custom-call | tf_op jit(solution)/shard_map/open/pallas_call | solution.py:663
  27.7 10.0 %look.1 = (bf16[512,256]{1,0:T(8,128)(2,1)}, bf16[512,256]{1,0:T(8,128)(2,1)}, bf16[512,256]{1,0:T(8,128)(2,1)}, bf16[512,256]{1,0:T(8,128)(2,1)}, bf16[512,256]...) custom-call(s32[2]{0:T(128)} %pad_add_fusion.1.scal, ...), custom_call_target="tpu_custom_call" | custom-call | bytes 31457280 | tf_op jit(solution)/shard_map/look/pallas_call | solution.py:138
  72.9 9.6 %collective-permute-done.6.rest_7_ = bf16[512,256]{1,0:T(8,128)(2,1)S(1)} collective-permute-done((bf16[512,256]{1,0:T(8,128)(2,1)S(1)}, bf16[512,256]{1,0:T(8,128)(2,1)S(1)}, u32[]{:S(2)}, u32[]{:S(2)}) %collective-permute-start.6) | collective-permute-done | bytes 262176 | tf_op jit(solution)/shard_map/ppermute | solution.py:69
  97.0 10.3 %collective-permute-done.8.refs_2_ = bf16[128,1024]{1,0:T(8,128)(2,1)S(1)} collective-permute-done((bf16[128,1024]{1,0:T(8,128)(2,1)}, bf16[128,1024]{1,0:T(8,128)(2,1)S(1)}, u32[]{:S(2)}, u32[]{:S(2)}) %collective-permute-start.8) | collective-permute-done | bytes 262176 | tf_op jit(solution)/shard_map/ppermute | solution.py:69
  125.7 8.3 %placetiles.1 = (bf16[1024,1024]{1,0:T(8,128)(2,1)}, bf16[512,1024]{1,0:T(8,128)(2,1)}, bf16[1024,1024]{1,0:T(8,128)(2,1)}, bf16[512,1024]{1,0:T(8,128)(2,1)}) custom-call(s32[1,192]{1,0:T(1,128)} %slot.3, bf16[8,3904,128]{2,1,0:T(8,128)(2,1)} %bitcast.336), custom_call_target="tpu_custom_call" | custom-call | bytes 14680064 | tf_op jit(solution)/shard_map/placetiles/pallas_call | solution.py:138
  147.9 11.9 %collective-permute-start.17 = (bf16[144,512]{1,0:T(8,128)(2,1)}, bf16[144,512]{1,0:T(8,128)(2,1)S(1)}, u32[]{:S(2)}, u32[]{:S(2)}) collective-permute-start(bf16[144,512]{1,0:T(8,128)(2,1)} %get-tuple-element.199), channel_id=1, source_target_pairs={{0,4},{4,8},{8,12},{16,20},{20,24},{24,28},{1,5},{5,9},{9,13},{17,... | collective-permute-start | bytes 442376 | tf_op jit(solution)/shard_map/ppermute | solution.py:1587
  191.3 12.8 %collective-permute-done.21.refs_2_ = bf16[128,1152]{1,0:T(8,128)(2,1)S(1)} collective-permute-done((bf16[128,1152]{1,0:T(8,128)(2,1)}, bf16[128,1152]{1,0:T(8,128)(2,1)S(1)}, u32[]{:S(2)}, u32[]{:S(2)}) %collective-permute-start.21) | collective-permute-done | bytes 294944 | tf_op jit(solution)/shard_map/ppermute | solution.py:69
  221.6 11.7 %collective-permute-done.24.rest_2_ = bf16[128,1024]{1,0:T(8,128)(2,1)S(1)} collective-permute-done((bf16[128,1024]{1,0:T(8,128)(2,1)}, bf16[128,1024]{1,0:T(8,128)(2,1)S(1)}, u32[]{:S(2)}, u32[]{:S(2)}) %collective-permute-start.24) | collective-permute-done | bytes 262176 | tf_op jit(solution)/shard_map/ppermute | solution.py:69
  271.3 13.2 %collective-permute-done.34.refs_2_ = bf16[128,1152]{1,0:T(8,128)(2,1)S(1)} collective-permute-done((bf16[128,1152]{1,0:T(8,128)(2,1)}, bf16[128,1152]{1,0:T(8,128)(2,1)S(1)}, u32[]{:S(2)}, u32[]{:S(2)}) %collective-permute-start.34) | collective-permute-done | bytes 294944 | tf_op jit(solution)/shard_map/ppermute | solution.py:69
  301.6 10.8 %collective-permute-done.37.rest_2_ = bf16[128,1024]{1,0:T(8,128)(2,1)S(1)} collective-permute-done((bf16[128,1024]{1,0:T(8,128)(2,1)}, bf16[128,1024]{1,0:T(8,128)(2,1)S(1)}, u32[]{:S(2)}, u32[]{:S(2)}) %collective-permute-start.37) | collective-permute-done | bytes 262176 | tf_op jit(solution)/shard_map/ppermute | solution.py:69
  313.2 24.7 %logits.1 = (bf16[2,6400,512]{2,1,0:T(8,128)(2,1)}, f32[5,64,512]{2,1,0:T(8,128)}, f32[8,512]{1,0:T(8,128)}) custom-call(s32[1,512]{1,0:T(1,128)} %bitcast.380, bf16[6400,2048]{1,0:T(8,128)(2,1)} %all-gather.4.cloned.1.call-done.table, bf16[128,1024]{1,0:T(8,128)(2,1)} %get-tuple-element.223.rest_0_, bf16[128,1024]{1,0:T(8,128)(2,1)} %copy-done.80, ...), custom_call_target="tpu_custom_call" | custom-call | flops 13421772800 | bytes 41943040 | tf_op jit(solution)/shard_map/logits/pallas_call | solution.py:1211
  352.4 20.1 %rowgrads.1 = (bf16[128,1024]{1,0:T(8,128)(2,1)}, bf16[128,1024]{1,0:T(8,128)(2,1)}, bf16[128,1024]{1,0:T(8,128)(2,1)}, bf16[128,1024]{1,0:T(8,128)(2,1)}) custom-call(s32[1,512]{1,0:T(1,128)} %bitcast.381, f32[5,64,512]{2,1,0:T(8,128)} %exponential_multiply_fusion.scale, f32[1,512]{1,0:T(1,128)} %compare_select_fusion.3.weight, ...), custom_call_target="tpu_custom_call" | custom-call | flops 13421772800 | bytes 41943040 | tf_op jit(solution)/shard_map/rowgrads/pallas_call | solution.py:1287
  376.9 20.8 %tablegrads.1 = bf16[6400,2048]{1,0:T(8,128)(2,1)} custom-call(s32[1,512]{1,0:T(1,128)} %bitcast.382, f32[5,64,512]{2,1,0:T(8,128)} %exponential_multiply_fusion.scale, f32[1,512]{1,0:T(1,128)} %compare_select_fusion.3.weight, bf16[2,6400,512]{2,1,0:T(8,128)(2,1)} %get-tuple-element.227.p_in, bf16[128,1024]{1,0:T(8,128)(2,1)} %get-tuple-element.223.rest_0_, ...), custom_call_target="tpu_custom_call" | custom-call | flops 13421772800 | bytes 41943040 | tf_op jit(solution)/shard_map/tablegrads/pallas_call | solution.py:1322
  413.6 9.3 %collective-permute-done.46.rest_2_ = bf16[128,1152]{1,0:T(8,128)(2,1)S(1)} collective-permute-done((bf16[128,1152]{1,0:T(8,128)(2,1)}, bf16[128,1152]{1,0:T(8,128)(2,1)S(1)}, u32[]{:S(2)}, u32[]{:S(2)}) %collective-permute-start.46) | collective-permute-done | bytes 294944 | tf_op jit(solution)/shard_map/ppermute | solution.py:69
  447.2 14.0 %back.2 = (bf16[528,1024]{1,0:T(8,128)(2,1)}, bf16[528,384]{1,0:T(8,128)(2,1)}, f32[8,512]{1,0:T(8,128)}, f32[8,256]{1,0:T(8,128)}, f32[8,128]{1,0:T(8,128)}, /*...) custom-call(s32[1]{0:T(128)} %bitcast.9.scal, ...), custom_call_target="tpu_custom_call" | custom-call | flops 2147483648 | bytes 16777216 | tf_op jit(solution)/shard_map/back/pallas_call | solution.py:138
  478.6 11.6 %collective-permute-done.52.refs_2_ = bf16[128,1024]{1,0:T(8,128)(2,1)S(1)} collective-permute-done((bf16[128,1024]{1,0:T(8,128)(2,1)}, bf16[128,1024]{1,0:T(8,128)(2,1)S(1)}, u32[]{:S(2)}, u32[]{:S(2)}) %collective-permute-start.52) | collective-permute-done | bytes 262176 | tf_op jit(solution)/shard_map/ppermute | solution.py:69
  507.6 13.6 %collective-permute-done.59.rest_2_ = bf16[128,1152]{1,0:T(8,128)(2,1)S(1)} collective-permute-done((bf16[128,1152]{1,0:T(8,128)(2,1)}, bf16[128,1152]{1,0:T(8,128)(2,1)S(1)}, u32[]{:S(2)}, u32[]{:S(2)}) %collective-permute-start.59) | collective-permute-done | bytes 294944 | tf_op jit(solution)/shard_map/ppermute | solution.py:69
  552.5 14.2 %back.3 = (bf16[528,1024]{1,0:T(8,128)(2,1)}, bf16[528,384]{1,0:T(8,128)(2,1)}, f32[8,512]{1,0:T(8,128)}, f32[8,256]{1,0:T(8,128)}, f32[8,128]{1,0:T(8,128)}, /*...) custom-call(s32[1]{0:T(128)} %bitcast.9.scal, ...), custom_call_target="tpu_custom_call" | custom-call | flops 2147483648 | bytes 16777216 | tf_op jit(solution)/shard_map/back/pallas_call | solution.py:138
  578.6 9.4 %packtiles.1 = bf16[8,3968,128]{2,1,0:T(8,128)(2,1)} custom-call(s32[1]{0:T(128)} %bitcast.9.scal, s32[1,192]{1,0:T(1,128)} %slot.3, bf16[1024,1024]{1,0:T(8,128)(2,1)} %convolution_convert_fusion.1.refs_0_, bf16[512,1024]{1,0:T(8,128)(2,1)} %convolution_convert_fusion.3.refs_1_, bf16[1024,1024]{1,0:T(8,128)(2,1)} %convolution_convert_fusion.refs_2_, ...), custom_call_target="tpu_custom_call" | custom-call | bytes 14680064 | tf_op jit(solution)/shard_map/packtiles/pallas_call | solution.py:138
  590.7 73.0 %finish.1.parts = bf16[8,512,256]{2,1,0:T(8,128)(2,1)S(1)} custom-call(bf16[128,1024]{1,0:T(8,128)(2,1)S(1)} %copy-done.7, bf16[128,1024]{1,0:T(8,128)(2,1)S(1)} %copy-done.8, bf16[128,1024]{1,0:T(8,128)(2,1)S(1)} %copy-done.9, bf16[128,1024]{1,0:T(8,128)(2,1)S(1)} %copy-done.10, bf16[16,1024]{1,0:T(8,128)(2,1)S(1)} %copy-done.14, ...), custom_call_target="tpu_custom_call" | custom-call | tf_op jit(solution)/shard_map/finish/pallas_call | solution.py:611
  665.1 11.7 %addrows.1 = (bf16[6286,256]{1,0:T(8,128)(2,1)}, f32[1,256]{1,0:T(1,128)}) custom-call(s32[2]{0:T(128)} %pad_add_fusion.1.scal, s32[4104]{0:T(1024)} %concatenate.45.code, s32[4096]{0:T(1024)} %select_bitcast_fusion.listed, s32[32]{0:T(128)} %copy-done.70, bf16[6400,256]{1,0:T(8,128)(2,1)} %reduce-scatter.3.cloned.1.call-done.share, bf16[8,512,256]{2,1,0:T(8,128)(2,1)} %copy-done), custom_call_target="tpu_custom_call" | custom-call | bytes 31457280 | tf_op jit(solution)/shard_map/addrows/pallas_call | solution.py:138
  694.8 9.9 %sumall.1.sums = f32[8,128]{1,0:T(8,128)S(1)} custom-call(f32[8,128]{1,0:T(8,128)S(1)} %and_select_fusion.1.refs_0_, f32[12,512]{1,0:T(8,128)S(1)} %reshape.605.refs_1_.refs_14_, f32[6,8]{1,0:T(8,128)S(1)} %reshape_squeeze.3.refs_2_.refs_18_, f32[1,256]{1,0:T(1,128)S(1)} %copy-done.18, f32[1,128]{1,0:T(1,128)S(1)} %copy-done.19, f32[64,288]{1,0:T(8,128)S(1)} %bitcast.319, ...), custom_call_target="tpu_custom_call" | custom-call | tf_op jit(solution)/shard_map/sumall/pallas_call | solution.py:733
  707.2 10.1 %update.1 = (f32[24,128,128]{2,1,0:T(8,128)}, bf16[24,128,128]{2,1,0:T(8,128)(2,1)}, f32[24,128,128]{2,1,0:T(8,128)}, f32[24,128,128]{2,1,0:T(8,128)}, f32[64,28...) custom-call(f32[2]{0:T(128)S(1)} %pad_maximum_fusion.20.fixes, ...), custom_call_target="tpu_custom_call" | custom-call | flops 1207959552 | bytes 16777216 | tf_op jit(solution)/shard_map/update/pallas_call | solution.py:1417
  721.0 16.4 %multiply_subtract_fusion = (f32[6286,256]{1,0:T(8,128)}, f32[6286,256]{1,0:T(8,128)}, f32[6286,256]{1,0:T(8,128)}) fusion(f32[6286,256]{1,0:T(8,128)} %table.1, f32[]{:T(128)} %bitcast.88, f32[]{:T(128)} %bitcast.87, f32[]{:T(128)} %bitcast.86, bf16[6286,256]{1,0:T(8,128)(2,1)} %get-tuple-element.309, f32[6286,256]{1,0:T(8,128)} %param.33, f32[6286,256]{1,0:T(8,128)} %param.32), kind=kLoop, calls=%fused_computation.3 | loop fusion | flops 27356672 | bytes 41839628 | tf_op jit(solution)/shard_map/sub | solution.py:1344
  (526 shorter events, 357.7 us)
Async XLA Ops:
  7.2 87.2 %all-gather.6.cloned.1.call-start = ((), (), s32[]{:S(2)}) async-start(), calls=%async_computation.5 | async-start | bytes 8994816 | tf_op jit(solution)/shard_map/all_gather | solution.py:1526
  23.9 288.5 %all-gather.4.cloned.1.call-start = ((), (), s32[]{:S(2)}) async-start(), calls=%async_computation.2 | async-start | bytes 29491200 | tf_op jit(solution)/shard_map/all_gather | solution.py:1550
  42.9 545.1 %reduce-scatter.3.cloned.1.call-start = ((), (), s32[]{:S(2)}) async-start(), calls=%async_computation.3 | async-start | bytes 29491200 | tf_op jit(solution)/shard_map/reduce_scatter | solution.py:1659
  46.0 21.7 %collective-permute-start.4 = (bf16[512,256]{1,0:T(8,128)(2,1)S(1)}, bf16[512,256]{1,0:T(8,128)(2,1)S(1)}, u32[]{:S(2)}, u32[]{:S(2)}) collective-permute-start(bf16[512,256]{1,0:T(8,128)(2,1)S(1)} %copy-done.85), channel_id=1, source_target_pairs={{0,20},{4,16},{8,28},{12,24},{16,4},{20,0},{24,12},{28,8},{1,21},{... | collective-permute-start | bytes 786440 | tf_op jit(solution)/shard_map/ppermute | solution.py:69
  47.3 25.6 %collective-permute-start.5 = (bf16[512,256]{1,0:T(8,128)(2,1)S(1)}, bf16[512,256]{1,0:T(8,128)(2,1)S(1)}, u32[]{:S(2)}, u32[]{:S(2)}) collective-permute-start(bf16[512,256]{1,0:T(8,128)(2,1)S(1)} %copy-done.84), channel_id=1, source_target_pairs={{0,24},{4,28},{8,16},{12,20},{16,8},{20,12},{24,0},{28,4},{1,25},{... | collective-permute-start | bytes 786440 | tf_op jit(solution)/shard_map/ppermute | solution.py:69
  52.9 29.6 %collective-permute-start.6 = (bf16[512,256]{1,0:T(8,128)(2,1)S(1)}, bf16[512,256]{1,0:T(8,128)(2,1)S(1)}, u32[]{:S(2)}, u32[]{:S(2)}) collective-permute-start(bf16[512,256]{1,0:T(8,128)(2,1)S(1)} %copy-done.83), channel_id=1, source_target_pairs={{0,28},{4,24},{8,20},{12,16},{16,12},{20,8},{24,4},{28,0},{1,29},{... | collective-permute-start | bytes 786440 | tf_op jit(solution)/shard_map/ppermute | solution.py:69
  85.9 21.4 %collective-permute-start.8 = (bf16[128,1024]{1,0:T(8,128)(2,1)}, bf16[128,1024]{1,0:T(8,128)(2,1)S(1)}, u32[]{:S(2)}, u32[]{:S(2)}) collective-permute-start(bf16[128,1024]{1,0:T(8,128)(2,1)} %get-tuple-element.194), channel_id=1, source_target_pairs={{0,2},{1,3},{2,0},{3,1},{4,6},{5,7},{6,4},{7,5},{8,10},{9,11},{10,... | collective-permute-start | bytes 786440 | tf_op jit(solution)/shard_map/ppermute | solution.py:69
  86.0 21.4 %collective-permute-start.9 = (bf16[128,1024]{1,0:T(8,128)(2,1)}, bf16[128,1024]{1,0:T(8,128)(2,1)S(1)}, u32[]{:S(2)}, u32[]{:S(2)}) collective-permute-start(bf16[128,1024]{1,0:T(8,128)(2,1)} %get-tuple-element.195), channel_id=1, source_target_pairs={{0,3},{1,2},{2,1},{3,0},{4,7},{5,6},{6,5},{7,4},{8,11},{9,10},{10,... | collective-permute-start | bytes 786440 | tf_op jit(solution)/shard_map/ppermute | solution.py:69
  110.4 23.6 %collective-permute-start.10 = (bf16[128,1024]{1,0:T(8,128)(2,1)}, bf16[128,1024]{1,0:T(8,128)(2,1)}, u32[]{:S(2)}, u32[]{:S(2)}) collective-permute-start(bf16[128,1024]{1,0:T(8,128)(2,1)} %get-tuple-element.197.rest_0_), channel_id=1, source_target_pairs={{0,1},{1,0},{2,3},{3,2},{4,5},{5,4},{6,7},{7,6},{8,9},{9,8},{10,11... | collective-permute-start | bytes 786440 | tf_op jit(solution)/shard_map/ppermute | solution.py:69
  116.5 23.1 %collective-permute-start.11 = (bf16[128,1024]{1,0:T(8,128)(2,1)}, bf16[128,1024]{1,0:T(8,128)(2,1)}, u32[]{:S(2)}, u32[]{:S(2)}) collective-permute-start(bf16[128,1024]{1,0:T(8,128)(2,1)} %get-tuple-element.197.rest_0_), channel_id=1, source_target_pairs={{0,2},{1,3},{2,0},{3,1},{4,6},{5,7},{6,4},{7,5},{8,10},{9,11},{10,... | collective-permute-start | bytes 786440 | tf_op jit(solution)/shard_map/ppermute | solution.py:69
  116.5 23.1 %collective-permute-start.12 = (bf16[128,1024]{1,0:T(8,128)(2,1)}, bf16[128,1024]{1,0:T(8,128)(2,1)}, u32[]{:S(2)}, u32[]{:S(2)}) collective-permute-start(bf16[128,1024]{1,0:T(8,128)(2,1)} %get-tuple-element.197.rest_0_), channel_id=1, source_target_pairs={{0,3},{1,2},{2,1},{3,0},{4,7},{5,6},{6,5},{7,4},{8,11},{9,10},{10,... | collective-permute-start | bytes 786440 | tf_op jit(solution)/shard_map/ppermute | solution.py:69
  181.6 22.4 %collective-permute-start.21 = (bf16[128,1152]{1,0:T(8,128)(2,1)}, bf16[128,1152]{1,0:T(8,128)(2,1)S(1)}, u32[]{:S(2)}, u32[]{:S(2)}) collective-permute-start(bf16[128,1152]{1,0:T(8,128)(2,1)} %get-tuple-element.207), channel_id=1, source_target_pairs={{0,2},{1,3},{2,0},{3,1},{4,6},{5,7},{6,4},{7,5},{8,10},{9,11},{10,... | collective-permute-start | bytes 884744 | tf_op jit(solution)/shard_map/ppermute | solution.py:69
  181.6 22.4 %collective-permute-start.22 = (bf16[128,1152]{1,0:T(8,128)(2,1)}, bf16[128,1152]{1,0:T(8,128)(2,1)S(1)}, u32[]{:S(2)}, u32[]{:S(2)}) collective-permute-start(bf16[128,1152]{1,0:T(8,128)(2,1)} %get-tuple-element.208), channel_id=1, source_target_pairs={{0,3},{1,2},{2,1},{3,0},{4,7},{5,6},{6,5},{7,4},{8,11},{9,10},{10,... | collective-permute-start | bytes 884744 | tf_op jit(solution)/shard_map/ppermute | solution.py:69
  261.2 23.3 %collective-permute-start.34 = (bf16[128,1152]{1,0:T(8,128)(2,1)}, bf16[128,1152]{1,0:T(8,128)(2,1)S(1)}, u32[]{:S(2)}, u32[]{:S(2)}) collective-permute-start(bf16[128,1152]{1,0:T(8,128)(2,1)} %get-tuple-element.220), channel_id=1, source_target_pairs={{0,2},{1,3},{2,0},{3,1},{4,6},{5,7},{6,4},{7,5},{8,10},{9,11},{10,... | collective-permute-start | bytes 884744 | tf_op jit(solution)/shard_map/ppermute | solution.py:69
  261.2 23.3 %collective-permute-start.35 = (bf16[128,1152]{1,0:T(8,128)(2,1)}, bf16[128,1152]{1,0:T(8,128)(2,1)S(1)}, u32[]{:S(2)}, u32[]{:S(2)}) collective-permute-start(bf16[128,1152]{1,0:T(8,128)(2,1)} %get-tuple-element.221), channel_id=1, source_target_pairs={{0,3},{1,2},{2,1},{3,0},{4,7},{5,6},{6,5},{7,4},{8,11},{9,10},{10,... | collective-permute-start | bytes 884744 | tf_op jit(solution)/shard_map/ppermute | solution.py:69
  372.6 25.2 %collective-permute-start.42 = (bf16[128,1024]{1,0:T(8,128)(2,1)}, bf16[128,1024]{1,0:T(8,128)(2,1)S(1)}, u32[]{:S(2)}, u32[]{:S(2)}) collective-permute-start(bf16[128,1024]{1,0:T(8,128)(2,1)} %get-tuple-element.229), channel_id=1, source_target_pairs={{0,1},{1,0},{2,3},{3,2},{4,5},{5,4},{6,7},{7,6},{8,9},{9,8},{10,11... | collective-permute-start | bytes 786440 | tf_op jit(solution)/shard_map/ppermute | solution.py:69
  372.6 25.2 %collective-permute-start.43 = (bf16[128,1024]{1,0:T(8,128)(2,1)}, bf16[128,1024]{1,0:T(8,128)(2,1)S(1)}, u32[]{:S(2)}, u32[]{:S(2)}) collective-permute-start(bf16[128,1024]{1,0:T(8,128)(2,1)} %get-tuple-element.230), channel_id=1, source_target_pairs={{0,2},{1,3},{2,0},{3,1},{4,6},{5,7},{6,4},{7,5},{8,10},{9,11},{10,... | collective-permute-start | bytes 786440 | tf_op jit(solution)/shard_map/ppermute | solution.py:69
  374.0 23.8 %collective-permute-start.44 = (bf16[128,1024]{1,0:T(8,128)(2,1)}, bf16[128,1024]{1,0:T(8,128)(2,1)S(1)}, u32[]{:S(2)}, u32[]{:S(2)}) collective-permute-start(bf16[128,1024]{1,0:T(8,128)(2,1)} %get-tuple-element.231), channel_id=1, source_target_pairs={{0,3},{1,2},{2,1},{3,0},{4,7},{5,6},{6,5},{7,4},{8,11},{9,10},{10,... | collective-permute-start | bytes 786440 | tf_op jit(solution)/shard_map/ppermute | solution.py:69
  398.6 281.9 %reduce-scatter.5.cloned.1.call-start = ((), (), s32[]{:S(2)}) async-start(), calls=%async_computation.4 | async-start | bytes 9142272 | tf_op jit(solution)/shard_map/reduce_scatter | solution.py:1740
  401.4 21.5 %collective-permute-start.46 = (bf16[128,1152]{1,0:T(8,128)(2,1)}, bf16[128,1152]{1,0:T(8,128)(2,1)S(1)}, u32[]{:S(2)}, u32[]{:S(2)}) collective-permute-start(bf16[128,1152]{1,0:T(8,128)(2,1)} %get-tuple-element.239.rest_0_), channel_id=1, source_target_pairs={{0,2},{1,3},{2,0},{3,1},{4,6},{5,7},{6,4},{7,5},{8,10},{9,11},{10,... | collective-permute-start | bytes 884744 | tf_op jit(solution)/shard_map/ppermute | solution.py:69
  498.4 22.8 %collective-permute-start.59 = (bf16[128,1152]{1,0:T(8,128)(2,1)}, bf16[128,1152]{1,0:T(8,128)(2,1)S(1)}, u32[]{:S(2)}, u32[]{:S(2)}) collective-permute-start(bf16[128,1152]{1,0:T(8,128)(2,1)} %get-tuple-element.261.rest_0_), channel_id=1, source_target_pairs={{0,2},{1,3},{2,0},{3,1},{4,6},{5,7},{6,4},{7,5},{8,10},{9,11},{10,... | collective-permute-start | bytes 884744 | tf_op jit(solution)/shard_map/ppermute | solution.py:69
  498.4 22.8 %collective-permute-start.60 = (bf16[128,1152]{1,0:T(8,128)(2,1)}, bf16[128,1152]{1,0:T(8,128)(2,1)S(1)}, u32[]{:S(2)}, u32[]{:S(2)}) collective-permute-start(bf16[128,1152]{1,0:T(8,128)(2,1)} %get-tuple-element.261.rest_0_), channel_id=1, source_target_pairs={{0,3},{1,2},{2,1},{3,0},{4,7},{5,6},{6,5},{7,4},{8,11},{9,10},{10,... | collective-permute-start | bytes 884744 | tf_op jit(solution)/shard_map/ppermute | solution.py:69
  528.9 21.8 %collective-permute-start.62 = (bf16[144,512]{1,0:T(8,128)(2,1)}, bf16[144,512]{1,0:T(8,128)(2,1)S(1)}, u32[]{:S(2)}, u32[]{:S(2)}) collective-permute-start(bf16[144,512]{1,0:T(8,128)(2,1)} %get-tuple-element.263), channel_id=1, source_target_pairs={{8,0},{12,4},{24,16},{28,20},{9,1},{13,5},{25,17},{29,21},{10,2},{... | collective-permute-start | bytes 442376 | tf_op jit(solution)/shard_map/ppermute | solution.py:1587
  530.2 21.6 %collective-permute-start.63 = (bf16[144,512]{1,0:T(8,128)(2,1)}, bf16[144,512]{1,0:T(8,128)(2,1)S(1)}, u32[]{:S(2)}, u32[]{:S(2)}) collective-permute-start(bf16[144,512]{1,0:T(8,128)(2,1)} %get-tuple-element.263), channel_id=1, source_target_pairs={{12,0},{28,16},{13,1},{29,17},{14,2},{30,18},{15,3},{31,19}} | collective-permute-start | bytes 442376 | tf_op jit(solution)/shard_map/ppermute | solution.py:1587
  (151 other events, 1295.9 us)
Sparse Core Ops, SparseCore 0:
  24.0 70.3 all-gather.5
  96.9 131.0 all-gather.3
  397.9 173.8 reduce-scatter.2
  588.2 92.2 reduce-scatter.4

commit v4 on v3

--- a/solution.py
+++ b/solution.py
@@ -302,7 +302,7 @@
     shared, lines, out, work = refs
     for layer in range(layers):
         zx, wout = mats[2 * layer], mats[2 * layer + 1]
-        zx_wide, out_wide = zx.shape[1] // BLK, wout.shape[1] // BLK
+        zx_wide, out_wide = zx.shape[1] // BLK, D // BLK
         zx_count = zx.shape[0] // BLK * zx_wide
         for at in range(per_layer):
             where = slot[0, layer * per_layer + at]
@@ -364,106 +364,6 @@
     return total
 
 
-def enter_kernel(count, *refs):
-    parts, (gain, residual, normed) = refs[:count], refs[count:]
-    total = total_of(parts)
-    residual[...] = total
-    normed[...] = norm_rows(total, gain[...]).astype(BF)
-
-
-def enter(parts, gain):
-    own = parts[0].shape[0]
-    return call(
-        functools.partial(enter_kernel, len(parts)),
-        "enter",
-        [sds((own, D), F32), sds((own, D), BF)],
-        (*parts, gain),
-        moved=2 * MIB,
-    )
-
-
-def join_residual_kernel(count, *refs):
-    parts, (before, gain, residual, branch, factor, normed) = refs[:count], refs[count:]
-    total = total_of(parts)
-    scale = lax.rsqrt(column3(total[:, D:]) / DI + NORM_EPS)
-    branch[...] = total[:, :D]
-    factor[...] = scale
-    after = before[...] + scale * total[:, :D]
-    residual[...] = after
-    normed[...] = norm_rows(after, gain[...]).astype(BF)
-
-
-def join_residual(parts, before, gain):
-    own = before.shape[0]
-    return call(
-        functools.partial(join_residual_kernel, len(parts)),
-        "residual",
-        [sds((own, D), F32), sds((own, D), F32), sds((own, 1), F32), sds((own, D), BF)],
-        (*parts, before, gain),
-        moved=3 * MIB,
-    )
-
-
-def back_rows_kernel(count, rim_count, last, *refs):
-    parts, refs = refs[:count], refs[count:]
-    rims, refs = refs[:rim_count], refs[rim_count:]
-    residual, gain, refs = refs[0], refs[1], refs[2:]
-    grad_in = None
-    if rim_count:
-        grad_in, refs = refs[0], refs[1:]
-    if not last:
-        branch, factor, refs = refs[0], refs[1], refs[2:]
-    if rim_count:
-        grad_out, payload, gain_grad, work = refs
-    else:
-        grad_out, payload, gain_grad = refs
-    grad = total_of(parts)
-    if rim_count:
-        work[...] = grad
-        own = work.shape[0]
-        work[own - RIM :, :] += total_of(rims)
-        grad = work[...]
-    values = residual[...]
-    inv = lax.rsqrt(jnp.mean(values * values, axis=-1, keepdims=True) + NORM_EPS)
-    gain_grad[...] = jnp.sum(grad * values * inv, axis=0, keepdims=True)
-    scaled = grad * gain[...]
-    result = inv * scaled - values * (inv * inv * inv) * jnp.mean(
-        scaled * values, axis=-1, keepdims=True
-    )
-    if grad_in is not None:
-        result = grad_in[...] + result
-    grad_out[...] = result
-    if last:
-        payload[...] = result.astype(BF)
-    else:
-        scale = factor[...]
-        payload[:, :D] = (scale * result).astype(BF)
-        inner_rows = jnp.sum(result * branch[...], axis=-1, keepdims=True)
-        payload[:, D:] = lanes3(scale * scale * scale * inner_rows / DI)
-
-
-def back_rows(parts, rims, residual, gain, grad_in, below):
-    own = residual.shape[0]
-    last = below is None
-    args = (*parts, *rims, residual, gain)
-    if rims:
-        args = (*args, grad_in)
-    if not last:
-        args = (*args, *below)
-    return call(
-        functools.partial(back_rows_kernel, len(parts), len(rims), last),
-        "backrows",
-        [
-            sds((own, D), F32),
-            sds((own, D if last else D + LANES), BF),
-            sds((1, D), F32),
-        ],
-        args,
-        scratch=[pltpu.VMEM((own, D), F32)] if rims else [],
-        moved=4 * MIB,
-    )
-
-
 def send(source, target, send_sem, recv_sem, device):
     copy = pltpu.make_async_remote_copy(
         src_ref=source,
@@ -477,11 +377,393 @@
     return copy
 
 
+def greet_shards(groups, shards, rims):
+    place, shard = lax.axis_index("dp"), lax.axis_index("tensor")
+    last = shard == shards - 1
+    barrier = pltpu.get_barrier_semaphore()
+
+    def greet(device):
+        pl.semaphore_signal(barrier, inc=1, device_id=device, device_id_type=pl.DeviceIdType.MESH)
+
+    for off in range(1, shards):
+        greet((place, shard ^ off))
+    if not rims:
+        pl.semaphore_wait(barrier, shards - 1)
+        return
+    greet((lax.rem(place + groups - 1, groups), shards - 1))
+
+    @pl.when(last)
+    def _():
+        for other in range(shards):
+            greet((lax.rem(place + 1, groups), other))
+
+    pl.semaphore_wait(barrier, shards - 1 + jnp.where(last, shards + 1, 1))
+
+
+def pass_along(rows, own, base, shards, sems):
+    place, shard = lax.axis_index("dp"), lax.axis_index("tensor")
+
+    def copy(way, hop, source, to):
+        at = pl.ds(pl.multiple_of(base + source * own, RIM), own)
+        return pltpu.make_async_remote_copy(
+            src_ref=rows.at[at, :],
+            dst_ref=rows.at[at, :],
+            send_sem=sems.at[0, way, hop],
+            recv_sem=sems.at[1, way, hop],
+            device_id=(place, to),
+            device_id_type=pl.DeviceIdType.MESH,
+        )
+
+    def up(hop):
+        return copy(0, hop, shard - hop, shard + 1)
+
+    def down(hop):
+        return copy(1, hop, shard + hop, shard - 1)
+
+    can_up, can_down = shard + 1 < shards, shard > 0
+    for hop in range(shards):
+        if hop > 0:
+
+            @pl.when(shard - hop >= 0)
+            def _():
+                copy(0, hop - 1, shard - hop, shard - 1).wait_recv()
+
+        if hop < shards - 1:
+
+            @pl.when(jnp.logical_and(shard - hop >= 0, can_up))
+            def _():
+                up(hop).start()
+
+        if hop > 0:
+
+            @pl.when(shard + hop < shards)
+            def _():
+                copy(1, hop - 1, shard + hop, shard + 1).wait_recv()
+
+        if hop < shards - 1:
+
+            @pl.when(jnp.logical_and(shard + hop < shards, can_down))
+            def _():
+                down(hop).start()
+
+    for hop in range(shards - 1):
+
+        @pl.when(jnp.logical_and(shard - hop >= 0, can_up))
+        def _():
+            up(hop).wait_send()
+
+        @pl.when(jnp.logical_and(shard + hop < shards, can_down))
+        def _():
+            down(hop).wait_send()
+
+
+def exchange_terms(parts, slots, work, sems):
+    place, shard = lax.axis_index("dp"), lax.axis_index("tensor")
+    shards = len(parts)
+
+    def copy(off, source, to, slot):
+        return pltpu.make_async_remote_copy(
+            src_ref=source,
+            dst_ref=slots.at[slot],
+            send_sem=sems.at[0, off],
+            recv_sem=sems.at[1, slot],
+            device_id=(place, to),
+            device_id_type=pl.DeviceIdType.MESH,
+        )
+
+    def direct(off):
+        return copy(off, parts[off], shard ^ off, off)
+
+    if shards != 4:
+        for off in range(1, shards):
+            direct(off).start()
+        for off in range(1, shards):
+            direct(off).wait()
+        total = parts[0][...].astype(F32)
+        for off in range(1, shards):
+            total = total + slots[off].astype(F32)
+        work[...] = total
+        return
+    relay, added = 0, 4
+    outer = jnp.logical_or(shard == 0, shard == shards - 1)
+    inner = jnp.logical_not(outer)
+
+    @pl.when(outer)
+    def _():
+        copy(3, parts[3], shard ^ 1, relay).start()
+        direct(2).start()
+        direct(1).start()
+
+    @pl.when(inner)
+    def _():
+        direct(3).start()
+        direct(1).start()
+        copy(0, parts[3], shard ^ 1, relay).wait_recv()
+        slots[added] = (slots[relay].astype(F32) + parts[2][...].astype(F32)).astype(BF)
+        copy(2, slots.at[added], shard ^ 2, 2).start()
+
+    direct(1).wait_recv()
+    total = parts[0][...].astype(F32) + slots[1].astype(F32)
+    direct(2).wait_recv()
+    work[...] = total + slots[2].astype(F32)
+
+    @pl.when(inner)
+    def _():
+        direct(3).wait_recv()
+        work[...] += slots[3].astype(F32)
+
+    for off in range(1, shards):
+        direct(off).wait_send()
+
+
+def term_scratch(shards, own, width):
+    return [
+        pltpu.VMEM((shards + 1, own, width), BF),
+        pltpu.VMEM((own, width), F32),
+        pltpu.SemaphoreType.DMA((2, shards + 1)),
+    ]
+
+
+def forward_kernel(groups, shards, chunks, packed, rims, *refs):
+    parts, refs = refs[:shards], refs[shards:]
+    if packed:
+        before, gain, residual, branch, factor, normed, *refs = refs
+    else:
+        gain, residual, normed, *refs = refs
+    slots, work, term_sems, row_sems, rim_sems = refs
+    own = parts[0].shape[0]
+    rows = own * shards
+    place, shard = lax.axis_index("dp"), lax.axis_index("tensor")
+    chunk = lax.rem(place, chunks)
+    greet_shards(groups, shards, rims)
+    exchange_terms(parts, slots, work, term_sems)
+    total = work[...]
+    if packed:
+        scale = lax.rsqrt(column3(total[:, D:]) / DI + NORM_EPS)
+        branch[...] = total[:, :D]
+        factor[...] = scale
+        total = before[...] + scale * total[:, :D]
+    residual[...] = total
+    at = pl.ds(pl.multiple_of(RIM + shard * own, RIM), own)
+    normed[at, :] = norm_rows(total, gain[...]).astype(BF)
+
+    def rim_copy(to, device):
+        return pltpu.make_async_remote_copy(
+            src_ref=normed.at[rows : rows + RIM, :],
+            dst_ref=normed.at[0:RIM, :],
+            send_sem=rim_sems.at[0, to],
+            recv_sem=rim_sems.at[1, 0],
+            device_id=device,
+            device_id_type=pl.DeviceIdType.MESH,
+        )
+
+    gives = jnp.logical_and(shard == shards - 1, chunk + 1 < chunks)
+    if rims:
+
+        @pl.when(gives)
+        def _():
+            for to in range(shards):
+                rim_copy(to, (place + 1, to)).start()
+
+        @pl.when(chunk == 0)
+        def _():
+            normed[0:RIM, :] = jnp.zeros((RIM, D), BF)
+
+    else:
+        normed[0:RIM, :] = jnp.zeros((RIM, D), BF)
+    pass_along(normed, own, RIM, shards, row_sems)
+    if rims:
+
+        @pl.when(chunk > 0)
+        def _():
+            rim_copy(0, (place - 1, shards - 1)).wait_recv()
+
+        @pl.when(gives)
+        def _():
+            for to in range(shards):
+                rim_copy(to, (place + 1, to)).wait_send()
+
+
+def forward_rows(parts, before, gain, groups, chunks, rims, cid):
+    shards = len(parts)
+    own, width = parts[0].shape
+    packed = before is not None
+    args = (*parts, before, gain) if packed else (*parts, gain)
+    vmem = pl.BlockSpec(memory_space=pltpu.VMEM)
+    outs = [sds((own, D), F32)]
+    if packed:
+        outs += [sds((own, D), F32), sds((own, 1), F32)]
+    outs += [sds((RIM + own * shards, D), BF)]
+    return pl.pallas_call(
+        functools.partial(forward_kernel, groups, shards, chunks, packed, rims),
+        out_shape=outs,
+        in_specs=[vmem] * len(args),
+        out_specs=[vmem] * len(outs),
+        scratch_shapes=[
+            *term_scratch(shards, own, width),
+            pltpu.SemaphoreType.DMA((2, 2, shards)),
+            pltpu.SemaphoreType.DMA((2, shards)),
+        ],
+        compiler_params=pltpu.CompilerParams(
+            collective_id=cid, has_side_effects=True, vmem_limit_bytes=32 * MIB
+        ),
+        name="forward",
+    )(*args)
+
+
+def backward_kernel(groups, shards, chunks, exchanged, *refs):
+    parts, refs = refs[:shards], refs[shards:]
+    if exchanged:
+        residual, gain, branch, factor, grad_out, rows_out, gain_grad, row_sems = refs
+    else:
+        rim, residual, gain, grad_in, branch, factor, grad_out, rows_out, refs = *refs[:8], refs[8:]
+        slots, work, term_sems, from_rims, rim_sems, row_sems = refs
+    own = parts[0].shape[0]
+    place, shard = lax.axis_index("dp"), lax.axis_index("tensor")
+    chunk = lax.rem(place, chunks)
+    greet_shards(groups, shards, not exchanged)
+    values = residual[...]
+    inv = lax.rsqrt(jnp.mean(values * values, axis=-1, keepdims=True) + NORM_EPS)
+    if exchanged:
+        grad = total_of(parts)
+        gain_grad[...] = jnp.sum(grad * values * inv, axis=0, keepdims=True)
+    else:
+
+        def rim_copy(slot, device):
+            return pltpu.make_async_remote_copy(
+                src_ref=rim,
+                dst_ref=from_rims.at[slot],
+                send_sem=rim_sems.at[0, slot],
+                recv_sem=rim_sems.at[1, slot],
+                device_id=device,
+                device_id_type=pl.DeviceIdType.MESH,
+            )
+
+        @pl.when(chunk > 0)
+        def _():
+            rim_copy(shard, (place - 1, shards - 1)).start()
+
+        exchange_terms(parts, slots, work, term_sems)
+
+        @pl.when(jnp.logical_and(shard == shards - 1, chunk + 1 < chunks))
+        def _():
+            for other in range(shards):
+                rim_copy(other, (place + 1, other)).wait_recv()
+            edge = from_rims[0].astype(F32)
+            for other in range(1, shards):
+                edge = edge + from_rims[other].astype(F32)
+            work[own - RIM :, :] += edge
+
+        @pl.when(chunk > 0)
+        def _():
+            rim_copy(shard, (place - 1, shards - 1)).wait_send()
+
+        grad = work[...]
+    scaled = grad * gain[...]
+    result = inv * scaled - values * (inv * inv * inv) * jnp.mean(
+        scaled * values, axis=-1, keepdims=True
+    )
+    if not exchanged:
+        result = grad_in[...] + result
+    grad_out[...] = result
+    scale = factor[...]
+    at = pl.ds(pl.multiple_of(shard * own, RIM), own)
+    rows_out[at, :D] = (scale * result).astype(BF)
+    inner_rows = jnp.sum(result * branch[...], axis=-1, keepdims=True)
+    rows_out[at, D:] = lanes3(scale * scale * scale * inner_rows / DI)
+    pass_along(rows_out, own, 0, shards, row_sems)
+
+
+def backward_rows(parts, rim, residual, gain, grad_in, branch, factor, groups, chunks, cid):
+    shards = len(parts)
+    own = residual.shape[0]
+    exchanged = rim is None
+    vmem = pl.BlockSpec(memory_space=pltpu.VMEM)
+    outs = [sds((own, D), F32), sds((own * shards, D + LANES), BF)]
+    row_sems = pltpu.SemaphoreType.DMA((2, 2, shards))
+    if exchanged:
+        args = (*parts, residual, gain, branch, factor)
+        outs.append(sds((1, D), F32))
+        scratch = [row_sems]
+    else:
+        args = (*parts, rim, residual, gain, grad_in, branch, factor)
+        scratch = [
+            *term_scratch(shards, own, D),
+            pltpu.VMEM((shards, RIM, D), BF),
+            pltpu.SemaphoreType.DMA((2, shards)),
+            row_sems,
+        ]
+    return pl.pallas_call(
+        functools.partial(backward_kernel, groups, shards, chunks, exchanged),
+        out_shape=outs,
+        in_specs=[vmem] * len(args),
+        out_specs=[vmem] * len(outs),
+        scratch_shapes=scratch,
+        compiler_params=pltpu.CompilerParams(
+            collective_id=cid, has_side_effects=True, vmem_limit_bytes=32 * MIB
+        ),
+        name="backward",
+    )(*args)
+
+
+def stats_kernel(shards, chunks, stats, tops, weight, scale_out, loss_out, slots, sems):
+    place, shard = lax.axis_index("dp"), lax.axis_index("tensor")
+    rows = weight.shape[1]
+    own = rows // shards
+    greet_shards(0, shards, False)
+    copies = [
+        send(stats, slots.at[off - 1], sems.at[0, off], sems.at[1, off], (place, shard ^ off))
+        for off in range(1, shards)
+    ]
+    for copy in copies:
+        copy.wait()
+    others = [stats[...]] + [slots[off] for off in range(shards - 1)]
+    best = others[0][0:1, :]
+    for one in others[1:]:
+        best = jnp.maximum(best, one[0:1, :])
+    summed, target, plain = jnp.zeros((1, rows), F32), jnp.zeros((1, rows), F32), jnp.zeros((1, rows), F32)
+    for one in others:
+        summed = summed + one[1:2, :] * jnp.exp(one[0:1, :] - best)
+        target = target + one[2:3, :]
+        plain = plain + one[3:4, :]
+    log_total = best + jnp.log(summed)
+    token_loss = (
+        log_total
+        - (1.0 - SMOOTHING) * target
+        - SMOOTHING / V * plain
+        + ZLOSS_WEIGHT * log_total * log_total
+    )
+    lane = iota((1, rows), 1)
+    mine = jnp.logical_and(lane >= shard * own, lane < (shard + 1) * own)
+    loss = jnp.sum(jnp.where(mine, weight[...] * token_loss, 0.0), axis=1, keepdims=True)
+    here = jnp.logical_and(iota((8, LANES), 0) == 0, iota((8, LANES), 1) == place // chunks)
+    loss_out[...] = jnp.where(here, loss, 0.0)
+    soft = weight[...] * (1.0 + 2.0 * ZLOSS_WEIGHT * log_total)
+    for step in range(tops.shape[0]):
+        scale_out[step] = soft * jnp.exp(tops[step] - log_total)
+
+
+def merge_stats(stats, tops, weight, shards, chunks):
+    vmem = pl.BlockSpec(memory_space=pltpu.VMEM)
+    return pl.pallas_call(
+        functools.partial(stats_kernel, shards, chunks),
+        out_shape=[sds(tops.shape, F32), sds((8, LANES), F32)],
+        in_specs=[vmem] * 3,
+        out_specs=[vmem] * 2,
+        scratch_shapes=[
+            pltpu.VMEM((shards - 1, *stats.shape), F32),
+            pltpu.SemaphoreType.DMA((2, shards)),
+        ],
+        compiler_params=pltpu.CompilerParams(
+            collective_id=9, has_side_effects=True, vmem_limit_bytes=8 * MIB
+        ),
+        name="stats",
+    )(stats, tops, weight)
+
+
 def finish_kernel(groups, shards, chunks, own, *refs):
     parts, rim, residual, gain, grad_in, out = refs[:shards], *refs[shards : shards + 5]
-    (from_shards, from_rims, payload, full, work, term_sems, rim_sems, row_sems, out_sems) = refs[
-        shards + 5 :
-    ]
+    slots, work, term_sems, from_rims, payload, full, rim_sems, row_sems, out_sems = refs[shards + 5 :]
     place, shard = lax.axis_index("dp"), lax.axis_index("tensor")
     half = groups // 2
     cols = out.shape[2]
@@ -522,24 +804,9 @@
     def _():
         rim_copy().start()
 
-    terms = [
-        send(
-            parts[off],
-            from_shards.at[off - 1],
-            term_sems.at[0, off],
-            term_sems.at[1, off],
-            shard_peers[off - 1],
-        )
-        for off in range(1, shards)
-    ]
     values = residual[...]
     inv = lax.rsqrt(jnp.mean(values * values, axis=-1, keepdims=True) + NORM_EPS)
-    for term in terms:
-        term.wait()
-    total = parts[0][...].astype(F32)
-    for off in range(1, shards):
-        total = total + from_shards[off - 1].astype(F32)
-    work[...] = total
+    exchange_terms(parts, slots, work, term_sems)
 
     @pl.when(jnp.logical_and(chunk + 1 < chunks, last))
     def _():
@@ -614,12 +881,10 @@
         in_specs=[vmem] * len(args),
         out_specs=vmem,
         scratch_shapes=[
-            pltpu.VMEM((shards - 1, own, D), BF),
+            *term_scratch(shards, own, D),
             pltpu.VMEM((shards, RIM, D), BF),
             pltpu.VMEM((own, D), BF),
             pltpu.VMEM((shards, own, D), BF),
-            pltpu.VMEM((own, D), F32),
-            pltpu.SemaphoreType.DMA((2, shards)),
             pltpu.SemaphoreType.DMA((2, shards)),
             pltpu.SemaphoreType.DMA((2, shards)),
             pltpu.SemaphoreType.DMA((2, shards, groups)),
@@ -631,46 +896,55 @@
     )(*args)
 
 
-def open_kernel(groups, shards, ids, piece, ids_out, pieces_out, send, recv):
+def open_kernel(groups, shards, ids, piece, share, ids_out, pieces_out, share_out, middle, sends, gets):
     place, shard = lax.axis_index("dp"), lax.axis_index("tensor")
-    peers = [(place, shard ^ off) for off in range(1, shards)]
-    peers += [(place ^ off, shard) for off in range(1, groups)]
+    near = [(place, shard ^ off) for off in range(1, shards)]
+    far = [(place ^ off, shard) for off in range(1, groups)]
     barrier = pltpu.get_barrier_semaphore()
-    for peer in peers:
+    for peer in near + far:
         pl.semaphore_signal(barrier, inc=1, device_id=peer, device_id_type=pl.DeviceIdType.MESH)
-    pl.semaphore_wait(barrier, len(peers))
-    copies = []
-    for i, peer in enumerate(peers):
-        copy = pltpu.make_async_remote_copy(
-            src_ref=piece if i < shards - 1 else ids,
-            dst_ref=pieces_out.at[shard] if i < shards - 1 else ids_out.at[place],
-            send_sem=send.at[i],
-            recv_sem=recv.at[i],
-            device_id=peer,
-            device_id_type=pl.DeviceIdType.MESH,
-        )
-        copy.start()
-        copies.append(copy)
+    pl.semaphore_wait(barrier, len(near) + len(far))
+    shares, others = [], []
+    for i, peer in enumerate(near):
+        shares.append(send(share, middle.at[shard], sends.at[0, i], gets.at[0, i], peer))
+    for i, peer in enumerate(far):
+        others.append(send(ids, ids_out.at[place], sends.at[1, i], gets.at[1, i], peer))
+    for i, peer in enumerate(near):
+        others.append(send(piece, pieces_out.at[shard], sends.at[2, i], gets.at[2, i], peer))
+    middle[shard] = share[...]
     ids_out[place] = ids[...]
     pieces_out[shard] = piece[...]
-    for copy in copies:
+    for copy in shares:
         copy.wait()
-
-
-def open_exchange(ids, piece, groups, shards):
-    count = groups + shards - 2
+    for i, peer in enumerate(far):
+        others.append(send(middle, share_out.at[place], sends.at[3, i], gets.at[3, i], peer))
+    share_out[place] = middle[...]
+    for copy in others:
+        copy.wait()
+
+
+def open_exchange(ids, piece, share, groups, shards):
+    count = max(groups, shards)
     vmem = pl.BlockSpec(memory_space=pltpu.VMEM)
     return pl.pallas_call(
         functools.partial(open_kernel, groups, shards),
-        out_shape=[sds((groups, *ids.shape), jnp.int32), sds((shards, *piece.shape), BF)],
-        in_specs=[vmem, vmem],
-        out_specs=[vmem, vmem],
-        scratch_shapes=[pltpu.SemaphoreType.DMA((count,)), pltpu.SemaphoreType.DMA((count,))],
+        out_shape=[
+            sds((groups, *ids.shape), jnp.int32),
+            sds((shards, *piece.shape), BF),
+            sds((groups, shards, *share.shape), BF),
+        ],
+        in_specs=[vmem] * 3,
+        out_specs=[vmem] * 3,
+        scratch_shapes=[
+            pltpu.VMEM((shards, *share.shape), BF),
+            pltpu.SemaphoreType.DMA((4, count)),
+            pltpu.SemaphoreType.DMA((4, count)),
+        ],
         compiler_params=pltpu.CompilerParams(
             collective_id=2, has_side_effects=True, vmem_limit_bytes=8 * MIB
         ),
         name="open",
-    )(ids, piece)
+    )(ids, piece, share)
 
 
 def sum_kernel(groups, shards, once, split, *refs):
@@ -757,21 +1031,10 @@
     return total
 
 
-def front_kernel(shards, own, scal, *rest):
-    blocks, rest = rest[:shards], rest[shards:]
-    rims, rest = rest[:shards], rest[shards:]
-    wzx, wside, chan, bcp, head = rest[:5]
-    normed, zx, side, yloc, final, c_out, cum_out, xs_scr = rest[5:]
-    shard = scal[0]
-    rows = own * shards
+def front_kernel(normed, wzx, wside, chan, bcp, head, *rest):
+    zx, side, yloc, final, c_out, cum_out, xs_scr = rest
+    rows = normed.shape[0] - RIM
     inner = chan.shape[1]
-    rim = rims[0][...]
-    for other in rims[1:]:
-        rim = rim + other[...]
-    normed[0:RIM, :] = rim
-    for off in range(shards):
-        at = pl.multiple_of(RIM + (shard ^ off) * own, RIM)
-        normed[pl.ds(at, own), :] = blocks[off][...]
     zx[...] = nn(normed[...], wzx[...])
     side[...] = nn(normed[...], wside[...])
     pre = conv_sum(zx, chan, rows, pl.ds(inner, inner))
@@ -823,16 +1086,13 @@
     final[N:, :] = rows3(base, inner)
 
 
-def mixer_front(scal, blocks, rims, wzx, wside, chan, bcp, head):
-    shards = len(blocks)
-    own = blocks[0].shape[0]
-    rows = own * shards
+def mixer_front(normed, wzx, wside, chan, bcp, head):
+    rows = normed.shape[0] - RIM
     inner = chan.shape[1]
     return call(
-        functools.partial(front_kernel, shards, own),
+        front_kernel,
         "front",
         [
-            sds((rows + RIM, D), BF),
             sds((rows + RIM, 2 * inner), F32),
             sds((rows + RIM, 2 * N + LANES), F32),
             sds((rows, inner), F32),
@@ -840,8 +1100,7 @@
             sds((rows, N), BF),
             sds((rows, LANES), F32),
         ],
-        (scal, *blocks, *rims, wzx, wside, chan, bcp, head),
-        smem=(0,),
+        (normed, wzx, wside, chan, bcp, head),
         scratch=[pltpu.VMEM((rows, inner), F32)],
         flops=8 * rows * D * inner,
         moved=12 * MIB,
@@ -895,17 +1154,11 @@
     )
 
 
-def gate_back_kernel(shards, own, scal, *rest):
-    blocks, rest = rest[:shards], rest[shards:]
-    wout, y_in, zx, c_in, cum, chan = rest[:6]
-    grads, u_out, dy_out, dz_out, state_out, gain_out, coef = rest[6:]
-    shard = scal[0]
+def gate_back_kernel(grads, wout, y_in, zx, c_in, cum, chan, *rest):
+    u_out, dy_out, dz_out, state_out, gain_out = rest
     inner = chan.shape[1]
-    for off in range(shards):
-        at = pl.multiple_of((shard ^ off) * own, own)
-        grads[pl.ds(at, own), :] = blocks[off][:, :D]
-        coef[pl.ds(at, own), :] = column3(blocks[off][:, D:].astype(F32))
-    du = nt_dot(grads[...], wout[...])
+    du = nt_dot(grads[:, :D], wout[...])
+    coef = column3(grads[:, D:].astype(F32))
     z = zx[RIM:, :inner]
     y = y_in[...]
     sig = sigmoid(z)
@@ -914,7 +1167,7 @@
     gain_out[...] = jnp.sum(du * gated, axis=0, keepdims=True)
     gain = chan[5:6, :]
     u_out[...] = (gated * gain).astype(BF)
-    dgated = du * gain - gated * coef[...]
+    dgated = du * gain - gated * coef
     dy = dgated * silu
     dy_out[...] = dy
     dz_out[...] = (dgated * y * (sig * (1.0 + z * (1.0 - sig)))).astype(BF)
@@ -924,24 +1177,19 @@
     state_out[N:, :] = rows3(cum[rows - 1 : rows, :], inner)
 
 
-def gate_back(scal, blocks, wout, y, zx, c_in, cum, chan):
-    shards = len(blocks)
-    own = blocks[0].shape[0]
+def gate_back(grads, wout, y, zx, c_in, cum, chan):
     rows, inner = y.shape
     return call(
-        functools.partial(gate_back_kernel, shards, own),
+        gate_back_kernel,
         "gateback",
         [
-            sds((rows, D), BF),
             sds((rows, inner), BF),
             sds((rows, inner), F32),
             sds((rows, inner), BF),
             sds((N + RIM, inner), BF),
             sds((1, inner), F32),
         ],
-        (scal, *blocks, wout, y, zx, c_in, cum, chan),
-        smem=(0,),
-        scratch=[pltpu.VMEM((rows, 1), F32)],
+        (grads, wout, y, zx, c_in, cum, chan),
         flops=2 * rows * D * inner,
         moved=10 * MIB,
     )
@@ -1159,16 +1407,14 @@
     )
 
 
-def logits_kernel(shards, own, vrows, label, table, *rest):
-    blocks, rest = rest[:shards], rest[shards:]
+def logits_kernel(vrows, label, table, normed, *rest):
     p_out, tops, stats, rows_scr, top, total, target, plain = rest
     step = pl.program_id(0)
-    rows = own * shards
+    rows = normed.shape[0] - RIM
 
     @pl.when(step == 0)
     def _():
-        for off in range(shards):
-            rows_scr[:, off * own : (off + 1) * own] = blocks[off][...].T
+        rows_scr[...] = normed[RIM:, :].T
         top[...] = jnp.full((1, rows), -1e30, F32)
         total[...] = jnp.zeros((1, rows), F32)
         target[...] = jnp.zeros((1, rows), F32)
@@ -1201,15 +1447,13 @@
     stats[...] = jnp.concatenate([highest, summed, hit, whole, jnp.zeros((4, rows), F32)], axis=0)
 
 
-def vocab_logits(label, table, blocks, vrows):
-    shards = len(blocks)
-    own = blocks[0].shape[0]
-    rows = own * shards
+def vocab_logits(label, table, normed, vrows):
+    rows = normed.shape[0] - RIM
     padded = table.shape[0]
     steps = padded // PAIRS
     whole = lambda i: (0, 0)
     return pl.pallas_call(
-        functools.partial(logits_kernel, shards, own, vrows),
+        functools.partial(logits_kernel, vrows),
         grid=(steps,),
         out_shape=[
             sds((2, padded, rows), BF),
@@ -1219,8 +1463,8 @@
         in_specs=[
             pl.BlockSpec((1, rows), whole),
             pl.BlockSpec((PAIRS, 2 * D), lambda i: (i, 0)),
-        ]
-        + [pl.BlockSpec((own, D), whole)] * shards,
+            pl.BlockSpec(normed.shape, whole),
+        ],
         out_specs=[
             pl.BlockSpec((2, PAIRS, rows), lambda i: (0, i, 0)),
             pl.BlockSpec((1, 16 * (PAIRS // PART), rows), lambda i: (i, 0, 0)),
@@ -1234,7 +1478,7 @@
             flops=4 * rows * D * padded, bytes_accessed=40 * MIB, transcendentals=2 * rows * padded
         ),
         name="logits",
-    )(label, table, *blocks)
+    )(label, table, normed)
 
 
 def logit_grads(step, label, scale, weight, p_in):
@@ -1253,7 +1497,7 @@
         yield half, jnp.concatenate(pieces, axis=0)
 
 
-def rows_kernel(shards, own, label, scale, weight, p_in, table, *rest):
+def rows_kernel(shards, own, scal, label, scale, weight, p_in, table, *rest):
     parts, acc = rest[:shards], rest[-1]
     step = pl.program_id(0)
 
@@ -1267,7 +1511,8 @@
     @pl.when(step == pl.num_programs(0) - 1)
     def _():
         for off in range(shards):
-            parts[off][...] = acc[off * own : (off + 1) * own, :].astype(BF)
+            at = pl.ds(pl.multiple_of((scal[0] ^ off) * own, own), own)
+            parts[off][...] = acc[at, :].astype(BF)
 
 
 def vocab_specs(rows):
@@ -1280,7 +1525,7 @@
     ]
 
 
-def vocab_rows(label, scale, weight, p_in, table, shards):
+def vocab_rows(scal, label, scale, weight, p_in, table, shards):
     _, padded, rows = p_in.shape
     own = rows // shards
     whole = lambda i: (0, 0)
@@ -1288,7 +1533,9 @@
         functools.partial(rows_kernel, shards, own),
         grid=(padded // PAIRS,),
         out_shape=[sds((own, D), BF)] * shards,
-        in_specs=vocab_specs(rows) + [pl.BlockSpec((PAIRS, 2 * D), lambda i: (i, 0))],
+        in_specs=[pl.BlockSpec(memory_space=pltpu.SMEM)]
+        + vocab_specs(rows)
+        + [pl.BlockSpec((PAIRS, 2 * D), lambda i: (i, 0))],
         out_specs=[pl.BlockSpec((own, D), whole)] * shards,
         scratch_shapes=[pltpu.VMEM((rows, D), F32)],
         compiler_params=pltpu.CompilerParams(
@@ -1298,32 +1545,28 @@
             flops=4 * rows * D * padded, bytes_accessed=40 * MIB, transcendentals=0
         ),
         name="rowgrads",
-    )(label, scale, weight, p_in, table)
-
-
-def table_kernel(shards, own, label, scale, weight, p_in, *rest):
-    blocks, out, rows_scr = rest[:shards], rest[shards], rest[-1]
+    )(scal, label, scale, weight, p_in, table)
+
+
+def table_kernel(label, scale, weight, p_in, normed, out, rows_scr):
     step = pl.program_id(0)
 
     @pl.when(step == 0)
     def _():
-        for off in range(shards):
-            rows_scr[off * own : (off + 1) * own, :] = blocks[off][...]
+        rows_scr[...] = normed[RIM:, :]
 
     for half, q in logit_grads(step, label, scale, weight, p_in):
         out[:, half * D : (half + 1) * D] = nn(q, rows_scr[...]).astype(BF)
 
 
-def vocab_table_grad(label, scale, weight, p_in, blocks):
+def vocab_table_grad(label, scale, weight, p_in, normed):
     _, padded, rows = p_in.shape
-    shards = len(blocks)
-    own = blocks[0].shape[0]
     whole = lambda i: (0, 0)
     return pl.pallas_call(
-        functools.partial(table_kernel, shards, own),
+        table_kernel,
         grid=(padded // PAIRS,),
         out_shape=sds((padded, 2 * D), BF),
-        in_specs=vocab_specs(rows) + [pl.BlockSpec((own, D), whole)] * shards,
+        in_specs=vocab_specs(rows) + [pl.BlockSpec(normed.shape, whole)],
         out_specs=pl.BlockSpec((PAIRS, 2 * D), lambda i: (i, 0)),
         scratch_shapes=[pltpu.VMEM((rows, D), BF)],
         compiler_params=pltpu.CompilerParams(
@@ -1333,7 +1576,7 @@
             flops=4 * rows * D * padded, bytes_accessed=40 * MIB, transcendentals=0
         ),
         name="tablegrads",
-    )(label, scale, weight, p_in, *blocks)
+    )(label, scale, weight, p_in, normed)
 
 
 def adam_update(weight_in, gradient, moment_one, moment_two, factor, fix_one, fix_two, decay_rate):
@@ -1503,17 +1746,13 @@
     share_size = shared_params.shape[0]
     share_pad = -(-share_size // 2048) * 2048
 
-    piece = jnp.concatenate(
-        [
-            jnp.pad(side_proj.astype(BF), ((0, 0), (0, 0), (0, LANES - H))).reshape(-1, LANES),
-            jnp.pad(shared_params.astype(BF), (0, share_pad - share_size)).reshape(-1, LANES),
-        ],
-        axis=0,
-    )
-    piece_rows = piece.shape[0]
-    side_part = piece_rows - share_pad // LANES
+    piece = jnp.pad(side_proj.astype(BF), ((0, 0), (0, 0), (0, LANES - H))).reshape(-1, LANES)
+    share = jnp.pad(shared_params.astype(BF), (0, share_pad - share_size)).reshape(-1, LANES)
+    side_part = piece.shape[0]
+    piece_rows = side_part + share.shape[0]
     ids = jnp.pad(jnp.concatenate([token_ids, labels], axis=0), ((0, 8 - 2 * seqs), (0, 0)))
-    ids_all, pieces = open_exchange(ids, piece, nd, nt)
+    ids_all, pieces, shared_all = open_exchange(ids, piece, share, nd, nt)
+    shared_full = shared_all.reshape(nd * nt, share_pad)[:, :share_size].reshape(-1).astype(F32)
     ids_all = ids_all.transpose(1, 0, 2).reshape(8, length)
     all_ids = ids_all[:seqs].reshape(-1)
     local_row = all_ids // 2 - shard * vrows
@@ -1535,18 +1774,18 @@
     table_now, parts = lax.optimization_barrier((vocab_table, parts))
     parts = [parts[0]] + [swap(parts[off], "dp", off) for off in range(1, nd)]
     table_low = jnp.pad(table_now.astype(BF), ((0, padded - vrows), (0, 0)))
+    parts = join_parts(scal, parts, nt, own)
+    residual, normed = forward_rows(
+        parts, None, shared_full[None, :D], nd, chunks, True, 4
+    )
+    gathered, normed = lax.optimization_barrier((gathered, normed))
     placed = place_tiles(block_slot, gathered, own_tiles, inner, zx_count, per_layer)
-    small = gathered[:, own_tiles * BLK :].reshape(nd, nt, piece_rows, LANES)
     side_full = (
-        small[:, :, :side_part]
+        gathered[:, own_tiles * BLK :]
         .reshape(nd, nt, L, side_rows, 2 * N + LANES)
         .transpose(2, 0, 1, 3, 4)
         .reshape(L, D, 2 * N + LANES)
     )
-    shared_full = small[:, :, side_part:].reshape(nd * nt, share_pad)[:, :share_size].reshape(-1)
-    shared_full = shared_full.astype(F32)
-
-    parts = join_parts(scal, parts, nt, own)
     table_all = lax.all_gather(table_low, "dp", axis=1, tiled=True)
 
     def layer_mats(layer_index):
@@ -1570,14 +1809,6 @@
         head = jnp.pad(head_params[layer_index], ((0, 5), (0, LANES - heads)))
         return (zx_part, out_part, side_here, gain, bcp, chan, head)
 
-    def spread(x):
-        return [x] + [swap(x, "tensor", off) for off in range(1, nt)]
-
-    def rim_pairs(to):
-        return [
-            (k * nt + nt - 1, (k + 1) * nt + to) for k in range(nd) if k % chunks + 1 < chunks
-        ]
-
     def hop(x, distance):
         pairs = [
             (k, k + distance)
@@ -1594,71 +1825,39 @@
     final_gain = shared_full[L * stride :][None, :]
     gains = [mats[layer_index][3][None, :] for layer_index in range(L)] + [final_gain]
     saved = []
-    residual, normed_own = enter(returned(parts), gains[0])
     for layer_index in range(L):
         wzx, wout, wside, gain, bcp, chan, head = mats[layer_index]
-        edge = normed_own[own - RIM :]
-        rims = [lax.ppermute(edge, both, rim_pairs(to)) for to in range(nt)]
-        normed, zx, side, yloc, final, c_out, cum = mixer_front(
-            scal_shard, spread(normed_own), rims, wzx, wside, chan, bcp, head
-        )
+        zx, side, yloc, final, c_out, cum = mixer_front(normed, wzx, wside, chan, bcp, head)
         states = [hop(final, k) for k in hops]
         result = mixer_middle(scal_shard, states, yloc, zx, c_out, cum, wout, chan, nt)
         y, s_in = result[:2]
+        below = normed
         before = residual
-        residual, branch, factor, normed_own = join_residual(
-            returned(result[2:]), before, gains[layer_index + 1]
+        inside = layer_index + 1 < L
+        residual, branch, factor, normed = forward_rows(
+            result[2:], before, gains[layer_index + 1], nd, chunks, inside, 5 + layer_index
         )
-        saved.append((before, normed, zx, side, c_out, cum, y, s_in, factor, branch))
-    final_rows = spread(normed_own)
+        saved.append((before, below, zx, side, c_out, cum, y, s_in, factor, branch))
 
     member = micro_batch[:, None] == jnp.arange(MB, dtype=jnp.int32)[None, :]
     batch_tokens = jnp.sum(jnp.where(member, seq_lengths[:, None], 0), axis=0).astype(F32)
     seq_weight = 1.0 / (MB * jnp.sum(jnp.where(member, batch_tokens[None, :], 0.0), axis=1))
-    block_order = shard ^ jnp.arange(nt, dtype=jnp.int32)
-    row_at = (
-        place * rows + block_order[:, None] * own + jnp.arange(own, dtype=jnp.int32)[None, :]
-    ).reshape(rows)
+    row_at = place * rows + jnp.arange(rows, dtype=jnp.int32)
     my_seq = place // chunks
     weight = jnp.where(row_at % length < seq_lengths[my_seq], seq_weight[my_seq], 0.0)
     all_labels = ids_all[seqs : 2 * seqs].reshape(-1)
-    label = (all_labels[row_at] - 2 * shard * vrows).reshape(1, rows)
-
-    p_low, tops, stats = vocab_logits(label, table_all, final_rows, vrows)
-    stats = stats.reshape(8, nt, own)
-    merged = (stats[0], stats[1], stats[2], stats[3])
-    others = [swap(stats, "tensor", off) for off in range(1, nt)]
-    best = stats[0]
-    for off in range(1, nt):
-        best = jnp.maximum(best, jnp.stack([others[off - 1][0, o ^ off] for o in range(nt)]))
-    summed = stats[1] * jnp.exp(stats[0] - best)
-    target = stats[2]
-    plain = stats[3]
-    for off in range(1, nt):
-        them = jnp.stack([others[off - 1][:, o ^ off] for o in range(nt)], axis=1)
-        summed = summed + them[1] * jnp.exp(them[0] - best)
-        target = target + them[2]
-        plain = plain + them[3]
-    log_total = best + jnp.log(summed)
-    token_loss = (
-        log_total
-        - (1.0 - SMOOTHING) * target
-        - SMOOTHING / V * plain
-        + ZLOSS_WEIGHT * log_total * log_total
-    )
-    loss_here = jnp.sum(weight[:own] * token_loss[0])
-    seq_part = jnp.where(
-        (iota((8, LANES), 0) == 0) & (iota((8, LANES), 1) == my_seq), loss_here, 0.0
-    )
-    soft = (weight.reshape(nt, own) * (1.0 + 2.0 * ZLOSS_WEIGHT * log_total)).reshape(1, 1, rows)
-    scale = soft * jnp.exp(tops - log_total.reshape(1, 1, rows))
+    label = (lax.dynamic_slice_in_dim(all_labels, place * rows, rows) - 2 * shard * vrows).reshape(
+        1, rows
+    )
     row_weight = weight.reshape(1, rows)
-    sent = returned(vocab_rows(label, scale, row_weight, p_low, table_all, nt))
-    table_grad = vocab_table_grad(label, scale, row_weight, p_low, final_rows)
+    p_low, tops, stats = vocab_logits(label, table_all, normed, vrows)
+    scale, seq_part = merge_stats(stats, tops, row_weight, nt, chunks)
+    sent = returned(vocab_rows(scal_shard, label, scale, row_weight, p_low, table_all, nt))
+    table_grad = vocab_table_grad(label, scale, row_weight, p_low, normed)
     sent, table_grad = lax.optimization_barrier((sent, table_grad))
     table_share = lax.psum_scatter(table_grad, "dp", scatter_dimension=1, tiled=True)
-    grad_res, payload, grad_final_gain = back_rows(
-        sent, [], residual, final_gain, None, (saved[L - 1][9], saved[L - 1][8])
+    grad_res, payload, grad_final_gain = backward_rows(
+        sent, None, residual, final_gain, None, saved[L - 1][9], saved[L - 1][8], nd, chunks, 10
     )
 
     block_pieces = [None] * (2 * L)
@@ -1669,11 +1868,9 @@
     for layer_index in reversed(range(L)):
         wzx, wout, wside, gain, bcp, chan, head = mats[layer_index]
         residual_in, normed, zx, side, c_out, cum, y, s_in, factor, branch = saved[layer_index]
-        grads, u_low, dy, dz, dstate, gain_grad = gate_back(
-            scal_shard, spread(payload), wout, y, zx, c_out, cum, chan
-        )
+        u_low, dy, dz, dstate, gain_grad = gate_back(payload, wout, y, zx, c_out, cum, chan)
         states = [hop(dstate, -k) for k in hops]
-        grad_out_w = tn(u_low, grads)
+        grad_out_w = tn(u_low, payload)
         inside = mixer_within(s_in, zx, side, dy, chan, bcp, head)
         result = mixer_back(
             scal_shard,
@@ -1739,16 +1936,17 @@
             )
             block_share = lax.psum_scatter(tile_grads, "dp", scatter_dimension=0, tiled=True)[0]
         if layer_index:
-            rims = [
-                lax.ppermute(rim_grad, both, [(b, a) for a, b in rim_pairs(to)]) for to in range(nt)
-            ]
-            grad_res, payload, _ = back_rows(
-                returned(parts_out),
-                rims,
+            grad_res, payload = backward_rows(
+                parts_out,
+                rim_grad,
                 residual_in,
                 gains[layer_index],
                 grad_res,
-                (saved[layer_index - 1][9], saved[layer_index - 1][8]),
+                saved[layer_index - 1][9],
+                saved[layer_index - 1][8],
+                nd,
+                chunks,
+                10 + layer_index,
             )
         else:
             embed = finish_rows(

time: 751 us -> 726 us (0.967)
  Pallas kernels: 315 us -> 506 us
  waiting for transfers between devices: 195 us -> 52.4 us
  starting transfers between devices: 114 us -> 36.2 us
  local copies, waits for them, and re-layouts: 40.5 us -> 56.1 us
    pallas_call x2 -> x8, Pallas kernels: 45.5 us -> 252 us  [the longest x3 129 us: forward_rows(): pl.pallas_call(functools.partial(forward_kernel, groups, shards, chunks,...]
    ppermute x43 -> x13, waiting for transfers between devices: 165 us -> 31.4 us  [swap(): return lax.ppermute(x, axis, [(i, i ^ offset) for i in range(size)])]
    ppermute x43 -> x13, starting transfers between devices: 76.7 us -> 14.6 us  [swap(): return lax.ppermute(x, axis, [(i, i ^ offset) for i in range(size)])]
    unnamed x236 -> x237, local copies, waits for them, and re-layouts: 19.9 us -> 39.7 us
    pallas_call x21 -> x16, Pallas kernels: 144 us -> 130 us  [call(): pl.pallas_call(kernel, out_shape=out_shape, in_specs=specs, out_specs=jax...]
    ppermute x12 -> x0, starting transfers between devices: 8.75 us -> none  [the longest x8 5.96 us: shards(): rims = [lax.ppermute(edge, both, rim_pairs(to)) for to in range(nt)]]
  transfers between devices with their start and end apart: 71 -> 29, of which waited for: 30 -> 13; matrix products, arithmetic and copies ran while one was open for 8% -> 6% of each run, Pallas kernels for 32% -> 59%
where the time goes in v4:
time: 726 us; the launch traced here: 720 us
  Pallas kernels  506 us (70%)
  local copies, waits for them, and re-layouts  56.1 us (8%)
  waiting for transfers between devices  52.4 us (7%)
  other arithmetic  36.7 us (5%)
  starting transfers between devices  36.2 us (5%)
  matrix products  16.6 us (2%)
  between operations  16.3 us (2%)
    pallas_call x16, Pallas kernels, call(): pl.pallas_call(kernel, out_shape=out_shape, in_specs=specs, out_specs=jax...  130 us
    pallas_call x3, Pallas kernels, forward_rows(): pl.pallas_call(functools.partial(forward_kernel, groups, shards, chunks,...  129 us
    pallas_call x2, Pallas kernels, backward_rows(): pl.pallas_call(functools.partial(backward_kernel, groups, shards, chunks,...  71.8 us
    pallas_call x1, Pallas kernels, finish_rows(): pl.pallas_call(functools.partial(finish_kernel, groups, shards, chunks, o...  71.4 us
    unnamed x237, local copies, waits for them, and re-layouts  39.7 us
    ppermute x13, waiting for transfers between devices, swap(): return lax.ppermute(x, axis, [(i, i ^ offset) for i in range(size)])  31.4 us
    pallas_call x1, Pallas kernels, vocab_logits(): pl.pallas_call(functools.partial(logits_kernel, vrows), grid=(steps,), ou...  24.9 us
    ppermute x12, starting transfers between devices, hop(): return lax.ppermute(x, 'dp', pairs)  21.5 us
  transfers between devices with their start and end apart: 29, of which 13 were waited for; matrix products, arithmetic and copies ran while one was open for 6% of the time, Pallas kernels for 59%

profile of v4, /device:TPU:0, one launch (start us, length us, event | category | flops | bytes accessed | tf_op | source)
XLA Modules:
  0.0 720.4 jit_solution(15991843214306912815)
XLA Ops:
  10.5 12.7 %open.1 = (s32[8,8,256]{2,1,0:T(8,128)S(1)}, bf16[4,192,128]{2,1,0:T(8,128)(2,1)S(1)}, bf16[8,4,16,128]{3,2,1,0:T(8,128)(2,1)S(1)}) custom-call(s32[8,256]{1,0:T(8,128)S(1)} %pad.51.ids, bf16[192,128]{1,0:T(8,128)(2,1)S(1)} %reshape.381.piece, bf16[16,128]{1,0:T(8,128)(2,1)S(1)} %pad_bitcast_fusion.share), custom_call_target="tpu_custom_call" | custom-call | tf_op jit(solution)/shard_map/open/pallas_call | solution.py:929
  28.0 9.7 %look.1 = (bf16[512,256]{1,0:T(8,128)(2,1)}, bf16[512,256]{1,0:T(8,128)(2,1)}, bf16[512,256]{1,0:T(8,128)(2,1)}, bf16[512,256]{1,0:T(8,128)(2,1)}, bf16[512,256]...) custom-call(s32[2]{0:T(128)} %pad_add_fusion.1.scal, ...), custom_call_target="tpu_custom_call" | custom-call | bytes 31457280 | tf_op jit(solution)/shard_map/look/pallas_call | solution.py:138
  74.3 9.3 %collective-permute-done.6.rest_7_ = bf16[512,256]{1,0:T(8,128)(2,1)S(1)} collective-permute-done((bf16[512,256]{1,0:T(8,128)(2,1)S(1)}, bf16[512,256]{1,0:T(8,128)(2,1)S(1)}, u32[]{:S(2)}, u32[]{:S(2)}) %collective-permute-start.6) | collective-permute-done | bytes 262176 | tf_op jit(solution)/shard_map/ppermute | solution.py:69
  90.9 44.6 %forward.3 = (f32[128,1024]{1,0:T(8,128)S(1)}, bf16[528,1024]{1,0:T(8,128)(2,1)S(1)}) custom-call(bf16[128,1024]{1,0:T(8,128)(2,1)S(1)} %copy-done.29, bf16[128,1024]{1,0:T(8,128)(2,1)S(1)} %copy-done.30, bf16[128,1024]{1,0:T(8,128)(2,1)S(1)} %copy-done.31, bf16[128,1024]{1,0:T(8,128)(2,1)S(1)} %copy-done.32, f32[1,1024]{1,0:T(1,128)S(1)} %bitcast.133), custom_call_target="tpu_custom_call" | custom-call | tf_op jit(solution)/shard_map/forward/pallas_call | solution.py:597
  138.0 8.3 %placetiles.1 = (bf16[1024,1024]{1,0:T(8,128)(2,1)}, bf16[512,1024]{1,0:T(8,128)(2,1)}, bf16[1024,1024]{1,0:T(8,128)(2,1)}, bf16[512,1024]{1,0:T(8,128)(2,1)}) custom-call(s32[1,192]{1,0:T(1,128)} %slot.3, bf16[8,3840,128]{2,1,0:T(8,128)(2,1)} %bitcast.148), custom_call_target="tpu_custom_call" | custom-call | bytes 14680064 | tf_op jit(solution)/shard_map/placetiles/pallas_call | solution.py:138
  151.4 7.9 %front.2 = (f32[528,1024]{1,0:T(8,128)}, f32[528,384]{1,0:T(8,128)}, f32[512,512]{1,0:T(8,128)}, bf16[144,512]{1,0:T(8,128)(2,1)}, bf16[512,128]{1,0:T(8,128)(2,1)}, /*index=5*/f32[512,128]{1,0:T(8,128)}) custom-call(bf16[528,1024]{1,0:T(8,128)(2,1)} %copy-done.8, bf16[1024,1024]{1,0:T(8,128)(2,1)} %get-tuple-element.202.wzx.rest_14_, ...), custom_call_target="tpu_custom_call" | custom-call | flops 2147483648 | bytes 12582912 | tf_op jit(solution)/shard_map/front/pallas_call | solution.py:138
  186.6 44.6 %forward.4 = (f32[128,1024]{1,0:T(8,128)S(1)}, f32[128,1024]{1,0:T(8,128)S(1)}, f32[128,1]{1,0:T(8,128)S(1)}, bf16[528,1024]{1,0:T(8,128)(2,1)S(1)}) custom-call(bf16[128,1152]{1,0:T(8,128)(2,1)S(1)} %copy-done.14, bf16[128,1152]{1,0:T(8,128)(2,1)S(1)} %copy-done.15, bf16[128,1152]{1,0:T(8,128)(2,1)S(1)} %copy-done.16, bf16[128,1152]{1,0:T(8,128)(2,1)S(1)} %copy-done.17, ...), custom_call_target="tpu_custom_call" | custom-call | tf_op jit(solution)/shard_map/forward/pallas_call | solution.py:597
  232.2 7.8 %front.3 = (f32[528,1024]{1,0:T(8,128)}, f32[528,384]{1,0:T(8,128)}, f32[512,512]{1,0:T(8,128)}, bf16[144,512]{1,0:T(8,128)(2,1)}, bf16[512,128]{1,0:T(8,128)(2,1)}, /*index=5*/f32[512,128]{1,0:T(8,128)}) custom-call(bf16[528,1024]{1,0:T(8,128)(2,1)} %copy-done.10, bf16[1024,1024]{1,0:T(8,128)(2,1)} %get-tuple-element.215.wzx.rest_14_, ...), custom_call_target="tpu_custom_call" | custom-call | flops 2147483648 | bytes 12582912 | tf_op jit(solution)/shard_map/front/pallas_call | solution.py:138
  260.9 39.5 %forward.5 = (f32[128,1024]{1,0:T(8,128)S(1)}, f32[128,1024]{1,0:T(8,128)S(1)}, f32[128,1]{1,0:T(8,128)S(1)}, bf16[528,1024]{1,0:T(8,128)(2,1)S(1)}) custom-call(bf16[128,1152]{1,0:T(8,128)(2,1)S(1)} %copy-done.18, bf16[128,1152]{1,0:T(8,128)(2,1)S(1)} %copy-done.19, bf16[128,1152]{1,0:T(8,128)(2,1)S(1)} %copy-done.20, bf16[128,1152]{1,0:T(8,128)(2,1)S(1)} %copy-done.21, ...), custom_call_target="tpu_custom_call" | custom-call | tf_op jit(solution)/shard_map/forward/pallas_call | solution.py:597
  301.4 24.9 %logits.1 = (bf16[2,6400,512]{2,1,0:T(8,128)(2,1)}, f32[5,64,512]{2,1,0:T(8,128)}, f32[8,512]{1,0:T(8,128)}) custom-call(s32[1,512]{1,0:T(1,128)} %bitcast.173, bf16[6400,2048]{1,0:T(8,128)(2,1)} %all-gather.4.cloned.1.call-done.table, bf16[528,1024]{1,0:T(8,128)(2,1)} %copy-done.54), custom_call_target="tpu_custom_call" | custom-call | flops 13421772800 | bytes 41943040 | tf_op jit(solution)/shard_map/logits/pallas_call | solution.py:1455
  335.0 20.1 %rowgrads.1 = (bf16[128,1024]{1,0:T(8,128)(2,1)}, bf16[128,1024]{1,0:T(8,128)(2,1)}, bf16[128,1024]{1,0:T(8,128)(2,1)}, bf16[128,1024]{1,0:T(8,128)(2,1)}) custom-call(s32[1]{0:T(128)} %bitcast.4.scal, s32[1,512]{1,0:T(1,128)} %bitcast.174, f32[5,64,512]{2,1,0:T(8,128)} %copy-done.55, f32[1,512]{1,0:T(1,128)} %copy-done.48, ...), custom_call_target="tpu_custom_call" | custom-call | flops 13421772800 | bytes 41943040 | tf_op jit(solution)/shard_map/rowgrads/pallas_call | solution.py:1532
  359.5 20.7 %tablegrads.1 = bf16[6400,2048]{1,0:T(8,128)(2,1)} custom-call(s32[1,512]{1,0:T(1,128)} %bitcast.175, f32[5,64,512]{2,1,0:T(8,128)} %copy-done.55, f32[1,512]{1,0:T(1,128)} %copy-done.48, bf16[2,6400,512]{2,1,0:T(8,128)(2,1)} %get-tuple-element.232.p_in, bf16[528,1024]{1,0:T(8,128)(2,1)} %copy-done.54), custom_call_target="tpu_custom_call" | custom-call | flops 13421772800 | bytes 41943040 | tf_op jit(solution)/shard_map/tablegrads/pallas_call | solution.py:1565
  382.9 22.4 %backward.2 = (f32[128,1024]{1,0:T(8,128)S(1)}, bf16[512,1152]{1,0:T(8,128)(2,1)S(1)}, f32[1,1024]{1,0:T(1,128)S(1)}) custom-call(bf16[128,1024]{1,0:T(8,128)(2,1)S(1)} %copy-done.26, bf16[128,1024]{1,0:T(8,128)(2,1)S(1)} %collective-permute-done.13.refs_1_, bf16[128,1024]{1,0:T(8,128)(2,1)S(1)} %collective-permute-done.14.refs_2_, ...), custom_call_target="tpu_custom_call" | custom-call | tf_op jit(solution)/shard_map/backward/pallas_call | solution.py:696
  420.3 7.8 %within.2 = (f32[512,512]{1,0:T(8,128)}, bf16[512,256]{1,0:T(8,128)(2,1)}, f32[512,128]{1,0:T(8,128)}, f32[2,128,512]{2,1,0:T(8,128)}, f32[512,512]{1,0:T(8,128)}, /*index=5*/f32[512,256]{1,0:T(8,128)}) custom-call(f32[128,512]{1,0:T(8,128)} %get-tuple-element.247.s_in, f32[528,1024]{1,0:T(8,128)} %get-tuple-element.218.rest_4_.zx.rest_9_, ...), custom_call_target="tpu_custom_call" | custom-call | flops 2147483648 | bytes 16777216 | tf_op jit(solution)/shard_map/within/pallas_call | solution.py:138
  432.5 14.0 %back.2 = (bf16[528,1024]{1,0:T(8,128)(2,1)}, bf16[528,384]{1,0:T(8,128)(2,1)}, f32[8,512]{1,0:T(8,128)}, f32[8,256]{1,0:T(8,128)}, f32[8,128]{1,0:T(8,128)}, /*...) custom-call(s32[1]{0:T(128)} %bitcast.4.scal, ...), custom_call_target="tpu_custom_call" | custom-call | flops 2147483648 | bytes 16777216 | tf_op jit(solution)/shard_map/back/pallas_call | solution.py:138
  451.1 49.3 %backward.3 = (f32[128,1024]{1,0:T(8,128)S(1)}, bf16[512,1152]{1,0:T(8,128)(2,1)S(1)}) custom-call(bf16[128,1024]{1,0:T(8,128)(2,1)S(1)} %copy-done.33, bf16[128,1024]{1,0:T(8,128)(2,1)S(1)} %copy-done.34, bf16[128,1024]{1,0:T(8,128)(2,1)S(1)} %copy-done.35, bf16[128,1024]{1,0:T(8,128)(2,1)S(1)} %copy-done.36, bf16[16,1024]{1,0:T(8,128)(2,1)S(1)} %copy-done.46, ...), custom_call_target="tpu_custom_call" | custom-call | tf_op jit(solution)/shard_map/backward/pallas_call | solution.py:696
  510.9 8.2 %within.3 = (f32[512,512]{1,0:T(8,128)}, bf16[512,256]{1,0:T(8,128)(2,1)}, f32[512,128]{1,0:T(8,128)}, f32[2,128,512]{2,1,0:T(8,128)}, f32[512,512]{1,0:T(8,128)}, /*index=5*/f32[512,256]{1,0:T(8,128)}) custom-call(f32[128,512]{1,0:T(8,128)} %get-tuple-element.268.s_in, f32[528,1024]{1,0:T(8,128)} %get-tuple-element.205.rest_4_.zx.rest_9_, ...), custom_call_target="tpu_custom_call" | custom-call | flops 2147483648 | bytes 16777216 | tf_op jit(solution)/shard_map/within/pallas_call | solution.py:138
  527.4 14.2 %back.3 = (bf16[528,1024]{1,0:T(8,128)(2,1)}, bf16[528,384]{1,0:T(8,128)(2,1)}, f32[8,512]{1,0:T(8,128)}, f32[8,256]{1,0:T(8,128)}, f32[8,128]{1,0:T(8,128)}, /*...) custom-call(s32[1]{0:T(128)} %bitcast.4.scal, ...), custom_call_target="tpu_custom_call" | custom-call | flops 2147483648 | bytes 16777216 | tf_op jit(solution)/shard_map/back/pallas_call | solution.py:138
  553.5 9.6 %packtiles.1 = bf16[8,3968,128]{2,1,0:T(8,128)(2,1)} custom-call(s32[1]{0:T(128)} %bitcast.4.scal, s32[1,192]{1,0:T(1,128)} %slot.3, bf16[1024,1024]{1,0:T(8,128)(2,1)} %convolution_convert_fusion.3.refs_0_, bf16[512,1152]{1,0:T(8,128)(2,1)} %convolution_convert_fusion.1.refs_1_, bf16[1024,1024]{1,0:T(8,128)(2,1)} %convolution_convert_fusion.2.refs_2_, ...), custom_call_target="tpu_custom_call" | custom-call | bytes 14680064 | tf_op jit(solution)/shard_map/packtiles/pallas_call | solution.py:138
  564.9 71.4 %finish.1.parts = bf16[8,512,256]{2,1,0:T(8,128)(2,1)S(1)} custom-call(bf16[128,1024]{1,0:T(8,128)(2,1)S(1)} %copy-done.22, bf16[128,1024]{1,0:T(8,128)(2,1)S(1)} %copy-done.23, bf16[128,1024]{1,0:T(8,128)(2,1)S(1)} %copy-done.24, bf16[128,1024]{1,0:T(8,128)(2,1)S(1)} %copy-done.25, bf16[16,1024]{1,0:T(8,128)(2,1)S(1)} %copy-done.45, ...), custom_call_target="tpu_custom_call" | custom-call | tf_op jit(solution)/shard_map/finish/pallas_call | solution.py:878
  637.7 11.0 %addrows.1 = (bf16[6286,256]{1,0:T(8,128)(2,1)}, f32[1,256]{1,0:T(1,128)}) custom-call(s32[2]{0:T(128)} %pad_add_fusion.1.scal, s32[4104]{0:T(1024)} %concatenate.41.code, s32[4096]{0:T(1024)} %select_bitcast_fusion.listed, s32[32]{0:T(128)} %copy-done.82, bf16[6400,256]{1,0:T(8,128)(2,1)} %reduce-scatter.3.cloned.1.call-done.share, bf16[8,512,256]{2,1,0:T(8,128)(2,1)} %copy-done), custom_call_target="tpu_custom_call" | custom-call | bytes 31457280 | tf_op jit(solution)/shard_map/addrows/pallas_call | solution.py:138
  670.9 9.9 %sumall.1.sums = f32[8,128]{1,0:T(8,128)S(1)} custom-call(f32[8,128]{1,0:T(8,128)S(1)} %get-tuple-element.230.refs_0_, f32[12,512]{1,0:T(8,128)S(1)} %reshape.399.refs_1_.refs_14_, f32[6,8]{1,0:T(8,128)S(1)} %reshape_squeeze.3.refs_2_.refs_18_, f32[1,256]{1,0:T(1,128)S(1)} %copy-done.52, f32[1,128]{1,0:T(1,128)S(1)} %copy-done.53, f32[64,288]{1,0:T(8,128)S(1)} %bitcast.126, ...), custom_call_target="tpu_custom_call" | custom-call | tf_op jit(solution)/shard_map/sumall/pallas_call | solution.py:1007
  683.4 10.1 %update.1 = (f32[24,128,128]{2,1,0:T(8,128)}, bf16[24,128,128]{2,1,0:T(8,128)(2,1)}, f32[24,128,128]{2,1,0:T(8,128)}, f32[24,128,128]{2,1,0:T(8,128)}, f32[64,28...) custom-call(f32[2]{0:T(128)S(1)} %pad_maximum_fusion.3.fixes, ...), custom_call_target="tpu_custom_call" | custom-call | flops 1207959552 | bytes 16777216 | tf_op jit(solution)/shard_map/update/pallas_call | solution.py:1660
  697.2 16.4 %multiply_subtract_fusion = (f32[6286,256]{1,0:T(8,128)}, f32[6286,256]{1,0:T(8,128)}, f32[6286,256]{1,0:T(8,128)}) fusion(f32[6286,256]{1,0:T(8,128)} %table.1, f32[]{:T(128)} %bitcast.42, f32[]{:T(128)} %bitcast.41, f32[]{:T(128)} %bitcast.40, bf16[6286,256]{1,0:T(8,128)(2,1)} %get-tuple-element.311, f32[6286,256]{1,0:T(8,128)} %param.33, f32[6286,256]{1,0:T(8,128)} %param.32), kind=kLoop, calls=%fused_computation.2 | loop fusion | flops 27356672 | bytes 41839628 | tf_op jit(solution)/shard_map/sub | solution.py:1587
  (421 shorter events, 209.7 us)
Async XLA Ops:
  7.2 129.3 %all-gather.6.cloned.1.call-start = ((), (), s32[]{:S(2)}) async-start(), calls=%async_computation.5 | async-start | bytes 8847360 | tf_op jit(solution)/shard_map/all_gather | solution.py:1765
  24.2 277.2 %all-gather.4.cloned.1.call-start = ((), (), s32[]{:S(2)}) async-start(), calls=%async_computation.2 | async-start | bytes 29491200 | tf_op jit(solution)/shard_map/all_gather | solution.py:1789
  42.9 520.2 %reduce-scatter.3.cloned.1.call-start = ((), (), s32[]{:S(2)}) async-start(), calls=%async_computation.3 | async-start | bytes 29491200 | tf_op jit(solution)/shard_map/reduce_scatter | solution.py:1858
  43.7 9.2 %collective-permute-start.1 = (bf16[512,256]{1,0:T(8,128)(2,1)S(1)}, bf16[512,256]{1,0:T(8,128)(2,1)S(1)}, u32[]{:S(2)}, u32[]{:S(2)}) collective-permute-start(bf16[512,256]{1,0:T(8,128)(2,1)S(1)} %copy-done.102), channel_id=1, source_target_pairs={{0,8},{4,12},{8,0},{12,4},{16,24},{20,28},{24,16},{28,20},{1,9},{5... | collective-permute-start | bytes 786440 | tf_op jit(solution)/shard_map/ppermute | solution.py:69
  44.8 17.2 %collective-permute-start.2 = (bf16[512,256]{1,0:T(8,128)(2,1)S(1)}, bf16[512,256]{1,0:T(8,128)(2,1)S(1)}, u32[]{:S(2)}, u32[]{:S(2)}) collective-permute-start(bf16[512,256]{1,0:T(8,128)(2,1)S(1)} %copy-done.101), channel_id=1, source_target_pairs={{0,12},{4,8},{8,4},{12,0},{16,28},{20,24},{24,20},{28,16},{1,13},{... | collective-permute-start | bytes 786440 | tf_op jit(solution)/shard_map/ppermute | solution.py:69
  45.0 17.0 %collective-permute-start.3 = (bf16[512,256]{1,0:T(8,128)(2,1)S(1)}, bf16[512,256]{1,0:T(8,128)(2,1)S(1)}, u32[]{:S(2)}, u32[]{:S(2)}) collective-permute-start(bf16[512,256]{1,0:T(8,128)(2,1)S(1)} %copy-done.100), channel_id=1, source_target_pairs={{0,16},{4,20},{8,24},{12,28},{16,0},{20,4},{24,8},{28,12},{1,17},{... | collective-permute-start | bytes 786440 | tf_op jit(solution)/shard_map/ppermute | solution.py:69
  46.5 23.1 %collective-permute-start.4 = (bf16[512,256]{1,0:T(8,128)(2,1)S(1)}, bf16[512,256]{1,0:T(8,128)(2,1)S(1)}, u32[]{:S(2)}, u32[]{:S(2)}) collective-permute-start(bf16[512,256]{1,0:T(8,128)(2,1)S(1)} %copy-done.99), channel_id=1, source_target_pairs={{0,20},{4,16},{8,28},{12,24},{16,4},{20,0},{24,12},{28,8},{1,21},{... | collective-permute-start | bytes 786440 | tf_op jit(solution)/shard_map/ppermute | solution.py:69
  47.8 26.5 %collective-permute-start.5 = (bf16[512,256]{1,0:T(8,128)(2,1)S(1)}, bf16[512,256]{1,0:T(8,128)(2,1)S(1)}, u32[]{:S(2)}, u32[]{:S(2)}) collective-permute-start(bf16[512,256]{1,0:T(8,128)(2,1)S(1)} %copy-done.98), channel_id=1, source_target_pairs={{0,24},{4,28},{8,16},{12,20},{16,8},{20,12},{24,0},{28,4},{1,25},{... | collective-permute-start | bytes 786440 | tf_op jit(solution)/shard_map/ppermute | solution.py:69
  52.9 30.7 %collective-permute-start.6 = (bf16[512,256]{1,0:T(8,128)(2,1)S(1)}, bf16[512,256]{1,0:T(8,128)(2,1)S(1)}, u32[]{:S(2)}, u32[]{:S(2)}) collective-permute-start(bf16[512,256]{1,0:T(8,128)(2,1)S(1)} %copy-done.97), channel_id=1, source_target_pairs={{0,28},{4,24},{8,20},{12,16},{16,12},{20,8},{24,4},{28,0},{1,29},{... | collective-permute-start | bytes 786440 | tf_op jit(solution)/shard_map/ppermute | solution.py:69
  159.4 9.5 %collective-permute-start.7 = (bf16[144,512]{1,0:T(8,128)(2,1)}, bf16[144,512]{1,0:T(8,128)(2,1)S(1)}, u32[]{:S(2)}, u32[]{:S(2)}) collective-permute-start(bf16[144,512]{1,0:T(8,128)(2,1)} %get-tuple-element.203), channel_id=1, source_target_pairs={{0,4},{4,8},{8,12},{16,20},{20,24},{24,28},{1,5},{5,9},{9,13},{17,... | collective-permute-start | bytes 442376 | tf_op jit(solution)/shard_map/ppermute | solution.py:1818
  160.7 11.1 %collective-permute-start.8 = (bf16[144,512]{1,0:T(8,128)(2,1)}, bf16[144,512]{1,0:T(8,128)(2,1)S(1)}, u32[]{:S(2)}, u32[]{:S(2)}) collective-permute-start(bf16[144,512]{1,0:T(8,128)(2,1)} %get-tuple-element.203), channel_id=1, source_target_pairs={{0,8},{4,12},{16,24},{20,28},{1,9},{5,13},{17,25},{21,29},{2,10},{... | collective-permute-start | bytes 442376 | tf_op jit(solution)/shard_map/ppermute | solution.py:1818
  164.1 13.1 %collective-permute-start.9 = (bf16[144,512]{1,0:T(8,128)(2,1)}, bf16[144,512]{1,0:T(8,128)(2,1)S(1)}, u32[]{:S(2)}, u32[]{:S(2)}) collective-permute-start(bf16[144,512]{1,0:T(8,128)(2,1)} %get-tuple-element.203), channel_id=1, source_target_pairs={{0,12},{16,28},{1,13},{17,29},{2,14},{18,30},{3,15},{19,31}} | collective-permute-start | bytes 442376 | tf_op jit(solution)/shard_map/ppermute | solution.py:1818
  240.0 9.6 %collective-permute-start.10 = (bf16[144,512]{1,0:T(8,128)(2,1)}, bf16[144,512]{1,0:T(8,128)(2,1)S(1)}, u32[]{:S(2)}, u32[]{:S(2)}) collective-permute-start(bf16[144,512]{1,0:T(8,128)(2,1)} %get-tuple-element.216), channel_id=1, source_target_pairs={{0,4},{4,8},{8,12},{16,20},{20,24},{24,28},{1,5},{5,9},{9,13},{17,... | collective-permute-start | bytes 442376 | tf_op jit(solution)/shard_map/ppermute | solution.py:1818
  355.1 25.1 %collective-permute-start.13 = (bf16[128,1024]{1,0:T(8,128)(2,1)}, bf16[128,1024]{1,0:T(8,128)(2,1)S(1)}, u32[]{:S(2)}, u32[]{:S(2)}) collective-permute-start(bf16[128,1024]{1,0:T(8,128)(2,1)} %get-tuple-element.234), channel_id=1, source_target_pairs={{0,1},{1,0},{2,3},{3,2},{4,5},{5,4},{6,7},{7,6},{8,9},{9,8},{10,11... | collective-permute-start | bytes 786440 | tf_op jit(solution)/shard_map/ppermute | solution.py:69
  355.5 24.7 %collective-permute-start.14 = (bf16[128,1024]{1,0:T(8,128)(2,1)}, bf16[128,1024]{1,0:T(8,128)(2,1)S(1)}, u32[]{:S(2)}, u32[]{:S(2)}) collective-permute-start(bf16[128,1024]{1,0:T(8,128)(2,1)} %get-tuple-element.235), channel_id=1, source_target_pairs={{0,2},{1,3},{2,0},{3,1},{4,6},{5,7},{6,4},{7,5},{8,10},{9,11},{10,... | collective-permute-start | bytes 786440 | tf_op jit(solution)/shard_map/ppermute | solution.py:69
  357.9 22.4 %collective-permute-start.15 = (bf16[128,1024]{1,0:T(8,128)(2,1)}, bf16[128,1024]{1,0:T(8,128)(2,1)S(1)}, u32[]{:S(2)}, u32[]{:S(2)}) collective-permute-start(bf16[128,1024]{1,0:T(8,128)(2,1)} %get-tuple-element.236), channel_id=1, source_target_pairs={{0,3},{1,2},{2,1},{3,0},{4,7},{5,6},{6,5},{7,4},{8,11},{9,10},{10,... | collective-permute-start | bytes 786440 | tf_op jit(solution)/shard_map/ppermute | solution.py:69
  381.0 274.2 %reduce-scatter.5.cloned.1.call-start = ((), (), s32[]{:S(2)}) async-start(), calls=%async_computation.4 | async-start | bytes 9142272 | tf_op jit(solution)/shard_map/reduce_scatter | solution.py:1937
  413.2 14.9 %collective-permute-start.16 = (bf16[144,512]{1,0:T(8,128)(2,1)}, bf16[144,512]{1,0:T(8,128)(2,1)S(1)}, u32[]{:S(2)}, u32[]{:S(2)}) collective-permute-start(bf16[144,512]{1,0:T(8,128)(2,1)} %get-tuple-element.246), channel_id=1, source_target_pairs={{4,0},{8,4},{12,8},{20,16},{24,20},{28,24},{5,1},{9,5},{13,9},{21,... | collective-permute-start | bytes 442376 | tf_op jit(solution)/shard_map/ppermute | solution.py:1818
  414.5 16.2 %collective-permute-start.17 = (bf16[144,512]{1,0:T(8,128)(2,1)}, bf16[144,512]{1,0:T(8,128)(2,1)S(1)}, u32[]{:S(2)}, u32[]{:S(2)}) collective-permute-start(bf16[144,512]{1,0:T(8,128)(2,1)} %get-tuple-element.246), channel_id=1, source_target_pairs={{8,0},{12,4},{24,16},{28,20},{9,1},{13,5},{25,17},{29,21},{10,2},{... | collective-permute-start | bytes 442376 | tf_op jit(solution)/shard_map/ppermute | solution.py:1818
  415.8 16.1 %collective-permute-start.18 = (bf16[144,512]{1,0:T(8,128)(2,1)}, bf16[144,512]{1,0:T(8,128)(2,1)S(1)}, u32[]{:S(2)}, u32[]{:S(2)}) collective-permute-start(bf16[144,512]{1,0:T(8,128)(2,1)} %get-tuple-element.246), channel_id=1, source_target_pairs={{12,0},{28,16},{13,1},{29,17},{14,2},{30,18},{15,3},{31,19}} | collective-permute-start | bytes 442376 | tf_op jit(solution)/shard_map/ppermute | solution.py:1818
  506.9 19.5 %collective-permute-start.19 = (bf16[144,512]{1,0:T(8,128)(2,1)}, bf16[144,512]{1,0:T(8,128)(2,1)S(1)}, u32[]{:S(2)}, u32[]{:S(2)}) collective-permute-start(bf16[144,512]{1,0:T(8,128)(2,1)} %get-tuple-element.267), channel_id=1, source_target_pairs={{4,0},{8,4},{12,8},{20,16},{24,20},{28,24},{5,1},{9,5},{13,9},{21,... | collective-permute-start | bytes 442376 | tf_op jit(solution)/shard_map/ppermute | solution.py:1818
  508.2 18.2 %collective-permute-start.20 = (bf16[144,512]{1,0:T(8,128)(2,1)}, bf16[144,512]{1,0:T(8,128)(2,1)S(1)}, u32[]{:S(2)}, u32[]{:S(2)}) collective-permute-start(bf16[144,512]{1,0:T(8,128)(2,1)} %get-tuple-element.267), channel_id=1, source_target_pairs={{8,0},{12,4},{24,16},{28,20},{9,1},{13,5},{25,17},{29,21},{10,2},{... | collective-permute-start | bytes 442376 | tf_op jit(solution)/shard_map/ppermute | solution.py:1818
  509.5 17.3 %collective-permute-start.21 = (bf16[144,512]{1,0:T(8,128)(2,1)}, bf16[144,512]{1,0:T(8,128)(2,1)S(1)}, u32[]{:S(2)}, u32[]{:S(2)}) collective-permute-start(bf16[144,512]{1,0:T(8,128)(2,1)} %get-tuple-element.267), channel_id=1, source_target_pairs={{12,0},{28,16},{13,1},{29,17},{14,2},{30,18},{15,3},{31,19}} | collective-permute-start | bytes 442376 | tf_op jit(solution)/shard_map/ppermute | solution.py:1818
  657.5 11.1 %collective-permute-start.24 = (bf16[208,128]{1,0:T(8,128)(2,1)}, bf16[208,128]{1,0:T(8,128)(2,1)S(1)}, u32[]{:S(2)}, u32[]{:S(2)}) collective-permute-start(bf16[208,128]{1,0:T(8,128)(2,1)} %get-tuple-element.423), channel_id=1, source_target_pairs={{0,3},{1,2},{2,1},{3,0},{4,7},{5,6},{6,5},{7,4},{8,11},{9,10},{10,... | collective-permute-start | bytes 159752 | tf_op jit(solution)/shard_map/ppermute | solution.py:69
  (110 other events, 989.8 us)
Sparse Core Ops, SparseCore 0:
  24.3 69.6 all-gather.5
  96.4 132.7 all-gather.3
  381.1 175.2 reduce-scatter.2
  563.4 91.7 reduce-scatter.4

commit v5 on v4

--- a/solution.py
+++ b/solution.py
@@ -178,8 +178,12 @@
 
 
 def look_kernel(groups, rows, scal, code, listed, count, table, *rest):
-    outs, work = rest[:groups], rest[groups]
+    outs, low, work = rest[:groups], rest[groups], rest[groups + 1]
     place = scal[0]
+    vrows = table.shape[0]
+    edge = vrows // RIM * RIM
+    low[edge:, :] = jnp.zeros((low.shape[0] - edge, low.shape[1]), BF)
+    low[0:vrows, :] = table[...].astype(BF)
 
     def fill(step, carry):
         work[pl.ds(pl.multiple_of(step * rows, rows), rows), :] = jnp.zeros((rows, table.shape[1]), F32)
@@ -196,42 +200,16 @@
         outs[off][...] = work[pl.ds(base, rows), :].astype(BF)
 
 
-def gather_rows(scal, code, listed, count, table, groups, rows):
+def gather_rows(scal, code, listed, count, table, groups, rows, padded):
     cols = table.shape[1]
     return call(
         functools.partial(look_kernel, groups, rows),
         "look",
-        [sds((rows, cols), BF)] * groups,
+        [sds((rows, cols), BF)] * groups + [sds((padded, cols), BF)],
         (scal, code, listed, count, table),
         smem=(0, 1, 2, 3),
         scratch=[pltpu.VMEM((groups * rows + 8, cols), F32)],
         moved=30 * MIB,
-    )
-
-
-def join_kernel(groups, shards, own, scal, *rest):
-    parts, outs, work = rest[:groups], rest[groups : groups + shards], rest[-1]
-    place, shard = scal[0], scal[1]
-    half = groups // 2
-    cols = parts[0].shape[1]
-    for off in range(half):
-        at = ((place ^ off) % half) * cols
-        work[:, pl.ds(pl.multiple_of(at, cols), cols)] = parts[off][...] + parts[off + half][...]
-    for off in range(shards):
-        at = pl.multiple_of((shard ^ off) * own, own)
-        outs[off][...] = work[pl.ds(at, own), :]
-
-
-def join_parts(scal, parts, shards, own):
-    rows = parts[0].shape[0]
-    return call(
-        functools.partial(join_kernel, len(parts), shards, own),
-        "join",
-        [sds((own, D), BF)] * shards,
-        (scal, *parts),
-        smem=(0,),
-        scratch=[pltpu.VMEM((rows, D), BF)],
-        moved=4 * MIB,
     )
 
 
@@ -377,7 +355,7 @@
     return copy
 
 
-def greet_shards(groups, shards, rims):
+def greet_shards(groups, shards, rims, wide=False):
     place, shard = lax.axis_index("dp"), lax.axis_index("tensor")
     last = shard == shards - 1
     barrier = pltpu.get_barrier_semaphore()
@@ -389,6 +367,21 @@
         greet((place, shard ^ off))
     if not rims:
         pl.semaphore_wait(barrier, shards - 1)
+        return
+    if wide:
+        for off in range(1, groups):
+            greet((place ^ off, shard))
+
+        @pl.when(jnp.logical_not(last))
+        def _():
+            greet((lax.rem(place + groups - 1, groups), shards - 1))
+
+        @pl.when(last)
+        def _():
+            for other in range(shards - 1):
+                greet((lax.rem(place + 1, groups), other))
+
+        pl.semaphore_wait(barrier, shards + groups - 2 + jnp.where(last, shards - 1, 1))
         return
     greet((lax.rem(place + groups - 1, groups), shards - 1))
 
@@ -457,7 +450,7 @@
             down(hop).wait_send()
 
 
-def exchange_terms(parts, slots, work, sems):
+def exchange_terms(parts, slots, work, sems, ready=None):
     place, shard = lax.axis_index("dp"), lax.axis_index("tensor")
     shards = len(parts)
 
@@ -475,8 +468,12 @@
         return copy(off, parts[off], shard ^ off, off)
 
     if shards != 4:
-        for off in range(1, shards):
+        for off in reversed(range(1, shards)):
+            if ready:
+                ready(off)
             direct(off).start()
+        if ready:
+            ready(0)
         for off in range(1, shards):
             direct(off).wait()
         total = parts[0][...].astype(F32)
@@ -488,19 +485,48 @@
     outer = jnp.logical_or(shard == 0, shard == shards - 1)
     inner = jnp.logical_not(outer)
 
-    @pl.when(outer)
-    def _():
-        copy(3, parts[3], shard ^ 1, relay).start()
-        direct(2).start()
-        direct(1).start()
-
-    @pl.when(inner)
-    def _():
-        direct(3).start()
-        direct(1).start()
+    def pass_relayed():
         copy(0, parts[3], shard ^ 1, relay).wait_recv()
         slots[added] = (slots[relay].astype(F32) + parts[2][...].astype(F32)).astype(BF)
         copy(2, slots.at[added], shard ^ 2, 2).start()
+
+    if ready:
+        ready(3)
+
+        @pl.when(outer)
+        def _():
+            copy(3, parts[3], shard ^ 1, relay).start()
+
+        @pl.when(inner)
+        def _():
+            direct(3).start()
+
+        ready(2)
+
+        @pl.when(outer)
+        def _():
+            direct(2).start()
+
+        @pl.when(inner)
+        def _():
+            pass_relayed()
+
+        ready(1)
+        direct(1).start()
+        ready(0)
+    else:
+
+        @pl.when(outer)
+        def _():
+            copy(3, parts[3], shard ^ 1, relay).start()
+            direct(2).start()
+            direct(1).start()
+
+        @pl.when(inner)
+        def _():
+            direct(3).start()
+            direct(1).start()
+            pass_relayed()
 
     direct(1).wait_recv()
     total = parts[0][...].astype(F32) + slots[1].astype(F32)
@@ -525,18 +551,49 @@
 
 
 def forward_kernel(groups, shards, chunks, packed, rims, *refs):
-    parts, refs = refs[:shards], refs[shards:]
+    ready = None
+    place, shard = lax.axis_index("dp"), lax.axis_index("tensor")
     if packed:
+        parts, refs = refs[:shards], refs[shards:]
         before, gain, residual, branch, factor, normed, *refs = refs
+        slots, work, term_sems, row_sems, rim_sems = refs
+        own = parts[0].shape[0]
+        greet_shards(groups, shards, rims)
     else:
+        looked, refs = refs[:groups], refs[groups:]
         gain, residual, normed, *refs = refs
-    slots, work, term_sems, row_sems, rim_sems = refs
-    own = parts[0].shape[0]
+        slots, work, term_sems, row_sems, rim_sems, arrived, terms, look_sems = refs
+        own = terms.shape[1]
+        half, cols = groups // 2, looked[0].shape[1]
+        parts = [terms.at[off] for off in range(shards)]
+        greet_shards(groups, shards, rims, True)
+
+        def block(off):
+            return pl.ds(pl.multiple_of((shard ^ off) * own, own), own)
+
+        copies = {
+            (off, other): send(
+                looked[other].at[block(off), :],
+                arrived.at[off, other],
+                look_sems.at[0, off, other],
+                look_sems.at[1, off, other],
+                (place ^ other, shard),
+            )
+            for off in reversed(range(shards))
+            for other in range(1, groups)
+        }
+
+        def ready(off):
+            for other in range(1, groups):
+                copies[off, other].wait()
+            arrived[off, 0] = looked[0][block(off), :]
+            for other in range(half):
+                at = pl.multiple_of(lax.rem(place ^ other, half) * cols, cols)
+                terms[off, :, pl.ds(at, cols)] = arrived[off, other] + arrived[off, other + half]
+
     rows = own * shards
-    place, shard = lax.axis_index("dp"), lax.axis_index("tensor")
     chunk = lax.rem(place, chunks)
-    greet_shards(groups, shards, rims)
-    exchange_terms(parts, slots, work, term_sems)
+    exchange_terms(parts, slots, work, term_sems, ready)
     total = work[...]
     if packed:
         scale = lax.rsqrt(column3(total[:, D:]) / DI + NORM_EPS)
@@ -584,11 +641,22 @@
                 rim_copy(to, (place + 1, to)).wait_send()
 
 
-def forward_rows(parts, before, gain, groups, chunks, rims, cid):
-    shards = len(parts)
-    own, width = parts[0].shape
+def forward_rows(parts, before, gain, groups, chunks, rims, cid, entry=0):
     packed = before is not None
-    args = (*parts, before, gain) if packed else (*parts, gain)
+    if packed:
+        shards = len(parts)
+        own, width = parts[0].shape
+        args = (*parts, before, gain)
+        extra = []
+    else:
+        shards = entry
+        own, width = parts[0].shape[0] // shards, D
+        args = (*parts, gain)
+        extra = [
+            pltpu.VMEM((shards, groups, own, parts[0].shape[1]), BF),
+            pltpu.VMEM((shards, own, D), BF),
+            pltpu.SemaphoreType.DMA((2, shards, groups)),
+        ]
     vmem = pl.BlockSpec(memory_space=pltpu.VMEM)
     outs = [sds((own, D), F32)]
     if packed:
@@ -603,11 +671,12 @@
             *term_scratch(shards, own, width),
             pltpu.SemaphoreType.DMA((2, 2, shards)),
             pltpu.SemaphoreType.DMA((2, shards)),
+            *extra,
         ],
         compiler_params=pltpu.CompilerParams(
-            collective_id=cid, has_side_effects=True, vmem_limit_bytes=32 * MIB
+            collective_id=cid, has_side_effects=True, vmem_limit_bytes=60 * MIB
         ),
-        name="forward",
+        name="forward" if packed else "enter",
     )(*args)
 
 
@@ -700,7 +769,7 @@
         out_specs=[vmem] * len(outs),
         scratch_shapes=scratch,
         compiler_params=pltpu.CompilerParams(
-            collective_id=cid, has_side_effects=True, vmem_limit_bytes=32 * MIB
+            collective_id=cid, has_side_effects=True, vmem_limit_bytes=60 * MIB
         ),
         name="backward",
     )(*args)
@@ -890,7 +959,7 @@
             pltpu.SemaphoreType.DMA((2, shards, groups)),
         ],
         compiler_params=pltpu.CompilerParams(
-            collective_id=3, has_side_effects=True, vmem_limit_bytes=32 * MIB
+            collective_id=3, has_side_effects=True, vmem_limit_bytes=60 * MIB
         ),
         name="finish",
     )(*args)
@@ -1656,7 +1725,9 @@
     each = 4 if count % 4 == 0 else 2
     tile_spec = pl.BlockSpec((each, BLK, BLK), lambda i: (i, 0, 0))
     base_spec = pl.BlockSpec((each, 2, BLK, BLK), lambda i: (i, 0, 0, 0))
-    whole = [pl.BlockSpec(x.shape, lambda i: (0, 0)) for group in little for x in group]
+    whole = [
+        pl.BlockSpec(x.shape, lambda i, rank=x.ndim: (0,) * rank) for group in little for x in group
+    ]
     return pl.pallas_call(
         functools.partial(last_kernel, len(little)),
         grid=(count // each,),
@@ -1770,14 +1841,13 @@
         axis=0,
         tiled=False,
     )
-    parts = gather_rows(scal, code, listed, count, vocab_table, nd, rows)
-    table_now, parts = lax.optimization_barrier((vocab_table, parts))
-    parts = [parts[0]] + [swap(parts[off], "dp", off) for off in range(1, nd)]
-    table_low = jnp.pad(table_now.astype(BF), ((0, padded - vrows), (0, 0)))
-    parts = join_parts(scal, parts, nt, own)
+    *parts, table_low = gather_rows(
+        scal, code, listed, count, vocab_table, nd, rows, padded
+    )
     residual, normed = forward_rows(
-        parts, None, shared_full[None, :D], nd, chunks, True, 4
-    )
+        parts, None, shared_full[None, :D], nd, chunks, True, 4, nt
+    )
+    table_low, normed = lax.optimization_barrier((table_low, normed))
     gathered, normed = lax.optimization_barrier((gathered, normed))
     placed = place_tiles(block_slot, gathered, own_tiles, inner, zx_count, per_layer)
     side_full = (
@@ -1996,8 +2066,8 @@
     little = [
         [flat(side_proj), side_share, flat(side_first), flat(side_second)],
         [flat(shared_params), shared_share, flat(shared_first), flat(shared_second)],
-        [flat(channel_params), channel_sum, flat(channel_first), flat(channel_second)],
-        [flat(head_params), head_sum, flat(head_first), flat(head_second)],
+        [channel_params, channel_sum.reshape(channel_params.shape), channel_first, channel_second],
+        [head_params, head_sum.reshape(head_params.shape), head_first, head_second],
     ]
     updated = last_update(
         jnp.stack([fix_one, fix_two]),

time: 726 us -> 690 us (0.950)
  Pallas kernels: 506 us -> 540 us
  local copies, waits for them, and re-layouts: 56.1 us -> 25.8 us
  waiting for transfers between devices: 52.4 us -> 24.5 us
    ppermute x13 -> x6, waiting for transfers between devices: 31.4 us -> 0.02 us  [swap(): return lax.ppermute(x, axis, [(i, i ^ offset) for i in range(size)])]
    pallas_call x3, Pallas kernels: 129 us -> 157 us  [forward_rows(): pl.pallas_call(functools.partial(forward_kernel, groups, shards, chunks,...]
    unnamed x237 -> x141, local copies, waits for them, and re-layouts: 39.7 us -> 13.4 us
    ppermute x13 -> x6, starting transfers between devices: 14.6 us -> 8.77 us  [swap(): return lax.ppermute(x, axis, [(i, i ^ offset) for i in range(size)])]
    pallas_call x16 -> x15, Pallas kernels: 130 us -> 131 us  [call(): pl.pallas_call(kernel, out_shape=out_shape, in_specs=specs, out_specs=jax...]
  transfers between devices with their start and end apart: 29 -> 22, of which waited for: 13 -> 5; matrix products, arithmetic and copies ran while one was open for 6% -> 6% of each run, Pallas kernels for 59% -> 67%
where the time goes in v5:
time: 690 us; the launch traced here: 685 us
  Pallas kernels  540 us (78%)
  other arithmetic  31.5 us (5%)
  starting transfers between devices  30.7 us (4%)
  local copies, waits for them, and re-layouts  25.8 us (4%)
  waiting for transfers between devices  24.5 us (4%)
  matrix products  16.6 us (2%)
  between operations  16 us (2%)
    pallas_call x3, Pallas kernels, forward_rows(): pl.pallas_call(functools.partial(forward_kernel, groups, shards, chunks,...  157 us
    pallas_call x15, Pallas kernels, call(): pl.pallas_call(kernel, out_shape=out_shape, in_specs=specs, out_specs=jax...  131 us
    pallas_call x2, Pallas kernels, backward_rows(): pl.pallas_call(functools.partial(backward_kernel, groups, shards, chunks,...  74.3 us
    pallas_call x1, Pallas kernels, finish_rows(): pl.pallas_call(functools.partial(finish_kernel, groups, shards, chunks, o...  74.1 us
    pallas_call x1, Pallas kernels, vocab_logits(): pl.pallas_call(functools.partial(logits_kernel, vrows), grid=(steps,), ou...  24.9 us
    ppermute x12, starting transfers between devices, hop(): return lax.ppermute(x, 'dp', pairs)  21.6 us
    pallas_call x1, Pallas kernels, vocab_table_grad(): pl.pallas_call(table_kernel, grid=(padded // PAIRS,), out_shape=sds((padd...  20.7 us
    pallas_call x1, Pallas kernels, vocab_rows(): pl.pallas_call(functools.partial(rows_kernel, shards, own), grid=(padded...  20 us
  transfers between devices with their start and end apart: 22, of which 5 were waited for; matrix products, arithmetic and copies ran while one was open for 6% of the time, Pallas kernels for 67%

profile of v5, /device:TPU:0, one launch (start us, length us, event | category | flops | bytes accessed | tf_op | source)
XLA Modules:
  0.0 685.5 jit_solution(7380629057964921993)
XLA Ops:
  10.5 12.7 %open.1 = (s32[8,8,256]{2,1,0:T(8,128)S(1)}, bf16[4,192,128]{2,1,0:T(8,128)(2,1)S(1)}, bf16[8,4,16,128]{3,2,1,0:T(8,128)(2,1)S(1)}) custom-call(s32[8,256]{1,0:T(8,128)S(1)} %pad.47.ids, bf16[192,128]{1,0:T(8,128)(2,1)S(1)} %reshape.346.piece, bf16[16,128]{1,0:T(8,128)(2,1)S(1)} %pad_bitcast_fusion.share), custom_call_target="tpu_custom_call" | custom-call | tf_op jit(solution)/shard_map/open/pallas_call | solution.py:998
  28.2 11.3 %look.1 = (bf16[512,256]{1,0:T(8,128)(2,1)}, bf16[512,256]{1,0:T(8,128)(2,1)}, bf16[512,256]{1,0:T(8,128)(2,1)}, bf16[512,256]{1,0:T(8,128)(2,1)}, bf16[512,256]...) custom-call(s32[2]{0:T(128)} %pad_add_fusion.1.scal, ...), custom_call_target="tpu_custom_call" | custom-call | bytes 31457280 | tf_op jit(solution)/shard_map/look/pallas_call | solution.py:138
  40.0 69.1 %enter.1 = (f32[128,1024]{1,0:T(8,128)}, bf16[528,1024]{1,0:T(8,128)(2,1)}) custom-call(bf16[512,256]{1,0:T(8,128)(2,1)} %get-tuple-element.167.refs_0_, bf16[512,256]{1,0:T(8,128)(2,1)} %get-tuple-element.168.refs_1_, bf16[512,256]{1,0:T(8,128)(2,1)} %get-tuple-element.169.refs_2_, bf16[512,256]{1,0:T(8,128)(2,1)} %get-tuple-element.170.refs_3_, ...), custom_call_target="tpu_custom_call" | custom-call | tf_op jit(solution)/shard_map/enter/pallas_call | solution.py:665
  113.8 9.7 %placetiles.1 = (bf16[1024,1024]{1,0:T(8,128)(2,1)}, bf16[512,1024]{1,0:T(8,128)(2,1)}, bf16[1024,1024]{1,0:T(8,128)(2,1)}, bf16[512,1024]{1,0:T(8,128)(2,1)}) custom-call(s32[1,192]{1,0:T(1,128)} %slot.3, bf16[8,3840,128]{2,1,0:T(8,128)(2,1)} %bitcast.142), custom_call_target="tpu_custom_call" | custom-call | bytes 14680064 | tf_op jit(solution)/shard_map/placetiles/pallas_call | solution.py:138
  126.0 7.8 %front.2 = (f32[528,1024]{1,0:T(8,128)}, f32[528,384]{1,0:T(8,128)}, f32[512,512]{1,0:T(8,128)}, bf16[144,512]{1,0:T(8,128)(2,1)}, bf16[512,128]{1,0:T(8,128)(2,1)}, /*index=5*/f32[512,128]{1,0:T(8,128)}) custom-call(bf16[528,1024]{1,0:T(8,128)(2,1)} %get-tuple-element.180.normed.rest_19_, bf16[1024,1024]{1,0:T(8,128)(2,1)} %get-tuple-element.182.wzx.rest_14_, ...), custom_call_target="tpu_custom_call" | custom-call | flops 2147483648 | bytes 12582912 | tf_op jit(solution)/shard_map/front/pallas_call | solution.py:138
  154.9 45.1 %forward.2 = (f32[128,1024]{1,0:T(8,128)}, f32[128,1024]{1,0:T(8,128)}, f32[128,1]{1,0:T(8,128)}, bf16[528,1024]{1,0:T(8,128)(2,1)}) custom-call(bf16[128,1152]{1,0:T(8,128)(2,1)} %get-tuple-element.189.refs_0_, bf16[128,1152]{1,0:T(8,128)(2,1)} %get-tuple-element.190.refs_1_, bf16[128,1152]{1,0:T(8,128)(2,1)} %get-tuple-element.191.refs_2_, ...), custom_call_target="tpu_custom_call" | custom-call | tf_op jit(solution)/shard_map/forward/pallas_call | solution.py:665
  200.1 7.8 %front.3 = (f32[528,1024]{1,0:T(8,128)}, f32[528,384]{1,0:T(8,128)}, f32[512,512]{1,0:T(8,128)}, bf16[144,512]{1,0:T(8,128)(2,1)}, bf16[512,128]{1,0:T(8,128)(2,1)}, /*index=5*/f32[512,128]{1,0:T(8,128)}) custom-call(bf16[528,1024]{1,0:T(8,128)(2,1)} %get-tuple-element.194.normed.rest_19_, bf16[1024,1024]{1,0:T(8,128)(2,1)} %get-tuple-element.195.wzx.rest_14_, ...), custom_call_target="tpu_custom_call" | custom-call | flops 2147483648 | bytes 12582912 | tf_op jit(solution)/shard_map/front/pallas_call | solution.py:138
  209.1 7.2 %collective-permute-start.4 = (bf16[144,512]{1,0:T(8,128)(2,1)}, bf16[144,512]{1,0:T(8,128)(2,1)S(1)}, u32[]{:S(2)}, u32[]{:S(2)}) collective-permute-start(bf16[144,512]{1,0:T(8,128)(2,1)} %get-tuple-element.196), channel_id=1, source_target_pairs={{0,8},{4,12},{16,24},{20,28},{1,9},{5,13},{17,25},{21,29},{2,10},{... | collective-permute-start | bytes 442376 | tf_op jit(solution)/shard_map/ppermute | solution.py:1888
  235.0 42.4 %forward.3 = (f32[128,1024]{1,0:T(8,128)}, f32[128,1024]{1,0:T(8,128)}, f32[128,1]{1,0:T(8,128)}, bf16[528,1024]{1,0:T(8,128)(2,1)}) custom-call(bf16[128,1152]{1,0:T(8,128)(2,1)} %get-tuple-element.202.refs_0_, bf16[128,1152]{1,0:T(8,128)(2,1)} %get-tuple-element.203.refs_1_, bf16[128,1152]{1,0:T(8,128)(2,1)} %get-tuple-element.204.refs_2_, ...), custom_call_target="tpu_custom_call" | custom-call | tf_op jit(solution)/shard_map/forward/pallas_call | solution.py:665
  277.4 24.9 %logits.1 = (bf16[2,6400,512]{2,1,0:T(8,128)(2,1)}, f32[5,64,512]{2,1,0:T(8,128)}, f32[8,512]{1,0:T(8,128)}) custom-call(s32[1,512]{1,0:T(1,128)} %bitcast.175, bf16[6400,2048]{1,0:T(8,128)(2,1)} %all-gather.4.cloned.1.call-done.table, bf16[528,1024]{1,0:T(8,128)(2,1)} %get-tuple-element.207.normed), custom_call_target="tpu_custom_call" | custom-call | flops 13421772800 | bytes 41943040 | tf_op jit(solution)/shard_map/logits/pallas_call | solution.py:1524
  311.1 20.0 %rowgrads.1 = (bf16[128,1024]{1,0:T(8,128)(2,1)}, bf16[128,1024]{1,0:T(8,128)(2,1)}, bf16[128,1024]{1,0:T(8,128)(2,1)}, bf16[128,1024]{1,0:T(8,128)(2,1)}) custom-call(s32[1]{0:T(128)} %bitcast.4.scal, s32[1,512]{1,0:T(1,128)} %bitcast.176, f32[5,64,512]{2,1,0:T(8,128)} %copy-done.14, f32[1,512]{1,0:T(1,128)} %copy-done.8, ...), custom_call_target="tpu_custom_call" | custom-call | flops 13421772800 | bytes 41943040 | tf_op jit(solution)/shard_map/rowgrads/pallas_call | solution.py:1601
  335.5 20.7 %tablegrads.1 = bf16[6400,2048]{1,0:T(8,128)(2,1)} custom-call(s32[1,512]{1,0:T(1,128)} %bitcast.177, f32[5,64,512]{2,1,0:T(8,128)} %copy-done.14, f32[1,512]{1,0:T(1,128)} %copy-done.8, bf16[2,6400,512]{2,1,0:T(8,128)(2,1)} %get-tuple-element.212.p_in, bf16[528,1024]{1,0:T(8,128)(2,1)} %get-tuple-element.207.normed), custom_call_target="tpu_custom_call" | custom-call | flops 13421772800 | bytes 41943040 | tf_op jit(solution)/shard_map/tablegrads/pallas_call | solution.py:1634
  357.1 24.9 %backward.2 = (f32[128,1024]{1,0:T(8,128)}, bf16[512,1152]{1,0:T(8,128)(2,1)}, f32[1,1024]{1,0:T(1,128)}) custom-call(bf16[128,1024]{1,0:T(8,128)(2,1)} %get-tuple-element.217.refs_0_, bf16[128,1024]{1,0:T(8,128)(2,1)} %copy-done.20, bf16[128,1024]{1,0:T(8,128)(2,1)} %copy-done.21, bf16[128,1024]{1,0:T(8,128)(2,1)} %copy-done.22, ...), custom_call_target="tpu_custom_call" | custom-call | tf_op jit(solution)/shard_map/backward/pallas_call | solution.py:765
  396.1 7.5 %within.2 = (f32[512,512]{1,0:T(8,128)}, bf16[512,256]{1,0:T(8,128)(2,1)}, f32[512,128]{1,0:T(8,128)}, f32[2,128,512]{2,1,0:T(8,128)}, f32[512,512]{1,0:T(8,128)}, /*index=5*/f32[512,256]{1,0:T(8,128)}) custom-call(f32[128,512]{1,0:T(8,128)} %get-tuple-element.227.s_in, f32[528,1024]{1,0:T(8,128)} %get-tuple-element.198.rest_4_.zx.rest_9_, ...), custom_call_target="tpu_custom_call" | custom-call | flops 2147483648 | bytes 16777216 | tf_op jit(solution)/shard_map/within/pallas_call | solution.py:138
  404.4 14.4 %back.2 = (bf16[528,1024]{1,0:T(8,128)(2,1)}, bf16[528,384]{1,0:T(8,128)(2,1)}, f32[8,512]{1,0:T(8,128)}, f32[8,256]{1,0:T(8,128)}, f32[8,128]{1,0:T(8,128)}, /*...) custom-call(s32[1]{0:T(128)} %bitcast.4.scal, ...), custom_call_target="tpu_custom_call" | custom-call | flops 2147483648 | bytes 16777216 | tf_op jit(solution)/shard_map/back/pallas_call | solution.py:138
  418.8 49.4 %backward.3 = (f32[128,1024]{1,0:T(8,128)}, bf16[512,1152]{1,0:T(8,128)(2,1)}) custom-call(bf16[128,1024]{1,0:T(8,128)(2,1)} %get-tuple-element.237.refs_0_, bf16[128,1024]{1,0:T(8,128)(2,1)} %get-tuple-element.238.refs_1_, bf16[128,1024]{1,0:T(8,128)(2,1)} %get-tuple-element.239.refs_2_, bf16[128,1024]{1,0:T(8,128)(2,1)} %get-tuple-element.240.refs_3_, ...), custom_call_target="tpu_custom_call" | custom-call | tf_op jit(solution)/shard_map/backward/pallas_call | solution.py:765
  477.7 8.6 %within.3 = (f32[512,512]{1,0:T(8,128)}, bf16[512,256]{1,0:T(8,128)(2,1)}, f32[512,128]{1,0:T(8,128)}, f32[2,128,512]{2,1,0:T(8,128)}, f32[512,512]{1,0:T(8,128)}, /*index=5*/f32[512,256]{1,0:T(8,128)}) custom-call(f32[128,512]{1,0:T(8,128)} %get-tuple-element.248.s_in, f32[528,1024]{1,0:T(8,128)} %get-tuple-element.185.rest_4_.zx.rest_9_, ...), custom_call_target="tpu_custom_call" | custom-call | flops 2147483648 | bytes 16777216 | tf_op jit(solution)/shard_map/within/pallas_call | solution.py:138
  494.3 14.2 %back.3 = (bf16[528,1024]{1,0:T(8,128)(2,1)}, bf16[528,384]{1,0:T(8,128)(2,1)}, f32[8,512]{1,0:T(8,128)}, f32[8,256]{1,0:T(8,128)}, f32[8,128]{1,0:T(8,128)}, /*...) custom-call(s32[1]{0:T(128)} %bitcast.4.scal, ...), custom_call_target="tpu_custom_call" | custom-call | flops 2147483648 | bytes 16777216 | tf_op jit(solution)/shard_map/back/pallas_call | solution.py:138
  520.4 9.6 %packtiles.1 = bf16[8,3968,128]{2,1,0:T(8,128)(2,1)} custom-call(s32[1]{0:T(128)} %bitcast.4.scal, s32[1,192]{1,0:T(1,128)} %slot.3, bf16[1024,1024]{1,0:T(8,128)(2,1)} %convolution_convert_fusion.3.refs_0_, bf16[512,1152]{1,0:T(8,128)(2,1)} %convolution_convert_fusion.1.refs_1_, bf16[1024,1024]{1,0:T(8,128)(2,1)} %convolution_convert_fusion.2.refs_2_, ...), custom_call_target="tpu_custom_call" | custom-call | bytes 14680064 | tf_op jit(solution)/shard_map/packtiles/pallas_call | solution.py:138
  531.0 74.1 %finish.1.parts = bf16[8,512,256]{2,1,0:T(8,128)(2,1)} custom-call(bf16[128,1024]{1,0:T(8,128)(2,1)} %get-tuple-element.283.refs_0_, bf16[128,1024]{1,0:T(8,128)(2,1)} %get-tuple-element.284.refs_1_, bf16[128,1024]{1,0:T(8,128)(2,1)} %get-tuple-element.285.refs_2_, bf16[128,1024]{1,0:T(8,128)(2,1)} %get-tuple-element.286.refs_3_, ...), custom_call_target="tpu_custom_call" | custom-call | tf_op jit(solution)/shard_map/finish/pallas_call | solution.py:947
  605.2 11.1 %addrows.1 = (bf16[6286,256]{1,0:T(8,128)(2,1)}, f32[1,256]{1,0:T(1,128)}) custom-call(s32[2]{0:T(128)} %pad_add_fusion.1.scal, s32[4104]{0:T(1024)} %concatenate.41.code, s32[4096]{0:T(1024)} %select_bitcast_fusion.listed, s32[32]{0:T(128)} %copy-done.39, bf16[6400,256]{1,0:T(8,128)(2,1)} %reduce-scatter.3.cloned.1.call-done.share, ...), custom_call_target="tpu_custom_call" | custom-call | bytes 31457280 | tf_op jit(solution)/shard_map/addrows/pallas_call | solution.py:138
  637.9 9.9 %sumall.1.sums = f32[8,128]{1,0:T(8,128)S(1)} custom-call(f32[8,128]{1,0:T(8,128)S(1)} %get-tuple-element.210.refs_0_, f32[12,512]{1,0:T(8,128)S(1)} %reshape.364.refs_1_, f32[6,8]{1,0:T(8,128)S(1)} %reshape_squeeze.3.refs_2_, f32[1,256]{1,0:T(1,128)S(1)} %copy-done.12, f32[1,128]{1,0:T(1,128)S(1)} %copy-done.13, f32[64,288]{1,0:T(8,128)S(1)} %bitcast.128, ...), custom_call_target="tpu_custom_call" | custom-call | tf_op jit(solution)/shard_map/sumall/pallas_call | solution.py:1076
  650.4 10.3 %update.1 = (f32[24,128,128]{2,1,0:T(8,128)}, bf16[24,128,128]{2,1,0:T(8,128)(2,1)}, f32[24,128,128]{2,1,0:T(8,128)}, f32[24,128,128]{2,1,0:T(8,128)}, f32[64,28...) custom-call(f32[2]{0:T(128)S(1)} %pad_maximum_fusion.3.fixes, ...), custom_call_target="tpu_custom_call" | custom-call | flops 1207959552 | bytes 16777216 | tf_op jit(solution)/shard_map/update/pallas_call | solution.py:1731
  664.3 14.4 %multiply_subtract_fusion = (f32[6286,256]{1,0:T(8,128)}, f32[6286,256]{1,0:T(8,128)}, f32[6286,256]{1,0:T(8,128)}) fusion(f32[6286,256]{1,0:T(8,128)} %table.1, f32[]{:T(128)} %bitcast.42, f32[]{:T(128)} %bitcast.41, f32[]{:T(128)} %bitcast.40, bf16[6286,256]{1,0:T(8,128)(2,1)S(1)} %copy-done.15, f32[6286,256]{1,0:T(8,128)} %param.33, f32[6286,256]{1,0:T(8,128)} %param.32), kind=kLoop, calls=%fused_computation.2 | loop fusion | flops 27356672 | bytes 41839628 | tf_op jit(solution)/shard_map/sub | solution.py:1656
  (298 shorter events, 142.4 us)
Async XLA Ops:
  7.2 105.0 %all-gather.6.cloned.1.call-start = ((), (), s32[]{:S(2)}) async-start(), calls=%async_computation.5 | async-start | bytes 8847360 | tf_op jit(solution)/shard_map/all_gather | solution.py:1836
  24.2 253.2 %all-gather.4.cloned.1.call-start = ((), (), s32[]{:S(2)}) async-start(), calls=%async_computation.2 | async-start | bytes 29491200 | tf_op jit(solution)/shard_map/all_gather | solution.py:1859
  109.2 420.8 %reduce-scatter.3.cloned.1.call-start = ((), (), s32[]{:S(2)}) async-start(), calls=%async_computation.3 | async-start | bytes 29491200 | tf_op jit(solution)/shard_map/reduce_scatter | solution.py:1928
  133.8 7.3 %collective-permute-start = (bf16[144,512]{1,0:T(8,128)(2,1)}, bf16[144,512]{1,0:T(8,128)(2,1)S(1)}, u32[]{:S(2)}, u32[]{:S(2)}) collective-permute-start(bf16[144,512]{1,0:T(8,128)(2,1)} %get-tuple-element.183), channel_id=1, source_target_pairs={{0,4},{4,8},{8,12},{16,20},{20,24},{24,28},{1,5},{5,9},{9,13},{17,... | collective-permute-start | bytes 442376 | tf_op jit(solution)/shard_map/ppermute | solution.py:1888
  135.1 8.9 %collective-permute-start.1 = (bf16[144,512]{1,0:T(8,128)(2,1)}, bf16[144,512]{1,0:T(8,128)(2,1)S(1)}, u32[]{:S(2)}, u32[]{:S(2)}) collective-permute-start(bf16[144,512]{1,0:T(8,128)(2,1)} %get-tuple-element.183), channel_id=1, source_target_pairs={{0,8},{4,12},{16,24},{20,28},{1,9},{5,13},{17,25},{21,29},{2,10},{... | collective-permute-start | bytes 442376 | tf_op jit(solution)/shard_map/ppermute | solution.py:1888
  136.4 13.0 %collective-permute-start.2 = (bf16[144,512]{1,0:T(8,128)(2,1)}, bf16[144,512]{1,0:T(8,128)(2,1)S(1)}, u32[]{:S(2)}, u32[]{:S(2)}) collective-permute-start(bf16[144,512]{1,0:T(8,128)(2,1)} %get-tuple-element.183), channel_id=1, source_target_pairs={{0,12},{16,28},{1,13},{17,29},{2,14},{18,30},{3,15},{19,31}} | collective-permute-start | bytes 442376 | tf_op jit(solution)/shard_map/ppermute | solution.py:1888
  207.8 11.8 %collective-permute-start.3 = (bf16[144,512]{1,0:T(8,128)(2,1)}, bf16[144,512]{1,0:T(8,128)(2,1)S(1)}, u32[]{:S(2)}, u32[]{:S(2)}) collective-permute-start(bf16[144,512]{1,0:T(8,128)(2,1)} %get-tuple-element.196), channel_id=1, source_target_pairs={{0,4},{4,8},{8,12},{16,20},{20,24},{24,28},{1,5},{5,9},{9,13},{17,... | collective-permute-start | bytes 442376 | tf_op jit(solution)/shard_map/ppermute | solution.py:1888
  209.1 14.9 %collective-permute-start.4 = (bf16[144,512]{1,0:T(8,128)(2,1)}, bf16[144,512]{1,0:T(8,128)(2,1)S(1)}, u32[]{:S(2)}, u32[]{:S(2)}) collective-permute-start(bf16[144,512]{1,0:T(8,128)(2,1)} %get-tuple-element.196), channel_id=1, source_target_pairs={{0,8},{4,12},{16,24},{20,28},{1,9},{5,13},{17,25},{21,29},{2,10},{... | collective-permute-start | bytes 442376 | tf_op jit(solution)/shard_map/ppermute | solution.py:1888
  216.4 13.1 %collective-permute-start.5 = (bf16[144,512]{1,0:T(8,128)(2,1)}, bf16[144,512]{1,0:T(8,128)(2,1)S(1)}, u32[]{:S(2)}, u32[]{:S(2)}) collective-permute-start(bf16[144,512]{1,0:T(8,128)(2,1)} %get-tuple-element.196), channel_id=1, source_target_pairs={{0,12},{16,28},{1,13},{17,29},{2,14},{18,30},{3,15},{19,31}} | collective-permute-start | bytes 442376 | tf_op jit(solution)/shard_map/ppermute | solution.py:1888
  219.0 83.4 %copy-start.8 = (f32[1,512]{1,0:T(1,128)}, f32[1,512]{1,0:T(1,128)S(1)}, u32[]{:S(2)}) copy-start(f32[1,512]{1,0:T(1,128)S(1)} %compare_select_fusion.2.weight) | copy-start | bytes 6148
  331.1 25.1 %collective-permute-start.6 = (bf16[128,1024]{1,0:T(8,128)(2,1)}, bf16[128,1024]{1,0:T(8,128)(2,1)S(1)}, u32[]{:S(2)}, u32[]{:S(2)}) collective-permute-start(bf16[128,1024]{1,0:T(8,128)(2,1)} %get-tuple-element.214), channel_id=1, source_target_pairs={{0,1},{1,0},{2,3},{3,2},{4,5},{5,4},{6,7},{7,6},{8,9},{9,8},{10,11... | collective-permute-start | bytes 786440 | tf_op jit(solution)/shard_map/ppermute | solution.py:69
  331.5 24.7 %collective-permute-start.7 = (bf16[128,1024]{1,0:T(8,128)(2,1)}, bf16[128,1024]{1,0:T(8,128)(2,1)S(1)}, u32[]{:S(2)}, u32[]{:S(2)}) collective-permute-start(bf16[128,1024]{1,0:T(8,128)(2,1)} %get-tuple-element.215), channel_id=1, source_target_pairs={{0,2},{1,3},{2,0},{3,1},{4,6},{5,7},{6,4},{7,5},{8,10},{9,11},{10,... | collective-permute-start | bytes 786440 | tf_op jit(solution)/shard_map/ppermute | solution.py:69
  333.9 22.4 %collective-permute-start.8 = (bf16[128,1024]{1,0:T(8,128)(2,1)}, bf16[128,1024]{1,0:T(8,128)(2,1)S(1)}, u32[]{:S(2)}, u32[]{:S(2)}) collective-permute-start(bf16[128,1024]{1,0:T(8,128)(2,1)} %get-tuple-element.216), channel_id=1, source_target_pairs={{0,3},{1,2},{2,1},{3,0},{4,7},{5,6},{6,5},{7,4},{8,11},{9,10},{10,... | collective-permute-start | bytes 786440 | tf_op jit(solution)/shard_map/ppermute | solution.py:69
  357.1 265.5 %reduce-scatter.5.cloned.1.call-start = ((), (), s32[]{:S(2)}) async-start(), calls=%async_computation.4 | async-start | bytes 9142272 | tf_op jit(solution)/shard_map/reduce_scatter | solution.py:2007
  389.1 14.6 %collective-permute-start.9 = (bf16[144,512]{1,0:T(8,128)(2,1)}, bf16[144,512]{1,0:T(8,128)(2,1)S(1)}, u32[]{:S(2)}, u32[]{:S(2)}) collective-permute-start(bf16[144,512]{1,0:T(8,128)(2,1)} %get-tuple-element.226), channel_id=1, source_target_pairs={{4,0},{8,4},{12,8},{20,16},{24,20},{28,24},{5,1},{9,5},{13,9},{21,... | collective-permute-start | bytes 442376 | tf_op jit(solution)/shard_map/ppermute | solution.py:1888
  390.4 13.3 %collective-permute-start.10 = (bf16[144,512]{1,0:T(8,128)(2,1)}, bf16[144,512]{1,0:T(8,128)(2,1)S(1)}, u32[]{:S(2)}, u32[]{:S(2)}) collective-permute-start(bf16[144,512]{1,0:T(8,128)(2,1)} %get-tuple-element.226), channel_id=1, source_target_pairs={{8,0},{12,4},{24,16},{28,20},{9,1},{13,5},{25,17},{29,21},{10,2},{... | collective-permute-start | bytes 442376 | tf_op jit(solution)/shard_map/ppermute | solution.py:1888
  391.7 12.0 %collective-permute-start.11 = (bf16[144,512]{1,0:T(8,128)(2,1)}, bf16[144,512]{1,0:T(8,128)(2,1)S(1)}, u32[]{:S(2)}, u32[]{:S(2)}) collective-permute-start(bf16[144,512]{1,0:T(8,128)(2,1)} %get-tuple-element.226), channel_id=1, source_target_pairs={{12,0},{28,16},{13,1},{29,17},{14,2},{30,18},{15,3},{31,19}} | collective-permute-start | bytes 442376 | tf_op jit(solution)/shard_map/ppermute | solution.py:1888
  473.7 19.9 %collective-permute-start.12 = (bf16[144,512]{1,0:T(8,128)(2,1)}, bf16[144,512]{1,0:T(8,128)(2,1)S(1)}, u32[]{:S(2)}, u32[]{:S(2)}) collective-permute-start(bf16[144,512]{1,0:T(8,128)(2,1)} %get-tuple-element.247), channel_id=1, source_target_pairs={{4,0},{8,4},{12,8},{20,16},{24,20},{28,24},{5,1},{9,5},{13,9},{21,... | collective-permute-start | bytes 442376 | tf_op jit(solution)/shard_map/ppermute | solution.py:1888
  475.0 18.6 %collective-permute-start.13 = (bf16[144,512]{1,0:T(8,128)(2,1)}, bf16[144,512]{1,0:T(8,128)(2,1)S(1)}, u32[]{:S(2)}, u32[]{:S(2)}) collective-permute-start(bf16[144,512]{1,0:T(8,128)(2,1)} %get-tuple-element.247), channel_id=1, source_target_pairs={{8,0},{12,4},{24,16},{28,20},{9,1},{13,5},{25,17},{29,21},{10,2},{... | collective-permute-start | bytes 442376 | tf_op jit(solution)/shard_map/ppermute | solution.py:1888
  476.3 17.3 %collective-permute-start.14 = (bf16[144,512]{1,0:T(8,128)(2,1)}, bf16[144,512]{1,0:T(8,128)(2,1)S(1)}, u32[]{:S(2)}, u32[]{:S(2)}) collective-permute-start(bf16[144,512]{1,0:T(8,128)(2,1)} %get-tuple-element.247), channel_id=1, source_target_pairs={{12,0},{28,16},{13,1},{29,17},{14,2},{30,18},{15,3},{31,19}} | collective-permute-start | bytes 442376 | tf_op jit(solution)/shard_map/ppermute | solution.py:1888
  494.3 19.8 %copy-start.18 = (bf16[528,1024]{1,0:T(8,128)(2,1)S(1)}, bf16[528,1024]{1,0:T(8,128)(2,1)}, u32[]{:S(2)}) copy-start(bf16[528,1024]{1,0:T(8,128)(2,1)} %get-tuple-element.180.normed.rest_19_) | copy-start | bytes 3244036
  625.0 11.2 %collective-permute-start.17 = (bf16[208,128]{1,0:T(8,128)(2,1)}, bf16[208,128]{1,0:T(8,128)(2,1)}, u32[]{:S(2)}, u32[]{:S(2)}) collective-permute-start(bf16[208,128]{1,0:T(8,128)(2,1)} %get-tuple-element.403), channel_id=1, source_target_pairs={{0,3},{1,2},{2,1},{3,0},{4,7},{5,6},{6,5},{7,4},{8,11},{9,10},{10,... | collective-permute-start | bytes 159752 | tf_op jit(solution)/shard_map/ppermute | solution.py:69
  628.3 7.9 %collective-permute-start.16 = (bf16[208,128]{1,0:T(8,128)(2,1)}, bf16[208,128]{1,0:T(8,128)(2,1)}, u32[]{:S(2)}, u32[]{:S(2)}) collective-permute-start(bf16[208,128]{1,0:T(8,128)(2,1)} %get-tuple-element.402), channel_id=1, source_target_pairs={{0,2},{1,3},{2,0},{3,1},{4,6},{5,7},{6,4},{7,5},{8,10},{9,11},{10,... | collective-permute-start | bytes 159752 | tf_op jit(solution)/shard_map/ppermute | solution.py:69
  628.3 7.9 %collective-permute-start.15 = (bf16[208,128]{1,0:T(8,128)(2,1)}, bf16[208,128]{1,0:T(8,128)(2,1)}, u32[]{:S(2)}, u32[]{:S(2)}) collective-permute-start(bf16[208,128]{1,0:T(8,128)(2,1)} %get-tuple-element.401), channel_id=1, source_target_pairs={{0,1},{1,0},{2,3},{3,2},{4,5},{5,4},{6,7},{7,6},{8,9},{9,8},{10,11... | collective-permute-start | bytes 159752 | tf_op jit(solution)/shard_map/ppermute | solution.py:69
  (55 other events, 328.0 us)
Sparse Core Ops, SparseCore 0:
  24.3 66.2 all-gather.5
  109.3 138.4 all-gather.3
  356.4 167.1 reduce-scatter.2
  530.2 92.3 reduce-scatter.4

commit v6 on v5

--- a/solution.py
+++ b/solution.py
@@ -246,29 +246,29 @@
     )
 
 
-def tiles_kernel(slots_each, zx_count, per_layer, layers, slot, tiles, *outs):
-    for layer in range(layers):
+def tiles_kernel(slots_each, zx_count, per_layer, first_layer, slot, tiles, *outs):
+    for layer in (first_layer,):
         for at in range(per_layer):
             where = slot[0, layer * per_layer + at]
             owner = where // slots_each
             first = pl.multiple_of((where % slots_each) * BLK, BLK)
             tile = tiles[owner, pl.ds(first, BLK), :]
             if at < zx_count:
-                wide = outs[2 * layer].shape[1] // BLK
+                wide = outs[0].shape[1] // BLK
                 row, col = at // wide, at % wide
-                out = outs[2 * layer]
+                out = outs[0]
             else:
                 wide = D // BLK
                 row, col = (at - zx_count) // wide, (at - zx_count) % wide
-                out = outs[2 * layer + 1]
+                out = outs[1]
             out[row * BLK : (row + 1) * BLK, col * BLK : (col + 1) * BLK] = tile
 
 
-def place_tiles(slot, tiles, slots_each, inner, zx_count, per_layer):
+def place_tiles(slot, tiles, slots_each, inner, zx_count, per_layer, layer):
     return call(
-        functools.partial(tiles_kernel, slots_each, zx_count, per_layer, L),
+        functools.partial(tiles_kernel, slots_each, zx_count, per_layer, layer),
         "placetiles",
-        [sds((D, 2 * inner), BF), sds((inner, D), BF)] * L,
+        [sds((D, 2 * inner), BF), sds((inner, D), BF)],
         (slot, tiles),
         smem=(0,),
         moved=14 * MIB,
@@ -824,7 +824,7 @@
             pltpu.SemaphoreType.DMA((2, shards)),
         ],
         compiler_params=pltpu.CompilerParams(
-            collective_id=9, has_side_effects=True, vmem_limit_bytes=8 * MIB
+            collective_id=9, has_side_effects=True, vmem_limit_bytes=60 * MIB
         ),
         name="stats",
     )(stats, tops, weight)
@@ -1010,7 +1010,7 @@
             pltpu.SemaphoreType.DMA((4, count)),
         ],
         compiler_params=pltpu.CompilerParams(
-            collective_id=2, has_side_effects=True, vmem_limit_bytes=8 * MIB
+            collective_id=2, has_side_effects=True, vmem_limit_bytes=60 * MIB
         ),
         name="open",
     )(ids, piece, share)
@@ -1087,7 +1087,7 @@
             pltpu.SemaphoreType.DMA((count,)),
         ],
         compiler_params=pltpu.CompilerParams(
-            collective_id=1, has_side_effects=True, vmem_limit_bytes=8 * MIB
+            collective_id=1, has_side_effects=True, vmem_limit_bytes=60 * MIB
         ),
         name="sumall",
     )(*args)
@@ -1101,12 +1101,13 @@
 
 
 def front_kernel(normed, wzx, wside, chan, bcp, head, *rest):
-    zx, side, yloc, final, c_out, cum_out, xs_scr = rest
+    z_out, xr, side, yloc, final, c_out, cum_out, xs_scr = rest
     rows = normed.shape[0] - RIM
     inner = chan.shape[1]
-    zx[...] = nn(normed[...], wzx[...])
+    z_out[...] = nn(normed[RIM:, :], wzx[:, :inner])
+    xr[...] = nn(normed[...], wzx[:, inner:])
     side[...] = nn(normed[...], wside[...])
-    pre = conv_sum(zx, chan, rows, pl.ds(inner, inner))
+    pre = conv_sum(xr, chan, rows, pl.ds(0, inner))
     xs_scr[...] = pre * sigmoid(pre)
     pre = conv_sum(side, bcp, rows, pl.ds(0, 2 * N))
     bc = (pre * sigmoid(pre)).astype(BF)
@@ -1162,7 +1163,8 @@
         front_kernel,
         "front",
         [
-            sds((rows + RIM, 2 * inner), F32),
+            sds((rows, inner), F32),
+            sds((rows + RIM, inner), F32),
             sds((rows + RIM, 2 * N + LANES), F32),
             sds((rows, inner), F32),
             sds((N + RIM, inner), BF),
@@ -1188,7 +1190,7 @@
 
 def middle_kernel(shards, own, hops, scal, *rest):
     states, rest = rest[:hops], rest[hops:]
-    yloc, zx, c_in, cum, wout, chan = rest[:6]
+    yloc, z_in, c_in, cum, wout, chan = rest[:6]
     y_out, s_out = rest[6:8]
     parts, work = rest[8 : 8 + shards], rest[-1]
     shard = scal[0]
@@ -1198,7 +1200,7 @@
     s_out[...] = state
     y = yloc[...] + widen(jnp.exp(cum[...]), expand) * nn(c_in[...], state.astype(BF))
     y_out[...] = y
-    z = zx[RIM:, :inner]
+    z = z_in[...]
     gated = y * (z * sigmoid(z))
     work[:, :D] = nn((gated * chan[5:6, :]).astype(BF), wout[...]).astype(BF)
     work[:, D:] = lanes3(jnp.sum(gated * gated, axis=1, keepdims=True))
@@ -1207,7 +1209,7 @@
         parts[off][...] = work[pl.ds(at, own), :]
 
 
-def mixer_middle(scal, states, yloc, zx, c_in, cum, wout, chan, shards):
+def mixer_middle(scal, states, yloc, z_in, c_in, cum, wout, chan, shards):
     rows, inner = yloc.shape
     own = rows // shards
     return call(
@@ -1215,7 +1217,7 @@
         "middle",
         [sds((rows, inner), F32), sds((N, inner), F32)]
         + [sds((own, D + LANES), BF)] * shards,
-        (scal, *states, yloc, zx, c_in, cum, wout, chan),
+        (scal, *states, yloc, z_in, c_in, cum, wout, chan),
         smem=(0,),
         scratch=[pltpu.VMEM((rows, D + LANES), BF)],
         flops=2 * rows * D * inner,
@@ -1223,12 +1225,12 @@
     )
 
 
-def gate_back_kernel(grads, wout, y_in, zx, c_in, cum, chan, *rest):
+def gate_back_kernel(grads, wout, y_in, z_in, c_in, cum, chan, *rest):
     u_out, dy_out, dz_out, state_out, gain_out = rest
     inner = chan.shape[1]
     du = nt_dot(grads[:, :D], wout[...])
     coef = column3(grads[:, D:].astype(F32))
-    z = zx[RIM:, :inner]
+    z = z_in[...]
     y = y_in[...]
     sig = sigmoid(z)
     silu = z * sig
@@ -1246,7 +1248,7 @@
     state_out[N:, :] = rows3(cum[rows - 1 : rows, :], inner)
 
 
-def gate_back(grads, wout, y, zx, c_in, cum, chan):
+def gate_back(grads, wout, y, z_in, c_in, cum, chan):
     rows, inner = y.shape
     return call(
         gate_back_kernel,
@@ -1258,7 +1260,7 @@
             sds((N + RIM, inner), BF),
             sds((1, inner), F32),
         ],
-        (grads, wout, y, zx, c_in, cum, chan),
+        (grads, wout, y, z_in, c_in, cum, chan),
         flops=2 * rows * D * inner,
         moved=10 * MIB,
     )
@@ -1284,11 +1286,11 @@
     return jnp.concatenate(grads, axis=0)
 
 
-def within_kernel(s_in, zx, side, dy_in, chan, bcp, head, *outs):
+def within_kernel(s_in, xr, side, dy_in, chan, bcp, head, *outs):
     xs_out, bc_out, cum_out, starts_out, dscaled_out, dbc_out = outs
     rows, inner = dy_in.shape
     expand = head_map(inner)
-    pre_x = conv_sum(zx, chan, rows, pl.ds(inner, inner))
+    pre_x = conv_sum(xr, chan, rows, pl.ds(0, inner))
     xs_out[...] = pre_x * sigmoid(pre_x)
     pre_bc = conv_sum(side, bcp, rows, pl.ds(0, 2 * N))
     bc = (pre_bc * sigmoid(pre_bc)).astype(BF)
@@ -1339,7 +1341,7 @@
         dbc_out[here, N:] = tn(dscores_low, keys) + nt_dot(dy_grown, start_low)
 
 
-def mixer_within(s_in, zx, side, dy, chan, bcp, head):
+def mixer_within(s_in, xr, side, dy, chan, bcp, head):
     rows, inner = dy.shape
     return call(
         within_kernel,
@@ -1352,7 +1354,7 @@
             sds((rows, inner), F32),
             sds((rows, 2 * N), F32),
         ],
-        (s_in, zx, side, dy, chan, bcp, head),
+        (s_in, xr, side, dy, chan, bcp, head),
         flops=8 * rows * D * inner,
         moved=16 * MIB,
     )
@@ -1361,7 +1363,7 @@
 def back_kernel(shards, own, hops, scal, *rest):
     states, rest = rest[:hops], rest[hops:]
     xs_in, bc_in, cum_in, starts, dscaled_in, dbc_in, rest = *rest[:6], rest[6:]
-    zx, side, dy_in, dz_in, y_in, wzx, wside, chan, bcp, head = rest[:10]
+    xr, side, dy_in, dz_in, y_in, wzx, wside, chan, bcp, head = rest[:10]
     normed, gain = rest[10:12]
     dzx, dside, chan_out, bcp_out, head_out, rim_out, gain_out = rest[12:19]
     parts, rest = rest[19 : 19 + shards], rest[19 + shards :]
@@ -1427,12 +1429,12 @@
             grown = widen(jnp.exp(cum), expand)
             dstate = tot_wide * dstate + tn(queries, (dy * grown).astype(BF))
     body = pl.ds(RIM, rows)
-    pre_x = conv_sum(zx, chan, rows, pl.ds(inner, inner))
+    pre_x = conv_sum(xr, chan, rows, pl.ds(0, inner))
     dsx[body, :] = dsx[body, :] * silu_slope(pre_x)
     pre_bc = conv_sum(side, bcp, rows, pl.ds(0, 2 * N))
     dsbc[body, :] = dsbc[body, :] * silu_slope(pre_bc)
     chan_out[...] = conv_back(
-        dsx, zx, chan, rows, pl.ds(inner, inner), inner, dzx, pl.ds(inner, inner)
+        dsx, xr, chan, rows, pl.ds(0, inner), inner, dzx, pl.ds(inner, inner)
     )
     bcp_out[...] = conv_back(dsbc, side, bcp, rows, pl.ds(0, 2 * N), 2 * N, dside, pl.ds(0, 2 * N))
     head_out[...] = jnp.concatenate([dbias, dgrow, dskip, jnp.zeros((5, LANES), F32)], axis=0)
@@ -1446,7 +1448,7 @@
 
 
 def mixer_back(
-    scal, states, inside, zx, side, dy, dz, y, wzx, wside, chan, bcp, head, normed, gain, shards
+    scal, states, inside, xr, side, dy, dz, y, wzx, wside, chan, bcp, head, normed, gain, shards
 ):
     rows, inner = dy.shape
     own = rows // shards
@@ -1464,7 +1466,7 @@
             sds((1, D), F32),
         ]
         + [sds((own, D), BF)] * shards,
-        (scal, *states, *inside, zx, side, dy, dz, y, wzx, wside, chan, bcp, head, normed, gain),
+        (scal, *states, *inside, xr, side, dy, dz, y, wzx, wside, chan, bcp, head, normed, gain),
         smem=(0,),
         scratch=[
             pltpu.VMEM((ext + RIM, inner), F32),
@@ -1656,30 +1658,48 @@
     return (weight_in - LEARN_RATE * (direction + decay_rate * weight_in), one_next, two_next)
 
 
-def turn_kernel(share, bases, turned, root):
-    count = bases.shape[0]
-    total = jnp.zeros((1, BLK), F32)
-
-    def turn(at, total):
-        grad = share[pl.ds(pl.multiple_of(at * BLK, BLK), BLK), :].astype(F32)
+def turn_kernel(share, bases, turned, root, total):
+    step = pl.program_id(0)
+
+    @pl.when(step == 0)
+    def _():
+        total[...] = jnp.zeros_like(total)
+
+    for at in range(bases.shape[0]):
+        grad = share[at * BLK : (at + 1) * BLK, :].astype(F32)
         half_turn = tn(bases[at, 0], grad, HIGHEST)
         turned[at] = nn(half_turn, bases[at, 1], HIGHEST)
-        return total + jnp.sum(grad * grad, axis=0, keepdims=True)
-
-    for at in range(count):
-        total = turn(at, total)
-    root[...] = jnp.sqrt(total)
+        total[...] += jnp.sum(grad * grad, axis=0, keepdims=True)
+
+    @pl.when(step == pl.num_programs(0) - 1)
+    def _():
+        root[...] = jnp.sqrt(total[...])
 
 
 def turn_tiles(share, bases):
     count = bases.shape[0]
-    return call(
+    each = 4 if count % 4 == 0 else 2
+    return pl.pallas_call(
         turn_kernel,
-        "turn",
-        [sds((count, BLK, BLK), F32), sds((1, BLK), F32)],
-        (share, bases),
-        moved=6 * MIB,
-    )
+        grid=(count // each,),
+        out_shape=[sds((count, BLK, BLK), F32), sds((1, BLK), F32)],
+        in_specs=[
+            pl.BlockSpec((each * BLK, LANES), lambda i: (i, 0)),
+            pl.BlockSpec((each, 2, BLK, BLK), lambda i: (i, 0, 0, 0)),
+        ],
+        out_specs=[
+            pl.BlockSpec((each, BLK, BLK), lambda i: (i, 0, 0)),
+            pl.BlockSpec((1, BLK), lambda i: (0, 0)),
+        ],
+        scratch_shapes=[pltpu.VMEM((1, BLK), F32)],
+        compiler_params=pltpu.CompilerParams(
+            dimension_semantics=("arbitrary",), vmem_limit_bytes=60 * MIB
+        ),
+        cost_estimate=pl.CostEstimate(
+            flops=24 * count * BLK * BLK * BLK, bytes_accessed=6 * MIB, transcendentals=0
+        ),
+        name="turn",
+    )(share, bases)
 
 
 def last_kernel(small, fixes, sums, *refs):
@@ -1742,7 +1762,7 @@
         out_specs=[tile_spec] * 4
         + [spec for which in range(len(little)) for spec in whole[4 * which : 4 * which + 3]],
         compiler_params=pltpu.CompilerParams(
-            dimension_semantics=("arbitrary",), vmem_limit_bytes=48 * MIB
+            dimension_semantics=("arbitrary",), vmem_limit_bytes=60 * MIB
         ),
         cost_estimate=pl.CostEstimate(
             flops=24 * count * BLK * BLK * BLK, bytes_accessed=16 * MIB, transcendentals=0
@@ -1849,7 +1869,6 @@
     )
     table_low, normed = lax.optimization_barrier((table_low, normed))
     gathered, normed = lax.optimization_barrier((gathered, normed))
-    placed = place_tiles(block_slot, gathered, own_tiles, inner, zx_count, per_layer)
     side_full = (
         gathered[:, own_tiles * BLK :]
         .reshape(nd, nt, L, side_rows, 2 * N + LANES)
@@ -1859,7 +1878,6 @@
     table_all = lax.all_gather(table_low, "dp", axis=1, tiled=True)
 
     def layer_mats(layer_index):
-        zx_part, out_part = placed[2 * layer_index], placed[2 * layer_index + 1]
         dt_part = lax.dynamic_slice_in_dim(
             side_full[layer_index], 2 * N + shard * heads, heads, 1
         )
@@ -1877,7 +1895,7 @@
         bcp = jnp.concatenate([taps, bias, jnp.zeros((3, 2 * N), F32)], axis=0)
         chan = jnp.pad(channel_params[layer_index], ((0, 2), (0, 0)))
         head = jnp.pad(head_params[layer_index], ((0, 5), (0, LANES - heads)))
-        return (zx_part, out_part, side_here, gain, bcp, chan, head)
+        return [None, None, side_here, gain, bcp, chan, head]
 
     def hop(x, distance):
         pairs = [
@@ -1895,11 +1913,16 @@
     final_gain = shared_full[L * stride :][None, :]
     gains = [mats[layer_index][3][None, :] for layer_index in range(L)] + [final_gain]
     saved = []
+    tiles_now = gathered
     for layer_index in range(L):
+        mats[layer_index][:2] = place_tiles(
+            block_slot, tiles_now, own_tiles, inner, zx_count, per_layer, layer_index
+        )
         wzx, wout, wside, gain, bcp, chan, head = mats[layer_index]
-        zx, side, yloc, final, c_out, cum = mixer_front(normed, wzx, wside, chan, bcp, head)
+        z, xr, side, yloc, final, c_out, cum = mixer_front(normed, wzx, wside, chan, bcp, head)
+        final, tiles_now = lax.optimization_barrier((final, tiles_now))
         states = [hop(final, k) for k in hops]
-        result = mixer_middle(scal_shard, states, yloc, zx, c_out, cum, wout, chan, nt)
+        result = mixer_middle(scal_shard, states, yloc, z, c_out, cum, wout, chan, nt)
         y, s_in = result[:2]
         below = normed
         before = residual
@@ -1907,7 +1930,7 @@
         residual, branch, factor, normed = forward_rows(
             result[2:], before, gains[layer_index + 1], nd, chunks, inside, 5 + layer_index
         )
-        saved.append((before, below, zx, side, c_out, cum, y, s_in, factor, branch))
+        saved.append((before, below, z, xr, side, c_out, cum, y, s_in, factor, branch))
 
     member = micro_batch[:, None] == jnp.arange(MB, dtype=jnp.int32)[None, :]
     batch_tokens = jnp.sum(jnp.where(member, seq_lengths[:, None], 0), axis=0).astype(F32)
@@ -1927,7 +1950,7 @@
     sent, table_grad = lax.optimization_barrier((sent, table_grad))
     table_share = lax.psum_scatter(table_grad, "dp", scatter_dimension=1, tiled=True)
     grad_res, payload, grad_final_gain = backward_rows(
-        sent, None, residual, final_gain, None, saved[L - 1][9], saved[L - 1][8], nd, chunks, 10
+        sent, None, residual, final_gain, None, saved[L - 1][10], saved[L - 1][9], nd, chunks, 10
     )
 
     block_pieces = [None] * (2 * L)
@@ -1937,16 +1960,16 @@
     shared_pieces = [None] * L
     for layer_index in reversed(range(L)):
         wzx, wout, wside, gain, bcp, chan, head = mats[layer_index]
-        residual_in, normed, zx, side, c_out, cum, y, s_in, factor, branch = saved[layer_index]
-        u_low, dy, dz, dstate, gain_grad = gate_back(payload, wout, y, zx, c_out, cum, chan)
+        residual_in, normed, z, xr, side, c_out, cum, y, s_in, factor, branch = saved[layer_index]
+        u_low, dy, dz, dstate, gain_grad = gate_back(payload, wout, y, z, c_out, cum, chan)
         states = [hop(dstate, -k) for k in hops]
         grad_out_w = tn(u_low, payload)
-        inside = mixer_within(s_in, zx, side, dy, chan, bcp, head)
+        inside = mixer_within(s_in, xr, side, dy, chan, bcp, head)
         result = mixer_back(
             scal_shard,
             states,
             inside,
-            zx,
+            xr,
             side,
             dy,
             dz,
@@ -2012,8 +2035,8 @@
                 residual_in,
                 gains[layer_index],
                 grad_res,
+                saved[layer_index - 1][10],
                 saved[layer_index - 1][9],
-                saved[layer_index - 1][8],
                 nd,
                 chunks,
                 10 + layer_index,

time: 690 us -> 701 us (1.016)
  local copies, waits for them, and re-layouts: 25.8 us -> 35.5 us
  waiting for transfers between devices: 24.5 us -> 16.2 us
    pallas_call x0 -> x1, Pallas kernels: none -> 7.62 us  [turn_tiles(): pl.pallas_call(turn_kernel, grid=(count // each,), out_shape=[sds((count,...]
    unnamed x141 -> x117, local copies, waits for them, and re-layouts: 13.4 us -> 16.7 us
  transfers between devices with their start and end apart: 22 -> 22, of which waited for: 5 -> 5; matrix products, arithmetic and copies ran while one was open for 6% -> 7% of each run, Pallas kernels for 67% -> 66%
where the time goes in v6:
time: 701 us; the launch traced here: 691 us
  Pallas kernels  544 us (78%)
  local copies, waits for them, and re-layouts  35.5 us (5%)
  other arithmetic  32.1 us (5%)
  starting transfers between devices  31.3 us (4%)
  matrix products  16.5 us (2%)
  waiting for transfers between devices  16.2 us (2%)
  between operations  15.7 us (2%)
    pallas_call x3, Pallas kernels, forward_rows(): pl.pallas_call(functools.partial(forward_kernel, groups, shards, chunks,...  156 us
    pallas_call x15, Pallas kernels, call(): pl.pallas_call(kernel, out_shape=out_shape, in_specs=specs, out_specs=jax...  125 us
    pallas_call x2, Pallas kernels, backward_rows(): pl.pallas_call(functools.partial(backward_kernel, groups, shards, chunks,...  74 us
    pallas_call x1, Pallas kernels, finish_rows(): pl.pallas_call(functools.partial(finish_kernel, groups, shards, chunks, o...  70.7 us
    pallas_call x1, Pallas kernels, vocab_logits(): pl.pallas_call(functools.partial(logits_kernel, vrows), grid=(steps,), ou...  24.9 us
    ppermute x12, starting transfers between devices, hop(): return lax.ppermute(x, 'dp', pairs)  22.4 us
    pallas_call x1, Pallas kernels, vocab_table_grad(): pl.pallas_call(table_kernel, grid=(padded // PAIRS,), out_shape=sds((padd...  20.7 us
    pallas_call x1, Pallas kernels, vocab_rows(): pl.pallas_call(functools.partial(rows_kernel, shards, own), grid=(padded...  20.1 us
  transfers between devices with their start and end apart: 22, of which 5 were waited for; matrix products, arithmetic and copies ran while one was open for 7% of the time, Pallas kernels for 66%

profile of v6, /device:TPU:0, one launch (start us, length us, event | category | flops | bytes accessed | tf_op | source)
XLA Modules:
  0.0 691.5 jit_solution(4996991024242945725)
XLA Ops:
  12.3 14.1 %open.1 = (s32[8,8,256]{2,1,0:T(8,128)}, bf16[4,192,128]{2,1,0:T(8,128)(2,1)}, bf16[8,4,16,128]{3,2,1,0:T(8,128)(2,1)}) custom-call(s32[8,256]{1,0:T(8,128)} %pad.47.ids, bf16[192,128]{1,0:T(8,128)(2,1)} %reshape.346.piece, bf16[16,128]{1,0:T(8,128)(2,1)} %pad_bitcast_fusion.share), custom_call_target="tpu_custom_call" | custom-call | tf_op jit(solution)/shard_map/open/pallas_call | solution.py:998
  32.4 11.1 %look.1 = (bf16[512,256]{1,0:T(8,128)(2,1)}, bf16[512,256]{1,0:T(8,128)(2,1)}, bf16[512,256]{1,0:T(8,128)(2,1)}, bf16[512,256]{1,0:T(8,128)(2,1)}, bf16[512,256]...) custom-call(s32[2]{0:T(128)} %pad_add_fusion.1.scal, ...), custom_call_target="tpu_custom_call" | custom-call | bytes 31457280 | tf_op jit(solution)/shard_map/look/pallas_call | solution.py:138
  44.1 69.8 %enter.1 = (f32[128,1024]{1,0:T(8,128)}, bf16[528,1024]{1,0:T(8,128)(2,1)}) custom-call(bf16[512,256]{1,0:T(8,128)(2,1)} %get-tuple-element.172.refs_0_, bf16[512,256]{1,0:T(8,128)(2,1)} %get-tuple-element.173.refs_1_, bf16[512,256]{1,0:T(8,128)(2,1)} %get-tuple-element.174.refs_2_, bf16[512,256]{1,0:T(8,128)(2,1)} %get-tuple-element.175.refs_3_, ...), custom_call_target="tpu_custom_call" | custom-call | tf_op jit(solution)/shard_map/enter/pallas_call | solution.py:665
  118.7 7.5 %placetiles.2 = (bf16[1024,1024]{1,0:T(8,128)(2,1)}, bf16[512,1024]{1,0:T(8,128)(2,1)}) custom-call(s32[1,192]{1,0:T(1,128)} %slot.5, bf16[8,3840,128]{2,1,0:T(8,128)(2,1)} %bitcast.127), custom_call_target="tpu_custom_call" | custom-call | bytes 14680064 | tf_op jit(solution)/shard_map/placetiles/pallas_call | solution.py:138
  128.6 8.1 %front.2 = (f32[512,512]{1,0:T(8,128)}, f32[528,512]{1,0:T(8,128)}, f32[528,384]{1,0:T(8,128)}, f32[512,512]{1,0:T(8,128)}, bf16[144,512]{1,0:T(8,128)(2,1)}, /*...) custom-call(bf16[528,1024]{1,0:T(8,128)(2,1)} %get-tuple-element.185.normed.rest_19_, ...), custom_call_target="tpu_custom_call" | custom-call | flops 2147483648 | bytes 12582912 | tf_op jit(solution)/shard_map/front/pallas_call | solution.py:138
  157.8 44.4 %forward.2 = (f32[128,1024]{1,0:T(8,128)}, f32[128,1024]{1,0:T(8,128)}, f32[128,1]{1,0:T(8,128)}, bf16[528,1024]{1,0:T(8,128)(2,1)}) custom-call(bf16[128,1152]{1,0:T(8,128)(2,1)} %get-tuple-element.195.refs_0_, bf16[128,1152]{1,0:T(8,128)(2,1)} %get-tuple-element.196.refs_1_, bf16[128,1152]{1,0:T(8,128)(2,1)} %get-tuple-element.197.refs_2_, ...), custom_call_target="tpu_custom_call" | custom-call | tf_op jit(solution)/shard_map/forward/pallas_call | solution.py:665
  202.2 8.0 %front.3 = (f32[512,512]{1,0:T(8,128)}, f32[528,512]{1,0:T(8,128)}, f32[528,384]{1,0:T(8,128)}, f32[512,512]{1,0:T(8,128)}, bf16[144,512]{1,0:T(8,128)(2,1)}, /*...) custom-call(bf16[528,1024]{1,0:T(8,128)(2,1)} %get-tuple-element.200.normed.rest_19_, ...), custom_call_target="tpu_custom_call" | custom-call | flops 2147483648 | bytes 12582912 | tf_op jit(solution)/shard_map/front/pallas_call | solution.py:138
  211.6 7.7 %collective-permute-start.4 = (bf16[144,512]{1,0:T(8,128)(2,1)}, bf16[144,512]{1,0:T(8,128)(2,1)S(1)}, u32[]{:S(2)}, u32[]{:S(2)}) collective-permute-start(bf16[144,512]{1,0:T(8,128)(2,1)} %get-tuple-element.204), channel_id=1, source_target_pairs={{0,8},{4,12},{16,24},{20,28},{1,9},{5,13},{17,25},{21,29},{2,10},{... | collective-permute-start | bytes 442376 | tf_op jit(solution)/shard_map/ppermute | solution.py:1906
  237.7 42.2 %forward.3 = (f32[128,1024]{1,0:T(8,128)}, f32[128,1024]{1,0:T(8,128)}, f32[128,1]{1,0:T(8,128)}, bf16[528,1024]{1,0:T(8,128)(2,1)}) custom-call(bf16[128,1152]{1,0:T(8,128)(2,1)} %get-tuple-element.210.refs_0_, bf16[128,1152]{1,0:T(8,128)(2,1)} %get-tuple-element.211.refs_1_, bf16[128,1152]{1,0:T(8,128)(2,1)} %get-tuple-element.212.refs_2_, ...), custom_call_target="tpu_custom_call" | custom-call | tf_op jit(solution)/shard_map/forward/pallas_call | solution.py:665
  279.9 24.9 %logits.1 = (bf16[2,6400,512]{2,1,0:T(8,128)(2,1)}, f32[5,64,512]{2,1,0:T(8,128)}, f32[8,512]{1,0:T(8,128)}) custom-call(s32[1,512]{1,0:T(1,128)} %bitcast.173, bf16[6400,2048]{1,0:T(8,128)(2,1)} %all-gather.4.cloned.1.call-done.table, bf16[528,1024]{1,0:T(8,128)(2,1)} %get-tuple-element.215.normed), custom_call_target="tpu_custom_call" | custom-call | flops 13421772800 | bytes 41943040 | tf_op jit(solution)/shard_map/logits/pallas_call | solution.py:1526
  304.7 8.1 %stats.1 = (f32[5,64,512]{2,1,0:T(8,128)}, f32[8,128]{1,0:T(8,128)}) custom-call(f32[8,512]{1,0:T(8,128)} %get-tuple-element.216.stats, f32[5,64,512]{2,1,0:T(8,128)} %get-tuple-element.217.tops, f32[1,512]{1,0:T(1,128)} %compare_select_fusion.2.weight), custom_call_target="tpu_custom_call" | custom-call | tf_op jit(solution)/shard_map/stats/pallas_call | solution.py:817
  312.8 20.1 %rowgrads.1 = (bf16[128,1024]{1,0:T(8,128)(2,1)}, bf16[128,1024]{1,0:T(8,128)(2,1)}, bf16[128,1024]{1,0:T(8,128)(2,1)}, bf16[128,1024]{1,0:T(8,128)(2,1)}) custom-call(s32[1]{0:T(128)} %bitcast.4.scal, s32[1,512]{1,0:T(1,128)} %bitcast.174, f32[5,64,512]{2,1,0:T(8,128)} %get-tuple-element.219.scale, f32[1,512]{1,0:T(1,128)} %compare_select_fusion.2.weight, ...), custom_call_target="tpu_custom_call" | custom-call | flops 13421772800 | bytes 41943040 | tf_op jit(solution)/shard_map/rowgrads/pallas_call | solution.py:1603
  337.3 20.7 %tablegrads.1 = bf16[6400,2048]{1,0:T(8,128)(2,1)} custom-call(s32[1,512]{1,0:T(1,128)} %bitcast.175, f32[5,64,512]{2,1,0:T(8,128)} %get-tuple-element.219.scale, f32[1,512]{1,0:T(1,128)} %compare_select_fusion.2.weight, bf16[2,6400,512]{2,1,0:T(8,128)(2,1)} %get-tuple-element.220.p_in, bf16[528,1024]{1,0:T(8,128)(2,1)} %get-tuple-element.215.normed), custom_call_target="tpu_custom_call" | custom-call | flops 13421772800 | bytes 41943040 | tf_op jit(solution)/shard_map/tablegrads/pallas_call | solution.py:1636
  358.8 24.9 %backward.2 = (f32[128,1024]{1,0:T(8,128)}, bf16[512,1152]{1,0:T(8,128)(2,1)}, f32[1,1024]{1,0:T(1,128)}) custom-call(bf16[128,1024]{1,0:T(8,128)(2,1)} %get-tuple-element.225.refs_0_, bf16[128,1024]{1,0:T(8,128)(2,1)} %copy-done.6, bf16[128,1024]{1,0:T(8,128)(2,1)} %copy-done.7, bf16[128,1024]{1,0:T(8,128)(2,1)} %copy-done.8, ...), custom_call_target="tpu_custom_call" | custom-call | tf_op jit(solution)/shard_map/backward/pallas_call | solution.py:765
  405.0 14.0 %back.2 = (bf16[528,1024]{1,0:T(8,128)(2,1)}, bf16[528,384]{1,0:T(8,128)(2,1)}, f32[8,512]{1,0:T(8,128)}, f32[8,256]{1,0:T(8,128)}, f32[8,128]{1,0:T(8,128)}, /*...) custom-call(s32[1]{0:T(128)} %bitcast.4.scal, ...), custom_call_target="tpu_custom_call" | custom-call | flops 2147483648 | bytes 16777216 | tf_op jit(solution)/shard_map/back/pallas_call | solution.py:138
  419.1 49.1 %backward.3 = (f32[128,1024]{1,0:T(8,128)}, bf16[512,1152]{1,0:T(8,128)(2,1)}) custom-call(bf16[128,1024]{1,0:T(8,128)(2,1)} %get-tuple-element.246.refs_0_, bf16[128,1024]{1,0:T(8,128)(2,1)} %get-tuple-element.247.refs_1_, bf16[128,1024]{1,0:T(8,128)(2,1)} %get-tuple-element.248.refs_2_, bf16[128,1024]{1,0:T(8,128)(2,1)} %get-tuple-element.249.refs_3_, ...), custom_call_target="tpu_custom_call" | custom-call | tf_op jit(solution)/shard_map/backward/pallas_call | solution.py:765
  493.1 13.7 %back.3 = (bf16[528,1024]{1,0:T(8,128)(2,1)}, bf16[528,384]{1,0:T(8,128)(2,1)}, f32[8,512]{1,0:T(8,128)}, f32[8,256]{1,0:T(8,128)}, f32[8,128]{1,0:T(8,128)}, /*...) custom-call(s32[1]{0:T(128)} %bitcast.4.scal, ...), custom_call_target="tpu_custom_call" | custom-call | flops 2147483648 | bytes 16777216 | tf_op jit(solution)/shard_map/back/pallas_call | solution.py:138
  518.7 9.5 %packtiles.1 = bf16[8,3968,128]{2,1,0:T(8,128)(2,1)} custom-call(s32[1]{0:T(128)} %bitcast.4.scal, s32[1,192]{1,0:T(1,128)} %slot.5, bf16[1024,1024]{1,0:T(8,128)(2,1)} %convolution_convert_fusion.3.refs_0_, bf16[512,1152]{1,0:T(8,128)(2,1)} %convolution_convert_fusion.1.refs_1_, bf16[1024,1024]{1,0:T(8,128)(2,1)} %convolution_convert_fusion.2.refs_2_, ...), custom_call_target="tpu_custom_call" | custom-call | bytes 14680064 | tf_op jit(solution)/shard_map/packtiles/pallas_call | solution.py:138
  532.6 70.7 %finish.1.parts = bf16[8,512,256]{2,1,0:T(8,128)(2,1)} custom-call(bf16[128,1024]{1,0:T(8,128)(2,1)} %get-tuple-element.293.refs_0_, bf16[128,1024]{1,0:T(8,128)(2,1)} %get-tuple-element.294.refs_1_, bf16[128,1024]{1,0:T(8,128)(2,1)} %get-tuple-element.295.refs_2_, bf16[128,1024]{1,0:T(8,128)(2,1)} %get-tuple-element.296.refs_3_, ...), custom_call_target="tpu_custom_call" | custom-call | tf_op jit(solution)/shard_map/finish/pallas_call | solution.py:947
  603.3 11.6 %addrows.1 = (bf16[6286,256]{1,0:T(8,128)(2,1)}, f32[1,256]{1,0:T(1,128)}) custom-call(s32[2]{0:T(128)} %pad_add_fusion.1.scal, s32[4104]{0:T(1024)} %concatenate.41.code, s32[4096]{0:T(1024)} %select_bitcast_fusion.listed, s32[32]{0:T(128)} %copy-done.27, bf16[6400,256]{1,0:T(8,128)(2,1)} %reduce-scatter.3.cloned.1.call-done.share, ...), custom_call_target="tpu_custom_call" | custom-call | bytes 31457280 | tf_op jit(solution)/shard_map/addrows/pallas_call | solution.py:138
  625.3 7.6 %turn.1 = (f32[24,128,128]{2,1,0:T(8,128)}, f32[1,128]{1,0:T(1,128)}) custom-call(bf16[3968,128]{1,0:T(8,128)(2,1)} %bitcast.163, f32[24,2,128,128]{3,2,1,0:T(8,128)} %bitcast.131), custom_call_target="tpu_custom_call" | custom-call | flops 1207959552 | bytes 6291456 | tf_op jit(solution)/shard_map/turn/pallas_call | solution.py:1682
  636.9 11.4 %sumall.1.sums = f32[8,128]{1,0:T(8,128)} custom-call(f32[8,128]{1,0:T(8,128)} %get-tuple-element.218.refs_0_, f32[12,512]{1,0:T(8,128)} %reshape.364.refs_1_, f32[6,8]{1,0:T(8,128)} %reshape_squeeze.3.refs_2_, f32[1,256]{1,0:T(1,128)} %get-tuple-element.299.refs_3_, f32[1,128]{1,0:T(1,128)} %get-tuple-element.300.refs_4_, f32[64,288]{1,0:T(8,128)} %bitcast.142, ...), custom_call_target="tpu_custom_call" | custom-call | tf_op jit(solution)/shard_map/sumall/pallas_call | solution.py:1076
  650.8 11.5 %update.1 = (f32[24,128,128]{2,1,0:T(8,128)}, bf16[24,128,128]{2,1,0:T(8,128)(2,1)}, f32[24,128,128]{2,1,0:T(8,128)}, f32[24,128,128]{2,1,0:T(8,128)}, f32[64,28...) custom-call(f32[2]{0:T(128)} %pad_maximum_fusion.3.fixes, ...), custom_call_target="tpu_custom_call" | custom-call | flops 1207959552 | bytes 16777216 | tf_op jit(solution)/shard_map/update/pallas_call | solution.py:1751
  670.3 14.4 %multiply_subtract_fusion = (f32[6286,256]{1,0:T(8,128)}, f32[6286,256]{1,0:T(8,128)}, f32[6286,256]{1,0:T(8,128)}) fusion(f32[6286,256]{1,0:T(8,128)} %table.1, f32[]{:T(128)} %bitcast.42, f32[]{:T(128)} %bitcast.41, f32[]{:T(128)} %bitcast.40, bf16[6286,256]{1,0:T(8,128)(2,1)S(1)} %copy-done, f32[6286,256]{1,0:T(8,128)} %param.33, f32[6286,256]{1,0:T(8,128)} %param.32), kind=kLoop, calls=%fused_computation.2 | loop fusion | flops 27356672 | bytes 41839628 | tf_op jit(solution)/shard_map/sub | solution.py:1658
  (275 shorter events, 150.6 us)
Async XLA Ops:
  7.2 109.7 %all-gather.6.cloned.1.call-start = ((), (), s32[]{:S(2)}) async-start(), calls=%async_computation.5 | async-start | bytes 8847360 | tf_op jit(solution)/shard_map/all_gather | solution.py:1856
  28.4 251.4 %all-gather.4.cloned.1.call-start = ((), (), s32[]{:S(2)}) async-start(), calls=%async_computation.2 | async-start | bytes 29491200 | tf_op jit(solution)/shard_map/all_gather | solution.py:1878
  113.9 414.3 %reduce-scatter.3.cloned.1.call-start = ((), (), s32[]{:S(2)}) async-start(), calls=%async_computation.3 | async-start | bytes 29491200 | tf_op jit(solution)/shard_map/reduce_scatter | solution.py:1951
  136.7 13.7 %collective-permute-start = (bf16[144,512]{1,0:T(8,128)(2,1)}, bf16[144,512]{1,0:T(8,128)(2,1)S(1)}, u32[]{:S(2)}, u32[]{:S(2)}) collective-permute-start(bf16[144,512]{1,0:T(8,128)(2,1)} %get-tuple-element.189), channel_id=1, source_target_pairs={{0,4},{4,8},{8,12},{16,20},{20,24},{24,28},{1,5},{5,9},{9,13},{17,... | collective-permute-start | bytes 442376 | tf_op jit(solution)/shard_map/ppermute | solution.py:1906
  138.0 12.3 %collective-permute-start.1 = (bf16[144,512]{1,0:T(8,128)(2,1)}, bf16[144,512]{1,0:T(8,128)(2,1)S(1)}, u32[]{:S(2)}, u32[]{:S(2)}) collective-permute-start(bf16[144,512]{1,0:T(8,128)(2,1)} %get-tuple-element.189), channel_id=1, source_target_pairs={{0,8},{4,12},{16,24},{20,28},{1,9},{5,13},{17,25},{21,29},{2,10},{... | collective-permute-start | bytes 442376 | tf_op jit(solution)/shard_map/ppermute | solution.py:1906
  139.3 13.3 %collective-permute-start.2 = (bf16[144,512]{1,0:T(8,128)(2,1)}, bf16[144,512]{1,0:T(8,128)(2,1)S(1)}, u32[]{:S(2)}, u32[]{:S(2)}) collective-permute-start(bf16[144,512]{1,0:T(8,128)(2,1)} %get-tuple-element.189), channel_id=1, source_target_pairs={{0,12},{16,28},{1,13},{17,29},{2,14},{18,30},{3,15},{19,31}} | collective-permute-start | bytes 442376 | tf_op jit(solution)/shard_map/ppermute | solution.py:1906
  210.3 12.9 %collective-permute-start.3 = (bf16[144,512]{1,0:T(8,128)(2,1)}, bf16[144,512]{1,0:T(8,128)(2,1)S(1)}, u32[]{:S(2)}, u32[]{:S(2)}) collective-permute-start(bf16[144,512]{1,0:T(8,128)(2,1)} %get-tuple-element.204), channel_id=1, source_target_pairs={{0,4},{4,8},{8,12},{16,20},{20,24},{24,28},{1,5},{5,9},{9,13},{17,... | collective-permute-start | bytes 442376 | tf_op jit(solution)/shard_map/ppermute | solution.py:1906
  211.6 15.4 %collective-permute-start.4 = (bf16[144,512]{1,0:T(8,128)(2,1)}, bf16[144,512]{1,0:T(8,128)(2,1)S(1)}, u32[]{:S(2)}, u32[]{:S(2)}) collective-permute-start(bf16[144,512]{1,0:T(8,128)(2,1)} %get-tuple-element.204), channel_id=1, source_target_pairs={{0,8},{4,12},{16,24},{20,28},{1,9},{5,13},{17,25},{21,29},{2,10},{... | collective-permute-start | bytes 442376 | tf_op jit(solution)/shard_map/ppermute | solution.py:1906
  219.3 13.1 %collective-permute-start.5 = (bf16[144,512]{1,0:T(8,128)(2,1)}, bf16[144,512]{1,0:T(8,128)(2,1)S(1)}, u32[]{:S(2)}, u32[]{:S(2)}) collective-permute-start(bf16[144,512]{1,0:T(8,128)(2,1)} %get-tuple-element.204), channel_id=1, source_target_pairs={{0,12},{16,28},{1,13},{17,29},{2,14},{18,30},{3,15},{19,31}} | collective-permute-start | bytes 442376 | tf_op jit(solution)/shard_map/ppermute | solution.py:1906
  332.9 25.1 %collective-permute-start.6 = (bf16[128,1024]{1,0:T(8,128)(2,1)}, bf16[128,1024]{1,0:T(8,128)(2,1)S(1)}, u32[]{:S(2)}, u32[]{:S(2)}) collective-permute-start(bf16[128,1024]{1,0:T(8,128)(2,1)} %get-tuple-element.222), channel_id=1, source_target_pairs={{0,1},{1,0},{2,3},{3,2},{4,5},{5,4},{6,7},{7,6},{8,9},{9,8},{10,11... | collective-permute-start | bytes 786440 | tf_op jit(solution)/shard_map/ppermute | solution.py:69
  333.3 24.7 %collective-permute-start.7 = (bf16[128,1024]{1,0:T(8,128)(2,1)}, bf16[128,1024]{1,0:T(8,128)(2,1)S(1)}, u32[]{:S(2)}, u32[]{:S(2)}) collective-permute-start(bf16[128,1024]{1,0:T(8,128)(2,1)} %get-tuple-element.223), channel_id=1, source_target_pairs={{0,2},{1,3},{2,0},{3,1},{4,6},{5,7},{6,4},{7,5},{8,10},{9,11},{10,... | collective-permute-start | bytes 786440 | tf_op jit(solution)/shard_map/ppermute | solution.py:69
  335.6 22.4 %collective-permute-start.8 = (bf16[128,1024]{1,0:T(8,128)(2,1)}, bf16[128,1024]{1,0:T(8,128)(2,1)S(1)}, u32[]{:S(2)}, u32[]{:S(2)}) collective-permute-start(bf16[128,1024]{1,0:T(8,128)(2,1)} %get-tuple-element.224), channel_id=1, source_target_pairs={{0,3},{1,2},{2,1},{3,0},{4,7},{5,6},{6,5},{7,4},{8,11},{9,10},{10,... | collective-permute-start | bytes 786440 | tf_op jit(solution)/shard_map/ppermute | solution.py:69
  358.8 260.3 %reduce-scatter.5.cloned.1.call-start = ((), (), s32[]{:S(2)}) async-start(), calls=%async_computation.4 | async-start | bytes 9142272 | tf_op jit(solution)/shard_map/reduce_scatter | solution.py:2030
  390.0 14.3 %collective-permute-start.9 = (bf16[144,512]{1,0:T(8,128)(2,1)}, bf16[144,512]{1,0:T(8,128)(2,1)S(1)}, u32[]{:S(2)}, u32[]{:S(2)}) collective-permute-start(bf16[144,512]{1,0:T(8,128)(2,1)} %get-tuple-element.234), channel_id=1, source_target_pairs={{4,0},{8,4},{12,8},{20,16},{24,20},{28,24},{5,1},{9,5},{13,9},{21,... | collective-permute-start | bytes 442376 | tf_op jit(solution)/shard_map/ppermute | solution.py:1906
  391.3 13.0 %collective-permute-start.10 = (bf16[144,512]{1,0:T(8,128)(2,1)}, bf16[144,512]{1,0:T(8,128)(2,1)S(1)}, u32[]{:S(2)}, u32[]{:S(2)}) collective-permute-start(bf16[144,512]{1,0:T(8,128)(2,1)} %get-tuple-element.234), channel_id=1, source_target_pairs={{8,0},{12,4},{24,16},{28,20},{9,1},{13,5},{25,17},{29,21},{10,2},{... | collective-permute-start | bytes 442376 | tf_op jit(solution)/shard_map/ppermute | solution.py:1906
  392.6 11.7 %collective-permute-start.11 = (bf16[144,512]{1,0:T(8,128)(2,1)}, bf16[144,512]{1,0:T(8,128)(2,1)S(1)}, u32[]{:S(2)}, u32[]{:S(2)}) collective-permute-start(bf16[144,512]{1,0:T(8,128)(2,1)} %get-tuple-element.234), channel_id=1, source_target_pairs={{12,0},{28,16},{13,1},{29,17},{14,2},{30,18},{15,3},{31,19}} | collective-permute-start | bytes 442376 | tf_op jit(solution)/shard_map/ppermute | solution.py:1906
  473.4 18.7 %collective-permute-start.12 = (bf16[144,512]{1,0:T(8,128)(2,1)}, bf16[144,512]{1,0:T(8,128)(2,1)S(1)}, u32[]{:S(2)}, u32[]{:S(2)}) collective-permute-start(bf16[144,512]{1,0:T(8,128)(2,1)} %get-tuple-element.256), channel_id=1, source_target_pairs={{4,0},{8,4},{12,8},{20,16},{24,20},{28,24},{5,1},{9,5},{13,9},{21,... | collective-permute-start | bytes 442376 | tf_op jit(solution)/shard_map/ppermute | solution.py:1906
  474.7 17.4 %collective-permute-start.13 = (bf16[144,512]{1,0:T(8,128)(2,1)}, bf16[144,512]{1,0:T(8,128)(2,1)S(1)}, u32[]{:S(2)}, u32[]{:S(2)}) collective-permute-start(bf16[144,512]{1,0:T(8,128)(2,1)} %get-tuple-element.256), channel_id=1, source_target_pairs={{8,0},{12,4},{24,16},{28,20},{9,1},{13,5},{25,17},{29,21},{10,2},{... | collective-permute-start | bytes 442376 | tf_op jit(solution)/shard_map/ppermute | solution.py:1906
  476.0 16.4 %collective-permute-start.14 = (bf16[144,512]{1,0:T(8,128)(2,1)}, bf16[144,512]{1,0:T(8,128)(2,1)S(1)}, u32[]{:S(2)}, u32[]{:S(2)}) collective-permute-start(bf16[144,512]{1,0:T(8,128)(2,1)} %get-tuple-element.256), channel_id=1, source_target_pairs={{12,0},{28,16},{13,1},{29,17},{14,2},{30,18},{15,3},{31,19}} | collective-permute-start | bytes 442376 | tf_op jit(solution)/shard_map/ppermute | solution.py:1906
  493.1 19.4 %copy-start.3 = (bf16[528,1024]{1,0:T(8,128)(2,1)S(1)}, bf16[528,1024]{1,0:T(8,128)(2,1)}, u32[]{:S(2)}) copy-start(bf16[528,1024]{1,0:T(8,128)(2,1)} %get-tuple-element.185.normed.rest_19_) | copy-start | bytes 3244036
  620.8 14.7 %collective-permute-start.17 = (bf16[208,128]{1,0:T(8,128)(2,1)S(1)}, bf16[208,128]{1,0:T(8,128)(2,1)S(1)}, u32[]{:S(2)}, u32[]{:S(2)}) collective-permute-start(bf16[208,128]{1,0:T(8,128)(2,1)S(1)} %get-tuple-element.413), channel_id=1, source_target_pairs={{0,3},{1,2},{2,1},{3,0},{4,7},{5,6},{6,5},{7,4},{8,11},{9,10},{10,... | collective-permute-start | bytes 159752 | tf_op jit(solution)/shard_map/ppermute | solution.py:69
  624.3 11.2 %collective-permute-start.16 = (bf16[208,128]{1,0:T(8,128)(2,1)S(1)}, bf16[208,128]{1,0:T(8,128)(2,1)S(1)}, u32[]{:S(2)}, u32[]{:S(2)}) collective-permute-start(bf16[208,128]{1,0:T(8,128)(2,1)S(1)} %get-tuple-element.412), channel_id=1, source_target_pairs={{0,2},{1,3},{2,0},{3,1},{4,6},{5,7},{6,4},{7,5},{8,10},{9,11},{10,... | collective-permute-start | bytes 159752 | tf_op jit(solution)/shard_map/ppermute | solution.py:69
  624.3 11.2 %collective-permute-start.15 = (bf16[208,128]{1,0:T(8,128)(2,1)S(1)}, bf16[208,128]{1,0:T(8,128)(2,1)S(1)}, u32[]{:S(2)}, u32[]{:S(2)}) collective-permute-start(bf16[208,128]{1,0:T(8,128)(2,1)S(1)} %get-tuple-element.411), channel_id=1, source_target_pairs={{0,1},{1,0},{2,3},{3,2},{4,5},{5,4},{6,7},{7,6},{8,9},{9,8},{10,11... | collective-permute-start | bytes 159752 | tf_op jit(solution)/shard_map/ppermute | solution.py:69
  650.8 19.5 %copy-start = (bf16[6286,256]{1,0:T(8,128)(2,1)S(1)}, bf16[6286,256]{1,0:T(8,128)(2,1)}, u32[]{:S(2)}) copy-start(bf16[6286,256]{1,0:T(8,128)(2,1)} %get-tuple-element.301) | copy-start | bytes 9655300
  (43 other events, 158.0 us)
Sparse Core Ops, SparseCore 0:
  28.6 66.4 all-gather.5
  114.1 138.3 all-gather.3
  358.1 165.6 reduce-scatter.2
  528.4 90.6 reduce-scatter.4

commit v7 on v6

--- a/solution.py
+++ b/solution.py
@@ -824,7 +824,7 @@
             pltpu.SemaphoreType.DMA((2, shards)),
         ],
         compiler_params=pltpu.CompilerParams(
-            collective_id=9, has_side_effects=True, vmem_limit_bytes=60 * MIB
+            collective_id=9, has_side_effects=True, vmem_limit_bytes=8 * MIB
         ),
         name="stats",
     )(stats, tops, weight)
@@ -1010,7 +1010,7 @@
             pltpu.SemaphoreType.DMA((4, count)),
         ],
         compiler_params=pltpu.CompilerParams(
-            collective_id=2, has_side_effects=True, vmem_limit_bytes=60 * MIB
+            collective_id=2, has_side_effects=True, vmem_limit_bytes=8 * MIB
         ),
         name="open",
     )(ids, piece, share)
@@ -1087,7 +1087,7 @@
             pltpu.SemaphoreType.DMA((count,)),
         ],
         compiler_params=pltpu.CompilerParams(
-            collective_id=1, has_side_effects=True, vmem_limit_bytes=60 * MIB
+            collective_id=1, has_side_effects=True, vmem_limit_bytes=8 * MIB
         ),
         name="sumall",
     )(*args)
@@ -1658,48 +1658,30 @@
     return (weight_in - LEARN_RATE * (direction + decay_rate * weight_in), one_next, two_next)
 
 
-def turn_kernel(share, bases, turned, root, total):
-    step = pl.program_id(0)
-
-    @pl.when(step == 0)
-    def _():
-        total[...] = jnp.zeros_like(total)
-
-    for at in range(bases.shape[0]):
-        grad = share[at * BLK : (at + 1) * BLK, :].astype(F32)
+def turn_kernel(share, bases, turned, root):
+    count = bases.shape[0]
+    total = jnp.zeros((1, BLK), F32)
+
+    def turn(at, total):
+        grad = share[pl.ds(pl.multiple_of(at * BLK, BLK), BLK), :].astype(F32)
         half_turn = tn(bases[at, 0], grad, HIGHEST)
         turned[at] = nn(half_turn, bases[at, 1], HIGHEST)
-        total[...] += jnp.sum(grad * grad, axis=0, keepdims=True)
-
-    @pl.when(step == pl.num_programs(0) - 1)
-    def _():
-        root[...] = jnp.sqrt(total[...])
+        return total + jnp.sum(grad * grad, axis=0, keepdims=True)
+
+    for at in range(count):
+        total = turn(at, total)
+    root[...] = jnp.sqrt(total)
 
 
 def turn_tiles(share, bases):
     count = bases.shape[0]
-    each = 4 if count % 4 == 0 else 2
-    return pl.pallas_call(
+    return call(
         turn_kernel,
-        grid=(count // each,),
-        out_shape=[sds((count, BLK, BLK), F32), sds((1, BLK), F32)],
-        in_specs=[
-            pl.BlockSpec((each * BLK, LANES), lambda i: (i, 0)),
-            pl.BlockSpec((each, 2, BLK, BLK), lambda i: (i, 0, 0, 0)),
-        ],
-        out_specs=[
-            pl.BlockSpec((each, BLK, BLK), lambda i: (i, 0, 0)),
-            pl.BlockSpec((1, BLK), lambda i: (0, 0)),
-        ],
-        scratch_shapes=[pltpu.VMEM((1, BLK), F32)],
-        compiler_params=pltpu.CompilerParams(
-            dimension_semantics=("arbitrary",), vmem_limit_bytes=60 * MIB
-        ),
-        cost_estimate=pl.CostEstimate(
-            flops=24 * count * BLK * BLK * BLK, bytes_accessed=6 * MIB, transcendentals=0
-        ),
-        name="turn",
-    )(share, bases)
+        "turn",
+        [sds((count, BLK, BLK), F32), sds((1, BLK), F32)],
+        (share, bases),
+        moved=6 * MIB,
+    )
 
 
 def last_kernel(small, fixes, sums, *refs):
@@ -1762,7 +1744,7 @@
         out_specs=[tile_spec] * 4
         + [spec for which in range(len(little)) for spec in whole[4 * which : 4 * which + 3]],
         compiler_params=pltpu.CompilerParams(
-            dimension_semantics=("arbitrary",), vmem_limit_bytes=60 * MIB
+            dimension_semantics=("arbitrary",), vmem_limit_bytes=48 * MIB
         ),
         cost_estimate=pl.CostEstimate(
             flops=24 * count * BLK * BLK * BLK, bytes_accessed=16 * MIB, transcendentals=0
@@ -2089,8 +2071,14 @@
     little = [
         [flat(side_proj), side_share, flat(side_first), flat(side_second)],
         [flat(shared_params), shared_share, flat(shared_first), flat(shared_second)],
-        [channel_params, channel_sum.reshape(channel_params.shape), channel_first, channel_second],
-        [head_params, head_sum.reshape(head_params.shape), head_first, head_second],
+        [
+            x.reshape(channel_params.shape).transpose(1, 0, 2)
+            for x in (channel_params, channel_sum, channel_first, channel_second)
+        ],
+        [
+            x.reshape(head_params.shape).transpose(1, 0, 2)
+            for x in (head_params, head_sum, head_first, head_second)
+        ],
     ]
     updated = last_update(
         jnp.stack([fix_one, fix_two]),
@@ -2113,8 +2101,9 @@
         WEIGHT_DECAY,
     )
     block_out = [x.reshape(layer_blocks.shape) for x in updated[:4]]
-    like = [side_proj] * 3 + [shared_params] * 3 + [channel_params] * 3 + [head_params] * 3
-    small_out = [x.reshape(y.shape) for x, y in zip(updated[4:], like)]
+    like = [side_proj] * 3 + [shared_params] * 3
+    small_out = [x.reshape(y.shape) for x, y in zip(updated[4:10], like)]
+    small_out += [x.transpose(1, 0, 2) for x in updated[10:]]
     return (
         seq_loss,
         clip_norm,

time: 701 us -> 684 us (0.976)
  local copies, waits for them, and re-layouts: 35.5 us -> 21 us
    unnamed x117 -> x129, local copies, waits for them, and re-layouts: 16.7 us -> 8.51 us
    pallas_call x1 -> x0, Pallas kernels: 7.62 us -> none  [turn_tiles(): pl.pallas_call(turn_kernel, grid=(count // each,), out_shape=[sds((count,...]
    pallas_call x15 -> x16, Pallas kernels: 125 us -> 131 us  [call(): pl.pallas_call(kernel, out_shape=out_shape, in_specs=specs, out_specs=jax...]
  transfers between devices with their start and end apart: 22 -> 22, of which waited for: 5 -> 5; matrix products, arithmetic and copies ran while one was open for 7% -> 6% of each run, Pallas kernels for 66% -> 67%
where the time goes in v7:
time: 684 us; the launch traced here: 675 us
  Pallas kernels  539 us (79%)
  other arithmetic  32.3 us (5%)
  starting transfers between devices  30.6 us (4%)
  local copies, waits for them, and re-layouts  21 us (3%)
  waiting for transfers between devices  20.2 us (3%)
  matrix products  16.5 us (2%)
  between operations  16 us (2%)
    pallas_call x3, Pallas kernels, forward_rows(): pl.pallas_call(functools.partial(forward_kernel, groups, shards, chunks,...  157 us
    pallas_call x16, Pallas kernels, call(): pl.pallas_call(kernel, out_shape=out_shape, in_specs=specs, out_specs=jax...  131 us
    pallas_call x1, Pallas kernels, finish_rows(): pl.pallas_call(functools.partial(finish_kernel, groups, shards, chunks, o...  73.9 us
    pallas_call x2, Pallas kernels, backward_rows(): pl.pallas_call(functools.partial(backward_kernel, groups, shards, chunks,...  72.3 us
    pallas_call x1, Pallas kernels, vocab_logits(): pl.pallas_call(functools.partial(logits_kernel, vrows), grid=(steps,), ou...  24.9 us
    ppermute x12, starting transfers between devices, hop(): return lax.ppermute(x, 'dp', pairs)  21.7 us
    pallas_call x1, Pallas kernels, vocab_table_grad(): pl.pallas_call(table_kernel, grid=(padded // PAIRS,), out_shape=sds((padd...  20.7 us
    pallas_call x1, Pallas kernels, vocab_rows(): pl.pallas_call(functools.partial(rows_kernel, shards, own), grid=(padded...  20.1 us
  transfers between devices with their start and end apart: 22, of which 5 were waited for; matrix products, arithmetic and copies ran while one was open for 6% of the time, Pallas kernels for 67%

profile of v7, /device:TPU:0, one launch (start us, length us, event | category | flops | bytes accessed | tf_op | source)
XLA Modules:
  0.0 675.5 jit_solution(5383651127182509975)
XLA Ops:
  10.5 12.7 %open.1 = (s32[8,8,256]{2,1,0:T(8,128)S(1)}, bf16[4,192,128]{2,1,0:T(8,128)(2,1)S(1)}, bf16[8,4,16,128]{3,2,1,0:T(8,128)(2,1)S(1)}) custom-call(s32[8,256]{1,0:T(8,128)S(1)} %pad.47.ids, bf16[192,128]{1,0:T(8,128)(2,1)S(1)} %reshape.346.piece, bf16[16,128]{1,0:T(8,128)(2,1)S(1)} %pad_bitcast_fusion.share), custom_call_target="tpu_custom_call" | custom-call | tf_op jit(solution)/shard_map/open/pallas_call | solution.py:998
  28.2 11.4 %look.1 = (bf16[512,256]{1,0:T(8,128)(2,1)}, bf16[512,256]{1,0:T(8,128)(2,1)}, bf16[512,256]{1,0:T(8,128)(2,1)}, bf16[512,256]{1,0:T(8,128)(2,1)}, bf16[512,256]...) custom-call(s32[2]{0:T(128)} %pad_add_fusion.1.scal, ...), custom_call_target="tpu_custom_call" | custom-call | bytes 31457280 | tf_op jit(solution)/shard_map/look/pallas_call | solution.py:138
  40.2 69.6 %enter.1 = (f32[128,1024]{1,0:T(8,128)}, bf16[528,1024]{1,0:T(8,128)(2,1)}) custom-call(bf16[512,256]{1,0:T(8,128)(2,1)} %get-tuple-element.172.refs_0_, bf16[512,256]{1,0:T(8,128)(2,1)} %get-tuple-element.173.refs_1_, bf16[512,256]{1,0:T(8,128)(2,1)} %get-tuple-element.174.refs_2_, bf16[512,256]{1,0:T(8,128)(2,1)} %get-tuple-element.175.refs_3_, ...), custom_call_target="tpu_custom_call" | custom-call | tf_op jit(solution)/shard_map/enter/pallas_call | solution.py:665
  114.6 7.5 %placetiles.2 = (bf16[1024,1024]{1,0:T(8,128)(2,1)}, bf16[512,1024]{1,0:T(8,128)(2,1)}) custom-call(s32[1,192]{1,0:T(1,128)} %slot.5, bf16[8,3840,128]{2,1,0:T(8,128)(2,1)} %bitcast.166), custom_call_target="tpu_custom_call" | custom-call | bytes 14680064 | tf_op jit(solution)/shard_map/placetiles/pallas_call | solution.py:138
  124.5 8.2 %front.2 = (f32[512,512]{1,0:T(8,128)}, f32[528,512]{1,0:T(8,128)}, f32[528,384]{1,0:T(8,128)}, f32[512,512]{1,0:T(8,128)}, bf16[144,512]{1,0:T(8,128)(2,1)}, /*...) custom-call(bf16[528,1024]{1,0:T(8,128)(2,1)} %get-tuple-element.185.normed.rest_19_, ...), custom_call_target="tpu_custom_call" | custom-call | flops 2147483648 | bytes 12582912 | tf_op jit(solution)/shard_map/front/pallas_call | solution.py:138
  153.4 45.0 %forward.2 = (f32[128,1024]{1,0:T(8,128)}, f32[128,1024]{1,0:T(8,128)}, f32[128,1]{1,0:T(8,128)}, bf16[528,1024]{1,0:T(8,128)(2,1)}) custom-call(bf16[128,1152]{1,0:T(8,128)(2,1)} %get-tuple-element.195.refs_0_, bf16[128,1152]{1,0:T(8,128)(2,1)} %get-tuple-element.196.refs_1_, bf16[128,1152]{1,0:T(8,128)(2,1)} %get-tuple-element.197.refs_2_, ...), custom_call_target="tpu_custom_call" | custom-call | tf_op jit(solution)/shard_map/forward/pallas_call | solution.py:665
  198.4 8.0 %front.3 = (f32[512,512]{1,0:T(8,128)}, f32[528,512]{1,0:T(8,128)}, f32[528,384]{1,0:T(8,128)}, f32[512,512]{1,0:T(8,128)}, bf16[144,512]{1,0:T(8,128)(2,1)}, /*...) custom-call(bf16[528,1024]{1,0:T(8,128)(2,1)} %get-tuple-element.200.normed.rest_19_, ...), custom_call_target="tpu_custom_call" | custom-call | flops 2147483648 | bytes 12582912 | tf_op jit(solution)/shard_map/front/pallas_call | solution.py:138
  207.8 7.1 %collective-permute-start.4 = (bf16[144,512]{1,0:T(8,128)(2,1)}, bf16[144,512]{1,0:T(8,128)(2,1)S(1)}, u32[]{:S(2)}, u32[]{:S(2)}) collective-permute-start(bf16[144,512]{1,0:T(8,128)(2,1)} %get-tuple-element.204), channel_id=1, source_target_pairs={{0,8},{4,12},{16,24},{20,28},{1,9},{5,13},{17,25},{21,29},{2,10},{... | collective-permute-start | bytes 442376 | tf_op jit(solution)/shard_map/ppermute | solution.py:1888
  233.2 42.2 %forward.3 = (f32[128,1024]{1,0:T(8,128)}, f32[128,1024]{1,0:T(8,128)}, f32[128,1]{1,0:T(8,128)}, bf16[528,1024]{1,0:T(8,128)(2,1)}) custom-call(bf16[128,1152]{1,0:T(8,128)(2,1)} %get-tuple-element.210.refs_0_, bf16[128,1152]{1,0:T(8,128)(2,1)} %get-tuple-element.211.refs_1_, bf16[128,1152]{1,0:T(8,128)(2,1)} %get-tuple-element.212.refs_2_, ...), custom_call_target="tpu_custom_call" | custom-call | tf_op jit(solution)/shard_map/forward/pallas_call | solution.py:665
  275.4 24.9 %logits.1 = (bf16[2,6400,512]{2,1,0:T(8,128)(2,1)}, f32[5,64,512]{2,1,0:T(8,128)}, f32[8,512]{1,0:T(8,128)}) custom-call(s32[1,512]{1,0:T(1,128)} %bitcast.202, bf16[6400,2048]{1,0:T(8,128)(2,1)} %all-gather.4.cloned.1.call-done.table, bf16[528,1024]{1,0:T(8,128)(2,1)} %get-tuple-element.215.normed), custom_call_target="tpu_custom_call" | custom-call | flops 13421772800 | bytes 41943040 | tf_op jit(solution)/shard_map/logits/pallas_call | solution.py:1526
  309.1 20.1 %rowgrads.1 = (bf16[128,1024]{1,0:T(8,128)(2,1)}, bf16[128,1024]{1,0:T(8,128)(2,1)}, bf16[128,1024]{1,0:T(8,128)(2,1)}, bf16[128,1024]{1,0:T(8,128)(2,1)}) custom-call(s32[1]{0:T(128)} %bitcast.4.scal, s32[1,512]{1,0:T(1,128)} %bitcast.203, f32[5,64,512]{2,1,0:T(8,128)} %copy-done.20, f32[1,512]{1,0:T(1,128)} %copy-done.12, ...), custom_call_target="tpu_custom_call" | custom-call | flops 13421772800 | bytes 41943040 | tf_op jit(solution)/shard_map/rowgrads/pallas_call | solution.py:1603
  333.6 20.7 %tablegrads.1 = bf16[6400,2048]{1,0:T(8,128)(2,1)} custom-call(s32[1,512]{1,0:T(1,128)} %bitcast.204, f32[5,64,512]{2,1,0:T(8,128)} %copy-done.20, f32[1,512]{1,0:T(1,128)} %copy-done.12, bf16[2,6400,512]{2,1,0:T(8,128)(2,1)} %get-tuple-element.220.p_in, bf16[528,1024]{1,0:T(8,128)(2,1)} %get-tuple-element.215.normed), custom_call_target="tpu_custom_call" | custom-call | flops 13421772800 | bytes 41943040 | tf_op jit(solution)/shard_map/tablegrads/pallas_call | solution.py:1636
  355.2 24.9 %backward.2 = (f32[128,1024]{1,0:T(8,128)}, bf16[512,1152]{1,0:T(8,128)(2,1)}, f32[1,1024]{1,0:T(1,128)}) custom-call(bf16[128,1024]{1,0:T(8,128)(2,1)} %get-tuple-element.225.refs_0_, bf16[128,1024]{1,0:T(8,128)(2,1)} %copy-done.26, bf16[128,1024]{1,0:T(8,128)(2,1)} %copy-done.27, bf16[128,1024]{1,0:T(8,128)(2,1)} %copy-done.28, ...), custom_call_target="tpu_custom_call" | custom-call | tf_op jit(solution)/shard_map/backward/pallas_call | solution.py:765
  393.3 7.3 %within.2 = (f32[512,512]{1,0:T(8,128)}, bf16[512,256]{1,0:T(8,128)(2,1)}, f32[512,128]{1,0:T(8,128)}, f32[2,128,512]{2,1,0:T(8,128)}, f32[512,512]{1,0:T(8,128)}, /*index=5*/f32[512,256]{1,0:T(8,128)}) custom-call(f32[128,512]{1,0:T(8,128)} %get-tuple-element.235.s_in, f32[528,512]{1,0:T(8,128)} %get-tuple-element.236.xr.rest_9_, ...), custom_call_target="tpu_custom_call" | custom-call | flops 2147483648 | bytes 16777216 | tf_op jit(solution)/shard_map/within/pallas_call | solution.py:138
  401.4 14.0 %back.2 = (bf16[528,1024]{1,0:T(8,128)(2,1)}, bf16[528,384]{1,0:T(8,128)(2,1)}, f32[8,512]{1,0:T(8,128)}, f32[8,256]{1,0:T(8,128)}, f32[8,128]{1,0:T(8,128)}, /*...) custom-call(s32[1]{0:T(128)} %bitcast.4.scal, ...), custom_call_target="tpu_custom_call" | custom-call | flops 2147483648 | bytes 16777216 | tf_op jit(solution)/shard_map/back/pallas_call | solution.py:138
  415.5 47.4 %backward.3 = (f32[128,1024]{1,0:T(8,128)}, bf16[512,1152]{1,0:T(8,128)(2,1)}) custom-call(bf16[128,1024]{1,0:T(8,128)(2,1)} %get-tuple-element.246.refs_0_, bf16[128,1024]{1,0:T(8,128)(2,1)} %get-tuple-element.247.refs_1_, bf16[128,1024]{1,0:T(8,128)(2,1)} %get-tuple-element.248.refs_2_, bf16[128,1024]{1,0:T(8,128)(2,1)} %get-tuple-element.249.refs_3_, ...), custom_call_target="tpu_custom_call" | custom-call | tf_op jit(solution)/shard_map/backward/pallas_call | solution.py:765
  471.9 7.4 %within.3 = (f32[512,512]{1,0:T(8,128)}, bf16[512,256]{1,0:T(8,128)(2,1)}, f32[512,128]{1,0:T(8,128)}, f32[2,128,512]{2,1,0:T(8,128)}, f32[512,512]{1,0:T(8,128)}, /*index=5*/f32[512,256]{1,0:T(8,128)}) custom-call(f32[128,512]{1,0:T(8,128)} %get-tuple-element.257.s_in, f32[528,512]{1,0:T(8,128)} %get-tuple-element.258.xr.rest_9_, ...), custom_call_target="tpu_custom_call" | custom-call | flops 2147483648 | bytes 16777216 | tf_op jit(solution)/shard_map/within/pallas_call | solution.py:138
  489.5 13.8 %back.3 = (bf16[528,1024]{1,0:T(8,128)(2,1)}, bf16[528,384]{1,0:T(8,128)(2,1)}, f32[8,512]{1,0:T(8,128)}, f32[8,256]{1,0:T(8,128)}, f32[8,128]{1,0:T(8,128)}, /*...) custom-call(s32[1]{0:T(128)} %bitcast.4.scal, ...), custom_call_target="tpu_custom_call" | custom-call | flops 2147483648 | bytes 16777216 | tf_op jit(solution)/shard_map/back/pallas_call | solution.py:138
  515.2 9.5 %packtiles.1 = bf16[8,3968,128]{2,1,0:T(8,128)(2,1)} custom-call(s32[1]{0:T(128)} %bitcast.4.scal, s32[1,192]{1,0:T(1,128)} %slot.5, bf16[1024,1024]{1,0:T(8,128)(2,1)} %convolution_convert_fusion.3.refs_0_, bf16[512,1152]{1,0:T(8,128)(2,1)} %convolution_convert_fusion.1.refs_1_, bf16[1024,1024]{1,0:T(8,128)(2,1)} %convolution_convert_fusion.2.refs_2_, ...), custom_call_target="tpu_custom_call" | custom-call | bytes 14680064 | tf_op jit(solution)/shard_map/packtiles/pallas_call | solution.py:138
  525.5 73.9 %finish.1.parts = bf16[8,512,256]{2,1,0:T(8,128)(2,1)} custom-call(bf16[128,1024]{1,0:T(8,128)(2,1)} %get-tuple-element.293.refs_0_, bf16[128,1024]{1,0:T(8,128)(2,1)} %get-tuple-element.294.refs_1_, bf16[128,1024]{1,0:T(8,128)(2,1)} %get-tuple-element.295.refs_2_, bf16[128,1024]{1,0:T(8,128)(2,1)} %get-tuple-element.296.refs_3_, ...), custom_call_target="tpu_custom_call" | custom-call | tf_op jit(solution)/shard_map/finish/pallas_call | solution.py:947
  599.4 11.3 %addrows.1 = (bf16[6286,256]{1,0:T(8,128)(2,1)}, f32[1,256]{1,0:T(1,128)}) custom-call(s32[2]{0:T(128)} %pad_add_fusion.1.scal, s32[4104]{0:T(1024)} %concatenate.41.code, s32[4096]{0:T(1024)} %select_bitcast_fusion.listed, s32[32]{0:T(128)} %copy-done.41, bf16[6400,256]{1,0:T(8,128)(2,1)} %reduce-scatter.3.cloned.1.call-done.share, ...), custom_call_target="tpu_custom_call" | custom-call | bytes 31457280 | tf_op jit(solution)/shard_map/addrows/pallas_call | solution.py:138
  632.1 9.9 %sumall.1.sums = f32[8,128]{1,0:T(8,128)S(1)} custom-call(f32[8,128]{1,0:T(8,128)S(1)} %get-tuple-element.218.refs_0_, f32[12,512]{1,0:T(8,128)S(1)} %reshape.364.refs_1_, f32[6,8]{1,0:T(8,128)S(1)} %reshape_squeeze.3.refs_2_, f32[1,256]{1,0:T(1,128)S(1)} %copy-done.18, f32[1,128]{1,0:T(1,128)S(1)} %copy-done.19, f32[64,288]{1,0:T(8,128)S(1)} %bitcast.146, ...), custom_call_target="tpu_custom_call" | custom-call | tf_op jit(solution)/shard_map/sumall/pallas_call | solution.py:1076
  643.2 15.0 %multiply_subtract_fusion = (f32[6286,256]{1,0:T(8,128)}, f32[6286,256]{1,0:T(8,128)}, f32[6286,256]{1,0:T(8,128)}) fusion(f32[6286,256]{1,0:T(8,128)} %table.1, f32[]{:T(128)} %bitcast.42, f32[]{:T(128)} %bitcast.41, f32[]{:T(128)} %bitcast.40, bf16[6286,256]{1,0:T(8,128)(2,1)S(1)} %copy-done.21, f32[6286,256]{1,0:T(8,128)} %param.33, f32[6286,256]{1,0:T(8,128)} %param.32), kind=kLoop, calls=%fused_computation.2 | loop fusion | flops 27356672 | bytes 41839628 | tf_op jit(solution)/shard_map/sub | solution.py:1658
  658.4 10.3 %update.1 = (f32[24,128,128]{2,1,0:T(8,128)}, bf16[24,128,128]{2,1,0:T(8,128)(2,1)}, f32[24,128,128]{2,1,0:T(8,128)}, f32[24,128,128]{2,1,0:T(8,128)}, f32[64,28...) custom-call(f32[2]{0:T(128)S(1)} %pad_maximum_fusion.3.fixes, ...), custom_call_target="tpu_custom_call" | custom-call | flops 1207959552 | bytes 16777216 | tf_op jit(solution)/shard_map/update/pallas_call | solution.py:1733
  (290 shorter events, 137.4 us)
Async XLA Ops:
  7.2 105.7 %all-gather.6.cloned.1.call-start = ((), (), s32[]{:S(2)}) async-start(), calls=%async_computation.5 | async-start | bytes 8847360 | tf_op jit(solution)/shard_map/all_gather | solution.py:1838
  24.2 251.2 %all-gather.4.cloned.1.call-start = ((), (), s32[]{:S(2)}) async-start(), calls=%async_computation.2 | async-start | bytes 29491200 | tf_op jit(solution)/shard_map/all_gather | solution.py:1860
  109.9 414.7 %reduce-scatter.3.cloned.1.call-start = ((), (), s32[]{:S(2)}) async-start(), calls=%async_computation.3 | async-start | bytes 29491200 | tf_op jit(solution)/shard_map/reduce_scatter | solution.py:1933
  132.7 13.6 %collective-permute-start = (bf16[144,512]{1,0:T(8,128)(2,1)}, bf16[144,512]{1,0:T(8,128)(2,1)S(1)}, u32[]{:S(2)}, u32[]{:S(2)}) collective-permute-start(bf16[144,512]{1,0:T(8,128)(2,1)} %get-tuple-element.189), channel_id=1, source_target_pairs={{0,4},{4,8},{8,12},{16,20},{20,24},{24,28},{1,5},{5,9},{9,13},{17,... | collective-permute-start | bytes 442376 | tf_op jit(solution)/shard_map/ppermute | solution.py:1888
  134.0 12.3 %collective-permute-start.1 = (bf16[144,512]{1,0:T(8,128)(2,1)}, bf16[144,512]{1,0:T(8,128)(2,1)S(1)}, u32[]{:S(2)}, u32[]{:S(2)}) collective-permute-start(bf16[144,512]{1,0:T(8,128)(2,1)} %get-tuple-element.189), channel_id=1, source_target_pairs={{0,8},{4,12},{16,24},{20,28},{1,9},{5,13},{17,25},{21,29},{2,10},{... | collective-permute-start | bytes 442376 | tf_op jit(solution)/shard_map/ppermute | solution.py:1888
  135.3 12.9 %collective-permute-start.2 = (bf16[144,512]{1,0:T(8,128)(2,1)}, bf16[144,512]{1,0:T(8,128)(2,1)S(1)}, u32[]{:S(2)}, u32[]{:S(2)}) collective-permute-start(bf16[144,512]{1,0:T(8,128)(2,1)} %get-tuple-element.189), channel_id=1, source_target_pairs={{0,12},{16,28},{1,13},{17,29},{2,14},{18,30},{3,15},{19,31}} | collective-permute-start | bytes 442376 | tf_op jit(solution)/shard_map/ppermute | solution.py:1888
  206.5 11.8 %collective-permute-start.3 = (bf16[144,512]{1,0:T(8,128)(2,1)}, bf16[144,512]{1,0:T(8,128)(2,1)S(1)}, u32[]{:S(2)}, u32[]{:S(2)}) collective-permute-start(bf16[144,512]{1,0:T(8,128)(2,1)} %get-tuple-element.204), channel_id=1, source_target_pairs={{0,4},{4,8},{8,12},{16,20},{20,24},{24,28},{1,5},{5,9},{9,13},{17,... | collective-permute-start | bytes 442376 | tf_op jit(solution)/shard_map/ppermute | solution.py:1888
  207.8 14.8 %collective-permute-start.4 = (bf16[144,512]{1,0:T(8,128)(2,1)}, bf16[144,512]{1,0:T(8,128)(2,1)S(1)}, u32[]{:S(2)}, u32[]{:S(2)}) collective-permute-start(bf16[144,512]{1,0:T(8,128)(2,1)} %get-tuple-element.204), channel_id=1, source_target_pairs={{0,8},{4,12},{16,24},{20,28},{1,9},{5,13},{17,25},{21,29},{2,10},{... | collective-permute-start | bytes 442376 | tf_op jit(solution)/shard_map/ppermute | solution.py:1888
  214.9 13.1 %collective-permute-start.5 = (bf16[144,512]{1,0:T(8,128)(2,1)}, bf16[144,512]{1,0:T(8,128)(2,1)S(1)}, u32[]{:S(2)}, u32[]{:S(2)}) collective-permute-start(bf16[144,512]{1,0:T(8,128)(2,1)} %get-tuple-element.204), channel_id=1, source_target_pairs={{0,12},{16,28},{1,13},{17,29},{2,14},{18,30},{3,15},{19,31}} | collective-permute-start | bytes 442376 | tf_op jit(solution)/shard_map/ppermute | solution.py:1888
  217.5 82.8 %copy-start.12 = (f32[1,512]{1,0:T(1,128)}, f32[1,512]{1,0:T(1,128)S(1)}, u32[]{:S(2)}) copy-start(f32[1,512]{1,0:T(1,128)S(1)} %compare_select_fusion.2.weight) | copy-start | bytes 6148
  329.2 25.1 %collective-permute-start.6 = (bf16[128,1024]{1,0:T(8,128)(2,1)}, bf16[128,1024]{1,0:T(8,128)(2,1)S(1)}, u32[]{:S(2)}, u32[]{:S(2)}) collective-permute-start(bf16[128,1024]{1,0:T(8,128)(2,1)} %get-tuple-element.222), channel_id=1, source_target_pairs={{0,1},{1,0},{2,3},{3,2},{4,5},{5,4},{6,7},{7,6},{8,9},{9,8},{10,11... | collective-permute-start | bytes 786440 | tf_op jit(solution)/shard_map/ppermute | solution.py:69
  329.6 24.7 %collective-permute-start.7 = (bf16[128,1024]{1,0:T(8,128)(2,1)}, bf16[128,1024]{1,0:T(8,128)(2,1)S(1)}, u32[]{:S(2)}, u32[]{:S(2)}) collective-permute-start(bf16[128,1024]{1,0:T(8,128)(2,1)} %get-tuple-element.223), channel_id=1, source_target_pairs={{0,2},{1,3},{2,0},{3,1},{4,6},{5,7},{6,4},{7,5},{8,10},{9,11},{10,... | collective-permute-start | bytes 786440 | tf_op jit(solution)/shard_map/ppermute | solution.py:69
  331.9 22.4 %collective-permute-start.8 = (bf16[128,1024]{1,0:T(8,128)(2,1)}, bf16[128,1024]{1,0:T(8,128)(2,1)S(1)}, u32[]{:S(2)}, u32[]{:S(2)}) collective-permute-start(bf16[128,1024]{1,0:T(8,128)(2,1)} %get-tuple-element.224), channel_id=1, source_target_pairs={{0,3},{1,2},{2,1},{3,0},{4,7},{5,6},{6,5},{7,4},{8,11},{9,10},{10,... | collective-permute-start | bytes 786440 | tf_op jit(solution)/shard_map/ppermute | solution.py:69
  355.2 261.7 %reduce-scatter.5.cloned.1.call-start = ((), (), s32[]{:S(2)}) async-start(), calls=%async_computation.4 | async-start | bytes 9142272 | tf_op jit(solution)/shard_map/reduce_scatter | solution.py:2012
  386.3 14.3 %collective-permute-start.9 = (bf16[144,512]{1,0:T(8,128)(2,1)}, bf16[144,512]{1,0:T(8,128)(2,1)S(1)}, u32[]{:S(2)}, u32[]{:S(2)}) collective-permute-start(bf16[144,512]{1,0:T(8,128)(2,1)} %get-tuple-element.234), channel_id=1, source_target_pairs={{4,0},{8,4},{12,8},{20,16},{24,20},{28,24},{5,1},{9,5},{13,9},{21,... | collective-permute-start | bytes 442376 | tf_op jit(solution)/shard_map/ppermute | solution.py:1888
  387.6 13.0 %collective-permute-start.10 = (bf16[144,512]{1,0:T(8,128)(2,1)}, bf16[144,512]{1,0:T(8,128)(2,1)S(1)}, u32[]{:S(2)}, u32[]{:S(2)}) collective-permute-start(bf16[144,512]{1,0:T(8,128)(2,1)} %get-tuple-element.234), channel_id=1, source_target_pairs={{8,0},{12,4},{24,16},{28,20},{9,1},{13,5},{25,17},{29,21},{10,2},{... | collective-permute-start | bytes 442376 | tf_op jit(solution)/shard_map/ppermute | solution.py:1888
  388.9 11.8 %collective-permute-start.11 = (bf16[144,512]{1,0:T(8,128)(2,1)}, bf16[144,512]{1,0:T(8,128)(2,1)S(1)}, u32[]{:S(2)}, u32[]{:S(2)}) collective-permute-start(bf16[144,512]{1,0:T(8,128)(2,1)} %get-tuple-element.234), channel_id=1, source_target_pairs={{12,0},{28,16},{13,1},{29,17},{14,2},{30,18},{15,3},{31,19}} | collective-permute-start | bytes 442376 | tf_op jit(solution)/shard_map/ppermute | solution.py:1888
  468.0 18.7 %collective-permute-start.12 = (bf16[144,512]{1,0:T(8,128)(2,1)}, bf16[144,512]{1,0:T(8,128)(2,1)S(1)}, u32[]{:S(2)}, u32[]{:S(2)}) collective-permute-start(bf16[144,512]{1,0:T(8,128)(2,1)} %get-tuple-element.256), channel_id=1, source_target_pairs={{4,0},{8,4},{12,8},{20,16},{24,20},{28,24},{5,1},{9,5},{13,9},{21,... | collective-permute-start | bytes 442376 | tf_op jit(solution)/shard_map/ppermute | solution.py:1888
  469.2 17.4 %collective-permute-start.13 = (bf16[144,512]{1,0:T(8,128)(2,1)}, bf16[144,512]{1,0:T(8,128)(2,1)S(1)}, u32[]{:S(2)}, u32[]{:S(2)}) collective-permute-start(bf16[144,512]{1,0:T(8,128)(2,1)} %get-tuple-element.256), channel_id=1, source_target_pairs={{8,0},{12,4},{24,16},{28,20},{9,1},{13,5},{25,17},{29,21},{10,2},{... | collective-permute-start | bytes 442376 | tf_op jit(solution)/shard_map/ppermute | solution.py:1888
  470.5 18.3 %collective-permute-start.14 = (bf16[144,512]{1,0:T(8,128)(2,1)}, bf16[144,512]{1,0:T(8,128)(2,1)S(1)}, u32[]{:S(2)}, u32[]{:S(2)}) collective-permute-start(bf16[144,512]{1,0:T(8,128)(2,1)} %get-tuple-element.256), channel_id=1, source_target_pairs={{12,0},{28,16},{13,1},{29,17},{14,2},{30,18},{15,3},{31,19}} | collective-permute-start | bytes 442376 | tf_op jit(solution)/shard_map/ppermute | solution.py:1888
  489.5 19.4 %copy-start.24 = (bf16[528,1024]{1,0:T(8,128)(2,1)S(1)}, bf16[528,1024]{1,0:T(8,128)(2,1)}, u32[]{:S(2)}) copy-start(bf16[528,1024]{1,0:T(8,128)(2,1)} %get-tuple-element.185.normed.rest_19_) | copy-start | bytes 3244036
  619.3 11.1 %collective-permute-start.17 = (bf16[208,128]{1,0:T(8,128)(2,1)}, bf16[208,128]{1,0:T(8,128)(2,1)}, u32[]{:S(2)}, u32[]{:S(2)}) collective-permute-start(bf16[208,128]{1,0:T(8,128)(2,1)} %get-tuple-element.329), channel_id=1, source_target_pairs={{0,3},{1,2},{2,1},{3,0},{4,7},{5,6},{6,5},{7,4},{8,11},{9,10},{10,... | collective-permute-start | bytes 159752 | tf_op jit(solution)/shard_map/ppermute | solution.py:69
  622.6 7.8 %collective-permute-start.16 = (bf16[208,128]{1,0:T(8,128)(2,1)}, bf16[208,128]{1,0:T(8,128)(2,1)}, u32[]{:S(2)}, u32[]{:S(2)}) collective-permute-start(bf16[208,128]{1,0:T(8,128)(2,1)} %get-tuple-element.328), channel_id=1, source_target_pairs={{0,2},{1,3},{2,0},{3,1},{4,6},{5,7},{6,4},{7,5},{8,10},{9,11},{10,... | collective-permute-start | bytes 159752 | tf_op jit(solution)/shard_map/ppermute | solution.py:69
  622.6 7.8 %collective-permute-start.15 = (bf16[208,128]{1,0:T(8,128)(2,1)}, bf16[208,128]{1,0:T(8,128)(2,1)}, u32[]{:S(2)}, u32[]{:S(2)}) collective-permute-start(bf16[208,128]{1,0:T(8,128)(2,1)} %get-tuple-element.327), channel_id=1, source_target_pairs={{0,1},{1,0},{2,3},{3,2},{4,5},{5,4},{6,7},{7,6},{8,9},{9,8},{10,11... | collective-permute-start | bytes 159752 | tf_op jit(solution)/shard_map/ppermute | solution.py:69
  (55 other events, 359.9 us)
Sparse Core Ops, SparseCore 0:
  24.3 66.3 all-gather.5
  110.0 138.4 all-gather.3
  354.5 165.7 reduce-scatter.2
  524.8 92.0 reduce-scatter.4

commit v8 on v7

--- a/solution.py
+++ b/solution.py
@@ -1724,7 +1724,7 @@
 
 def last_update(fixes, sums, tiles, turned, bases, tile_one, tile_two, little):
     count = tiles.shape[0]
-    each = 4 if count % 4 == 0 else 2
+    each = 6 if count % 6 == 0 else 2
     tile_spec = pl.BlockSpec((each, BLK, BLK), lambda i: (i, 0, 0))
     base_spec = pl.BlockSpec((each, 2, BLK, BLK), lambda i: (i, 0, 0, 0))
     whole = [

time: 684 us -> 685 us (level)
  no operation moved by 1% of the time
where the time goes in v8:
time: 685 us; the launch traced here: 675 us
  Pallas kernels  537 us (78%)
  other arithmetic  32.3 us (5%)
  starting transfers between devices  32 us (5%)
  local copies, waits for them, and re-layouts  21.1 us (3%)
  waiting for transfers between devices  20.6 us (3%)
  matrix products  16.5 us (2%)
  between operations  15.9 us (2%)
    pallas_call x3, Pallas kernels, forward_rows(): pl.pallas_call(functools.partial(forward_kernel, groups, shards, chunks,...  156 us
    pallas_call x16, Pallas kernels, call(): pl.pallas_call(kernel, out_shape=out_shape, in_specs=specs, out_specs=jax...  131 us
    pallas_call x1, Pallas kernels, finish_rows(): pl.pallas_call(functools.partial(finish_kernel, groups, shards, chunks, o...  74.1 us
    pallas_call x2, Pallas kernels, backward_rows(): pl.pallas_call(functools.partial(backward_kernel, groups, shards, chunks,...  72.4 us
    pallas_call x1, Pallas kernels, vocab_logits(): pl.pallas_call(functools.partial(logits_kernel, vrows), grid=(steps,), ou...  24.9 us
    ppermute x12, starting transfers between devices, hop(): return lax.ppermute(x, 'dp', pairs)  23.1 us
    pallas_call x1, Pallas kernels, vocab_table_grad(): pl.pallas_call(table_kernel, grid=(padded // PAIRS,), out_shape=sds((padd...  20.7 us
    pallas_call x1, Pallas kernels, vocab_rows(): pl.pallas_call(functools.partial(rows_kernel, shards, own), grid=(padded...  20.1 us
  transfers between devices with their start and end apart: 22, of which 5 were waited for; matrix products, arithmetic and copies ran while one was open for 6% of the time, Pallas kernels for 67%

profile of v8, /device:TPU:0, one launch (start us, length us, event | category | flops | bytes accessed | tf_op | source)
XLA Modules:
  0.0 675.5 jit_solution(2553206328079020494)
XLA Ops:
  10.5 12.7 %open.1 = (s32[8,8,256]{2,1,0:T(8,128)S(1)}, bf16[4,192,128]{2,1,0:T(8,128)(2,1)S(1)}, bf16[8,4,16,128]{3,2,1,0:T(8,128)(2,1)S(1)}) custom-call(s32[8,256]{1,0:T(8,128)S(1)} %pad.47.ids, bf16[192,128]{1,0:T(8,128)(2,1)S(1)} %reshape.346.piece, bf16[16,128]{1,0:T(8,128)(2,1)S(1)} %pad_bitcast_fusion.share), custom_call_target="tpu_custom_call" | custom-call | tf_op jit(solution)/shard_map/open/pallas_call | solution.py:998
  28.2 11.2 %look.1 = (bf16[512,256]{1,0:T(8,128)(2,1)}, bf16[512,256]{1,0:T(8,128)(2,1)}, bf16[512,256]{1,0:T(8,128)(2,1)}, bf16[512,256]{1,0:T(8,128)(2,1)}, bf16[512,256]...) custom-call(s32[2]{0:T(128)} %pad_add_fusion.1.scal, ...), custom_call_target="tpu_custom_call" | custom-call | bytes 31457280 | tf_op jit(solution)/shard_map/look/pallas_call | solution.py:138
  40.0 70.0 %enter.1 = (f32[128,1024]{1,0:T(8,128)}, bf16[528,1024]{1,0:T(8,128)(2,1)}) custom-call(bf16[512,256]{1,0:T(8,128)(2,1)} %get-tuple-element.172.refs_0_, bf16[512,256]{1,0:T(8,128)(2,1)} %get-tuple-element.173.refs_1_, bf16[512,256]{1,0:T(8,128)(2,1)} %get-tuple-element.174.refs_2_, bf16[512,256]{1,0:T(8,128)(2,1)} %get-tuple-element.175.refs_3_, ...), custom_call_target="tpu_custom_call" | custom-call | tf_op jit(solution)/shard_map/enter/pallas_call | solution.py:665
  114.9 7.4 %placetiles.2 = (bf16[1024,1024]{1,0:T(8,128)(2,1)}, bf16[512,1024]{1,0:T(8,128)(2,1)}) custom-call(s32[1,192]{1,0:T(1,128)} %slot.5, bf16[8,3840,128]{2,1,0:T(8,128)(2,1)} %bitcast.166), custom_call_target="tpu_custom_call" | custom-call | bytes 14680064 | tf_op jit(solution)/shard_map/placetiles/pallas_call | solution.py:138
  124.7 8.2 %front.2 = (f32[512,512]{1,0:T(8,128)}, f32[528,512]{1,0:T(8,128)}, f32[528,384]{1,0:T(8,128)}, f32[512,512]{1,0:T(8,128)}, bf16[144,512]{1,0:T(8,128)(2,1)}, /*...) custom-call(bf16[528,1024]{1,0:T(8,128)(2,1)} %get-tuple-element.185.normed.rest_19_, ...), custom_call_target="tpu_custom_call" | custom-call | flops 2147483648 | bytes 12582912 | tf_op jit(solution)/shard_map/front/pallas_call | solution.py:138
  153.9 44.1 %forward.2 = (f32[128,1024]{1,0:T(8,128)}, f32[128,1024]{1,0:T(8,128)}, f32[128,1]{1,0:T(8,128)}, bf16[528,1024]{1,0:T(8,128)(2,1)}) custom-call(bf16[128,1152]{1,0:T(8,128)(2,1)} %get-tuple-element.195.refs_0_, bf16[128,1152]{1,0:T(8,128)(2,1)} %get-tuple-element.196.refs_1_, bf16[128,1152]{1,0:T(8,128)(2,1)} %get-tuple-element.197.refs_2_, ...), custom_call_target="tpu_custom_call" | custom-call | tf_op jit(solution)/shard_map/forward/pallas_call | solution.py:665
  197.9 8.0 %front.3 = (f32[512,512]{1,0:T(8,128)}, f32[528,512]{1,0:T(8,128)}, f32[528,384]{1,0:T(8,128)}, f32[512,512]{1,0:T(8,128)}, bf16[144,512]{1,0:T(8,128)(2,1)}, /*...) custom-call(bf16[528,1024]{1,0:T(8,128)(2,1)} %get-tuple-element.200.normed.rest_19_, ...), custom_call_target="tpu_custom_call" | custom-call | flops 2147483648 | bytes 12582912 | tf_op jit(solution)/shard_map/front/pallas_call | solution.py:138
  207.3 8.1 %collective-permute-start.4 = (bf16[144,512]{1,0:T(8,128)(2,1)}, bf16[144,512]{1,0:T(8,128)(2,1)S(1)}, u32[]{:S(2)}, u32[]{:S(2)}) collective-permute-start(bf16[144,512]{1,0:T(8,128)(2,1)} %get-tuple-element.204), channel_id=1, source_target_pairs={{0,8},{4,12},{16,24},{20,28},{1,9},{5,13},{17,25},{21,29},{2,10},{... | collective-permute-start | bytes 442376 | tf_op jit(solution)/shard_map/ppermute | solution.py:1888
  233.7 41.9 %forward.3 = (f32[128,1024]{1,0:T(8,128)}, f32[128,1024]{1,0:T(8,128)}, f32[128,1]{1,0:T(8,128)}, bf16[528,1024]{1,0:T(8,128)(2,1)}) custom-call(bf16[128,1152]{1,0:T(8,128)(2,1)} %get-tuple-element.210.refs_0_, bf16[128,1152]{1,0:T(8,128)(2,1)} %get-tuple-element.211.refs_1_, bf16[128,1152]{1,0:T(8,128)(2,1)} %get-tuple-element.212.refs_2_, ...), custom_call_target="tpu_custom_call" | custom-call | tf_op jit(solution)/shard_map/forward/pallas_call | solution.py:665
  275.6 24.9 %logits.1 = (bf16[2,6400,512]{2,1,0:T(8,128)(2,1)}, f32[5,64,512]{2,1,0:T(8,128)}, f32[8,512]{1,0:T(8,128)}) custom-call(s32[1,512]{1,0:T(1,128)} %bitcast.202, bf16[6400,2048]{1,0:T(8,128)(2,1)} %all-gather.4.cloned.1.call-done.table, bf16[528,1024]{1,0:T(8,128)(2,1)} %get-tuple-element.215.normed), custom_call_target="tpu_custom_call" | custom-call | flops 13421772800 | bytes 41943040 | tf_op jit(solution)/shard_map/logits/pallas_call | solution.py:1526
  309.3 20.1 %rowgrads.1 = (bf16[128,1024]{1,0:T(8,128)(2,1)}, bf16[128,1024]{1,0:T(8,128)(2,1)}, bf16[128,1024]{1,0:T(8,128)(2,1)}, bf16[128,1024]{1,0:T(8,128)(2,1)}) custom-call(s32[1]{0:T(128)} %bitcast.4.scal, s32[1,512]{1,0:T(1,128)} %bitcast.203, f32[5,64,512]{2,1,0:T(8,128)} %copy-done.20, f32[1,512]{1,0:T(1,128)} %copy-done.12, ...), custom_call_target="tpu_custom_call" | custom-call | flops 13421772800 | bytes 41943040 | tf_op jit(solution)/shard_map/rowgrads/pallas_call | solution.py:1603
  333.8 20.7 %tablegrads.1 = bf16[6400,2048]{1,0:T(8,128)(2,1)} custom-call(s32[1,512]{1,0:T(1,128)} %bitcast.204, f32[5,64,512]{2,1,0:T(8,128)} %copy-done.20, f32[1,512]{1,0:T(1,128)} %copy-done.12, bf16[2,6400,512]{2,1,0:T(8,128)(2,1)} %get-tuple-element.220.p_in, bf16[528,1024]{1,0:T(8,128)(2,1)} %get-tuple-element.215.normed), custom_call_target="tpu_custom_call" | custom-call | flops 13421772800 | bytes 41943040 | tf_op jit(solution)/shard_map/tablegrads/pallas_call | solution.py:1636
  355.4 25.0 %backward.2 = (f32[128,1024]{1,0:T(8,128)}, bf16[512,1152]{1,0:T(8,128)(2,1)}, f32[1,1024]{1,0:T(1,128)}) custom-call(bf16[128,1024]{1,0:T(8,128)(2,1)} %get-tuple-element.225.refs_0_, bf16[128,1024]{1,0:T(8,128)(2,1)} %copy-done.26, bf16[128,1024]{1,0:T(8,128)(2,1)} %copy-done.27, bf16[128,1024]{1,0:T(8,128)(2,1)} %copy-done.28, ...), custom_call_target="tpu_custom_call" | custom-call | tf_op jit(solution)/shard_map/backward/pallas_call | solution.py:765
  393.7 7.3 %within.2 = (f32[512,512]{1,0:T(8,128)}, bf16[512,256]{1,0:T(8,128)(2,1)}, f32[512,128]{1,0:T(8,128)}, f32[2,128,512]{2,1,0:T(8,128)}, f32[512,512]{1,0:T(8,128)}, /*index=5*/f32[512,256]{1,0:T(8,128)}) custom-call(f32[128,512]{1,0:T(8,128)} %get-tuple-element.235.s_in, f32[528,512]{1,0:T(8,128)} %get-tuple-element.236.xr.rest_9_, ...), custom_call_target="tpu_custom_call" | custom-call | flops 2147483648 | bytes 16777216 | tf_op jit(solution)/shard_map/within/pallas_call | solution.py:138
  401.8 13.8 %back.2 = (bf16[528,1024]{1,0:T(8,128)(2,1)}, bf16[528,384]{1,0:T(8,128)(2,1)}, f32[8,512]{1,0:T(8,128)}, f32[8,256]{1,0:T(8,128)}, f32[8,128]{1,0:T(8,128)}, /*...) custom-call(s32[1]{0:T(128)} %bitcast.4.scal, ...), custom_call_target="tpu_custom_call" | custom-call | flops 2147483648 | bytes 16777216 | tf_op jit(solution)/shard_map/back/pallas_call | solution.py:138
  415.7 47.5 %backward.3 = (f32[128,1024]{1,0:T(8,128)}, bf16[512,1152]{1,0:T(8,128)(2,1)}) custom-call(bf16[128,1024]{1,0:T(8,128)(2,1)} %get-tuple-element.246.refs_0_, bf16[128,1024]{1,0:T(8,128)(2,1)} %get-tuple-element.247.refs_1_, bf16[128,1024]{1,0:T(8,128)(2,1)} %get-tuple-element.248.refs_2_, bf16[128,1024]{1,0:T(8,128)(2,1)} %get-tuple-element.249.refs_3_, ...), custom_call_target="tpu_custom_call" | custom-call | tf_op jit(solution)/shard_map/backward/pallas_call | solution.py:765
  472.2 7.4 %within.3 = (f32[512,512]{1,0:T(8,128)}, bf16[512,256]{1,0:T(8,128)(2,1)}, f32[512,128]{1,0:T(8,128)}, f32[2,128,512]{2,1,0:T(8,128)}, f32[512,512]{1,0:T(8,128)}, /*index=5*/f32[512,256]{1,0:T(8,128)}) custom-call(f32[128,512]{1,0:T(8,128)} %get-tuple-element.257.s_in, f32[528,512]{1,0:T(8,128)} %get-tuple-element.258.xr.rest_9_, ...), custom_call_target="tpu_custom_call" | custom-call | flops 2147483648 | bytes 16777216 | tf_op jit(solution)/shard_map/within/pallas_call | solution.py:138
  489.9 14.1 %back.3 = (bf16[528,1024]{1,0:T(8,128)(2,1)}, bf16[528,384]{1,0:T(8,128)(2,1)}, f32[8,512]{1,0:T(8,128)}, f32[8,256]{1,0:T(8,128)}, f32[8,128]{1,0:T(8,128)}, /*...) custom-call(s32[1]{0:T(128)} %bitcast.4.scal, ...), custom_call_target="tpu_custom_call" | custom-call | flops 2147483648 | bytes 16777216 | tf_op jit(solution)/shard_map/back/pallas_call | solution.py:138
  515.8 9.4 %packtiles.1 = bf16[8,3968,128]{2,1,0:T(8,128)(2,1)} custom-call(s32[1]{0:T(128)} %bitcast.4.scal, s32[1,192]{1,0:T(1,128)} %slot.5, bf16[1024,1024]{1,0:T(8,128)(2,1)} %convolution_convert_fusion.3.refs_0_, bf16[512,1152]{1,0:T(8,128)(2,1)} %convolution_convert_fusion.1.refs_1_, bf16[1024,1024]{1,0:T(8,128)(2,1)} %convolution_convert_fusion.2.refs_2_, ...), custom_call_target="tpu_custom_call" | custom-call | bytes 14680064 | tf_op jit(solution)/shard_map/packtiles/pallas_call | solution.py:138
  526.1 74.1 %finish.1.parts = bf16[8,512,256]{2,1,0:T(8,128)(2,1)} custom-call(bf16[128,1024]{1,0:T(8,128)(2,1)} %get-tuple-element.293.refs_0_, bf16[128,1024]{1,0:T(8,128)(2,1)} %get-tuple-element.294.refs_1_, bf16[128,1024]{1,0:T(8,128)(2,1)} %get-tuple-element.295.refs_2_, bf16[128,1024]{1,0:T(8,128)(2,1)} %get-tuple-element.296.refs_3_, ...), custom_call_target="tpu_custom_call" | custom-call | tf_op jit(solution)/shard_map/finish/pallas_call | solution.py:947
  600.2 11.0 %addrows.1 = (bf16[6286,256]{1,0:T(8,128)(2,1)}, f32[1,256]{1,0:T(1,128)}) custom-call(s32[2]{0:T(128)} %pad_add_fusion.1.scal, s32[4104]{0:T(1024)} %concatenate.41.code, s32[4096]{0:T(1024)} %select_bitcast_fusion.listed, s32[32]{0:T(128)} %copy-done.41, bf16[6400,256]{1,0:T(8,128)(2,1)} %reduce-scatter.3.cloned.1.call-done.share, ...), custom_call_target="tpu_custom_call" | custom-call | bytes 31457280 | tf_op jit(solution)/shard_map/addrows/pallas_call | solution.py:138
  632.9 9.9 %sumall.1.sums = f32[8,128]{1,0:T(8,128)S(1)} custom-call(f32[8,128]{1,0:T(8,128)S(1)} %get-tuple-element.218.refs_0_, f32[12,512]{1,0:T(8,128)S(1)} %reshape.364.refs_1_, f32[6,8]{1,0:T(8,128)S(1)} %reshape_squeeze.3.refs_2_, f32[1,256]{1,0:T(1,128)S(1)} %copy-done.18, f32[1,128]{1,0:T(1,128)S(1)} %copy-done.19, f32[64,288]{1,0:T(8,128)S(1)} %bitcast.146, ...), custom_call_target="tpu_custom_call" | custom-call | tf_op jit(solution)/shard_map/sumall/pallas_call | solution.py:1076
  644.0 15.0 %multiply_subtract_fusion = (f32[6286,256]{1,0:T(8,128)}, f32[6286,256]{1,0:T(8,128)}, f32[6286,256]{1,0:T(8,128)}) fusion(f32[6286,256]{1,0:T(8,128)} %table.1, f32[]{:T(128)} %bitcast.42, f32[]{:T(128)} %bitcast.41, f32[]{:T(128)} %bitcast.40, bf16[6286,256]{1,0:T(8,128)(2,1)S(1)} %copy-done.21, f32[6286,256]{1,0:T(8,128)} %param.33, f32[6286,256]{1,0:T(8,128)} %param.32), kind=kLoop, calls=%fused_computation.2 | loop fusion | flops 27356672 | bytes 41839628 | tf_op jit(solution)/shard_map/sub | solution.py:1658
  659.2 9.6 %update.1 = (f32[24,128,128]{2,1,0:T(8,128)}, bf16[24,128,128]{2,1,0:T(8,128)(2,1)}, f32[24,128,128]{2,1,0:T(8,128)}, f32[24,128,128]{2,1,0:T(8,128)}, f32[64,28...) custom-call(f32[2]{0:T(128)S(1)} %pad_maximum_fusion.3.fixes, ...), custom_call_target="tpu_custom_call" | custom-call | flops 1207959552 | bytes 16777216 | tf_op jit(solution)/shard_map/update/pallas_call | solution.py:1733
  (290 shorter events, 138.4 us)
Async XLA Ops:
  7.2 105.8 %all-gather.6.cloned.1.call-start = ((), (), s32[]{:S(2)}) async-start(), calls=%async_computation.5 | async-start | bytes 8847360 | tf_op jit(solution)/shard_map/all_gather | solution.py:1838
  24.2 251.4 %all-gather.4.cloned.1.call-start = ((), (), s32[]{:S(2)}) async-start(), calls=%async_computation.2 | async-start | bytes 29491200 | tf_op jit(solution)/shard_map/all_gather | solution.py:1860
  110.1 415.2 %reduce-scatter.3.cloned.1.call-start = ((), (), s32[]{:S(2)}) async-start(), calls=%async_computation.3 | async-start | bytes 29491200 | tf_op jit(solution)/shard_map/reduce_scatter | solution.py:1933
  132.8 13.9 %collective-permute-start = (bf16[144,512]{1,0:T(8,128)(2,1)}, bf16[144,512]{1,0:T(8,128)(2,1)S(1)}, u32[]{:S(2)}, u32[]{:S(2)}) collective-permute-start(bf16[144,512]{1,0:T(8,128)(2,1)} %get-tuple-element.189), channel_id=1, source_target_pairs={{0,4},{4,8},{8,12},{16,20},{20,24},{24,28},{1,5},{5,9},{9,13},{17,... | collective-permute-start | bytes 442376 | tf_op jit(solution)/shard_map/ppermute | solution.py:1888
  134.1 12.6 %collective-permute-start.1 = (bf16[144,512]{1,0:T(8,128)(2,1)}, bf16[144,512]{1,0:T(8,128)(2,1)S(1)}, u32[]{:S(2)}, u32[]{:S(2)}) collective-permute-start(bf16[144,512]{1,0:T(8,128)(2,1)} %get-tuple-element.189), channel_id=1, source_target_pairs={{0,8},{4,12},{16,24},{20,28},{1,9},{5,13},{17,25},{21,29},{2,10},{... | collective-permute-start | bytes 442376 | tf_op jit(solution)/shard_map/ppermute | solution.py:1888
  135.4 13.2 %collective-permute-start.2 = (bf16[144,512]{1,0:T(8,128)(2,1)}, bf16[144,512]{1,0:T(8,128)(2,1)S(1)}, u32[]{:S(2)}, u32[]{:S(2)}) collective-permute-start(bf16[144,512]{1,0:T(8,128)(2,1)} %get-tuple-element.189), channel_id=1, source_target_pairs={{0,12},{16,28},{1,13},{17,29},{2,14},{18,30},{3,15},{19,31}} | collective-permute-start | bytes 442376 | tf_op jit(solution)/shard_map/ppermute | solution.py:1888
  206.0 12.7 %collective-permute-start.3 = (bf16[144,512]{1,0:T(8,128)(2,1)}, bf16[144,512]{1,0:T(8,128)(2,1)S(1)}, u32[]{:S(2)}, u32[]{:S(2)}) collective-permute-start(bf16[144,512]{1,0:T(8,128)(2,1)} %get-tuple-element.204), channel_id=1, source_target_pairs={{0,4},{4,8},{8,12},{16,20},{20,24},{24,28},{1,5},{5,9},{9,13},{17,... | collective-permute-start | bytes 442376 | tf_op jit(solution)/shard_map/ppermute | solution.py:1888
  207.3 15.7 %collective-permute-start.4 = (bf16[144,512]{1,0:T(8,128)(2,1)}, bf16[144,512]{1,0:T(8,128)(2,1)S(1)}, u32[]{:S(2)}, u32[]{:S(2)}) collective-permute-start(bf16[144,512]{1,0:T(8,128)(2,1)} %get-tuple-element.204), channel_id=1, source_target_pairs={{0,8},{4,12},{16,24},{20,28},{1,9},{5,13},{17,25},{21,29},{2,10},{... | collective-permute-start | bytes 442376 | tf_op jit(solution)/shard_map/ppermute | solution.py:1888
  215.3 13.1 %collective-permute-start.5 = (bf16[144,512]{1,0:T(8,128)(2,1)}, bf16[144,512]{1,0:T(8,128)(2,1)S(1)}, u32[]{:S(2)}, u32[]{:S(2)}) collective-permute-start(bf16[144,512]{1,0:T(8,128)(2,1)} %get-tuple-element.204), channel_id=1, source_target_pairs={{0,12},{16,28},{1,13},{17,29},{2,14},{18,30},{3,15},{19,31}} | collective-permute-start | bytes 442376 | tf_op jit(solution)/shard_map/ppermute | solution.py:1888
  218.0 82.5 %copy-start.12 = (f32[1,512]{1,0:T(1,128)}, f32[1,512]{1,0:T(1,128)S(1)}, u32[]{:S(2)}) copy-start(f32[1,512]{1,0:T(1,128)S(1)} %compare_select_fusion.2.weight) | copy-start | bytes 6148
  329.4 25.1 %collective-permute-start.6 = (bf16[128,1024]{1,0:T(8,128)(2,1)}, bf16[128,1024]{1,0:T(8,128)(2,1)S(1)}, u32[]{:S(2)}, u32[]{:S(2)}) collective-permute-start(bf16[128,1024]{1,0:T(8,128)(2,1)} %get-tuple-element.222), channel_id=1, source_target_pairs={{0,1},{1,0},{2,3},{3,2},{4,5},{5,4},{6,7},{7,6},{8,9},{9,8},{10,11... | collective-permute-start | bytes 786440 | tf_op jit(solution)/shard_map/ppermute | solution.py:69
  329.8 24.7 %collective-permute-start.7 = (bf16[128,1024]{1,0:T(8,128)(2,1)}, bf16[128,1024]{1,0:T(8,128)(2,1)S(1)}, u32[]{:S(2)}, u32[]{:S(2)}) collective-permute-start(bf16[128,1024]{1,0:T(8,128)(2,1)} %get-tuple-element.223), channel_id=1, source_target_pairs={{0,2},{1,3},{2,0},{3,1},{4,6},{5,7},{6,4},{7,5},{8,10},{9,11},{10,... | collective-permute-start | bytes 786440 | tf_op jit(solution)/shard_map/ppermute | solution.py:69
  332.1 22.4 %collective-permute-start.8 = (bf16[128,1024]{1,0:T(8,128)(2,1)}, bf16[128,1024]{1,0:T(8,128)(2,1)S(1)}, u32[]{:S(2)}, u32[]{:S(2)}) collective-permute-start(bf16[128,1024]{1,0:T(8,128)(2,1)} %get-tuple-element.224), channel_id=1, source_target_pairs={{0,3},{1,2},{2,1},{3,0},{4,7},{5,6},{6,5},{7,4},{8,11},{9,10},{10,... | collective-permute-start | bytes 786440 | tf_op jit(solution)/shard_map/ppermute | solution.py:69
  355.4 262.4 %reduce-scatter.5.cloned.1.call-start = ((), (), s32[]{:S(2)}) async-start(), calls=%async_computation.4 | async-start | bytes 9142272 | tf_op jit(solution)/shard_map/reduce_scatter | solution.py:2012
  386.5 14.5 %collective-permute-start.9 = (bf16[144,512]{1,0:T(8,128)(2,1)}, bf16[144,512]{1,0:T(8,128)(2,1)S(1)}, u32[]{:S(2)}, u32[]{:S(2)}) collective-permute-start(bf16[144,512]{1,0:T(8,128)(2,1)} %get-tuple-element.234), channel_id=1, source_target_pairs={{4,0},{8,4},{12,8},{20,16},{24,20},{28,24},{5,1},{9,5},{13,9},{21,... | collective-permute-start | bytes 442376 | tf_op jit(solution)/shard_map/ppermute | solution.py:1888
  387.8 13.3 %collective-permute-start.10 = (bf16[144,512]{1,0:T(8,128)(2,1)}, bf16[144,512]{1,0:T(8,128)(2,1)S(1)}, u32[]{:S(2)}, u32[]{:S(2)}) collective-permute-start(bf16[144,512]{1,0:T(8,128)(2,1)} %get-tuple-element.234), channel_id=1, source_target_pairs={{8,0},{12,4},{24,16},{28,20},{9,1},{13,5},{25,17},{29,21},{10,2},{... | collective-permute-start | bytes 442376 | tf_op jit(solution)/shard_map/ppermute | solution.py:1888
  389.1 12.0 %collective-permute-start.11 = (bf16[144,512]{1,0:T(8,128)(2,1)}, bf16[144,512]{1,0:T(8,128)(2,1)S(1)}, u32[]{:S(2)}, u32[]{:S(2)}) collective-permute-start(bf16[144,512]{1,0:T(8,128)(2,1)} %get-tuple-element.234), channel_id=1, source_target_pairs={{12,0},{28,16},{13,1},{29,17},{14,2},{30,18},{15,3},{31,19}} | collective-permute-start | bytes 442376 | tf_op jit(solution)/shard_map/ppermute | solution.py:1888
  468.2 18.7 %collective-permute-start.12 = (bf16[144,512]{1,0:T(8,128)(2,1)}, bf16[144,512]{1,0:T(8,128)(2,1)S(1)}, u32[]{:S(2)}, u32[]{:S(2)}) collective-permute-start(bf16[144,512]{1,0:T(8,128)(2,1)} %get-tuple-element.256), channel_id=1, source_target_pairs={{4,0},{8,4},{12,8},{20,16},{24,20},{28,24},{5,1},{9,5},{13,9},{21,... | collective-permute-start | bytes 442376 | tf_op jit(solution)/shard_map/ppermute | solution.py:1888
  469.5 17.4 %collective-permute-start.13 = (bf16[144,512]{1,0:T(8,128)(2,1)}, bf16[144,512]{1,0:T(8,128)(2,1)S(1)}, u32[]{:S(2)}, u32[]{:S(2)}) collective-permute-start(bf16[144,512]{1,0:T(8,128)(2,1)} %get-tuple-element.256), channel_id=1, source_target_pairs={{8,0},{12,4},{24,16},{28,20},{9,1},{13,5},{25,17},{29,21},{10,2},{... | collective-permute-start | bytes 442376 | tf_op jit(solution)/shard_map/ppermute | solution.py:1888
  470.8 18.4 %collective-permute-start.14 = (bf16[144,512]{1,0:T(8,128)(2,1)}, bf16[144,512]{1,0:T(8,128)(2,1)S(1)}, u32[]{:S(2)}, u32[]{:S(2)}) collective-permute-start(bf16[144,512]{1,0:T(8,128)(2,1)} %get-tuple-element.256), channel_id=1, source_target_pairs={{12,0},{28,16},{13,1},{29,17},{14,2},{30,18},{15,3},{31,19}} | collective-permute-start | bytes 442376 | tf_op jit(solution)/shard_map/ppermute | solution.py:1888
  489.9 19.7 %copy-start.24 = (bf16[528,1024]{1,0:T(8,128)(2,1)S(1)}, bf16[528,1024]{1,0:T(8,128)(2,1)}, u32[]{:S(2)}) copy-start(bf16[528,1024]{1,0:T(8,128)(2,1)} %get-tuple-element.185.normed.rest_19_) | copy-start | bytes 3244036
  620.1 11.1 %collective-permute-start.17 = (bf16[208,128]{1,0:T(8,128)(2,1)}, bf16[208,128]{1,0:T(8,128)(2,1)}, u32[]{:S(2)}, u32[]{:S(2)}) collective-permute-start(bf16[208,128]{1,0:T(8,128)(2,1)} %get-tuple-element.329), channel_id=1, source_target_pairs={{0,3},{1,2},{2,1},{3,0},{4,7},{5,6},{6,5},{7,4},{8,11},{9,10},{10,... | collective-permute-start | bytes 159752 | tf_op jit(solution)/shard_map/ppermute | solution.py:69
  623.4 7.8 %collective-permute-start.16 = (bf16[208,128]{1,0:T(8,128)(2,1)}, bf16[208,128]{1,0:T(8,128)(2,1)}, u32[]{:S(2)}, u32[]{:S(2)}) collective-permute-start(bf16[208,128]{1,0:T(8,128)(2,1)} %get-tuple-element.328), channel_id=1, source_target_pairs={{0,2},{1,3},{2,0},{3,1},{4,6},{5,7},{6,4},{7,5},{8,10},{9,11},{10,... | collective-permute-start | bytes 159752 | tf_op jit(solution)/shard_map/ppermute | solution.py:69
  623.4 7.8 %collective-permute-start.15 = (bf16[208,128]{1,0:T(8,128)(2,1)}, bf16[208,128]{1,0:T(8,128)(2,1)}, u32[]{:S(2)}, u32[]{:S(2)}) collective-permute-start(bf16[208,128]{1,0:T(8,128)(2,1)} %get-tuple-element.327), channel_id=1, source_target_pairs={{0,1},{1,0},{2,3},{3,2},{4,5},{5,4},{6,7},{7,6},{8,9},{9,8},{10,11... | collective-permute-start | bytes 159752 | tf_op jit(solution)/shard_map/ppermute | solution.py:69
  (55 other events, 360.3 us)
Sparse Core Ops, SparseCore 0:
  24.3 66.3 all-gather.5
  110.2 137.8 all-gather.3
  354.7 165.8 reduce-scatter.2
  525.4 92.2 reduce-scatter.4
